TPU v7x, 32 devices: a whole 2x2x4 slice. The times are simulated.
32 devices in a mesh: expert: 8 (over z, y), dp: 4 (over x, core).
Axes of the slice: x: 2, y: 2, z: 4, core: 2. Of those that a mesh axis runs over, the one named last changes fastest.
Arguments:
- tokens: bfloat16 [1024, 4096], P(('expert', 'dp')), may hold values from -6 to 6
- out_grad: bfloat16 [1024, 4096], P(('expert', 'dp')), may hold values from -6 to 6
- gate_probs: bfloat16 [1024, 8], P(('expert', 'dp')), may hold values from 0.049804688 to 0.5
- route_ids: int32 [1024, 8], P(('expert', 'dp')), may hold values from 0 to 127, all different within a row; in each aligned block of 32 rows (0 to 31, 32 to 63, ...) at most 4 rows name the same one
- w_gate: bfloat16 [8, 1536, 4096], P('expert', 'dp'), may hold values from -0.09375 to 0.09375
- w_up: bfloat16 [8, 1536, 4096], P('expert', 'dp'), may hold values from -0.09375 to 0.09375
- w_down: bfloat16 [8, 1536, 4096], P('expert', 'dp'), may hold values from -0.15625 to 0.15625
Outputs:
- token_grad: bfloat16 [1024, 4096], P(('expert', 'dp'))
- gate_grad: float32 [1024, 8], P(('expert', 'dp'))
- grad_gate: bfloat16 [8, 1536, 4096], P('expert', 'dp')
- grad_up: bfloat16 [8, 1536, 4096], P('expert', 'dp')
- grad_down: bfloat16 [8, 1536, 4096], P('expert', 'dp')
Inputs may be any that keep to these rules, and one draw needn't show every extreme that they name: `route_ids`: the 8 ids of a token differ. In each aligned block of 32 rows (the tokens of one device) no id is named by more than 4 rows, a bound that some block reaches.
All inputs are finite; a program needn't handle non-finite values.
Results may differ from a plain program's by a relative error of at most 0.014.
Values may be sent and summed in bfloat16 or wider, within the bound.
No kernel may reach another device: no remote copies, remote signals or barrier semaphores. Data moves between devices by JAX's collectives and lax.ppermute only.
A program may use at most 128 MiB of HBM per device.

v0:
```python
import jax
import jax.numpy as jnp
from jax import lax
from jax.sharding import PartitionSpec as P

EXPERTS = 128
CAP = 4


CONTRACT_LAST = (((1,), (1,)), ((), ()))
CONTRACT_FIRST = (((0,), (0,)), ((), ()))


def route_table(route_ids, n_targets):
    per_device = EXPERTS // n_targets
    flat_ids = route_ids.reshape(-1)
    active = flat_ids % per_device == 0
    target = flat_ids // per_device
    onehot = jnp.logical_and(
        target[:, None] == jnp.arange(n_targets, dtype=jnp.int32)[None, :], active[:, None]
    ).astype(jnp.int32)
    slot_rank = jnp.sum((jnp.cumsum(onehot, axis=0) - onehot) * onehot, axis=1)
    slot_index = target * CAP + slot_rank
    placed = jnp.logical_and(
        slot_index[:, None] == jnp.arange(n_targets * CAP, dtype=jnp.int32)[None, :],
        active[:, None],
    )
    return placed.astype(jnp.float32).reshape(
        route_ids.shape[0], route_ids.shape[1], n_targets * CAP
    )


def dispatch_rows(routing, tokens, out_grad, gate_probs):
    picked = jnp.sum(routing, axis=1).astype(jnp.bfloat16)
    rows_token = lax.dot_general(
        picked, tokens, CONTRACT_FIRST, preferred_element_type=jnp.float32
    ).astype(jnp.bfloat16)
    rows_grad = lax.dot_general(
        picked, out_grad, CONTRACT_FIRST, preferred_element_type=jnp.float32
    ).astype(jnp.bfloat16)
    rows_gate = jnp.einsum(
        "tks,tk->s", routing, gate_probs.astype(jnp.float32), precision=lax.Precision.HIGHEST
    ).astype(jnp.bfloat16)
    return (rows_token, rows_grad, rows_gate)


def backward_rows(weights, portion):
    gate_weight, up_weight, down_weight = weights
    row_tokens, row_grads, row_gates = portion
    pre_gate = lax.dot_general(
        gate_weight, row_tokens, CONTRACT_LAST, preferred_element_type=jnp.float32
    )
    pre_up = lax.dot_general(
        up_weight, row_tokens, CONTRACT_LAST, preferred_element_type=jnp.float32
    )
    back_proj = lax.dot_general(
        down_weight, row_grads, CONTRACT_LAST, preferred_element_type=jnp.float32
    )
    squash = jax.nn.sigmoid(pre_gate)
    activated = pre_gate * squash
    hidden = (activated * pre_up).astype(jnp.bfloat16)
    gate_terms = jnp.sum(hidden.astype(jnp.float32) * back_proj, axis=0)
    gate_row = row_gates.astype(jnp.float32)
    out_scaled = (gate_row[:, None] * row_grads.astype(jnp.float32)).astype(jnp.bfloat16)
    hidden_grad = gate_row[None, :] * back_proj
    up_pre_grad = (hidden_grad * activated).astype(jnp.bfloat16)
    gate_pre_grad = (hidden_grad * pre_up * squash * (1.0 + pre_gate * (1.0 - squash))).astype(
        jnp.bfloat16
    )
    grad_down = jnp.dot(hidden, out_scaled, preferred_element_type=jnp.float32)
    grad_gate = jnp.dot(gate_pre_grad, row_tokens, preferred_element_type=jnp.float32)
    grad_up = jnp.dot(up_pre_grad, row_tokens, preferred_element_type=jnp.float32)
    return (grad_gate, grad_up, grad_down, gate_pre_grad, up_pre_grad, gate_terms)


def body(tokens, out_grad, gate_probs, route_ids, w_gate, w_up, w_down):
    n_targets = lax.axis_size("expert")
    token_rows, model_width = tokens.shape
    slot_count = n_targets * CAP
    weights = (w_gate[0], w_up[0], w_down[0])
    routing = route_table(route_ids, n_targets)
    outgoing = dispatch_rows(routing, tokens, out_grad, gate_probs)
    arrived = (
        lax.all_to_all(
            outgoing[0].reshape(n_targets, CAP, model_width),
            "expert",
            split_axis=0,
            concat_axis=0,
            tiled=True,
        ),
        lax.all_to_all(
            outgoing[1].reshape(n_targets, CAP, model_width),
            "expert",
            split_axis=0,
            concat_axis=0,
            tiled=True,
        ),
        lax.all_to_all(
            outgoing[2].reshape(n_targets, CAP), "expert", split_axis=0, concat_axis=0, tiled=True
        ),
    )
    own_rows = (
        arrived[0].reshape(slot_count, model_width),
        arrived[1].reshape(slot_count, model_width),
        arrived[2].reshape(slot_count),
    )
    totals = backward_rows(
        weights,
        (
            lax.all_gather(own_rows[0], "dp", axis=0, tiled=True),
            lax.all_gather(own_rows[1], "dp", axis=0, tiled=True),
            lax.all_gather(own_rows[2], "dp", axis=0, tiled=True),
        ),
    )
    grad_gate, grad_up, grad_down, gate_pre_all, up_pre_all, gate_terms_all = totals
    term = lax.dot_general(
        gate_pre_all, weights[0], CONTRACT_FIRST, preferred_element_type=jnp.float32
    )
    slot_grads = lax.psum_scatter(
        (
            term
            + lax.dot_general(
                up_pre_all, weights[1], CONTRACT_FIRST, preferred_element_type=jnp.float32
            )
        ).astype(jnp.bfloat16),
        "dp",
        scatter_dimension=0,
        tiled=True,
    ).astype(jnp.float32)
    slot_gates = lax.psum_scatter(gate_terms_all, "dp", scatter_dimension=0, tiled=True)
    returned = (
        lax.all_to_all(
            slot_grads.reshape(n_targets, CAP, model_width).astype(jnp.bfloat16),
            "expert",
            split_axis=0,
            concat_axis=0,
            tiled=True,
        ).astype(jnp.float32),
        lax.all_to_all(
            slot_gates.reshape(n_targets, CAP).astype(jnp.bfloat16),
            "expert",
            split_axis=0,
            concat_axis=0,
            tiled=True,
        ).astype(jnp.float32),
    )
    returned_rows = returned[0].reshape(slot_count, model_width)
    returned_gates = returned[1].reshape(slot_count)
    token_grad = jnp.dot(
        jnp.sum(routing, axis=1),
        returned_rows,
        precision=lax.Precision.HIGHEST,
        preferred_element_type=jnp.float32,
    )
    gate_grad = jnp.einsum("tks,s->tk", routing, returned_gates, precision=lax.Precision.HIGHEST)
    return (
        token_grad.astype(jnp.bfloat16),
        gate_grad,
        grad_gate.astype(jnp.bfloat16)[None],
        grad_up.astype(jnp.bfloat16)[None],
        grad_down.astype(jnp.bfloat16)[None],
    )


def solution(mesh):
    in_specs = (
        P(("expert", "dp"), None),
        P(("expert", "dp"), None),
        P(("expert", "dp"), None),
        P(("expert", "dp"), None),
        P("expert", "dp", None),
        P("expert", "dp", None),
        P("expert", "dp", None),
    )
    out_specs = (
        P(("expert", "dp"), None),
        P(("expert", "dp"), None),
        P("expert", "dp", None),
        P("expert", "dp", None),
        P("expert", "dp", None),
    )
    return jax.shard_map(body, mesh=mesh, in_specs=in_specs, out_specs=out_specs, check_vma=False)
```

profile of v0, /device:TPU:0, one launch (start us, length us, event | category | flops | bytes accessed | tf_op | source)
XLA Modules:
  0.0 125.1 jit_solution(4770145596119895603)
XLA Ops:
  9.7 1.9 %convolution_convert_fusion.4 = bf16[32,4096]{1,0:T(8,128)(2,1)} fusion(bf16[32,4096]{1,0:T(8,128)(2,1)} %param.7, f32[32,32]{1,0:T(8,128)S(1)} %convert_reduce_fusion), kind=kOutput, calls=%fused_computation.9 | convolution fusion | flops 8520704 | bytes 528384 | tf_op jit(solution)/shard_map/dot_general | solution.py:35
  12.6 16.1 %all_to_all.31 = bf16[8,4,4096]{2,1,0:T(4,128)(2,1)} all-to-all(bf16[8,4,4096]{2,1,0:T(4,128)(2,1)S(1)} %reshape.201), channel_id=1, replica_groups=mesh['expert'=8,'dp'=4] {'expert'}, dimensions={0} | all-to-all | bytes 524288 | tf_op jit(solution)/shard_map/all_to_all | solution.py:84
  28.7 1.7 %reshape.202 = bf16[32,4096]{1,0:T(8,128)(2,1)} reshape(bf16[8,4,4096]{2,1,0:T(4,128)(2,1)} %all_to_all.31) | data formatting | bytes 524288 | tf_op jit(solution)/shard_map/reshape | solution.py:103
  30.5 1.9 %convolution_convert_fusion.5 = bf16[32,4096]{1,0:T(8,128)(2,1)} fusion(bf16[32,4096]{1,0:T(8,128)(2,1)} %param.8, f32[32,32]{1,0:T(8,128)S(1)} %convert_reduce_fusion), kind=kOutput, calls=%fused_computation.10 | convolution fusion | flops 8520704 | bytes 528384 | tf_op jit(solution)/shard_map/dot_general | solution.py:38
  33.5 12.1 %all_to_all.32 = bf16[8,4,4096]{2,1,0:T(4,128)(2,1)} all-to-all(bf16[8,4,4096]{2,1,0:T(4,128)(2,1)S(1)} %reshape.199), channel_id=1, replica_groups=mesh['expert'=8,'dp'=4] {'expert'}, dimensions={0} | all-to-all | bytes 524288 | tf_op jit(solution)/shard_map/all_to_all | solution.py:91
  45.5 1.7 %reshape.200 = bf16[32,4096]{1,0:T(8,128)(2,1)} reshape(bf16[8,4,4096]{2,1,0:T(4,128)(2,1)} %all_to_all.32) | data formatting | bytes 524288 | tf_op jit(solution)/shard_map/reshape | solution.py:104
  48.3 3.6 %all-to-all-start = ((bf16[8,1,4]{2,1,0:T(2,128)(2,1)}), bf16[8,1,4]{2,1,0:T(2,128)(2,1)S(1)}, u32[]{:S(2)}, u32[]{:S(2)}) async-start(bf16[8,1,4]{2,1,0:T(2,128)(2,1)} %all_to_all.25), calls=%async_computation | async-start | bytes 8192 | tf_op jit(solution)/shard_map/all_to_all | solution.py:98
  53.2 5.1 %all-to-all-done = bf16[8,1,4]{2,1,0:T(2,128)(2,1)S(1)} async-done(((bf16[8,1,4]{2,1,0:T(2,128)(2,1)}), bf16[8,1,4]{2,1,0:T(2,128)(2,1)S(1)}, u32[]{:S(2)}, u32[]{:S(2)}) %all-to-all-start) | async-done | bytes 96 | tf_op jit(solution)/shard_map/all_to_all | solution.py:98
  58.6 6.1 %all-reduce = bf16[128]{0:T(256)(128)(2,1)S(1)} all-reduce(bf16[128]{0:T(256)(128)(2,1)S(1)} %dynamic-update-slice), channel_id=1, replica_groups=mesh['expert'=8,'dp'=4] {'dp'}, use_global_device_ids=true, to_apply=%add | all-reduce | flops 128 | bytes 512
  64.8 3.1 %fusion.19 = f32[384,128]{0,1:T(8,128)} fusion(bf16[128,4096]{1,0:T(8,128)(2,1)} %all-gather.5.cloned.1.call-done, bf16[1,384,4096]{2,1,0:T(8,128)(2,1)S(1)} %copy-done), kind=kOutput, calls=%fused_computation.23 | convolution fusion | flops 402653184 | bytes 4390912 | tf_op jit(solution)/shard_map/dot_general | solution.py:50
  67.9 1.8 %fusion.16 = f32[384,128]{0,1:T(8,128)} fusion(bf16[128,4096]{1,0:T(8,128)(2,1)S(1)} %copy-done.1, bf16[1,384,4096]{2,1,0:T(8,128)(2,1)S(1)} %copy-done.2), kind=kOutput, calls=%fused_computation.22 | convolution fusion | flops 402653184 | bytes 4390912 | tf_op jit(solution)/shard_map/dot_general | solution.py:53
  69.7 4.0 %multiply_reduce_fusion = (f32[128]{0:T(128)S(1)}, bf16[384,128]{0,1:T(8,128)(2,1)}, bf16[384,128]{0,1:T(8,128)(2,1)S(1)}, bf16[384,128]{0,1:T(8,128)(2,1)S(1)}) fusion(f32[384,128]{0,1:T(8,128)} %fusion.16, f32[384,128]{0,1:T(8,128)} %fusion.19, f32[128]{0:T(128)S(1)} %convert_element_type.84, bf16[128,4096]{1,0:T(8,128)(2,1)} %all-gather.3.cloned.1.call-done, ...), kind=kOutput, calls=%fused_computation.27 | convolution fusion | flops 403586944 | bytes 4883456 | tf_op jit(solution)/shard_map/dot_general | solution.py:56
  74.4 1.2 copy-done.3
  75.5 1.7 %fusion.3 = bf16[128,4096]{1,0:T(8,128)(2,1)} fusion(f32[128,4096]{1,0:T(8,128)S(1)} %fusion.4, bf16[384,128]{0,1:T(8,128)(2,1)S(1)} %get-tuple-element.8, bf16[1,384,4096]{2,1,0:T(8,128)(2,1)S(1)} %copy-done.3), kind=kOutput, calls=%fused_computation.7 | convolution fusion | flops 403701760 | bytes 6389760 | tf_op jit(solution)/shard_map/dot_general | solution.py:122
  78.7 6.2 %all-reduce.1 = bf16[128]{0:T(256)(128)(2,1)S(1)} all-reduce(f32[128]{0:T(128)S(1)} %get-tuple-element.5), channel_id=3, replica_groups=mesh['expert'=8,'dp'=4] {'dp'}, use_global_device_ids=true, to_apply=%region_6.7.clone | all-reduce | flops 128 | bytes 768
  85.6 3.3 %all-to-all-start.4 = ((bf16[8,1,4]{2,1,0:T(2,128)(2,1)}), bf16[8,1,4]{2,1,0:T(2,128)(2,1)S(1)}, u32[]{:S(2)}, u32[]{:S(2)}) async-start(bf16[8,1,4]{2,1,0:T(2,128)(2,1)} %convert_element_type.102), calls=%async_computation.5 | async-start | bytes 8192 | tf_op jit(solution)/shard_map/all_to_all | solution.py:139
  88.9 3.9 %fusion.1 = bf16[1,384,4096]{2,1,0:T(8,128)(2,1)} fusion(bf16[384,128]{0,1:T(8,128)(2,1)S(1)} %get-tuple-element.8, bf16[128,4096]{1,0:T(8,128)(2,1)} %all-gather.5.cloned.1.call-done), kind=kOutput, calls=%fused_computation.4 | convolution fusion | flops 404226048 | bytes 4292608 | tf_op jit(solution)/shard_map/dot_general | solution.py:72
  92.8 6.8 %reduce-scatter.2.cloned.1.call-done = bf16[32,4096]{1,0:T(8,128)(2,1)} async-done(((bf16[128,4096]{1,0:T(8,128)(2,1)}), bf16[32,4096]{1,0:T(8,128)(2,1)}) %reduce-scatter.2.cloned.1.call-update) | async-done | bytes 262160 | tf_op jit(solution)/shard_map/reduce_scatter | solution.py:119
  99.6 1.8 %convert_element_type.91 = bf16[8,4,4096]{2,1,0:T(4,128)(2,1)} reshape(bf16[32,4096]{1,0:T(8,128)(2,1)} %reduce-scatter.2.cloned.1.call-done) | data formatting | bytes 524288 | tf_op jit(solution)/shard_map/convert_element_type | solution.py:133
  101.4 5.5 %all-to-all-start.3 = ((bf16[8,4,4096]{2,1,0:T(4,128)(2,1)}), bf16[8,4,4096]{2,1,0:T(4,128)(2,1)S(1)}, u32[]{:S(2)}, u32[]{:S(2)}) async-start(bf16[8,4,4096]{2,1,0:T(4,128)(2,1)} %convert_element_type.91), calls=%async_computation.4 | async-start | bytes 524288 | tf_op jit(solution)/shard_map/all_to_all | solution.py:132
  106.9 4.0 %fusion = bf16[1,384,4096]{2,1,0:T(8,128)(2,1)} fusion(bf16[384,128]{0,1:T(8,128)(2,1)S(1)} %get-tuple-element.7, bf16[128,4096]{1,0:T(8,128)(2,1)} %all-gather.5.cloned.1.call-done), kind=kOutput, calls=%fused_computation.3 | convolution fusion | flops 404226048 | bytes 4292608 | tf_op jit(solution)/shard_map/dot_general | solution.py:71
  110.9 2.7 %fusion.2 = bf16[1,384,4096]{2,1,0:T(8,128)(2,1)} fusion(bf16[384,128]{0,1:T(8,128)(2,1)S(1)} %copy-done.5, bf16[128,4096]{1,0:T(8,128)(2,1)S(1)} %copy-done.4, f32[128]{0:T(128)S(1)} %convert_element_type.84), kind=kOutput, calls=%fused_computation.5 | convolution fusion | flops 405798912 | bytes 4293120 | tf_op jit(solution)/shard_map/dot_general | solution.py:70
  114.6 1.3 %all-to-all-done.3 = bf16[8,4,4096]{2,1,0:T(4,128)(2,1)S(1)} async-done(((bf16[8,4,4096]{2,1,0:T(4,128)(2,1)}), bf16[8,4,4096]{2,1,0:T(4,128)(2,1)S(1)}, u32[]{:S(2)}, u32[]{:S(2)}) %all-to-all-start.3) | async-done | bytes 262176 | tf_op jit(solution)/shard_map/all_to_all | solution.py:132
  116.6 2.0 %convolution_convert_fusion.3 = bf16[32,4096]{1,0:T(8,128)(2,1)} fusion(f32[32,32]{1,0:T(8,128)S(1)} %convert_reduce_fusion, bf16[32,4096]{1,0:T(8,128)(2,1)} %reshape.203), kind=kOutput, calls=%fused_computation.8 | convolution fusion | flops 50462720 | bytes 528384 | tf_op jit(solution)/shard_map/dot_general | solution.py:149
  (62 shorter events, 10.5 us)
Async XLA Ops:
  7.2 57.6 %copy-start = (bf16[1,384,4096]{2,1,0:T(8,128)(2,1)S(1)}, bf16[1,384,4096]{2,1,0:T(8,128)(2,1)}, u32[]{:S(2)}) copy-start(bf16[1,384,4096]{2,1,0:T(8,128)(2,1)} %param.11) | copy-start | bytes 9437188
  7.2 44.8 %copy-start.7 = (u32[32]{0:T(128)S(1)}, u32[32]{0:T(128)}, u32[]{:S(2)}) copy-start(u32[32]{0:T(128)} %constant.44) | copy-start | bytes 388
  7.2 40.2 %copy-start.8 = (bf16[32,8]{0,1:T(8,128)(2,1)S(1)}, bf16[32,8]{0,1:T(8,128)(2,1)}, u32[]{:S(2)}) copy-start(bf16[32,8]{0,1:T(8,128)(2,1)} %param.9) | copy-start | bytes 1540
  7.2 57.5 %all-gather.5.cloned.1.call-start = ((), (), s32[]{:S(2)}) async-start(), calls=%async_computation.7 | async-start | bytes 1310720 | tf_op jit(solution)/shard_map/all_gather | solution.py:110
  30.5 39.2 %all-gather.3.cloned.1.call-start = ((), (), s32[]{:S(2)}) async-start(), calls=%async_computation.6 | async-start | bytes 1310720 | tf_op jit(solution)/shard_map/all_gather | solution.py:111
  48.3 10.0 %all-to-all-start = ((bf16[8,1,4]{2,1,0:T(2,128)(2,1)}), bf16[8,1,4]{2,1,0:T(2,128)(2,1)S(1)}, u32[]{:S(2)}, u32[]{:S(2)}) async-start(bf16[8,1,4]{2,1,0:T(2,128)(2,1)} %all_to_all.25), calls=%async_computation | async-start | bytes 8192 | tf_op jit(solution)/shard_map/all_to_all | solution.py:98
  51.9 47.7 %reduce-scatter.2.cloned.1.call-start = ((), (), s32[]{:S(2)}) async-start(), calls=%async_computation.8 | async-start | bytes 1310720 | tf_op jit(solution)/shard_map/reduce_scatter | solution.py:119
  64.8 3.1 %copy-start.1 = (bf16[128,4096]{1,0:T(8,128)(2,1)S(1)}, bf16[128,4096]{1,0:T(8,128)(2,1)}, u32[]{:S(2)}) copy-start(bf16[128,4096]{1,0:T(8,128)(2,1)} %all-gather.5.cloned.1.call-done) | copy-start | bytes 3145732
  64.8 3.1 %copy-start.2 = (bf16[1,384,4096]{2,1,0:T(8,128)(2,1)S(1)}, bf16[1,384,4096]{2,1,0:T(8,128)(2,1)}, u32[]{:S(2)}) copy-start(bf16[1,384,4096]{2,1,0:T(8,128)(2,1)} %param.12) | copy-start | bytes 9437188
  73.6 1.9 %copy-start.3 = (bf16[1,384,4096]{2,1,0:T(8,128)(2,1)S(1)}, bf16[1,384,4096]{2,1,0:T(8,128)(2,1)}, u32[]{:S(2)}) copy-start(bf16[1,384,4096]{2,1,0:T(8,128)(2,1)} %param.12) | copy-start | bytes 9437188
  85.6 15.8 %all-to-all-start.4 = ((bf16[8,1,4]{2,1,0:T(2,128)(2,1)}), bf16[8,1,4]{2,1,0:T(2,128)(2,1)S(1)}, u32[]{:S(2)}, u32[]{:S(2)}) async-start(bf16[8,1,4]{2,1,0:T(2,128)(2,1)} %convert_element_type.102), calls=%async_computation.5 | async-start | bytes 8192 | tf_op jit(solution)/shard_map/all_to_all | solution.py:139
  101.4 14.5 %all-to-all-start.3 = ((bf16[8,4,4096]{2,1,0:T(4,128)(2,1)}), bf16[8,4,4096]{2,1,0:T(4,128)(2,1)S(1)}, u32[]{:S(2)}, u32[]{:S(2)}) async-start(bf16[8,4,4096]{2,1,0:T(4,128)(2,1)} %convert_element_type.91), calls=%async_computation.4 | async-start | bytes 524288 | tf_op jit(solution)/shard_map/all_to_all | solution.py:132
  106.9 4.0 %copy-start.4 = (bf16[128,4096]{1,0:T(8,128)(2,1)S(1)}, bf16[128,4096]{1,0:T(8,128)(2,1)}, u32[]{:S(2)}) copy-start(bf16[128,4096]{1,0:T(8,128)(2,1)} %all-gather.3.cloned.1.call-done) | copy-start | bytes 3145732
  106.9 4.0 %copy-start.5 = (bf16[384,128]{0,1:T(8,128)(2,1)S(1)}, bf16[384,128]{0,1:T(8,128)(2,1)}, u32[]{:S(2)}) copy-start(bf16[384,128]{0,1:T(8,128)(2,1)} %get-tuple-element.6) | copy-start | bytes 294916
  110.9 2.8 %copy-start.6 = (pred[32,8,32]{2,1,0:T(8,128)(4,1)S(1)}, pred[32,8,32]{2,1,0:T(8,128)(4,1)}, u32[]{:S(2)}) copy-start(pred[32,8,32]{2,1,0:T(8,128)(4,1)} %fusion.27) | copy-start | bytes 24580
Sparse Core Ops, SparseCore 0:
  30.6 15.7 all-gather.4
  48.5 16.8 all-gather.2
  77.4 22.1 reduce-scatter.1
where the time goes:
time: 126 us; the launch traced here: 125 us
  blocking collectives  40.4 us (32%)
  matrix products  28.7 us (23%)
  between operations  15.2 us (12%)
  waiting for transfers between devices  13.3 us (11%)
  local copies, waits for them, and re-layouts  13.1 us (10%)
  starting transfers between devices  12.5 us (10%)
  other arithmetic  1.89 us (2%)
    all_to_all x1, blocking collectives, body(): lax.all_to_all(outgoing[0].reshape(n_targets, CAP, model_width), 'expert'...  16.1 us
    unnamed x2, blocking collectives  12.2 us
    all_to_all x1, blocking collectives, body(): lax.all_to_all(outgoing[1].reshape(n_targets, CAP, model_width), 'expert'...  12.1 us
    reduce_scatter x1, waiting for transfers between devices, body(): lax.psum_scatter((term + lax.dot_general(up_pre_all, weights[1], CONTRACT...  6.84 us
    all_to_all x1, starting transfers between devices, body(): lax.all_to_all(slot_grads.reshape(n_targets, CAP, model_width).astype(jnp...  5.53 us
    all_to_all x1, waiting for transfers between devices, body(): lax.all_to_all(outgoing[2].reshape(n_targets, CAP), 'expert', split_axis=...  5.09 us
    dot_general x1, matrix products, backward_rows(): jnp.dot(gate_pre_grad, row_tokens, preferred_element_type=jnp.float32)  3.98 us
    dot_general x1, matrix products, backward_rows(): lax.dot_general(down_weight, row_grads, CONTRACT_LAST, preferred_element_...  3.98 us
  transfers between devices with their start and end apart: 6, of which 3 were waited for; matrix products, arithmetic and copies ran while one was open for 20% of the time, Pallas kernels for 0%

commit v1 on v0

v1 whole, which is shorter than its diff:
```python
import functools

import jax
import jax.numpy as jnp
from jax import lax
from jax.experimental import pallas as pl
from jax.experimental.pallas import tpu as pltpu
from jax.sharding import PartitionSpec as P

EXPERTS = 128
CAP = 4
BLOCK = 2 * CAP
LANES = 128

CONTRACT_LAST = (((1,), (1,)), ((), ()))
CONTRACT_FIRST = (((0,), (0,)), ((), ()))


def choice_table(ids, n_targets):
    rows, choices = ids.shape
    width = n_targets * BLOCK
    per_device = EXPERTS // n_targets
    lane = lax.broadcasted_iota(jnp.int32, (rows, width), 1)
    wanted = (lane // BLOCK) * per_device
    slot = lane % BLOCK
    matches = [ids[:, k : k + 1] == wanted for k in range(choices)]
    hit = functools.reduce(jnp.logical_or, matches)
    earlier = lax.broadcasted_iota(jnp.int32, (rows, rows), 1) < lax.broadcasted_iota(
        jnp.int32, (rows, rows), 0
    )
    rank = jnp.dot(
        earlier.astype(jnp.bfloat16), hit.astype(jnp.bfloat16), preferred_element_type=jnp.float32
    ).astype(jnp.int32)
    first = jnp.logical_and(hit, rank == slot)
    second = jnp.logical_and(hit, rank == slot - CAP)
    return matches, first, second


def dispatch_kernel(n_targets, ids_ref, gates_ref, tokens_ref, grads_ref, send_ref):
    matches, first, second = choice_table(ids_ref[...], n_targets)
    gates = gates_ref[...].astype(jnp.float32)
    scale = jnp.zeros(first.shape, jnp.float32)
    for k, match in enumerate(matches):
        scale = scale + jnp.where(match, gates[:, k : k + 1], 0.0)
    pick_tokens = first.astype(jnp.float32).astype(jnp.bfloat16)
    pick_grads = jnp.where(second, scale, 0.0).astype(jnp.bfloat16)
    rows = lax.dot_general(
        pick_tokens, tokens_ref[...], CONTRACT_FIRST, preferred_element_type=jnp.float32
    )
    rows = rows + lax.dot_general(
        pick_grads, grads_ref[...], CONTRACT_FIRST, preferred_element_type=jnp.float32
    )
    send_ref[...] = rows.astype(jnp.bfloat16)


def dispatch(n_targets, route_ids, gate_probs, tokens, out_grad):
    width = tokens.shape[1]
    return pl.pallas_call(
        functools.partial(dispatch_kernel, n_targets),
        out_shape=jax.ShapeDtypeStruct((n_targets * BLOCK, width), jnp.bfloat16),
        compiler_params=pltpu.CompilerParams(vmem_limit_bytes=32 * 2**20),
        name="dispatch",
    )(route_ids, gate_probs, tokens, out_grad)


def expert_kernel(count, *refs):
    pieces = refs[:count]
    weights = refs[count : count + 3]
    parts = refs[count + 3 : 2 * count + 3]
    gate_out, up_out, down_out = refs[2 * count + 3 : 2 * count + 6]
    x_s, w_s, sems = refs[2 * count + 6 :]
    piece_rows = pieces[0].shape[0]
    units, width = weights[0].shape
    half = width // 2
    rows = count * piece_rows
    copies = []
    for i, piece in enumerate(pieces):
        copies.append(
            pltpu.make_async_copy(piece, x_s.at[pl.ds(i * piece_rows, piece_rows)], sems.at[i])
        )
    for i, weight in enumerate(weights):
        copies.append(
            pltpu.make_async_copy(weight, w_s.at[pl.ds(i * units, units)], sems.at[count + i])
        )
    for copy in copies:
        copy.start()
    for copy in copies[:count]:
        copy.wait()
    x = x_s[...]
    projected = []
    for i in range(3):
        copies[count + i].wait()
        projected.append(
            lax.dot_general(
                w_s[pl.ds(i * units, units), :],
                x,
                CONTRACT_LAST,
                preferred_element_type=jnp.float32,
            )
        )
    pre_gate, pre_up, back = projected
    back = pltpu.roll(back, rows - CAP, 1)
    is_token = lax.broadcasted_iota(jnp.int32, (1, rows), 1) % BLOCK < CAP
    squash = 1.0 / (1.0 + jnp.exp(-pre_gate))
    activated = pre_gate * squash
    hidden = jnp.where(is_token, activated * pre_up, 0.0).astype(jnp.bfloat16).astype(jnp.float32)
    gate_terms = jnp.sum(hidden * back, axis=0, keepdims=True)
    up_pre = jnp.where(is_token, back * activated, 0.0)
    gate_pre = jnp.where(
        is_token, back * pre_up * squash * (1.0 + pre_gate * (1.0 - squash)), 0.0
    )
    gate_out[...] = gate_pre.astype(jnp.bfloat16)
    up_out[...] = up_pre.astype(jnp.bfloat16)
    down_out[...] = pltpu.roll(hidden, CAP, 1).astype(jnp.bfloat16)
    both = jnp.concatenate([gate_pre, up_pre], axis=0)
    low = both.T.astype(jnp.bfloat16)
    high = pltpu.roll(both, CAP, 1).T.astype(jnp.bfloat16)
    gate_column = jnp.broadcast_to(gate_terms, (LANES, rows)).T.astype(jnp.bfloat16)
    for i in range(count):
        parts[i][:, half:] = gate_column[i * piece_rows : (i + 1) * piece_rows]
    chunk = 512 if half % 512 == 0 else half

    @pl.loop(0, half // chunk)
    def _(step):
        start = pl.multiple_of(step * chunk, chunk)
        total = jnp.dot(
            low, w_s[: 2 * units, pl.ds(start, chunk)], preferred_element_type=jnp.float32
        )
        total = total + jnp.dot(
            high, w_s[: 2 * units, pl.ds(half + start, chunk)], preferred_element_type=jnp.float32
        )
        total = total.astype(jnp.bfloat16)
        for i in range(count):
            parts[i][:, pl.ds(start, chunk)] = total[i * piece_rows : (i + 1) * piece_rows]


def expert_rows(pieces, weights):
    count = len(pieces)
    piece_rows, width = pieces[0].shape
    units = weights[0].shape[0]
    rows = count * piece_rows
    anywhere = pl.BlockSpec(memory_space=pl.ANY)
    inside = pl.BlockSpec(memory_space=pltpu.VMEM)
    part = jax.ShapeDtypeStruct((piece_rows, width // 2 + LANES), jnp.bfloat16)
    kept = jax.ShapeDtypeStruct((units, rows), jnp.bfloat16)
    outs = pl.pallas_call(
        functools.partial(expert_kernel, count),
        out_shape=[part] * count + [kept] * 3,
        in_specs=[anywhere] * (count + 3),
        out_specs=[inside] * (count + 3),
        scratch_shapes=[
            pltpu.VMEM((rows, width), jnp.bfloat16),
            pltpu.VMEM((3 * units, width), jnp.bfloat16),
            pltpu.SemaphoreType.DMA((count + 3,)),
        ],
        compiler_params=pltpu.CompilerParams(vmem_limit_bytes=56 * 2**20),
        cost_estimate=pl.CostEstimate(
            flops=10 * rows * units * width,
            bytes_accessed=6 * units * width + 3 * rows * width,
            transcendentals=rows * units,
        ),
        name="expert_rows",
    )(*pieces, *weights)
    return outs[:count], outs[count:]


def weight_kernel(count, *refs):
    factors = refs[:3]
    pieces = refs[3 : 3 + count]
    outs = refs[3 + count :]
    x = jnp.concatenate([piece[...] for piece in pieces], axis=0)
    for factor, out in zip(factors, outs):
        out[...] = jnp.dot(factor[...], x, preferred_element_type=jnp.float32).astype(jnp.bfloat16)


def weight_grads(factors, pieces):
    count = len(pieces)
    piece_rows, width = pieces[0].shape
    units, rows = factors[0].shape
    chunk = 512 if width % 512 == 0 else width
    grad = jax.ShapeDtypeStruct((units, width), jnp.bfloat16)
    return pl.pallas_call(
        functools.partial(weight_kernel, count),
        grid=(width // chunk,),
        out_shape=[grad] * 3,
        in_specs=[pl.BlockSpec((units, rows), lambda i: (0, 0))] * 3
        + [pl.BlockSpec((piece_rows, chunk), lambda i: (0, i))] * count,
        out_specs=[pl.BlockSpec((units, chunk), lambda i: (0, i))] * 3,
        compiler_params=pltpu.CompilerParams(vmem_limit_bytes=32 * 2**20),
        cost_estimate=pl.CostEstimate(
            flops=6 * rows * units * width,
            bytes_accessed=6 * units * width + 2 * rows * width,
            transcendentals=0,
        ),
        name="weight_grads",
    )(*factors, *pieces)


def combine_kernel(n_targets, ids_ref, gates_ref, back_ref, token_ref, gate_ref):
    half = token_ref.shape[1] // 2
    token_rows, choices = ids_ref.shape
    matches, first, second = choice_table(ids_ref[...], n_targets)
    pick_first = first.astype(jnp.float32).astype(jnp.bfloat16)
    pick_second = second.astype(jnp.float32).astype(jnp.bfloat16)
    rows = back_ref[:, :half]
    token_ref[:, :half] = jnp.dot(
        pick_first, rows, preferred_element_type=jnp.float32
    ).astype(jnp.bfloat16)
    token_ref[:, half:] = jnp.dot(
        pick_second, rows, preferred_element_type=jnp.float32
    ).astype(jnp.bfloat16)
    lane = lax.broadcasted_iota(jnp.int32, (token_rows, LANES), 1)
    terms = jnp.zeros((token_rows, LANES), jnp.float32)
    for k in range(choices):
        chosen = jnp.logical_and(matches[k], first).astype(jnp.float32).astype(jnp.bfloat16)
        term = jnp.dot(chosen, back_ref[:, half:], preferred_element_type=jnp.float32)
        terms = terms + jnp.where(lane == k, term, 0.0)
    gate_ref[...] = terms[:, :choices] / gates_ref[...].astype(jnp.float32)


def combine(n_targets, route_ids, gate_probs, returned, width):
    token_rows, choices = route_ids.shape
    return pl.pallas_call(
        functools.partial(combine_kernel, n_targets),
        out_shape=[
            jax.ShapeDtypeStruct((token_rows, width), jnp.bfloat16),
            jax.ShapeDtypeStruct((token_rows, choices), jnp.float32),
        ],
        compiler_params=pltpu.CompilerParams(vmem_limit_bytes=32 * 2**20),
        name="combine",
    )(route_ids, gate_probs, returned)


def flip(value, axis, bit):
    size = lax.axis_size(axis)
    return lax.ppermute(value, axis, [(i, i ^ bit) for i in range(size)])


def exchange(value, n_targets):
    rows, width = value.shape
    blocks = value.reshape(n_targets, rows // n_targets, width)
    blocks = lax.all_to_all(blocks, "expert", split_axis=0, concat_axis=0, tiled=True)
    return blocks.reshape(rows, width)


def body(tokens, out_grad, gate_probs, route_ids, w_gate, w_up, w_down):
    n_targets = lax.axis_size("expert")
    n_dp = lax.axis_size("dp")
    width = tokens.shape[1]
    bits = [1 << i for i in range(1, n_dp.bit_length() - 1)] + [1]
    sent = dispatch(n_targets, route_ids, gate_probs, tokens, out_grad)
    held = {0: exchange(sent, n_targets)}
    for bit in bits:
        for mask in list(held):
            held[mask | bit] = flip(held[mask], "dp", bit)
    masks = sorted(held)
    pieces = [held[mask] for mask in masks]
    parts, factors = expert_rows(pieces, (w_gate[0], w_up[0], w_down[0]))
    grad_gate, grad_up, grad_down = weight_grads(factors, pieces)
    sums = dict(zip(masks, parts))
    for bit in reversed(bits):
        for mask in [m for m in sums if m & bit]:
            sums[mask ^ bit] = sums[mask ^ bit] + flip(sums.pop(mask), "dp", bit)
    returned = exchange(sums[0], n_targets)
    token_grad, gate_grad = combine(n_targets, route_ids, gate_probs, returned, width)
    return (token_grad, gate_grad, grad_gate[None], grad_up[None], grad_down[None])


def solution(mesh):
    in_specs = (
        P(("expert", "dp"), None),
        P(("expert", "dp"), None),
        P(("expert", "dp"), None),
        P(("expert", "dp"), None),
        P("expert", "dp", None),
        P("expert", "dp", None),
        P("expert", "dp", None),
    )
    out_specs = (
        P(("expert", "dp"), None),
        P(("expert", "dp"), None),
        P("expert", "dp", None),
        P("expert", "dp", None),
        P("expert", "dp", None),
    )
    return jax.shard_map(body, mesh=mesh, in_specs=in_specs, out_specs=out_specs, check_vma=False)
```

time: 126 us -> 86 us (0.68)
  matrix products: 28.7 us -> 0 us
  Pallas kernels: 0 us -> 19 us
  blocking collectives: 40.4 us -> 21.6 us
  between operations: 15.2 us -> 0.69 us
  waiting for transfers between devices: 13.3 us -> 21.4 us
  starting transfers between devices: 12.5 us -> 8 us
  local copies, waits for them, and re-layouts: 13.1 us -> 11.8 us
    dot_general x13 -> x0, matrix products: 28.7 us -> none  [the longest x1 3.98 us: backward_rows(): jnp.dot(gate_pre_grad, row_tokens, preferred_element_type=jnp.float32)]
    ppermute x0 -> x6, waiting for transfers between devices: none -> 21.4 us  [flip(): return lax.ppermute(value, axis, [(i, i ^ bit) for i in range(size)])]
    pallas_call x0 -> x4, Pallas kernels: none -> 19 us  [the longest x1 11.1 us: expert_rows(): pl.pallas_call(functools.partial(expert_kernel, count), out_shape=[part]...]
    unnamed x2 -> x0, blocking collectives: 12.2 us -> none
    unnamed x23 -> x29, local copies, waits for them, and re-layouts: 3.05 us -> 11.8 us
    all_to_all x3 -> x1, starting transfers between devices: 12.4 us -> 4.37 us  [exchange(): lax.all_to_all(blocks, 'expert', split_axis=0, concat_axis=0, tiled=True)]
    reduce_scatter x1 -> x0, waiting for transfers between devices: 6.84 us -> none  [body(): lax.psum_scatter((term + lax.dot_general(up_pre_all, weights[1], CONTRACT...]
    reshape x9 -> x0, local copies, waits for them, and re-layouts: 6.64 us -> none  [the longest x1 1.72 us: body(): arrived[1].reshape(slot_count, model_width)]
  transfers between devices with their start and end apart: 6 -> 7, of which waited for: 3 -> 4; matrix products, arithmetic and copies ran while one was open for 20% -> 1% of each run, Pallas kernels for 0% -> 7%
where the time goes in v1:
time: 86 us; the launch traced here: 85.3 us
  blocking collectives  21.6 us (25%)
  waiting for transfers between devices  21.4 us (25%)
  Pallas kernels  19 us (22%)
  local copies, waits for them, and re-layouts  11.8 us (14%)
  starting transfers between devices  8 us (9%)
  other arithmetic  2.76 us (3%)
    all_to_all x1, blocking collectives, exchange(): lax.all_to_all(blocks, 'expert', split_axis=0, concat_axis=0, tiled=True)  21.6 us
    ppermute x6, waiting for transfers between devices, flip(): return lax.ppermute(value, axis, [(i, i ^ bit) for i in range(size)])  21.4 us
    unnamed x29, local copies, waits for them, and re-layouts  11.8 us
    pallas_call x1, Pallas kernels, expert_rows(): pl.pallas_call(functools.partial(expert_kernel, count), out_shape=[part]...  11.1 us
    pallas_call x1, Pallas kernels, weight_grads(): pl.pallas_call(functools.partial(weight_kernel, count), grid=(width // ch...  6.09 us
    all_to_all x1, starting transfers between devices, exchange(): lax.all_to_all(blocks, 'expert', split_axis=0, concat_axis=0, tiled=True)  4.37 us
    ppermute x6, starting transfers between devices, flip(): return lax.ppermute(value, axis, [(i, i ^ bit) for i in range(size)])  3.63 us
    reshape x1, other arithmetic, exchange(): blocks = value.reshape(n_targets, rows // n_targets, width)  1.74 us
  transfers between devices with their start and end apart: 7, of which 4 were waited for; matrix products, arithmetic and copies ran while one was open for 1% of the time, Pallas kernels for 7%

profile of v1, /device:TPU:0, one launch (start us, length us, event | category | flops | bytes accessed | tf_op | source)
XLA Modules:
  0.0 85.3 jit_solution(6940177110315372784)
XLA Ops:
  0.6 0.8 copy.15.gates_ref
  2.2 0.9 %copy-done.2 = bf16[32,4096]{1,0:T(8,128)(2,1)S(1)} copy-done((bf16[32,4096]{1,0:T(8,128)(2,1)S(1)}, bf16[32,4096]{1,0:T(8,128)(2,1)}, u32[]{:S(2)}) %copy-start.2) | copy-done | bytes 262168
  3.1 0.9 %copy-done.3 = bf16[32,4096]{1,0:T(8,128)(2,1)S(1)} copy-done((bf16[32,4096]{1,0:T(8,128)(2,1)S(1)}, bf16[32,4096]{1,0:T(8,128)(2,1)}, u32[]{:S(2)}) %copy-start.3) | copy-done | bytes 262168
  4.8 21.6 %all_to_all.10 = bf16[8,8,4096]{2,1,0:T(8,128)(2,1)S(1)} all-to-all(bf16[8,8,4096]{2,1,0:T(8,128)(2,1)S(1)} %bitcast.11), channel_id=1, replica_groups=mesh['expert'=8,'dp'=4] {'expert'}, dimensions={0} | all-to-all | bytes 1048576 | tf_op jit(solution)/shard_map/all_to_all | solution.py:242
  26.4 1.5 %collective-permute-start.1 = (bf16[64,4096]{1,0:T(8,128)(2,1)S(1)}, bf16[64,4096]{1,0:T(8,128)(2,1)S(1)}, u32[]{:S(2)}, u32[]{:S(2)}) collective-permute-start(bf16[64,4096]{1,0:T(8,128)(2,1)S(1)} %bitcast.13), channel_id=1, source_target_pairs={{0,2},{1,3},{2,0},{3,1},{4,6},{5,7},{6,4},{7,5},{8,10},{9,11},{10,... | collective-permute-start | bytes 1572872 | tf_op jit(solution)/shard_map/ppermute | solution.py:236
  27.9 11.0 %collective-permute-done.1.refs_2_.refs_5_ = bf16[64,4096]{1,0:T(8,128)(2,1)S(1)} collective-permute-done((bf16[64,4096]{1,0:T(8,128)(2,1)S(1)}, bf16[64,4096]{1,0:T(8,128)(2,1)S(1)}, u32[]{:S(2)}, u32[]{:S(2)}) %collective-permute-start.1) | collective-permute-done | bytes 524320 | tf_op jit(solution)/shard_map/ppermute | solution.py:236
  38.9 1.9 %collective-permute-done.2.refs_3_.refs_6_ = bf16[64,4096]{1,0:T(8,128)(2,1)S(1)} collective-permute-done((bf16[64,4096]{1,0:T(8,128)(2,1)S(1)}, bf16[64,4096]{1,0:T(8,128)(2,1)S(1)}, u32[]{:S(2)}, u32[]{:S(2)}) %collective-permute-start.2) | collective-permute-done | bytes 524320 | tf_op jit(solution)/shard_map/ppermute | solution.py:236
  40.8 0.8 copy-done.8
  41.6 11.1 %expert_rows.1 = (bf16[64,2176]{1,0:T(8,128)(2,1)}, bf16[64,2176]{1,0:T(8,128)(2,1)}, bf16[64,2176]{1,0:T(8,128)(2,1)}, bf16[64,2176]{1,0:T(8,128)(2,1)}, bf16[3...) custom-call(bf16[64,4096]{1,0:T(8,128)(2,1)} %bitcast.15, bf16[64,4096]{1,0:T(8,128)(2,1)} %copy-done.6, ...), custom_call_target="tpu_custom_call" | custom-call | flops 4026531840 | bytes 12582912 | tf_op jit(solution)/shard_map/expert_rows/pallas_call | solution.py:146
  53.3 1.3 %collective-permute-done.4 = bf16[64,2176]{1,0:T(8,128)(2,1)S(1)} collective-permute-done((bf16[64,2176]{1,0:T(8,128)(2,1)}, bf16[64,2176]{1,0:T(8,128)(2,1)S(1)}, u32[]{:S(2)}, u32[]{:S(2)}) %collective-permute-start.4) | collective-permute-done | bytes 278560 | tf_op jit(solution)/shard_map/ppermute | solution.py:236
  54.6 1.0 %add.10 = bf16[64,2176]{1,0:T(8,128)(2,1)S(1)} add(bf16[64,2176]{1,0:T(8,128)(2,1)} %get-tuple-element.19, bf16[64,2176]{1,0:T(8,128)(2,1)S(1)} %collective-permute-done.4) | non-fusion elementwise | flops 139264 | bytes 835584 | tf_op jit(solution)/shard_map/add | solution.py:263
  55.6 1.6 %collective-permute-start.5 = (bf16[64,2176]{1,0:T(8,128)(2,1)S(1)}, bf16[64,2176]{1,0:T(8,128)(2,1)S(1)}, u32[]{:S(2)}, u32[]{:S(2)}) collective-permute-start(bf16[64,2176]{1,0:T(8,128)(2,1)S(1)} %add.10), channel_id=1, source_target_pairs={{0,2},{1,3},{2,0},{3,1},{4,6},{5,7},{6,4},{7,5},{8,10},{9,11},{10,... | collective-permute-start | bytes 835592 | tf_op jit(solution)/shard_map/ppermute | solution.py:236
  57.2 7.2 %collective-permute-done.5 = bf16[64,2176]{1,0:T(8,128)(2,1)S(1)} collective-permute-done((bf16[64,2176]{1,0:T(8,128)(2,1)S(1)}, bf16[64,2176]{1,0:T(8,128)(2,1)S(1)}, u32[]{:S(2)}, u32[]{:S(2)}) %collective-permute-start.5) | collective-permute-done | bytes 278560 | tf_op jit(solution)/shard_map/ppermute | solution.py:236
  64.4 1.7 %add_bitcast_fusion = bf16[8,8,2176]{2,1,0:T(8,128)(2,1)} fusion(bf16[64,2176]{1,0:T(8,128)(2,1)S(1)} %collective-permute-done.5, bf16[64,2176]{1,0:T(8,128)(2,1)} %get-tuple-element.17, bf16[64,2176]{1,0:T(8,128)(2,1)S(1)} %collective-permute-done.3), kind=kLoop, calls=%fused_computation | loop fusion | flops 278528 | bytes 1114112 | tf_op jit(solution)/shard_map/reshape | solution.py:241
  66.1 4.4 %all-to-all-start.1 = ((bf16[8,8,2176]{2,1,0:T(8,128)(2,1)}), bf16[8,8,2176]{2,1,0:T(8,128)(2,1)S(1)}, u32[]{:S(2)}, u32[]{:S(2)}) async-start(bf16[8,8,2176]{2,1,0:T(8,128)(2,1)} %add_bitcast_fusion), calls=%async_computation.1 | async-start | bytes 557056 | tf_op jit(solution)/shard_map/all_to_all | solution.py:242
  70.5 1.0 %copy-done.1 = bf16[8,8,4096]{2,1,0:T(8,128)(2,1)S(1)} copy-done((bf16[8,8,4096]{2,1,0:T(8,128)(2,1)S(1)}, bf16[8,8,4096]{2,1,0:T(8,128)(2,1)}, u32[]{:S(2)}) %copy-start.1) | copy-done | bytes 524312
  71.5 1.0 %copy-done.5 = bf16[64,4096]{1,0:T(8,128)(2,1)S(1)} copy-done((bf16[64,4096]{1,0:T(8,128)(2,1)S(1)}, bf16[64,4096]{1,0:T(8,128)(2,1)}, u32[]{:S(2)}) %copy-start.5) | copy-done | bytes 524312
  72.6 1.0 %copy-done.7 = bf16[64,4096]{1,0:T(8,128)(2,1)S(1)} copy-done((bf16[64,4096]{1,0:T(8,128)(2,1)S(1)}, bf16[64,4096]{1,0:T(8,128)(2,1)}, u32[]{:S(2)}) %copy-start.7) | copy-done | bytes 524312
  73.6 1.0 %copy-done.9 = bf16[64,4096]{1,0:T(8,128)(2,1)S(1)} copy-done((bf16[64,4096]{1,0:T(8,128)(2,1)S(1)}, bf16[64,4096]{1,0:T(8,128)(2,1)}, u32[]{:S(2)}) %copy-start.9) | copy-done | bytes 524312
  74.6 0.9 %copy-done.10 = bf16[384,256]{1,0:T(8,128)(2,1)S(1)} copy-done((bf16[384,256]{1,0:T(8,128)(2,1)S(1)}, bf16[384,256]{1,0:T(8,128)(2,1)}, u32[]{:S(2)}) %copy-start.10) | copy-done | bytes 196632
  75.6 0.9 %copy-done.11 = bf16[384,256]{1,0:T(8,128)(2,1)S(1)} copy-done((bf16[384,256]{1,0:T(8,128)(2,1)S(1)}, bf16[384,256]{1,0:T(8,128)(2,1)}, u32[]{:S(2)}) %copy-start.11) | copy-done | bytes 196632
  76.5 0.9 %copy-done.12 = bf16[384,256]{1,0:T(8,128)(2,1)S(1)} copy-done((bf16[384,256]{1,0:T(8,128)(2,1)S(1)}, bf16[384,256]{1,0:T(8,128)(2,1)}, u32[]{:S(2)}) %copy-start.12) | copy-done | bytes 196632
  77.4 6.1 %weight_grads.1 = (bf16[384,4096]{1,0:T(8,128)(2,1)}, bf16[384,4096]{1,0:T(8,128)(2,1)}, bf16[384,4096]{1,0:T(8,128)(2,1)}) custom-call(bf16[384,256]{1,0:T(8,128)(2,1)S(1)} %copy-done.10, bf16[384,256]{1,0:T(8,128)(2,1)S(1)} %copy-done.11, bf16[384,256]{1,0:T(8,128)(2,1)S(1)} %copy-done.12, bf16[64,4096]{1,0:T(8,128)(2,1)S(1)} %bitcast.16, ...), custom_call_target="tpu_custom_call" | custom-call | flops 2415919104 | bytes 11534336 | tf_op jit(solution)/shard_map/weight_grads/pallas_call | solution.py:182
  83.5 1.2 %combine.1 = (bf16[32,4096]{1,0:T(8,128)(2,1)}, f32[32,8]{1,0:T(8,128)S(1)}) custom-call(s32[32,8]{1,0:T(8,128)S(1)} %copy.14.ids_ref, bf16[32,8]{1,0:T(8,128)(2,1)S(1)} %copy.15.gates_ref, bf16[64,2176]{1,0:T(8,128)(2,1)S(1)} %bitcast.12), custom_call_target="tpu_custom_call" | custom-call | tf_op jit(solution)/shard_map/combine/pallas_call | solution.py:223
  (26 shorter events, 2.7 us)
Async XLA Ops:
  2.2 0.9 %copy-start.2 = (bf16[32,4096]{1,0:T(8,128)(2,1)S(1)}, bf16[32,4096]{1,0:T(8,128)(2,1)}, u32[]{:S(2)}) copy-start(bf16[32,4096]{1,0:T(8,128)(2,1)} %tokens_ref.1) | copy-start | bytes 786436
  3.1 0.9 %copy-start.3 = (bf16[32,4096]{1,0:T(8,128)(2,1)S(1)}, bf16[32,4096]{1,0:T(8,128)(2,1)}, u32[]{:S(2)}) copy-start(bf16[32,4096]{1,0:T(8,128)(2,1)} %grads_ref.1) | copy-start | bytes 786436
  26.4 14.5 %copy-start = (bf16[8,8,4096]{2,1,0:T(8,128)(2,1)}, bf16[8,8,4096]{2,1,0:T(8,128)(2,1)S(1)}, u32[]{:S(2)}) copy-start(bf16[8,8,4096]{2,1,0:T(8,128)(2,1)S(1)} %all_to_all.10) | copy-start | bytes 1572868
  26.4 12.5 %collective-permute-start.1 = (bf16[64,4096]{1,0:T(8,128)(2,1)S(1)}, bf16[64,4096]{1,0:T(8,128)(2,1)S(1)}, u32[]{:S(2)}, u32[]{:S(2)}) collective-permute-start(bf16[64,4096]{1,0:T(8,128)(2,1)S(1)} %bitcast.13), channel_id=1, source_target_pairs={{0,2},{1,3},{2,0},{3,1},{4,6},{5,7},{6,4},{7,5},{8,10},{9,11},{10,... | collective-permute-start | bytes 1572872 | tf_op jit(solution)/shard_map/ppermute | solution.py:236
  27.9 11.1 %collective-permute-start = (bf16[64,4096]{1,0:T(8,128)(2,1)S(1)}, bf16[64,4096]{1,0:T(8,128)(2,1)S(1)}, u32[]{:S(2)}, u32[]{:S(2)}) collective-permute-start(bf16[64,4096]{1,0:T(8,128)(2,1)S(1)} %bitcast.14), channel_id=1, source_target_pairs={{0,1},{1,0},{2,3},{3,2},{4,5},{5,4},{6,7},{7,6},{8,9},{9,8},{10,11... | collective-permute-start | bytes 1572872 | tf_op jit(solution)/shard_map/ppermute | solution.py:236
  38.9 1.9 %copy-start.4 = (bf16[64,4096]{1,0:T(8,128)(2,1)}, bf16[64,4096]{1,0:T(8,128)(2,1)S(1)}, u32[]{:S(2)}) copy-start(bf16[64,4096]{1,0:T(8,128)(2,1)S(1)} %collective-permute-done.1.refs_2_.refs_5_) | copy-start | bytes 1572868
  38.9 1.9 %collective-permute-start.2 = (bf16[64,4096]{1,0:T(8,128)(2,1)S(1)}, bf16[64,4096]{1,0:T(8,128)(2,1)S(1)}, u32[]{:S(2)}, u32[]{:S(2)}) collective-permute-start(bf16[64,4096]{1,0:T(8,128)(2,1)S(1)} %collective-permute-done.1.refs_2_.refs_5_), channel_id=1, source_target_pairs={{0,1},{1,0},{2,3},{3,2},{4,5},{5,4},{6,7},{7,6},{8,9},{9,8},{10,11... | collective-permute-start | bytes 1572872 | tf_op jit(solution)/shard_map/ppermute | solution.py:236
  38.9 1.9 %copy-start.6 = (bf16[64,4096]{1,0:T(8,128)(2,1)}, bf16[64,4096]{1,0:T(8,128)(2,1)S(1)}, u32[]{:S(2)}) copy-start(bf16[64,4096]{1,0:T(8,128)(2,1)S(1)} %collective-permute-done.refs_1_.refs_4_) | copy-start | bytes 1572868
  40.8 0.8 copy-start.8
  52.7 1.8 %collective-permute-start.4 = (bf16[64,2176]{1,0:T(8,128)(2,1)}, bf16[64,2176]{1,0:T(8,128)(2,1)S(1)}, u32[]{:S(2)}, u32[]{:S(2)}) collective-permute-start(bf16[64,2176]{1,0:T(8,128)(2,1)} %get-tuple-element.20), channel_id=1, source_target_pairs={{0,1},{1,0},{2,3},{3,2},{4,5},{5,4},{6,7},{7,6},{8,9},{9,8},{10,11... | collective-permute-start | bytes 835592 | tf_op jit(solution)/shard_map/ppermute | solution.py:236
  52.9 4.2 %collective-permute-start.3 = (bf16[64,2176]{1,0:T(8,128)(2,1)}, bf16[64,2176]{1,0:T(8,128)(2,1)S(1)}, u32[]{:S(2)}, u32[]{:S(2)}) collective-permute-start(bf16[64,2176]{1,0:T(8,128)(2,1)} %get-tuple-element.18), channel_id=1, source_target_pairs={{0,1},{1,0},{2,3},{3,2},{4,5},{5,4},{6,7},{7,6},{8,9},{9,8},{10,11... | collective-permute-start | bytes 835592 | tf_op jit(solution)/shard_map/ppermute | solution.py:236
  55.6 8.8 %collective-permute-start.5 = (bf16[64,2176]{1,0:T(8,128)(2,1)S(1)}, bf16[64,2176]{1,0:T(8,128)(2,1)S(1)}, u32[]{:S(2)}, u32[]{:S(2)}) collective-permute-start(bf16[64,2176]{1,0:T(8,128)(2,1)S(1)} %add.10), channel_id=1, source_target_pairs={{0,2},{1,3},{2,0},{3,1},{4,6},{5,7},{6,4},{7,5},{8,10},{9,11},{10,... | collective-permute-start | bytes 835592 | tf_op jit(solution)/shard_map/ppermute | solution.py:236
  66.1 17.4 %all-to-all-start.1 = ((bf16[8,8,2176]{2,1,0:T(8,128)(2,1)}), bf16[8,8,2176]{2,1,0:T(8,128)(2,1)S(1)}, u32[]{:S(2)}, u32[]{:S(2)}) async-start(bf16[8,8,2176]{2,1,0:T(8,128)(2,1)} %add_bitcast_fusion), calls=%async_computation.1 | async-start | bytes 557056 | tf_op jit(solution)/shard_map/all_to_all | solution.py:242
  70.5 1.0 %copy-start.1 = (bf16[8,8,4096]{2,1,0:T(8,128)(2,1)S(1)}, bf16[8,8,4096]{2,1,0:T(8,128)(2,1)}, u32[]{:S(2)}) copy-start(bf16[8,8,4096]{2,1,0:T(8,128)(2,1)} %copy-done) | copy-start | bytes 1572868
  71.5 1.0 %copy-start.5 = (bf16[64,4096]{1,0:T(8,128)(2,1)S(1)}, bf16[64,4096]{1,0:T(8,128)(2,1)}, u32[]{:S(2)}) copy-start(bf16[64,4096]{1,0:T(8,128)(2,1)} %copy-done.4) | copy-start | bytes 1572868
  72.6 1.0 %copy-start.7 = (bf16[64,4096]{1,0:T(8,128)(2,1)S(1)}, bf16[64,4096]{1,0:T(8,128)(2,1)}, u32[]{:S(2)}) copy-start(bf16[64,4096]{1,0:T(8,128)(2,1)} %copy-done.6) | copy-start | bytes 1572868
  73.6 1.0 %copy-start.9 = (bf16[64,4096]{1,0:T(8,128)(2,1)S(1)}, bf16[64,4096]{1,0:T(8,128)(2,1)}, u32[]{:S(2)}) copy-start(bf16[64,4096]{1,0:T(8,128)(2,1)} %copy-done.8) | copy-start | bytes 1572868
  74.6 0.9 %copy-start.10 = (bf16[384,256]{1,0:T(8,128)(2,1)S(1)}, bf16[384,256]{1,0:T(8,128)(2,1)}, u32[]{:S(2)}) copy-start(bf16[384,256]{1,0:T(8,128)(2,1)} %get-tuple-element.23.refs_0_) | copy-start | bytes 589828
  75.6 0.9 %copy-start.11 = (bf16[384,256]{1,0:T(8,128)(2,1)S(1)}, bf16[384,256]{1,0:T(8,128)(2,1)}, u32[]{:S(2)}) copy-start(bf16[384,256]{1,0:T(8,128)(2,1)} %get-tuple-element.24.refs_1_) | copy-start | bytes 589828
  76.5 0.9 %copy-start.12 = (bf16[384,256]{1,0:T(8,128)(2,1)S(1)}, bf16[384,256]{1,0:T(8,128)(2,1)}, u32[]{:S(2)}) copy-start(bf16[384,256]{1,0:T(8,128)(2,1)} %get-tuple-element.25.refs_2_) | copy-start | bytes 589828

commit v2 on v1

v2 whole, which is shorter than its diff:
```python
import functools

import jax
import jax.numpy as jnp
from jax import lax
from jax.experimental import pallas as pl
from jax.experimental.pallas import tpu as pltpu
from jax.sharding import PartitionSpec as P

EXPERTS = 128
CAP = 4
BLOCK = 2 * CAP
LANES = 128
MIB = 2**20
SMALL_ROWS = 512
COVER = 12

CONTRACT_LAST = (((1,), (1,)), ((), ()))
CONTRACT_FIRST = (((0,), (0,)), ((), ()))

HBM = pl.BlockSpec(memory_space=pltpu.HBM)
ANY = pl.BlockSpec(memory_space=pl.ANY)
VMEM = pl.BlockSpec(memory_space=pltpu.VMEM)


def as_bf16(mask):
    return mask.astype(jnp.float32).astype(jnp.bfloat16)


def choice_table(ids, n_targets):
    choices, tokens = ids.shape
    height = n_targets * BLOCK
    per_device = EXPERTS // n_targets
    row = lax.broadcasted_iota(jnp.int32, (height, 1), 0)
    wanted = ((row // BLOCK) ^ lax.axis_index("expert")) * per_device
    slot = row % BLOCK
    matches = [ids[k : k + 1, :] == wanted for k in range(choices)]
    hit = functools.reduce(jnp.logical_or, matches)
    earlier = lax.broadcasted_iota(jnp.int32, (tokens, tokens), 0) < lax.broadcasted_iota(
        jnp.int32, (tokens, tokens), 1
    )
    rank = jnp.dot(as_bf16(hit), as_bf16(earlier), preferred_element_type=jnp.float32)
    rank = rank.astype(jnp.int32)
    first = jnp.logical_and(hit, rank == slot)
    second = jnp.logical_and(hit, rank == slot - CAP)
    return matches, first, second


def fetch(sources, targets, sems):
    copies = [
        pltpu.make_async_copy(source, target, sems.at[i])
        for i, (source, target) in enumerate(zip(sources, targets))
    ]
    for copy in copies:
        copy.start()
    for copy in copies:
        copy.wait()


def dispatch_kernel(n_targets, ids_hbm, gates_hbm, tokens_hbm, grads_hbm, *refs):
    outs = refs[:n_targets]
    ids_ref, gates_ref, tokens_ref, grads_ref, sems = refs[n_targets:]
    fetch(
        (ids_hbm, gates_hbm, tokens_hbm, grads_hbm),
        (ids_ref, gates_ref, tokens_ref, grads_ref),
        sems,
    )
    matches, first, second = choice_table(ids_ref[...], n_targets)
    gates = gates_ref[...].astype(jnp.float32)
    scale = jnp.zeros(first.shape, jnp.float32)
    for k, match in enumerate(matches):
        scale = scale + jnp.where(match, gates[k : k + 1, :], 0.0)
    pick_grads = jnp.where(second, scale, 0.0).astype(jnp.bfloat16)
    rows = jnp.dot(as_bf16(first), tokens_ref[...], preferred_element_type=jnp.float32)
    rows = rows + jnp.dot(pick_grads, grads_ref[...], preferred_element_type=jnp.float32)
    for k, out in enumerate(outs):
        out[...] = rows[k * BLOCK : (k + 1) * BLOCK].astype(jnp.bfloat16)


def dispatch(n_targets, ids, gates, tokens, out_grad):
    width = tokens.shape[1]
    arrays = (ids, gates, tokens, out_grad)
    return pl.pallas_call(
        functools.partial(dispatch_kernel, n_targets),
        out_shape=[jax.ShapeDtypeStruct((BLOCK, width), jnp.bfloat16)] * n_targets,
        in_specs=[HBM] * 4,
        out_specs=[VMEM] * n_targets,
        scratch_shapes=[pltpu.VMEM(a.shape, a.dtype) for a in arrays]
        + [pltpu.SemaphoreType.DMA((4,))],
        compiler_params=pltpu.CompilerParams(vmem_limit_bytes=60 * MIB),
        name="dispatch",
    )(*arrays)


def placement_kernel(n_targets, ids_ref, first_ref, second_ref, choice_ref):
    matches, first, second = choice_table(ids_ref[...], n_targets)
    first_ref[...] = as_bf16(first)
    second_ref[...] = as_bf16(second)
    choice = jnp.full(first.shape, -1, jnp.int32)
    for k, match in enumerate(matches):
        choice = jnp.where(jnp.logical_and(match, first), k, choice)
    choice_ref[...] = choice


def placement(n_targets, ids):
    table = (n_targets * BLOCK, ids.shape[1])
    return pl.pallas_call(
        functools.partial(placement_kernel, n_targets),
        out_shape=[
            jax.ShapeDtypeStruct(table, jnp.bfloat16),
            jax.ShapeDtypeStruct(table, jnp.bfloat16),
            jax.ShapeDtypeStruct(table, jnp.int32),
        ],
        in_specs=[VMEM],
        out_specs=[VMEM] * 3,
        compiler_params=pltpu.CompilerParams(vmem_limit_bytes=4 * MIB),
        cost_estimate=pl.CostEstimate(
            flops=COVER * 10**9, bytes_accessed=COVER * 10**6, transcendentals=0
        ),
        name="placement",
    )(ids)


def row_grads(low, high, gate_w, up_w, received, parts, half):
    units = gate_w.shape[0]
    chunk = 512 if half % 512 == 0 else half
    block = parts[0].shape[0]

    @pl.loop(0, half // chunk)
    def _(step):
        near = pl.ds(pl.multiple_of(step * chunk, chunk), chunk)
        far = pl.ds(pl.multiple_of(half + step * chunk, chunk), chunk)
        total = None
        for rows, columns in ((low, near), (high, far)):
            for i, weight in enumerate((gate_w, up_w)):
                term = jnp.dot(
                    rows[:, i * units : (i + 1) * units],
                    weight[:, columns],
                    preferred_element_type=jnp.float32,
                )
                total = term if total is None else total + term
        for i, part in enumerate(parts):
            value = total[i * block : (i + 1) * block]
            if received is not None:
                value = value + received[i][:, near].astype(jnp.float32)
            part[:, near] = value.astype(jnp.bfloat16)


def expert_kernel(count, *refs):
    pieces = refs[:count]
    gate_w, up_w, down_w = refs[count : count + 3]
    part, x_out, gate_out, up_out, down_out, low_out, high_out, gates_out = refs[count + 3 : -1]
    width = gate_w.shape[1]
    half = width // 2
    rows = count * BLOCK
    if rows > SMALL_ROWS:
        spots = [x_out.at[pl.ds(i * BLOCK, BLOCK)] for i in range(count)]
        fetch(pieces, spots, refs[-1])
    else:
        for i in range(0, count, 2):
            x_out[i * BLOCK : (i + 2) * BLOCK, :] = jnp.concatenate(
                [pieces[i][...], pieces[i + 1][...]], axis=0
            )

    def project(weight):
        return lax.dot_general(
            weight[...], x_out[...], CONTRACT_LAST, preferred_element_type=jnp.float32
        )

    pre_gate, pre_up, back = project(gate_w), project(up_w), project(down_w)
    back = pltpu.roll(back, rows - CAP, 1)
    is_token = lax.broadcasted_iota(jnp.int32, (1, rows), 1) % BLOCK < CAP
    squash = 1.0 / (1.0 + jnp.exp(-pre_gate))
    activated = pre_gate * squash
    hidden = jnp.where(is_token, activated * pre_up, 0.0).astype(jnp.bfloat16).astype(jnp.float32)
    gate_terms = jnp.sum(hidden * back, axis=0, keepdims=True)
    up_pre = jnp.where(is_token, back * activated, 0.0)
    gate_pre = jnp.where(
        is_token, back * pre_up * squash * (1.0 + pre_gate * (1.0 - squash)), 0.0
    )
    both = jnp.concatenate([gate_pre, up_pre], axis=0)
    low = both.T.astype(jnp.bfloat16)
    high = pltpu.roll(both, CAP, 1).T.astype(jnp.bfloat16)
    gate_column = jnp.broadcast_to(gate_terms, (LANES, rows)).T.astype(jnp.bfloat16)
    mine = rows // 2
    part[:, half:] = gate_column[mine:]
    row_grads(low[mine:], high[mine:], gate_w, up_w, None, (part,), half)
    low_out[...] = low[:mine]
    high_out[...] = high[:mine]
    gates_out[...] = gate_column[:mine]
    gate_out[...] = gate_pre.astype(jnp.bfloat16)
    up_out[...] = up_pre.astype(jnp.bfloat16)
    down_out[...] = pltpu.roll(hidden, CAP, 1).astype(jnp.bfloat16)


def expert_rows(pieces, weights):
    count = len(pieces)
    width = pieces[0].shape[1]
    units = weights[0].shape[0]
    rows = count * BLOCK
    mine = rows // 2
    shapes = [
        (mine, width // 2 + LANES),
        (rows, width),
        (units, rows),
        (units, rows),
        (units, rows),
        (mine, 2 * units),
        (mine, 2 * units),
        (mine, LANES),
    ]
    return pl.pallas_call(
        functools.partial(expert_kernel, count),
        out_shape=[jax.ShapeDtypeStruct(shape, jnp.bfloat16) for shape in shapes],
        in_specs=[VMEM if rows <= SMALL_ROWS else ANY] * count + [VMEM] * 3,
        out_specs=[VMEM] * len(shapes),
        scratch_shapes=[pltpu.SemaphoreType.DMA((count,))],
        compiler_params=pltpu.CompilerParams(
            vmem_limit_bytes=4 * MIB
            + 2 * sum(height * across for height, across in shapes)
            + 64 * rows * units
        ),
        cost_estimate=pl.CostEstimate(
            flops=8 * rows * units * width,
            bytes_accessed=6 * units * width,
            transcendentals=rows * units,
        ),
        name="expert_rows",
    )(*pieces, *weights)


def own_kernel(groups, low, high, gates, gate_w, up_w, received, *parts):
    half = gate_w.shape[1] // 2
    block = parts[0].shape[0]
    for i, part in enumerate(parts):
        span = pl.ds(i * block, block)
        part[:, half:] = (
            gates[span, :].astype(jnp.float32) + received[span, half:].astype(jnp.float32)
        ).astype(jnp.bfloat16)
    views = [received.at[pl.ds(i * block, block)] for i in range(groups)]
    row_grads(low[...], high[...], gate_w, up_w, views, parts, half)


def own_rows(groups, low, high, gates, gate_w, up_w, received):
    rows, width = received.shape
    units = gate_w.shape[0]
    return pl.pallas_call(
        functools.partial(own_kernel, groups),
        out_shape=[jax.ShapeDtypeStruct((rows // groups, width), jnp.bfloat16)] * groups,
        in_specs=[VMEM] * 6,
        out_specs=[VMEM] * groups,
        compiler_params=pltpu.CompilerParams(vmem_limit_bytes=8 * MIB + 8 * rows * width),
        cost_estimate=pl.CostEstimate(
            flops=4 * rows * units * gate_w.shape[1],
            bytes_accessed=4 * units * gate_w.shape[1],
            transcendentals=0,
        ),
        name="own_rows",
    )(low, high, gates, gate_w, up_w, received)


def add_kernel(count, left, right, *outs):
    for i, out in enumerate(outs):
        span = pl.ds(i * (left.shape[0] // count), left.shape[0] // count)
        out[...] = (
            left[span, :].astype(jnp.float32) + right[span, :].astype(jnp.float32)
        ).astype(jnp.bfloat16)


def add_rows(left, right, count):
    rows, width = left.shape
    return pl.pallas_call(
        functools.partial(add_kernel, count),
        out_shape=[jax.ShapeDtypeStruct((rows // count, width), jnp.bfloat16)] * count,
        in_specs=[VMEM] * 2,
        out_specs=[VMEM] * count,
        compiler_params=pltpu.CompilerParams(vmem_limit_bytes=4 * MIB + 8 * rows * width),
        name="add_rows",
    )(left, right)


def weight_kernel(chunk, factor, x, out, stage, sems):
    copies = []
    for i in range(x.shape[1] // chunk):
        span = pl.ds(i * chunk, chunk)
        stage[:, span] = jnp.dot(
            factor[...], x[:, span], preferred_element_type=jnp.float32
        ).astype(jnp.bfloat16)
        copies.append(pltpu.make_async_copy(stage.at[:, span], out.at[:, span], sems.at[i]))
        copies[-1].start()
    for copy in copies:
        copy.wait()


def weight_grad(factor, x):
    units, rows = factor.shape
    width = x.shape[1]
    chunk = 512 if width % 512 == 0 else width
    return pl.pallas_call(
        functools.partial(weight_kernel, chunk),
        out_shape=jax.ShapeDtypeStruct((units, width), jnp.bfloat16),
        in_specs=[VMEM] * 2,
        out_specs=HBM,
        scratch_shapes=[
            pltpu.VMEM((units, width), jnp.bfloat16),
            pltpu.SemaphoreType.DMA((width // chunk,)),
        ],
        compiler_params=pltpu.CompilerParams(vmem_limit_bytes=12 * MIB),
        cost_estimate=pl.CostEstimate(
            flops=2 * rows * units * width,
            bytes_accessed=2 * units * width,
            transcendentals=0,
        ),
        name="weight_grad",
    )(factor, x)


def combine_kernel(n_targets, first, second, choice_ref, gates_ref, *refs):
    blocks = refs[:n_targets]
    token_ref, gate_ref = refs[n_targets:]
    half = token_ref.shape[1] // 2
    choices, tokens = gates_ref.shape
    back = jnp.concatenate([block[...] for block in blocks], axis=0)
    rows = back[:, :half]
    token_ref[:, :half] = lax.dot_general(
        first[...], rows, CONTRACT_FIRST, preferred_element_type=jnp.float32
    ).astype(jnp.bfloat16)
    token_ref[:, half:] = lax.dot_general(
        second[...], rows, CONTRACT_FIRST, preferred_element_type=jnp.float32
    ).astype(jnp.bfloat16)
    terms = back[:, half : half + tokens].astype(jnp.float32)
    choice = choice_ref[...]
    for k in range(choices):
        chosen = jnp.where(choice == k, terms, 0.0)
        gate = gates_ref[k : k + 1, :].astype(jnp.float32)
        gate_ref[k : k + 1, :] = jnp.sum(chosen, axis=0, keepdims=True) / gate


def combine(n_targets, table, gates, blocks, width):
    choices, tokens = gates.shape
    return pl.pallas_call(
        functools.partial(combine_kernel, n_targets),
        out_shape=[
            jax.ShapeDtypeStruct((tokens, width), jnp.bfloat16),
            jax.ShapeDtypeStruct((choices, tokens), jnp.float32),
        ],
        in_specs=[VMEM] * (4 + n_targets),
        out_specs=[VMEM] * 2,
        compiler_params=pltpu.CompilerParams(
            vmem_limit_bytes=4 * MIB + 16 * n_targets * BLOCK * width
        ),
        name="combine",
    )(*table, gates, *blocks)


def flip(value, axis, bit):
    size = lax.axis_size(axis)
    return lax.ppermute(value, axis, [(i, i ^ bit) for i in range(size)])


def spread(block, bits):
    held = {0: block}
    for bit in bits:
        for mask in list(held):
            held[mask | bit] = flip(held[mask], "dp", bit)
    return held


def body(tokens, out_grad, gate_probs, route_ids, w_gate, w_up, w_down):
    n_targets = lax.axis_size("expert")
    n_dp = lax.axis_size("dp")
    width = tokens.shape[1]
    ids, gates = route_ids.T, gate_probs.T
    far_bits = [1 << i for i in range(1, n_dp.bit_length() - 1)]
    weights = (w_gate[0], w_up[0], w_down[0])

    sent = dispatch(n_targets, ids, gates, tokens, out_grad)
    arrived = [sent[0]] + [flip(sent[k], "expert", k) for k in range(1, n_targets)]
    ids_after, _ = lax.optimization_barrier((ids, sent[0]))
    arrived[-1], *table = lax.optimization_barrier((arrived[-1], *placement(n_targets, ids_after)))
    held = [spread(block, far_bits + [1]) for block in arrived]
    masks = sorted(held[0], key=lambda mask: (mask & 1, mask))
    pieces = [held[k][mask] for mask in masks for k in range(n_targets)]

    part, x, gate_f, up_f, down_f, low, high, gate_column = expert_rows(pieces, weights)
    received = flip(part, "dp", 1)
    grad_gate = weight_grad(gate_f, x)
    received, grad_gate = lax.optimization_barrier((received, grad_gate))
    mine = [mask for mask in masks if not mask & 1]
    sums = dict(
        zip(mine, own_rows(len(mine), low, high, gate_column, weights[0], weights[1], received))
    )
    grad_up = weight_grad(up_f, x)
    for bit in reversed(far_bits):
        moved = {mask: flip(sums.pop(mask), "dp", bit) for mask in list(sums) if mask & bit}
        if bit == far_bits[0]:
            moved, grad_up = lax.optimization_barrier((moved, grad_up))
        for mask, value in moved.items():
            count = n_targets if bit == far_bits[0] else 1
            total = add_rows(sums[mask ^ bit], value, count)
            sums[mask ^ bit] = total if count > 1 else total[0]
    blocks = sums[0]
    returned = [blocks[0]] + [flip(blocks[k], "expert", k) for k in range(1, n_targets)]
    grad_down = weight_grad(down_f, x)
    returned, grad_down = lax.optimization_barrier((returned, grad_down))
    token_grad, gate_grad = combine(n_targets, table, gates, returned, width)
    return (token_grad, gate_grad.T, grad_gate[None], grad_up[None], grad_down[None])


def solution(mesh):
    in_specs = (
        P(("expert", "dp"), None),
        P(("expert", "dp"), None),
        P(("expert", "dp"), None),
        P(("expert", "dp"), None),
        P("expert", "dp", None),
        P("expert", "dp", None),
        P("expert", "dp", None),
    )
    out_specs = (
        P(("expert", "dp"), None),
        P(("expert", "dp"), None),
        P("expert", "dp", None),
        P("expert", "dp", None),
        P("expert", "dp", None),
    )
    return jax.shard_map(body, mesh=mesh, in_specs=in_specs, out_specs=out_specs, check_vma=False)
```

time: 86 us -> 74 us (0.86)
  starting transfers between devices: 8 us -> 39.6 us
  blocking collectives: 21.6 us -> 0 us
  local copies, waits for them, and re-layouts: 11.8 us -> 1.34 us
  waiting for transfers between devices: 21.4 us -> 15.1 us
  other arithmetic: 2.76 us -> 0 us
  Pallas kernels: 19 us -> 16.9 us
    ppermute x6 -> x40, starting transfers between devices: 3.63 us -> 39.6 us  [flip(): return lax.ppermute(value, axis, [(i, i ^ bit) for i in range(size)])]
    all_to_all x1 -> x0, blocking collectives: 21.6 us -> none  [exchange(): lax.all_to_all(blocks, 'expert', split_axis=0, concat_axis=0, tiled=True)]
    unnamed x29 -> x14, local copies, waits for them, and re-layouts: 11.8 us -> 1.34 us
    ppermute x6 -> x40, waiting for transfers between devices: 21.4 us -> 15.1 us  [flip(): return lax.ppermute(value, axis, [(i, i ^ bit) for i in range(size)])]
    all_to_all x1 -> x0, starting transfers between devices: 4.37 us -> none  [exchange(): lax.all_to_all(blocks, 'expert', split_axis=0, concat_axis=0, tiled=True)]
    pallas_call x3 -> x8, Pallas kernels: 17.9 us -> 16 us  [the longest x3 5.97 us: weight_grad(): pl.pallas_call(functools.partial(weight_kernel, chunk), out_shape=jax.Sha...]
    reshape x1 -> x0, other arithmetic: 1.74 us -> none  [exchange(): blocks = value.reshape(n_targets, rows // n_targets, width)]
    add x1 -> x0, other arithmetic: 1.03 us -> none  [body(): sums[mask ^ bit] = sums[mask ^ bit] + flip(sums.pop(mask), 'dp', bit)]
  transfers between devices with their start and end apart: 7 -> 40, of which waited for: 4 -> 13; matrix products, arithmetic and copies ran while one was open for 1% -> 0% of each run, Pallas kernels for 7% -> 8%
where the time goes in v2:
time: 74 us; the launch traced here: 73.8 us
  starting transfers between devices  39.6 us (54%)
  Pallas kernels  16.9 us (23%)
  waiting for transfers between devices  15.1 us (20%)
  local copies, waits for them, and re-layouts  1.34 us (2%)
  between operations  0.81 us (1%)
    ppermute x40, starting transfers between devices, flip(): return lax.ppermute(value, axis, [(i, i ^ bit) for i in range(size)])  39.6 us
    ppermute x40, waiting for transfers between devices, flip(): return lax.ppermute(value, axis, [(i, i ^ bit) for i in range(size)])  15.1 us
    pallas_call x3, Pallas kernels, weight_grad(): pl.pallas_call(functools.partial(weight_kernel, chunk), out_shape=jax.Sha...  5.97 us
    pallas_call x1, Pallas kernels, expert_rows(): pl.pallas_call(functools.partial(expert_kernel, count), out_shape=[jax.Sh...  5.49 us
    pallas_call x1, Pallas kernels, dispatch(): pl.pallas_call(functools.partial(dispatch_kernel, n_targets), out_shape=[...  2.43 us
    pallas_call x1, Pallas kernels, own_rows(): pl.pallas_call(functools.partial(own_kernel, groups), out_shape=[jax.Shap...  1.83 us
  transfers between devices with their start and end apart: 40, of which 13 were waited for; matrix products, arithmetic and copies ran while one was open for 0% of the time, Pallas kernels for 8%

profile of v2, /device:TPU:0, one launch (start us, length us, event | category | flops | bytes accessed | tf_op | source)
XLA Modules:
  0.0 73.8 jit_solution(8278959512681034177)
XLA Ops:
  0.6 2.4 %dispatch.1 = (bf16[8,4096]{1,0:T(8,128)(2,1)}, bf16[8,4096]{1,0:T(8,128)(2,1)}, bf16[8,4096]{1,0:T(8,128)(2,1)}, bf16[8,4096]{1,0:T(8,128)(2,1)}, bf16[8,4096]{...) custom-call(s32[8,32]{1,0:T(8,128)} %bitcast.15, ...), custom_call_target="tpu_custom_call" | custom-call | tf_op jit(solution)/shard_map/dispatch/pallas_call | solution.py:83
  3.1 6.1 %collective-permute-start = (bf16[8,4096]{1,0:T(8,128)(2,1)}, bf16[8,4096]{1,0:T(8,128)(2,1)S(1)}, u32[]{:S(2)}, u32[]{:S(2)}) collective-permute-start(bf16[8,4096]{1,0:T(8,128)(2,1)} %get-tuple-element.54), channel_id=1, source_target_pairs={{0,28},{4,24},{8,20},{12,16},{16,12},{20,8},{24,4},{28,0},{1,29},{... | collective-permute-start | bytes 196616 | tf_op jit(solution)/shard_map/ppermute | solution.py:358
  9.6 3.0 %collective-permute-start.3 = (bf16[8,4096]{1,0:T(8,128)(2,1)}, bf16[8,4096]{1,0:T(8,128)(2,1)S(1)}, u32[]{:S(2)}, u32[]{:S(2)}) collective-permute-start(bf16[8,4096]{1,0:T(8,128)(2,1)} %get-tuple-element.65), channel_id=1, source_target_pairs={{0,12},{4,8},{8,4},{12,0},{16,28},{20,24},{24,20},{28,16},{1,13},{... | collective-permute-start | bytes 196616 | tf_op jit(solution)/shard_map/ppermute | solution.py:358
  12.6 2.9 %collective-permute-start.5 = (bf16[8,4096]{1,0:T(8,128)(2,1)}, bf16[8,4096]{1,0:T(8,128)(2,1)S(1)}, u32[]{:S(2)}, u32[]{:S(2)}) collective-permute-start(bf16[8,4096]{1,0:T(8,128)(2,1)} %get-tuple-element.67), channel_id=1, source_target_pairs={{0,20},{4,16},{8,28},{12,24},{16,4},{20,0},{24,12},{28,8},{1,21},{... | collective-permute-start | bytes 196616 | tf_op jit(solution)/shard_map/ppermute | solution.py:358
  18.1 1.6 %collective-permute-start.7 = (bf16[8,4096]{1,0:T(8,128)(2,1)S(1)}, bf16[8,4096]{1,0:T(8,128)(2,1)S(1)}, u32[]{:S(2)}, u32[]{:S(2)}) collective-permute-start(bf16[8,4096]{1,0:T(8,128)(2,1)S(1)} %copy-done.5), channel_id=1, source_target_pairs={{0,2},{1,3},{2,0},{3,1},{4,6},{5,7},{6,4},{7,5},{8,10},{9,11},{10,... | collective-permute-start | bytes 196616 | tf_op jit(solution)/shard_map/ppermute | solution.py:358
  19.8 2.0 %collective-permute-done.5.refs_5_ = bf16[8,4096]{1,0:T(8,128)(2,1)S(1)} collective-permute-done((bf16[8,4096]{1,0:T(8,128)(2,1)}, bf16[8,4096]{1,0:T(8,128)(2,1)S(1)}, u32[]{:S(2)}, u32[]{:S(2)}) %collective-permute-start.5) | collective-permute-done | bytes 65568 | tf_op jit(solution)/shard_map/ppermute | solution.py:358
  21.8 1.5 %collective-permute-start.14 = (bf16[8,4096]{1,0:T(8,128)(2,1)S(1)}, bf16[8,4096]{1,0:T(8,128)(2,1)S(1)}, u32[]{:S(2)}, u32[]{:S(2)}) collective-permute-start(bf16[8,4096]{1,0:T(8,128)(2,1)S(1)} %collective-permute-done.refs_7_), channel_id=1, source_target_pairs={{0,2},{1,3},{2,0},{3,1},{4,6},{5,7},{6,4},{7,5},{8,10},{9,11},{10,... | collective-permute-start | bytes 196616 | tf_op jit(solution)/shard_map/ppermute | solution.py:358
  23.3 1.4 %collective-permute-start.8 = (bf16[8,4096]{1,0:T(8,128)(2,1)S(1)}, bf16[8,4096]{1,0:T(8,128)(2,1)S(1)}, u32[]{:S(2)}, u32[]{:S(2)}) collective-permute-start(bf16[8,4096]{1,0:T(8,128)(2,1)S(1)} %collective-permute-done.1.refs_1_), channel_id=1, source_target_pairs={{0,2},{1,3},{2,0},{3,1},{4,6},{5,7},{6,4},{7,5},{8,10},{9,11},{10,... | collective-permute-start | bytes 196616 | tf_op jit(solution)/shard_map/ppermute | solution.py:358
  26.1 1.5 %collective-permute-start.10 = (bf16[8,4096]{1,0:T(8,128)(2,1)S(1)}, bf16[8,4096]{1,0:T(8,128)(2,1)S(1)}, u32[]{:S(2)}, u32[]{:S(2)}) collective-permute-start(bf16[8,4096]{1,0:T(8,128)(2,1)S(1)} %collective-permute-done.3.refs_3_), channel_id=1, source_target_pairs={{0,2},{1,3},{2,0},{3,1},{4,6},{5,7},{6,4},{7,5},{8,10},{9,11},{10,... | collective-permute-start | bytes 196616 | tf_op jit(solution)/shard_map/ppermute | solution.py:358
  27.9 1.7 %collective-permute-start.11 = (bf16[8,4096]{1,0:T(8,128)(2,1)S(1)}, bf16[8,4096]{1,0:T(8,128)(2,1)S(1)}, u32[]{:S(2)}, u32[]{:S(2)}) collective-permute-start(bf16[8,4096]{1,0:T(8,128)(2,1)S(1)} %collective-permute-done.4.refs_4_), channel_id=1, source_target_pairs={{0,2},{1,3},{2,0},{3,1},{4,6},{5,7},{6,4},{7,5},{8,10},{9,11},{10,... | collective-permute-start | bytes 196616 | tf_op jit(solution)/shard_map/ppermute | solution.py:358
  30.8 1.3 %collective-permute-start.13 = (bf16[8,4096]{1,0:T(8,128)(2,1)S(1)}, bf16[8,4096]{1,0:T(8,128)(2,1)S(1)}, u32[]{:S(2)}, u32[]{:S(2)}) collective-permute-start(bf16[8,4096]{1,0:T(8,128)(2,1)S(1)} %collective-permute-done.6.refs_6_), channel_id=1, source_target_pairs={{0,2},{1,3},{2,0},{3,1},{4,6},{5,7},{6,4},{7,5},{8,10},{9,11},{10,... | collective-permute-start | bytes 196616 | tf_op jit(solution)/shard_map/ppermute | solution.py:358
  32.9 1.6 %collective-permute-done.12.refs_13_ = bf16[8,4096]{1,0:T(8,128)(2,1)S(1)} collective-permute-done((bf16[8,4096]{1,0:T(8,128)(2,1)S(1)}, bf16[8,4096]{1,0:T(8,128)(2,1)S(1)}, u32[]{:S(2)}, u32[]{:S(2)}) %collective-permute-start.12) | collective-permute-done | bytes 65568 | tf_op jit(solution)/shard_map/ppermute | solution.py:358
  37.5 5.5 %expert_rows.1 = (bf16[128,2176]{1,0:T(8,128)(2,1)S(1)}, bf16[256,4096]{1,0:T(8,128)(2,1)S(1)}, bf16[384,256]{1,0:T(8,128)(2,1)S(1)}, bf16[384,256]{1,0:T(8,128)...) custom-call(bf16[8,4096]{1,0:T(8,128)(2,1)S(1)} %copy-done.5, ...), custom_call_target="tpu_custom_call" | custom-call | flops 3221225472 | bytes 9437184 | tf_op jit(solution)/shard_map/expert_rows/pallas_call | solution.py:212
  43.4 2.0 %weight_grad.3 = bf16[384,4096]{1,0:T(8,128)(2,1)} custom-call(bf16[384,256]{1,0:T(8,128)(2,1)S(1)} %get-tuple-element.74.factor, bf16[256,4096]{1,0:T(8,128)(2,1)S(1)} %get-tuple-element.75.x), custom_call_target="tpu_custom_call" | custom-call | flops 805306368 | bytes 3145728 | tf_op jit(solution)/shard_map/weight_grad/pallas_call | solution.py:299
  45.4 1.8 %own_rows.1 = (bf16[64,2176]{1,0:T(8,128)(2,1)S(1)}, bf16[64,2176]{1,0:T(8,128)(2,1)S(1)}) custom-call(bf16[128,768]{1,0:T(8,128)(2,1)S(1)} %get-tuple-element.70.low, bf16[128,768]{1,0:T(8,128)(2,1)S(1)} %get-tuple-element.71.high, bf16[128,128]{1,0:T(8,128)(2,1)S(1)} %get-tuple-element.72.gates, bf16[384,4096]{1,0:T(8,128)(2,1)S(1)} %bitcast.10, ...), custom_call_target="tpu_custom_call" | custom-call | flops 805306368 | bytes 6291456 | tf_op jit(solution)/shard_map/own_rows/pallas_call | solution.py:247
  47.2 1.4 %collective-permute-start.32 = (bf16[64,2176]{1,0:T(8,128)(2,1)S(1)}, bf16[64,2176]{1,0:T(8,128)(2,1)S(1)}, u32[]{:S(2)}, u32[]{:S(2)}) collective-permute-start(bf16[64,2176]{1,0:T(8,128)(2,1)S(1)} %get-tuple-element.78), channel_id=1, source_target_pairs={{0,2},{1,3},{2,0},{3,1},{4,6},{5,7},{6,4},{7,5},{8,10},{9,11},{10,... | collective-permute-start | bytes 835592 | tf_op jit(solution)/shard_map/ppermute | solution.py:358
  48.7 2.0 %weight_grad.4 = bf16[384,4096]{1,0:T(8,128)(2,1)} custom-call(bf16[384,256]{1,0:T(8,128)(2,1)S(1)} %get-tuple-element.79.factor, bf16[256,4096]{1,0:T(8,128)(2,1)S(1)} %get-tuple-element.75.x), custom_call_target="tpu_custom_call" | custom-call | flops 805306368 | bytes 3145728 | tf_op jit(solution)/shard_map/weight_grad/pallas_call | solution.py:299
  50.7 5.3 %collective-permute-done.32.right = bf16[64,2176]{1,0:T(8,128)(2,1)S(1)} collective-permute-done((bf16[64,2176]{1,0:T(8,128)(2,1)S(1)}, bf16[64,2176]{1,0:T(8,128)(2,1)S(1)}, u32[]{:S(2)}, u32[]{:S(2)}) %collective-permute-start.32) | collective-permute-done | bytes 278560 | tf_op jit(solution)/shard_map/ppermute | solution.py:358
  56.1 1.5 %collective-permute-start.33 = (bf16[8,2176]{1,0:T(8,128)(2,1)S(1)}, bf16[8,2176]{1,0:T(8,128)(2,1)S(1)}, u32[]{:S(2)}, u32[]{:S(2)}) collective-permute-start(bf16[8,2176]{1,0:T(8,128)(2,1)S(1)} %get-tuple-element.82), channel_id=1, source_target_pairs={{0,4},{4,0},{8,12},{12,8},{16,20},{20,16},{24,28},{28,24},{1,5},{5... | collective-permute-start | bytes 104456 | tf_op jit(solution)/shard_map/ppermute | solution.py:358
  57.6 2.1 %collective-permute-start.35 = (bf16[8,2176]{1,0:T(8,128)(2,1)S(1)}, bf16[8,2176]{1,0:T(8,128)(2,1)S(1)}, u32[]{:S(2)}, u32[]{:S(2)}) collective-permute-start(bf16[8,2176]{1,0:T(8,128)(2,1)S(1)} %get-tuple-element.84), channel_id=1, source_target_pairs={{0,12},{4,8},{8,4},{12,0},{16,28},{20,24},{24,20},{28,16},{1,13},{... | collective-permute-start | bytes 104456 | tf_op jit(solution)/shard_map/ppermute | solution.py:358
  60.9 2.5 %collective-permute-start.37 = (bf16[8,2176]{1,0:T(8,128)(2,1)S(1)}, bf16[8,2176]{1,0:T(8,128)(2,1)S(1)}, u32[]{:S(2)}, u32[]{:S(2)}) collective-permute-start(bf16[8,2176]{1,0:T(8,128)(2,1)S(1)} %get-tuple-element.86), channel_id=1, source_target_pairs={{0,20},{4,16},{8,28},{12,24},{16,4},{20,0},{24,12},{28,8},{1,21},{... | collective-permute-start | bytes 104456 | tf_op jit(solution)/shard_map/ppermute | solution.py:358
  63.4 2.7 %collective-permute-start.38 = (bf16[8,2176]{1,0:T(8,128)(2,1)S(1)}, bf16[8,2176]{1,0:T(8,128)(2,1)S(1)}, u32[]{:S(2)}, u32[]{:S(2)}) collective-permute-start(bf16[8,2176]{1,0:T(8,128)(2,1)S(1)} %get-tuple-element.87), channel_id=1, source_target_pairs={{0,24},{4,28},{8,16},{12,20},{16,8},{20,12},{24,0},{28,4},{1,25},{... | collective-permute-start | bytes 104456 | tf_op jit(solution)/shard_map/ppermute | solution.py:358
  67.3 2.0 %weight_grad.5 = bf16[384,4096]{1,0:T(8,128)(2,1)} custom-call(bf16[384,256]{1,0:T(8,128)(2,1)S(1)} %get-tuple-element.89.factor, bf16[256,4096]{1,0:T(8,128)(2,1)S(1)} %get-tuple-element.75.x), custom_call_target="tpu_custom_call" | custom-call | flops 805306368 | bytes 3145728 | tf_op jit(solution)/shard_map/weight_grad/pallas_call | solution.py:299
  69.3 3.5 %collective-permute-done.39.refs_7_ = bf16[8,2176]{1,0:T(8,128)(2,1)S(1)} collective-permute-done((bf16[8,2176]{1,0:T(8,128)(2,1)S(1)}, bf16[8,2176]{1,0:T(8,128)(2,1)S(1)}, u32[]{:S(2)}, u32[]{:S(2)}) %collective-permute-start.39) | collective-permute-done | bytes 34848 | tf_op jit(solution)/shard_map/ppermute | solution.py:358
  (79 shorter events, 13.8 us)
Async XLA Ops:
  3.1 9.6 %collective-permute-start = (bf16[8,4096]{1,0:T(8,128)(2,1)}, bf16[8,4096]{1,0:T(8,128)(2,1)S(1)}, u32[]{:S(2)}, u32[]{:S(2)}) collective-permute-start(bf16[8,4096]{1,0:T(8,128)(2,1)} %get-tuple-element.54), channel_id=1, source_target_pairs={{0,28},{4,24},{8,20},{12,16},{16,12},{20,8},{24,4},{28,0},{1,29},{... | collective-permute-start | bytes 196616 | tf_op jit(solution)/shard_map/ppermute | solution.py:358
  9.1 7.3 %collective-permute-start.1 = (bf16[8,4096]{1,0:T(8,128)(2,1)}, bf16[8,4096]{1,0:T(8,128)(2,1)S(1)}, u32[]{:S(2)}, u32[]{:S(2)}) collective-permute-start(bf16[8,4096]{1,0:T(8,128)(2,1)} %get-tuple-element.63), channel_id=1, source_target_pairs={{0,4},{4,0},{8,12},{12,8},{16,20},{20,16},{24,28},{28,24},{1,5},{5... | collective-permute-start | bytes 196616 | tf_op jit(solution)/shard_map/ppermute | solution.py:358
  9.6 8.4 %collective-permute-start.2 = (bf16[8,4096]{1,0:T(8,128)(2,1)}, bf16[8,4096]{1,0:T(8,128)(2,1)S(1)}, u32[]{:S(2)}, u32[]{:S(2)}) collective-permute-start(bf16[8,4096]{1,0:T(8,128)(2,1)} %get-tuple-element.64), channel_id=1, source_target_pairs={{0,8},{4,12},{8,0},{12,4},{16,24},{20,28},{24,16},{28,20},{1,9},{5... | collective-permute-start | bytes 196616 | tf_op jit(solution)/shard_map/ppermute | solution.py:358
  9.6 8.4 %collective-permute-start.3 = (bf16[8,4096]{1,0:T(8,128)(2,1)}, bf16[8,4096]{1,0:T(8,128)(2,1)S(1)}, u32[]{:S(2)}, u32[]{:S(2)}) collective-permute-start(bf16[8,4096]{1,0:T(8,128)(2,1)} %get-tuple-element.65), channel_id=1, source_target_pairs={{0,12},{4,8},{8,4},{12,0},{16,28},{20,24},{24,20},{28,16},{1,13},{... | collective-permute-start | bytes 196616 | tf_op jit(solution)/shard_map/ppermute | solution.py:358
  12.6 7.1 %collective-permute-start.4 = (bf16[8,4096]{1,0:T(8,128)(2,1)}, bf16[8,4096]{1,0:T(8,128)(2,1)S(1)}, u32[]{:S(2)}, u32[]{:S(2)}) collective-permute-start(bf16[8,4096]{1,0:T(8,128)(2,1)} %get-tuple-element.66), channel_id=1, source_target_pairs={{0,16},{4,20},{8,24},{12,28},{16,0},{20,4},{24,8},{28,12},{1,17},{... | collective-permute-start | bytes 196616 | tf_op jit(solution)/shard_map/ppermute | solution.py:358
  12.6 9.2 %collective-permute-start.5 = (bf16[8,4096]{1,0:T(8,128)(2,1)}, bf16[8,4096]{1,0:T(8,128)(2,1)S(1)}, u32[]{:S(2)}, u32[]{:S(2)}) collective-permute-start(bf16[8,4096]{1,0:T(8,128)(2,1)} %get-tuple-element.67), channel_id=1, source_target_pairs={{0,20},{4,16},{8,28},{12,24},{16,4},{20,0},{24,12},{28,8},{1,21},{... | collective-permute-start | bytes 196616 | tf_op jit(solution)/shard_map/ppermute | solution.py:358
  17.0 6.3 %collective-permute-start.6 = (bf16[8,4096]{1,0:T(8,128)(2,1)S(1)}, bf16[8,4096]{1,0:T(8,128)(2,1)S(1)}, u32[]{:S(2)}, u32[]{:S(2)}) collective-permute-start(bf16[8,4096]{1,0:T(8,128)(2,1)S(1)} %copy-done.6), channel_id=1, source_target_pairs={{0,24},{4,28},{8,16},{12,20},{16,8},{20,12},{24,0},{28,4},{1,25},{... | collective-permute-start | bytes 196616 | tf_op jit(solution)/shard_map/ppermute | solution.py:358
  18.1 5.3 %collective-permute-start.15 = (bf16[8,4096]{1,0:T(8,128)(2,1)S(1)}, bf16[8,4096]{1,0:T(8,128)(2,1)S(1)}, u32[]{:S(2)}, u32[]{:S(2)}) collective-permute-start(bf16[8,4096]{1,0:T(8,128)(2,1)S(1)} %copy-done.5), channel_id=1, source_target_pairs={{0,1},{1,0},{2,3},{3,2},{4,5},{5,4},{6,7},{7,6},{8,9},{9,8},{10,11... | collective-permute-start | bytes 196616 | tf_op jit(solution)/shard_map/ppermute | solution.py:358
  18.1 6.6 %collective-permute-start.7 = (bf16[8,4096]{1,0:T(8,128)(2,1)S(1)}, bf16[8,4096]{1,0:T(8,128)(2,1)S(1)}, u32[]{:S(2)}, u32[]{:S(2)}) collective-permute-start(bf16[8,4096]{1,0:T(8,128)(2,1)S(1)} %copy-done.5), channel_id=1, source_target_pairs={{0,2},{1,3},{2,0},{3,1},{4,6},{5,7},{6,4},{7,5},{8,10},{9,11},{10,... | collective-permute-start | bytes 196616 | tf_op jit(solution)/shard_map/ppermute | solution.py:358
  19.7 5.2 %collective-permute-start.22 = (bf16[8,4096]{1,0:T(8,128)(2,1)S(1)}, bf16[8,4096]{1,0:T(8,128)(2,1)S(1)}, u32[]{:S(2)}, u32[]{:S(2)}) collective-permute-start(bf16[8,4096]{1,0:T(8,128)(2,1)S(1)} %collective-permute-done.refs_7_), channel_id=1, source_target_pairs={{0,1},{1,0},{2,3},{3,2},{4,5},{5,4},{6,7},{7,6},{8,9},{9,8},{10,11... | collective-permute-start | bytes 196616 | tf_op jit(solution)/shard_map/ppermute | solution.py:358
  23.3 4.6 %collective-permute-start.8 = (bf16[8,4096]{1,0:T(8,128)(2,1)S(1)}, bf16[8,4096]{1,0:T(8,128)(2,1)S(1)}, u32[]{:S(2)}, u32[]{:S(2)}) collective-permute-start(bf16[8,4096]{1,0:T(8,128)(2,1)S(1)} %collective-permute-done.1.refs_1_), channel_id=1, source_target_pairs={{0,2},{1,3},{2,0},{3,1},{4,6},{5,7},{6,4},{7,5},{8,10},{9,11},{10,... | collective-permute-start | bytes 196616 | tf_op jit(solution)/shard_map/ppermute | solution.py:358
  24.9 4.7 %collective-permute-start.9 = (bf16[8,4096]{1,0:T(8,128)(2,1)S(1)}, bf16[8,4096]{1,0:T(8,128)(2,1)S(1)}, u32[]{:S(2)}, u32[]{:S(2)}) collective-permute-start(bf16[8,4096]{1,0:T(8,128)(2,1)S(1)} %collective-permute-done.2.refs_2_), channel_id=1, source_target_pairs={{0,2},{1,3},{2,0},{3,1},{4,6},{5,7},{6,4},{7,5},{8,10},{9,11},{10,... | collective-permute-start | bytes 196616 | tf_op jit(solution)/shard_map/ppermute | solution.py:358
  26.1 4.5 %collective-permute-start.10 = (bf16[8,4096]{1,0:T(8,128)(2,1)S(1)}, bf16[8,4096]{1,0:T(8,128)(2,1)S(1)}, u32[]{:S(2)}, u32[]{:S(2)}) collective-permute-start(bf16[8,4096]{1,0:T(8,128)(2,1)S(1)} %collective-permute-done.3.refs_3_), channel_id=1, source_target_pairs={{0,2},{1,3},{2,0},{3,1},{4,6},{5,7},{6,4},{7,5},{8,10},{9,11},{10,... | collective-permute-start | bytes 196616 | tf_op jit(solution)/shard_map/ppermute | solution.py:358
  27.9 4.5 %collective-permute-start.11 = (bf16[8,4096]{1,0:T(8,128)(2,1)S(1)}, bf16[8,4096]{1,0:T(8,128)(2,1)S(1)}, u32[]{:S(2)}, u32[]{:S(2)}) collective-permute-start(bf16[8,4096]{1,0:T(8,128)(2,1)S(1)} %collective-permute-done.4.refs_4_), channel_id=1, source_target_pairs={{0,2},{1,3},{2,0},{3,1},{4,6},{5,7},{6,4},{7,5},{8,10},{9,11},{10,... | collective-permute-start | bytes 196616 | tf_op jit(solution)/shard_map/ppermute | solution.py:358
  29.8 4.7 %collective-permute-start.12 = (bf16[8,4096]{1,0:T(8,128)(2,1)S(1)}, bf16[8,4096]{1,0:T(8,128)(2,1)S(1)}, u32[]{:S(2)}, u32[]{:S(2)}) collective-permute-start(bf16[8,4096]{1,0:T(8,128)(2,1)S(1)} %collective-permute-done.5.refs_5_), channel_id=1, source_target_pairs={{0,2},{1,3},{2,0},{3,1},{4,6},{5,7},{6,4},{7,5},{8,10},{9,11},{10,... | collective-permute-start | bytes 196616 | tf_op jit(solution)/shard_map/ppermute | solution.py:358
  30.8 4.7 %collective-permute-start.13 = (bf16[8,4096]{1,0:T(8,128)(2,1)S(1)}, bf16[8,4096]{1,0:T(8,128)(2,1)S(1)}, u32[]{:S(2)}, u32[]{:S(2)}) collective-permute-start(bf16[8,4096]{1,0:T(8,128)(2,1)S(1)} %collective-permute-done.6.refs_6_), channel_id=1, source_target_pairs={{0,2},{1,3},{2,0},{3,1},{4,6},{5,7},{6,4},{7,5},{8,10},{9,11},{10,... | collective-permute-start | bytes 196616 | tf_op jit(solution)/shard_map/ppermute | solution.py:358
  47.2 8.8 %collective-permute-start.32 = (bf16[64,2176]{1,0:T(8,128)(2,1)S(1)}, bf16[64,2176]{1,0:T(8,128)(2,1)S(1)}, u32[]{:S(2)}, u32[]{:S(2)}) collective-permute-start(bf16[64,2176]{1,0:T(8,128)(2,1)S(1)} %get-tuple-element.78), channel_id=1, source_target_pairs={{0,2},{1,3},{2,0},{3,1},{4,6},{5,7},{6,4},{7,5},{8,10},{9,11},{10,... | collective-permute-start | bytes 835592 | tf_op jit(solution)/shard_map/ppermute | solution.py:358
  56.1 7.3 %collective-permute-start.33 = (bf16[8,2176]{1,0:T(8,128)(2,1)S(1)}, bf16[8,2176]{1,0:T(8,128)(2,1)S(1)}, u32[]{:S(2)}, u32[]{:S(2)}) collective-permute-start(bf16[8,2176]{1,0:T(8,128)(2,1)S(1)} %get-tuple-element.82), channel_id=1, source_target_pairs={{0,4},{4,0},{8,12},{12,8},{16,20},{20,16},{24,28},{28,24},{1,5},{5... | collective-permute-start | bytes 104456 | tf_op jit(solution)/shard_map/ppermute | solution.py:358
  57.6 8.6 %collective-permute-start.34 = (bf16[8,2176]{1,0:T(8,128)(2,1)S(1)}, bf16[8,2176]{1,0:T(8,128)(2,1)S(1)}, u32[]{:S(2)}, u32[]{:S(2)}) collective-permute-start(bf16[8,2176]{1,0:T(8,128)(2,1)S(1)} %get-tuple-element.83), channel_id=1, source_target_pairs={{0,8},{4,12},{8,0},{12,4},{16,24},{20,28},{24,16},{28,20},{1,9},{5... | collective-permute-start | bytes 104456 | tf_op jit(solution)/shard_map/ppermute | solution.py:358
  57.6 11.7 %collective-permute-start.35 = (bf16[8,2176]{1,0:T(8,128)(2,1)S(1)}, bf16[8,2176]{1,0:T(8,128)(2,1)S(1)}, u32[]{:S(2)}, u32[]{:S(2)}) collective-permute-start(bf16[8,2176]{1,0:T(8,128)(2,1)S(1)} %get-tuple-element.84), channel_id=1, source_target_pairs={{0,12},{4,8},{8,4},{12,0},{16,28},{20,24},{24,20},{28,16},{1,13},{... | collective-permute-start | bytes 104456 | tf_op jit(solution)/shard_map/ppermute | solution.py:358
  59.6 9.7 %collective-permute-start.36 = (bf16[8,2176]{1,0:T(8,128)(2,1)S(1)}, bf16[8,2176]{1,0:T(8,128)(2,1)S(1)}, u32[]{:S(2)}, u32[]{:S(2)}) collective-permute-start(bf16[8,2176]{1,0:T(8,128)(2,1)S(1)} %get-tuple-element.85), channel_id=1, source_target_pairs={{0,16},{4,20},{8,24},{12,28},{16,0},{20,4},{24,8},{28,12},{1,17},{... | collective-permute-start | bytes 104456 | tf_op jit(solution)/shard_map/ppermute | solution.py:358
  60.9 8.4 %collective-permute-start.37 = (bf16[8,2176]{1,0:T(8,128)(2,1)S(1)}, bf16[8,2176]{1,0:T(8,128)(2,1)S(1)}, u32[]{:S(2)}, u32[]{:S(2)}) collective-permute-start(bf16[8,2176]{1,0:T(8,128)(2,1)S(1)} %get-tuple-element.86), channel_id=1, source_target_pairs={{0,20},{4,16},{8,28},{12,24},{16,4},{20,0},{24,12},{28,8},{1,21},{... | collective-permute-start | bytes 104456 | tf_op jit(solution)/shard_map/ppermute | solution.py:358
  63.4 5.9 %collective-permute-start.38 = (bf16[8,2176]{1,0:T(8,128)(2,1)S(1)}, bf16[8,2176]{1,0:T(8,128)(2,1)S(1)}, u32[]{:S(2)}, u32[]{:S(2)}) collective-permute-start(bf16[8,2176]{1,0:T(8,128)(2,1)S(1)} %get-tuple-element.87), channel_id=1, source_target_pairs={{0,24},{4,28},{8,16},{12,20},{16,8},{20,12},{24,0},{28,4},{1,25},{... | collective-permute-start | bytes 104456 | tf_op jit(solution)/shard_map/ppermute | solution.py:358
  66.2 6.6 %collective-permute-start.39 = (bf16[8,2176]{1,0:T(8,128)(2,1)S(1)}, bf16[8,2176]{1,0:T(8,128)(2,1)S(1)}, u32[]{:S(2)}, u32[]{:S(2)}) collective-permute-start(bf16[8,2176]{1,0:T(8,128)(2,1)S(1)} %get-tuple-element.88), channel_id=1, source_target_pairs={{0,28},{4,24},{8,20},{12,16},{16,12},{20,8},{24,4},{28,0},{1,29},{... | collective-permute-start | bytes 104456 | tf_op jit(solution)/shard_map/ppermute | solution.py:358
  (23 other events, 138.0 us)

commit v3 on v2

v3 whole, which is shorter than its diff:
```python
import functools

import jax
import jax.numpy as jnp
from jax import lax
from jax.experimental import pallas as pl
from jax.experimental.pallas import tpu as pltpu
from jax.sharding import PartitionSpec as P

EXPERTS = 128
CAP = 4
BLOCK = 2 * CAP
LANES = 128
MIB = 2**20
COVER = 12

CONTRACT_LAST = (((1,), (1,)), ((), ()))
CONTRACT_FIRST = (((0,), (0,)), ((), ()))

HBM = pl.BlockSpec(memory_space=pltpu.HBM)
VMEM = pl.BlockSpec(memory_space=pltpu.VMEM)


def struct(shape, dtype=jnp.bfloat16):
    return jax.ShapeDtypeStruct(shape, dtype)


def as_bf16(mask):
    return mask.astype(jnp.float32).astype(jnp.bfloat16)


def choice_table(ids, n_targets):
    choices, tokens = ids.shape
    height = n_targets * BLOCK
    per_device = EXPERTS // n_targets
    row = lax.broadcasted_iota(jnp.int32, (height, 1), 0)
    wanted = (row // BLOCK) * per_device
    slot = row % BLOCK
    matches = [ids[k : k + 1, :] == wanted for k in range(choices)]
    hit = functools.reduce(jnp.logical_or, matches)
    earlier = lax.broadcasted_iota(jnp.int32, (tokens, tokens), 0) < lax.broadcasted_iota(
        jnp.int32, (tokens, tokens), 1
    )
    rank = jnp.dot(as_bf16(hit), as_bf16(earlier), preferred_element_type=jnp.float32)
    rank = rank.astype(jnp.int32)
    first = jnp.logical_and(hit, rank == slot)
    second = jnp.logical_and(hit, rank == slot - CAP)
    return matches, first, second


def pick_rows(first, second, rows_ref):
    half = rows_ref.shape[1] // 2
    low = jnp.dot(first, rows_ref[:, :half], preferred_element_type=jnp.float32)
    high = jnp.dot(second, rows_ref[:, half:], preferred_element_type=jnp.float32)
    return (low + high).astype(jnp.bfloat16)


def send_tokens_kernel(n_targets, ids_hbm, tokens_hbm, out, ids_ref, tokens_ref, sems):
    ids_copy = pltpu.make_async_copy(ids_hbm, ids_ref, sems.at[0])
    tokens_copy = pltpu.make_async_copy(tokens_hbm, tokens_ref, sems.at[1])
    ids_copy.start()
    tokens_copy.start()
    ids_copy.wait()
    _, first, second = choice_table(ids_ref[...], n_targets)
    tokens_copy.wait()
    out[...] = pick_rows(as_bf16(first), as_bf16(second), tokens_ref)


def send_tokens(n_targets, ids, tokens):
    return pl.pallas_call(
        functools.partial(send_tokens_kernel, n_targets),
        out_shape=struct((n_targets * BLOCK, tokens.shape[1] // 2)),
        in_specs=[HBM] * 2,
        out_specs=VMEM,
        scratch_shapes=[pltpu.VMEM(a.shape, a.dtype) for a in (ids, tokens)]
        + [pltpu.SemaphoreType.DMA((2,))],
        compiler_params=pltpu.CompilerParams(vmem_limit_bytes=60 * MIB),
        name="send_tokens",
    )(ids, tokens)


def send_grads_kernel(n_targets, ids_ref, gates_ref, grads_ref, out):
    matches, first, second = choice_table(ids_ref[...], n_targets)
    gates = gates_ref[...].astype(jnp.float32)
    scale = jnp.zeros(first.shape, jnp.float32)
    for k, match in enumerate(matches):
        scale = scale + jnp.where(match, gates[k : k + 1, :], 0.0)
    first = jnp.where(first, scale, 0.0).astype(jnp.bfloat16)
    second = jnp.where(second, scale, 0.0).astype(jnp.bfloat16)
    out[...] = pick_rows(first, second, grads_ref)


def send_grads(n_targets, ids, gates, out_grad):
    return pl.pallas_call(
        functools.partial(send_grads_kernel, n_targets),
        out_shape=struct((n_targets * BLOCK, out_grad.shape[1] // 2)),
        in_specs=[VMEM] * 3,
        out_specs=VMEM,
        compiler_params=pltpu.CompilerParams(
            vmem_limit_bytes=4 * MIB + 8 * n_targets * BLOCK * out_grad.shape[1]
        ),
        name="send_grads",
    )(ids, gates, out_grad)


def placement_kernel(n_targets, ids_ref, first_ref, second_ref, choice_ref):
    matches, first, second = choice_table(ids_ref[...], n_targets)
    first_ref[...] = as_bf16(first)
    second_ref[...] = as_bf16(second)
    choice = jnp.full(first.shape, -1, jnp.int32)
    for k, match in enumerate(matches):
        choice = jnp.where(jnp.logical_and(match, first), k, choice)
    choice_ref[...] = choice


def placement(n_targets, ids):
    table = (n_targets * BLOCK, ids.shape[1])
    return pl.pallas_call(
        functools.partial(placement_kernel, n_targets),
        out_shape=[struct(table), struct(table), struct(table, jnp.int32)],
        in_specs=[VMEM],
        out_specs=[VMEM] * 3,
        compiler_params=pltpu.CompilerParams(vmem_limit_bytes=4 * MIB),
        cost_estimate=pl.CostEstimate(
            flops=COVER * 10**9, bytes_accessed=COVER * 10**6, transcendentals=0
        ),
        name="placement",
    )(ids)


def gather_pieces(pieces, out):
    block = pieces[0].shape[0]
    for i, piece in enumerate(pieces):
        out[pl.ds(i * block, block), :] = piece[...]


def project(weight, halves):
    half = halves.shape[1]
    rows = halves.shape[0]
    low = lax.dot_general(
        weight[:, :half], halves[...], CONTRACT_LAST, preferred_element_type=jnp.float32
    )
    high = lax.dot_general(
        weight[:, half:], halves[...], CONTRACT_LAST, preferred_element_type=jnp.float32
    )
    return low + pltpu.roll(high, rows - CAP, 1)


def forward_kernel(count, *refs):
    pieces = refs[:count]
    gate_w, up_w, halves, activated_out, slope_out, hidden_out = refs[count:]
    gather_pieces(pieces, halves)
    pre_gate, pre_up = project(gate_w, halves), project(up_w, halves)
    is_slot = lax.broadcasted_iota(jnp.int32, (1, halves.shape[0]), 1) % BLOCK < CAP
    squash = 1.0 / (1.0 + jnp.exp(-pre_gate))
    activated = jnp.where(is_slot, pre_gate * squash, 0.0)
    slope = pre_up * squash * (1.0 + pre_gate * (1.0 - squash))
    activated_out[...] = activated
    slope_out[...] = jnp.where(is_slot, slope, 0.0)
    hidden_out[...] = (activated * pre_up).astype(jnp.bfloat16)


def forward(pieces, gate_w, up_w):
    count = len(pieces)
    units, width = gate_w.shape
    rows = count * pieces[0].shape[0]
    kept = (units, rows)
    return pl.pallas_call(
        functools.partial(forward_kernel, count),
        out_shape=[
            struct((rows, width // 2)),
            struct(kept, jnp.float32),
            struct(kept, jnp.float32),
            struct(kept),
        ],
        in_specs=[VMEM] * (count + 2),
        out_specs=[VMEM] * 4,
        compiler_params=pltpu.CompilerParams(
            vmem_limit_bytes=4 * MIB + rows * width + 40 * rows * units
        ),
        cost_estimate=pl.CostEstimate(
            flops=4 * rows * units * width,
            bytes_accessed=4 * units * width,
            transcendentals=rows * units,
        ),
        name="forward",
    )(*pieces, gate_w, up_w)


def row_grads(low, high, gate_w, up_w, received, parts, half):
    units = gate_w.shape[0]
    block = parts[0].shape[0]
    chunk = 512 if half % 512 == 0 else half

    @pl.loop(0, half // chunk)
    def _(step):
        near = pl.ds(pl.multiple_of(step * chunk, chunk), chunk)
        far = pl.ds(pl.multiple_of(half + step * chunk, chunk), chunk)
        total = None
        for rows, columns in ((low, near), (high, far)):
            for i, weight in enumerate((gate_w, up_w)):
                term = jnp.dot(
                    rows[:, i * units : (i + 1) * units],
                    weight[:, columns],
                    preferred_element_type=jnp.float32,
                )
                total = term if total is None else total + term
        if received is not None:
            total = total + received[:, near].astype(jnp.float32)
        total = total.astype(jnp.bfloat16)
        for i, part in enumerate(parts):
            part[:, near] = total[i * block : (i + 1) * block]


def backward_kernel(count, *refs):
    pieces = refs[:count]
    activated, slope, hidden, gate_w, up_w, down_w = refs[count : count + 6]
    part, halves, gate_out, up_out, low_out, high_out, gates_out = refs[count + 6 :]
    half = halves.shape[1]
    rows = halves.shape[0]
    mine = rows // 2
    gather_pieces(pieces, halves)
    back = project(down_w, halves)
    gate_terms = jnp.sum(hidden[...].astype(jnp.float32) * back, axis=0, keepdims=True)
    up_pre = back * activated[...]
    gate_pre = back * slope[...]
    both = jnp.concatenate([gate_pre, up_pre], axis=0)
    low = both.T.astype(jnp.bfloat16)
    high = pltpu.roll(both, CAP, 1).T.astype(jnp.bfloat16)
    gate_column = jnp.broadcast_to(gate_terms, (LANES, rows)).T.astype(jnp.bfloat16)
    part[:, half:] = gate_column[mine:]
    row_grads(low[mine:], high[mine:], gate_w, up_w, None, (part,), half)
    low_out[...] = low[:mine]
    high_out[...] = high[:mine]
    gates_out[...] = gate_column[:mine]
    gate_out[...] = gate_pre.astype(jnp.bfloat16)
    up_out[...] = up_pre.astype(jnp.bfloat16)


def backward(pieces, activated, slope, hidden, weights):
    count = len(pieces)
    units, width = weights[0].shape
    rows = count * pieces[0].shape[0]
    mine = rows // 2
    shapes = [
        (mine, width // 2 + LANES),
        (rows, width // 2),
        (units, rows),
        (units, rows),
        (mine, 2 * units),
        (mine, 2 * units),
        (mine, LANES),
    ]
    return pl.pallas_call(
        functools.partial(backward_kernel, count),
        out_shape=[struct(shape) for shape in shapes],
        in_specs=[VMEM] * (count + 6),
        out_specs=[VMEM] * len(shapes),
        compiler_params=pltpu.CompilerParams(
            vmem_limit_bytes=4 * MIB
            + 2 * sum(height * across for height, across in shapes)
            + 40 * rows * units
        ),
        cost_estimate=pl.CostEstimate(
            flops=4 * rows * units * width,
            bytes_accessed=2 * units * width,
            transcendentals=0,
        ),
        name="backward",
    )(*pieces, activated, slope, hidden, *weights)


def own_kernel(low, high, gates, gate_w, up_w, received, *parts):
    half = gate_w.shape[1] // 2
    block = parts[0].shape[0]
    for i, part in enumerate(parts):
        span = pl.ds(i * block, block)
        part[:, half:] = (
            gates[span, :].astype(jnp.float32) + received[span, half:].astype(jnp.float32)
        ).astype(jnp.bfloat16)
    row_grads(low[...], high[...], gate_w, up_w, received, parts, half)


def own_rows(count, low, high, gates, gate_w, up_w, received):
    rows, width = received.shape
    units = gate_w.shape[0]
    return pl.pallas_call(
        own_kernel,
        out_shape=[struct((rows // count, width))] * count,
        in_specs=[VMEM] * 6,
        out_specs=[VMEM] * count,
        compiler_params=pltpu.CompilerParams(vmem_limit_bytes=8 * MIB + 8 * rows * width),
        cost_estimate=pl.CostEstimate(
            flops=4 * rows * units * gate_w.shape[1],
            bytes_accessed=4 * units * gate_w.shape[1],
            transcendentals=0,
        ),
        name="own_rows",
    )(low, high, gates, gate_w, up_w, received)


def add_kernel(left, right, out):
    out[...] = (left[...].astype(jnp.float32) + right[...].astype(jnp.float32)).astype(
        jnp.bfloat16
    )


def add_rows(left, right):
    return pl.pallas_call(
        add_kernel,
        out_shape=struct(right.shape),
        in_specs=[VMEM] * 2,
        out_specs=VMEM,
        compiler_params=pltpu.CompilerParams(vmem_limit_bytes=4 * MIB + 16 * right.size),
        name="add_rows",
    )(left, right)


def weight_kernel(chunk, factor_ref, halves, out, stage, sems):
    half = halves.shape[1]
    low = factor_ref[...]
    high = pltpu.roll(low.astype(jnp.float32), CAP, 1).astype(jnp.bfloat16)
    copies = []
    for factor, base in ((low, 0), (high, half)):
        for start in range(0, half, chunk):
            span = pl.ds(base + start, chunk)
            stage[:, span] = jnp.dot(
                factor, halves[:, pl.ds(start, chunk)], preferred_element_type=jnp.float32
            ).astype(jnp.bfloat16)
            copies.append(
                pltpu.make_async_copy(
                    stage.at[:, span], out.at[:, span], sems.at[len(copies)]
                )
            )
            copies[-1].start()
    for copy in copies:
        copy.wait()


def weight_grad(factor, halves):
    units, rows = factor.shape
    half = halves.shape[1]
    chunk = 512 if half % 512 == 0 else half
    return pl.pallas_call(
        functools.partial(weight_kernel, chunk),
        out_shape=struct((units, 2 * half)),
        in_specs=[VMEM] * 2,
        out_specs=HBM,
        scratch_shapes=[
            pltpu.VMEM((units, 2 * half), jnp.bfloat16),
            pltpu.SemaphoreType.DMA((2 * half // chunk,)),
        ],
        compiler_params=pltpu.CompilerParams(
            vmem_limit_bytes=8 * MIB + 4 * units * half + 8 * units * rows
        ),
        cost_estimate=pl.CostEstimate(
            flops=4 * rows * units * half,
            bytes_accessed=4 * units * half,
            transcendentals=0,
        ),
        name="weight_grad",
    )(factor, halves)


def combine_kernel(first, second, choice_ref, gates_ref, back, token_ref, gate_ref):
    half = token_ref.shape[1] // 2
    choices, tokens = gates_ref.shape
    rows = back[:, :half]
    token_ref[:, :half] = lax.dot_general(
        first[...], rows, CONTRACT_FIRST, preferred_element_type=jnp.float32
    ).astype(jnp.bfloat16)
    token_ref[:, half:] = lax.dot_general(
        second[...], rows, CONTRACT_FIRST, preferred_element_type=jnp.float32
    ).astype(jnp.bfloat16)
    terms = back[:, half : half + tokens].astype(jnp.float32)
    choice = choice_ref[...]
    for k in range(choices):
        chosen = jnp.where(choice == k, terms, 0.0)
        gate = gates_ref[k : k + 1, :].astype(jnp.float32)
        gate_ref[k : k + 1, :] = jnp.sum(chosen, axis=0, keepdims=True) / gate


def combine(table, gates, returned, width):
    choices, tokens = gates.shape
    return pl.pallas_call(
        combine_kernel,
        out_shape=[struct((tokens, width)), struct((choices, tokens), jnp.float32)],
        in_specs=[VMEM] * 5,
        out_specs=[VMEM] * 2,
        compiler_params=pltpu.CompilerParams(vmem_limit_bytes=4 * MIB + 16 * returned.size),
        name="combine",
    )(*table, gates, returned)


def flip(value, axis, bit):
    size = lax.axis_size(axis)
    return lax.ppermute(value, axis, [(i, i ^ bit) for i in range(size)])


def exchange(value):
    n_targets = lax.axis_size("expert")
    rows, width = value.shape
    blocks = value.reshape(n_targets, rows // n_targets, width)
    blocks = lax.all_to_all(blocks, "expert", split_axis=0, concat_axis=0, tiled=True)
    return blocks.reshape(rows, width)


def cross(block, far_bits):
    held = {0: block}
    for bit in far_bits:
        for mask in list(held):
            held[mask | bit] = flip(held[mask], "dp", bit)
    return held


def body(tokens, out_grad, gate_probs, route_ids, w_gate, w_up, w_down):
    n_targets = lax.axis_size("expert")
    n_dp = lax.axis_size("dp")
    width = tokens.shape[1]
    ids, gates = route_ids.T, gate_probs.T
    far_bits = [1 << i for i in range(1, n_dp.bit_length() - 1)]
    weights = (w_gate[0], w_up[0], w_down[0])
    tie = lax.optimization_barrier

    token_rows = send_tokens(n_targets, ids, tokens)
    ids_after, token_rows = tie((ids, token_rows))
    token_rows = exchange(token_rows)
    grad_rows = send_grads(n_targets, ids_after, gates, out_grad)
    table_ids, token_rows = tie((ids_after, token_rows))
    grad_rows, *table = tie((grad_rows, *placement(n_targets, table_ids)))
    grad_rows = exchange(grad_rows)

    token_held = cross(token_rows, far_bits)
    near = sorted(token_held)
    token_near = [token_held[mask] for mask in near]
    token_far = [flip(token_near[0], "dp", 1)]
    grad_rows, *token_near[1:] = tie((grad_rows, *token_near[1:]))
    grad_held = cross(grad_rows, far_bits)
    token_far += [flip(value, "dp", 1) for value in token_near[1:]]
    grad_near = [grad_held[mask] for mask in near]
    token_halves, activated, slope, hidden = forward(
        token_near + token_far, weights[0], weights[1]
    )
    activated, slope, hidden, *grad_near = tie((activated, slope, hidden, *grad_near))
    grad_far = [flip(value, "dp", 1) for value in grad_near]

    part, grad_halves, gate_f, up_f, low, high, gate_column = backward(
        grad_near + grad_far, activated, slope, hidden, weights
    )
    received = flip(part, "dp", 1)
    grad_gate = weight_grad(gate_f, token_halves)
    received, grad_gate = tie((received, grad_gate))
    totals = own_rows(len(near), low, high, gate_column, weights[0], weights[1], received)
    sums = dict(zip(near, totals))
    grad_up = weight_grad(up_f, token_halves)
    for bit in reversed(far_bits):
        moved = {mask: flip(sums.pop(mask), "dp", bit) for mask in list(sums) if mask & bit}
        if bit == far_bits[0]:
            moved, grad_up = tie((moved, grad_up))
        for mask, value in moved.items():
            sums[mask ^ bit] = add_rows(sums[mask ^ bit], value)
    returned = exchange(sums[0])
    grad_down = weight_grad(hidden, grad_halves)
    returned, grad_down = tie((returned, grad_down))
    token_grad, gate_grad = combine(table, gates, returned, width)
    return (token_grad, gate_grad.T, grad_gate[None], grad_up[None], grad_down[None])


def solution(mesh):
    in_specs = (
        P(("expert", "dp"), None),
        P(("expert", "dp"), None),
        P(("expert", "dp"), None),
        P(("expert", "dp"), None),
        P("expert", "dp", None),
        P("expert", "dp", None),
        P("expert", "dp", None),
    )
    out_specs = (
        P(("expert", "dp"), None),
        P(("expert", "dp"), None),
        P("expert", "dp", None),
        P("expert", "dp", None),
        P("expert", "dp", None),
    )
    return jax.shard_map(body, mesh=mesh, in_specs=in_specs, out_specs=out_specs, check_vma=False)
```

time: 74 us -> 75.4 us (1.019)
  starting transfers between devices: 39.6 us -> 21.2 us
  waiting for transfers between devices: 15.1 us -> 28.5 us
  local copies, waits for them, and re-layouts: 1.34 us -> 5.63 us
  Pallas kernels: 16.9 us -> 18.7 us
    ppermute x40 -> x8, starting transfers between devices: 39.6 us -> 5.26 us  [flip(): return lax.ppermute(value, axis, [(i, i ^ bit) for i in range(size)])]
    all_to_all x0 -> x3, starting transfers between devices: none -> 15.9 us  [exchange(): lax.all_to_all(blocks, 'expert', split_axis=0, concat_axis=0, tiled=True)]
    all_to_all x0 -> x3, waiting for transfers between devices: none -> 13.4 us  [exchange(): lax.all_to_all(blocks, 'expert', split_axis=0, concat_axis=0, tiled=True)]
    unnamed x14 -> x28, local copies, waits for them, and re-layouts: 1.34 us -> 5.63 us
    pallas_call x8 -> x10, Pallas kernels: 16.7 us -> 18.5 us  [the longest x3 5.97 us: weight_grad(): pl.pallas_call(functools.partial(weight_kernel, chunk), out_shape=struct(...]
    ppermute x40 -> x8, waiting for transfers between devices: 15.1 us -> 15.2 us  [flip(): return lax.ppermute(value, axis, [(i, i ^ bit) for i in range(size)])]
  transfers between devices with their start and end apart: 40 -> 11, of which waited for: 13 -> 9; matrix products, arithmetic and copies ran while one was open for 0% -> 0% of each run, Pallas kernels for 8% -> 13%
where the time goes in v3:
time: 75.4 us; the launch traced here: 74.8 us
  waiting for transfers between devices  28.5 us (38%)
  starting transfers between devices  21.2 us (28%)
  Pallas kernels  18.7 us (25%)
  local copies, waits for them, and re-layouts  5.63 us (7%)
  between operations  0.8 us (1%)
    all_to_all x3, starting transfers between devices, exchange(): lax.all_to_all(blocks, 'expert', split_axis=0, concat_axis=0, tiled=True)  15.9 us
    ppermute x8, waiting for transfers between devices, flip(): return lax.ppermute(value, axis, [(i, i ^ bit) for i in range(size)])  15.2 us
    all_to_all x3, waiting for transfers between devices, exchange(): lax.all_to_all(blocks, 'expert', split_axis=0, concat_axis=0, tiled=True)  13.4 us
    pallas_call x3, Pallas kernels, weight_grad(): pl.pallas_call(functools.partial(weight_kernel, chunk), out_shape=struct(...  5.97 us
    unnamed x28, local copies, waits for them, and re-layouts  5.63 us
    ppermute x8, starting transfers between devices, flip(): return lax.ppermute(value, axis, [(i, i ^ bit) for i in range(size)])  5.26 us
    pallas_call x1, Pallas kernels, backward(): pl.pallas_call(functools.partial(backward_kernel, count), out_shape=[stru...  3.37 us
    pallas_call x1, Pallas kernels, forward(): pl.pallas_call(functools.partial(forward_kernel, count), out_shape=[struc...  3.21 us
  transfers between devices with their start and end apart: 11, of which 9 were waited for; matrix products, arithmetic and copies ran while one was open for 0% of the time, Pallas kernels for 13%

profile of v3, /device:TPU:0, one launch (start us, length us, event | category | flops | bytes accessed | tf_op | source)
XLA Modules:
  0.0 74.8 jit_solution(4974566919595391932)
XLA Ops:
  0.6 2.0 %send_tokens.1 = bf16[64,2048]{1,0:T(8,128)(2,1)} custom-call(s32[8,32]{1,0:T(8,128)} %bitcast.27, bf16[32,4096]{1,0:T(8,128)(2,1)} %tokens_hbm.1), custom_call_target="tpu_custom_call" | custom-call | tf_op jit(solution)/shard_map/send_tokens/pallas_call | solution.py:70
  2.6 7.3 %all-to-all-start = ((bf16[8,8,2048]{2,1,0:T(8,128)(2,1)}), bf16[8,8,2048]{2,1,0:T(8,128)(2,1)}, u32[]{:S(2)}, u32[]{:S(2)}) async-start(bf16[8,8,2048]{2,1,0:T(8,128)(2,1)} %bitcast.35), calls=%async_computation | async-start | bytes 524288 | tf_op jit(solution)/shard_map/all_to_all | solution.py:404
  9.9 0.9 %copy-done.9 = bf16[32,4096]{1,0:T(8,128)(2,1)S(1)} copy-done((bf16[32,4096]{1,0:T(8,128)(2,1)S(1)}, bf16[32,4096]{1,0:T(8,128)(2,1)}, u32[]{:S(2)}) %copy-start.9) | copy-done | bytes 262168
  13.3 5.6 %all-to-all-done = bf16[8,8,2048]{2,1,0:T(8,128)(2,1)} async-done(((bf16[8,8,2048]{2,1,0:T(8,128)(2,1)}), bf16[8,8,2048]{2,1,0:T(8,128)(2,1)}, u32[]{:S(2)}, u32[]{:S(2)}) %all-to-all-start) | async-done | bytes 262176 | tf_op jit(solution)/shard_map/all_to_all | solution.py:404
  19.8 3.7 %all-to-all-start.1 = ((bf16[8,8,2048]{2,1,0:T(8,128)(2,1)}), bf16[8,8,2048]{2,1,0:T(8,128)(2,1)S(1)}, u32[]{:S(2)}, u32[]{:S(2)}) async-start(bf16[8,8,2048]{2,1,0:T(8,128)(2,1)} %bitcast.26), calls=%async_computation.1 | async-start | bytes 524288 | tf_op jit(solution)/shard_map/all_to_all | solution.py:404
  23.5 1.5 %collective-permute-start = (bf16[64,2048]{1,0:T(8,128)(2,1)}, bf16[64,2048]{1,0:T(8,128)(2,1)}, u32[]{:S(2)}, u32[]{:S(2)}) collective-permute-start(bf16[64,2048]{1,0:T(8,128)(2,1)} %bitcast.3.refs_0_), channel_id=1, source_target_pairs={{0,2},{1,3},{2,0},{3,1},{4,6},{5,7},{6,4},{7,5},{8,10},{9,11},{10,... | collective-permute-start | bytes 786440 | tf_op jit(solution)/shard_map/ppermute | solution.py:397
  25.0 6.2 %collective-permute-done.refs_1_ = bf16[64,2048]{1,0:T(8,128)(2,1)} collective-permute-done((bf16[64,2048]{1,0:T(8,128)(2,1)}, bf16[64,2048]{1,0:T(8,128)(2,1)}, u32[]{:S(2)}, u32[]{:S(2)}) %collective-permute-start) | collective-permute-done | bytes 262176 | tf_op jit(solution)/shard_map/ppermute | solution.py:397
  31.3 0.8 %all-to-all-done.1 = bf16[8,8,2048]{2,1,0:T(8,128)(2,1)S(1)} async-done(((bf16[8,8,2048]{2,1,0:T(8,128)(2,1)}), bf16[8,8,2048]{2,1,0:T(8,128)(2,1)S(1)}, u32[]{:S(2)}, u32[]{:S(2)}) %all-to-all-start.1) | async-done | bytes 262176 | tf_op jit(solution)/shard_map/all_to_all | solution.py:404
  32.1 1.5 %collective-permute-start.3 = (bf16[64,2048]{1,0:T(8,128)(2,1)S(1)}, bf16[64,2048]{1,0:T(8,128)(2,1)S(1)}, u32[]{:S(2)}, u32[]{:S(2)}) collective-permute-start(bf16[64,2048]{1,0:T(8,128)(2,1)S(1)} %bitcast.23), channel_id=1, source_target_pairs={{0,2},{1,3},{2,0},{3,1},{4,6},{5,7},{6,4},{7,5},{8,10},{9,11},{10,... | collective-permute-start | bytes 786440 | tf_op jit(solution)/shard_map/ppermute | solution.py:397
  33.8 1.9 %copy-done.1 = bf16[1,384,4096]{2,1,0:T(8,128)(2,1)S(1)} copy-done((bf16[1,384,4096]{2,1,0:T(8,128)(2,1)S(1)}, bf16[1,384,4096]{2,1,0:T(8,128)(2,1)}, u32[]{:S(2)}) %copy-start.1) | copy-done | bytes 3145752
  35.7 3.2 %forward.1 = (bf16[256,2048]{1,0:T(8,128)(2,1)S(1)}, f32[384,256]{1,0:T(8,128)S(1)}, f32[384,256]{1,0:T(8,128)S(1)}, bf16[384,256]{1,0:T(8,128)(2,1)S(1)}) custom-call(bf16[64,2048]{1,0:T(8,128)(2,1)} %bitcast.3.refs_0_, bf16[64,2048]{1,0:T(8,128)(2,1)} %collective-permute-done.refs_1_, bf16[64,2048]{1,0:T(8,128)(2,1)} %collective-permute-done.1.refs_2_, ...), custom_call_target="tpu_custom_call" | custom-call | flops 1610612736 | bytes 6291456 | tf_op jit(solution)/shard_map/forward/pallas_call | solution.py:168
  39.0 1.8 %collective-permute-done.3.refs_1_ = bf16[64,2048]{1,0:T(8,128)(2,1)S(1)} collective-permute-done((bf16[64,2048]{1,0:T(8,128)(2,1)S(1)}, bf16[64,2048]{1,0:T(8,128)(2,1)S(1)}, u32[]{:S(2)}, u32[]{:S(2)}) %collective-permute-start.3) | collective-permute-done | bytes 262176 | tf_op jit(solution)/shard_map/ppermute | solution.py:397
  41.3 1.0 %collective-permute-done.4.refs_2_ = bf16[64,2048]{1,0:T(8,128)(2,1)S(1)} collective-permute-done((bf16[64,2048]{1,0:T(8,128)(2,1)S(1)}, bf16[64,2048]{1,0:T(8,128)(2,1)S(1)}, u32[]{:S(2)}, u32[]{:S(2)}) %collective-permute-start.4) | collective-permute-done | bytes 262176 | tf_op jit(solution)/shard_map/ppermute | solution.py:397
  42.7 3.4 %backward.1 = (bf16[128,2176]{1,0:T(8,128)(2,1)S(1)}, bf16[256,2048]{1,0:T(8,128)(2,1)S(1)}, bf16[384,256]{1,0:T(8,128)(2,1)S(1)}, bf16[384,256]{1,0:T(8,128)(2,...) custom-call(bf16[64,2048]{1,0:T(8,128)(2,1)S(1)} %bitcast.25, ...), custom_call_target="tpu_custom_call" | custom-call | flops 1610612736 | bytes 3145728 | tf_op jit(solution)/shard_map/backward/pallas_call | solution.py:254
  46.4 2.0 %weight_grad.3 = bf16[384,4096]{1,0:T(8,128)(2,1)} custom-call(bf16[384,256]{1,0:T(8,128)(2,1)S(1)} %get-tuple-element.69.factor_ref, bf16[256,2048]{1,0:T(8,128)(2,1)S(1)} %get-tuple-element.70.halves), custom_call_target="tpu_custom_call" | custom-call | flops 805306368 | bytes 3145728 | tf_op jit(solution)/shard_map/weight_grad/pallas_call | solution.py:344
  48.4 1.8 %own_rows.1 = (bf16[64,2176]{1,0:T(8,128)(2,1)S(1)}, bf16[64,2176]{1,0:T(8,128)(2,1)S(1)}) custom-call(bf16[128,768]{1,0:T(8,128)(2,1)S(1)} %get-tuple-element.65.low, bf16[128,768]{1,0:T(8,128)(2,1)S(1)} %get-tuple-element.66.high, bf16[128,128]{1,0:T(8,128)(2,1)S(1)} %get-tuple-element.67.gates, bf16[384,4096]{1,0:T(8,128)(2,1)S(1)} %bitcast.17, ...), custom_call_target="tpu_custom_call" | custom-call | flops 805306368 | bytes 6291456 | tf_op jit(solution)/shard_map/own_rows/pallas_call | solution.py:287
  50.2 1.6 %collective-permute-start.7 = (bf16[64,2176]{1,0:T(8,128)(2,1)S(1)}, bf16[64,2176]{1,0:T(8,128)(2,1)S(1)}, u32[]{:S(2)}, u32[]{:S(2)}) collective-permute-start(bf16[64,2176]{1,0:T(8,128)(2,1)S(1)} %get-tuple-element.73), channel_id=1, source_target_pairs={{0,2},{1,3},{2,0},{3,1},{4,6},{5,7},{6,4},{7,5},{8,10},{9,11},{10,... | collective-permute-start | bytes 835592 | tf_op jit(solution)/shard_map/ppermute | solution.py:397
  51.8 2.0 %weight_grad.4 = bf16[384,4096]{1,0:T(8,128)(2,1)} custom-call(bf16[384,256]{1,0:T(8,128)(2,1)S(1)} %get-tuple-element.74.factor_ref, bf16[256,2048]{1,0:T(8,128)(2,1)S(1)} %get-tuple-element.70.halves), custom_call_target="tpu_custom_call" | custom-call | flops 805306368 | bytes 3145728 | tf_op jit(solution)/shard_map/weight_grad/pallas_call | solution.py:344
  53.8 5.4 %collective-permute-done.7.right = bf16[64,2176]{1,0:T(8,128)(2,1)S(1)} collective-permute-done((bf16[64,2176]{1,0:T(8,128)(2,1)S(1)}, bf16[64,2176]{1,0:T(8,128)(2,1)S(1)}, u32[]{:S(2)}, u32[]{:S(2)}) %collective-permute-start.7) | collective-permute-done | bytes 278560 | tf_op jit(solution)/shard_map/ppermute | solution.py:397
  59.2 0.8 %add_rows.1 = bf16[64,2176]{1,0:T(8,128)(2,1)} custom-call(bf16[64,2176]{1,0:T(8,128)(2,1)S(1)} %get-tuple-element.72.left, bf16[64,2176]{1,0:T(8,128)(2,1)S(1)} %collective-permute-done.7.right), custom_call_target="tpu_custom_call" | custom-call | tf_op jit(solution)/shard_map/add_rows/pallas_call | solution.py:309
  60.0 4.9 %all-to-all-start.2 = ((bf16[8,8,2176]{2,1,0:T(8,128)(2,1)}), bf16[8,8,2176]{2,1,0:T(8,128)(2,1)S(1)}, u32[]{:S(2)}, u32[]{:S(2)}) async-start(bf16[8,8,2176]{2,1,0:T(8,128)(2,1)} %bitcast.9), calls=%async_computation.2 | async-start | bytes 557056 | tf_op jit(solution)/shard_map/all_to_all | solution.py:404
  64.9 2.0 %weight_grad.5 = bf16[384,4096]{1,0:T(8,128)(2,1)} custom-call(bf16[384,256]{1,0:T(8,128)(2,1)S(1)} %copy-done.8, bf16[256,2048]{1,0:T(8,128)(2,1)S(1)} %copy-done.6), custom_call_target="tpu_custom_call" | custom-call | flops 805306368 | bytes 3145728 | tf_op jit(solution)/shard_map/weight_grad/pallas_call | solution.py:344
  66.9 6.9 %all-to-all-done.2 = bf16[8,8,2176]{2,1,0:T(8,128)(2,1)S(1)} async-done(((bf16[8,8,2176]{2,1,0:T(8,128)(2,1)}), bf16[8,8,2176]{2,1,0:T(8,128)(2,1)S(1)}, u32[]{:S(2)}, u32[]{:S(2)}) %all-to-all-start.2) | async-done | bytes 278560 | tf_op jit(solution)/shard_map/all_to_all | solution.py:404
  73.8 1.0 %combine.1 = (bf16[32,4096]{1,0:T(8,128)(2,1)}, f32[8,32]{1,0:T(8,128)}) custom-call(bf16[64,32]{1,0:T(8,128)(2,1)S(1)} %get-tuple-element.50.first, bf16[64,32]{1,0:T(8,128)(2,1)S(1)} %get-tuple-element.51.second, s32[64,32]{1,0:T(8,128)S(1)} %get-tuple-element.52.choice_ref, bf16[8,32]{1,0:T(8,128)(2,1)S(1)} %bitcast.31, bf16[64,2176]{1,0:T(8,128)(2,1)S(1)} %bitcast.22), custom_call_target="tpu_custom_call" | custom-call | tf_op jit(solution)/shard_map/combine/pallas_call | solution.py:385
  (37 shorter events, 4.8 us)
Async XLA Ops:
  2.6 16.3 %all-to-all-start = ((bf16[8,8,2048]{2,1,0:T(8,128)(2,1)}), bf16[8,8,2048]{2,1,0:T(8,128)(2,1)}, u32[]{:S(2)}, u32[]{:S(2)}) async-start(bf16[8,8,2048]{2,1,0:T(8,128)(2,1)} %bitcast.35), calls=%async_computation | async-start | bytes 524288 | tf_op jit(solution)/shard_map/all_to_all | solution.py:404
  9.9 0.9 %copy-start.9 = (bf16[32,4096]{1,0:T(8,128)(2,1)S(1)}, bf16[32,4096]{1,0:T(8,128)(2,1)}, u32[]{:S(2)}) copy-start(bf16[32,4096]{1,0:T(8,128)(2,1)} %grads_ref.1) | copy-start | bytes 786436
  10.8 0.7 copy-start.10
  12.6 0.7 copy-start.4
  18.9 0.7 copy-start.11
  19.6 14.2 %copy-start = (bf16[1,384,4096]{2,1,0:T(8,128)(2,1)S(1)}, bf16[1,384,4096]{2,1,0:T(8,128)(2,1)}, u32[]{:S(2)}) copy-start(bf16[1,384,4096]{2,1,0:T(8,128)(2,1)} %param.11) | copy-start | bytes 9437188
  19.8 12.3 %all-to-all-start.1 = ((bf16[8,8,2048]{2,1,0:T(8,128)(2,1)}), bf16[8,8,2048]{2,1,0:T(8,128)(2,1)S(1)}, u32[]{:S(2)}, u32[]{:S(2)}) async-start(bf16[8,8,2048]{2,1,0:T(8,128)(2,1)} %bitcast.26), calls=%async_computation.1 | async-start | bytes 524288 | tf_op jit(solution)/shard_map/all_to_all | solution.py:404
  23.5 7.7 %collective-permute-start = (bf16[64,2048]{1,0:T(8,128)(2,1)}, bf16[64,2048]{1,0:T(8,128)(2,1)}, u32[]{:S(2)}, u32[]{:S(2)}) collective-permute-start(bf16[64,2048]{1,0:T(8,128)(2,1)} %bitcast.3.refs_0_), channel_id=1, source_target_pairs={{0,2},{1,3},{2,0},{3,1},{4,6},{5,7},{6,4},{7,5},{8,10},{9,11},{10,... | collective-permute-start | bytes 786440 | tf_op jit(solution)/shard_map/ppermute | solution.py:397
  25.0 8.6 %collective-permute-start.1 = (bf16[64,2048]{1,0:T(8,128)(2,1)}, bf16[64,2048]{1,0:T(8,128)(2,1)}, u32[]{:S(2)}, u32[]{:S(2)}) collective-permute-start(bf16[64,2048]{1,0:T(8,128)(2,1)} %bitcast.3.refs_0_), channel_id=1, source_target_pairs={{0,1},{1,0},{2,3},{3,2},{4,5},{5,4},{6,7},{7,6},{8,9},{9,8},{10,11... | collective-permute-start | bytes 786440 | tf_op jit(solution)/shard_map/ppermute | solution.py:397
  32.1 1.7 %collective-permute-start.2 = (bf16[64,2048]{1,0:T(8,128)(2,1)}, bf16[64,2048]{1,0:T(8,128)(2,1)S(1)}, u32[]{:S(2)}, u32[]{:S(2)}) collective-permute-start(bf16[64,2048]{1,0:T(8,128)(2,1)} %collective-permute-done.refs_1_), channel_id=1, source_target_pairs={{0,1},{1,0},{2,3},{3,2},{4,5},{5,4},{6,7},{7,6},{8,9},{9,8},{10,11... | collective-permute-start | bytes 786440 | tf_op jit(solution)/shard_map/ppermute | solution.py:397
  32.1 8.7 %collective-permute-start.3 = (bf16[64,2048]{1,0:T(8,128)(2,1)S(1)}, bf16[64,2048]{1,0:T(8,128)(2,1)S(1)}, u32[]{:S(2)}, u32[]{:S(2)}) collective-permute-start(bf16[64,2048]{1,0:T(8,128)(2,1)S(1)} %bitcast.23), channel_id=1, source_target_pairs={{0,2},{1,3},{2,0},{3,1},{4,6},{5,7},{6,4},{7,5},{8,10},{9,11},{10,... | collective-permute-start | bytes 786440 | tf_op jit(solution)/shard_map/ppermute | solution.py:397
  33.8 1.9 %copy-start.1 = (bf16[1,384,4096]{2,1,0:T(8,128)(2,1)S(1)}, bf16[1,384,4096]{2,1,0:T(8,128)(2,1)}, u32[]{:S(2)}) copy-start(bf16[1,384,4096]{2,1,0:T(8,128)(2,1)} %param.12) | copy-start | bytes 9437188
  35.7 7.0 %copy-start.2 = (bf16[1,384,4096]{2,1,0:T(8,128)(2,1)S(1)}, bf16[1,384,4096]{2,1,0:T(8,128)(2,1)}, u32[]{:S(2)}) copy-start(bf16[1,384,4096]{2,1,0:T(8,128)(2,1)} %param.12) | copy-start | bytes 9437188
  35.7 7.0 %copy-start.3 = (bf16[1,384,4096]{2,1,0:T(8,128)(2,1)S(1)}, bf16[1,384,4096]{2,1,0:T(8,128)(2,1)}, u32[]{:S(2)}) copy-start(bf16[1,384,4096]{2,1,0:T(8,128)(2,1)} %param.13) | copy-start | bytes 9437188
  39.0 7.2 %copy-start.7 = (bf16[384,256]{1,0:T(8,128)(2,1)}, bf16[384,256]{1,0:T(8,128)(2,1)S(1)}, u32[]{:S(2)}) copy-start(bf16[384,256]{1,0:T(8,128)(2,1)S(1)} %get-tuple-element.64.refs_6_.factor_ref) | copy-start | bytes 589828
  40.8 1.5 %collective-permute-start.4 = (bf16[64,2048]{1,0:T(8,128)(2,1)S(1)}, bf16[64,2048]{1,0:T(8,128)(2,1)S(1)}, u32[]{:S(2)}, u32[]{:S(2)}) collective-permute-start(bf16[64,2048]{1,0:T(8,128)(2,1)S(1)} %bitcast.24), channel_id=1, source_target_pairs={{0,1},{1,0},{2,3},{3,2},{4,5},{5,4},{6,7},{7,6},{8,9},{9,8},{10,11... | collective-permute-start | bytes 786440 | tf_op jit(solution)/shard_map/ppermute | solution.py:397
  40.8 1.9 %collective-permute-start.5 = (bf16[64,2048]{1,0:T(8,128)(2,1)S(1)}, bf16[64,2048]{1,0:T(8,128)(2,1)S(1)}, u32[]{:S(2)}, u32[]{:S(2)}) collective-permute-start(bf16[64,2048]{1,0:T(8,128)(2,1)S(1)} %collective-permute-done.3.refs_1_), channel_id=1, source_target_pairs={{0,1},{1,0},{2,3},{3,2},{4,5},{5,4},{6,7},{7,6},{8,9},{9,8},{10,11... | collective-permute-start | bytes 786440 | tf_op jit(solution)/shard_map/ppermute | solution.py:397
  46.1 4.1 %copy-start.5 = (bf16[256,2048]{1,0:T(8,128)(2,1)}, bf16[256,2048]{1,0:T(8,128)(2,1)S(1)}, u32[]{:S(2)}) copy-start(bf16[256,2048]{1,0:T(8,128)(2,1)S(1)} %get-tuple-element.76.halves) | copy-start | bytes 3145732
  46.1 2.2 %collective-permute-start.6 = (bf16[128,2176]{1,0:T(8,128)(2,1)S(1)}, bf16[128,2176]{1,0:T(8,128)(2,1)S(1)}, u32[]{:S(2)}, u32[]{:S(2)}) collective-permute-start(bf16[128,2176]{1,0:T(8,128)(2,1)S(1)} %get-tuple-element.68), channel_id=1, source_target_pairs={{0,1},{1,0},{2,3},{3,2},{4,5},{5,4},{6,7},{7,6},{8,9},{9,8},{10,11... | collective-permute-start | bytes 1671176 | tf_op jit(solution)/shard_map/ppermute | solution.py:397
  50.2 14.7 %copy-start.8 = (bf16[384,256]{1,0:T(8,128)(2,1)S(1)}, bf16[384,256]{1,0:T(8,128)(2,1)}, u32[]{:S(2)}) copy-start(bf16[384,256]{1,0:T(8,128)(2,1)} %copy-done.7) | copy-start | bytes 589828
  50.2 14.7 %copy-start.6 = (bf16[256,2048]{1,0:T(8,128)(2,1)S(1)}, bf16[256,2048]{1,0:T(8,128)(2,1)}, u32[]{:S(2)}) copy-start(bf16[256,2048]{1,0:T(8,128)(2,1)} %copy-done.5) | copy-start | bytes 3145732
  50.2 9.0 %collective-permute-start.7 = (bf16[64,2176]{1,0:T(8,128)(2,1)S(1)}, bf16[64,2176]{1,0:T(8,128)(2,1)S(1)}, u32[]{:S(2)}, u32[]{:S(2)}) collective-permute-start(bf16[64,2176]{1,0:T(8,128)(2,1)S(1)} %get-tuple-element.73), channel_id=1, source_target_pairs={{0,2},{1,3},{2,0},{3,1},{4,6},{5,7},{6,4},{7,5},{8,10},{9,11},{10,... | collective-permute-start | bytes 835592 | tf_op jit(solution)/shard_map/ppermute | solution.py:397
  53.8 20.0 %copy-start.13 = (bf16[32,8]{0,1:T(8,128)(2,1)S(1)}, bf16[32,8]{0,1:T(8,128)(2,1)}, u32[]{:S(2)}) copy-start(bf16[32,8]{0,1:T(8,128)(2,1)} %param.9) | copy-start | bytes 1540
  60.0 13.9 %all-to-all-start.2 = ((bf16[8,8,2176]{2,1,0:T(8,128)(2,1)}), bf16[8,8,2176]{2,1,0:T(8,128)(2,1)S(1)}, u32[]{:S(2)}, u32[]{:S(2)}) async-start(bf16[8,8,2176]{2,1,0:T(8,128)(2,1)} %bitcast.9), calls=%async_computation.2 | async-start | bytes 557056 | tf_op jit(solution)/shard_map/all_to_all | solution.py:404
  (1 other events, 0.7 us)

commit v4 on v3

--- a/solution.py
+++ b/solution.py
@@ -12,7 +12,7 @@
 BLOCK = 2 * CAP
 LANES = 128
 MIB = 2**20
-COVER = 12
+COVER = 40
 
 CONTRACT_LAST = (((1,), (1,)), ((), ()))
 CONTRACT_FIRST = (((0,), (0,)), ((), ()))
@@ -55,52 +55,42 @@
     return (low + high).astype(jnp.bfloat16)
 
 
-def send_tokens_kernel(n_targets, ids_hbm, tokens_hbm, out, ids_ref, tokens_ref, sems):
-    ids_copy = pltpu.make_async_copy(ids_hbm, ids_ref, sems.at[0])
-    tokens_copy = pltpu.make_async_copy(tokens_hbm, tokens_ref, sems.at[1])
-    ids_copy.start()
-    tokens_copy.start()
-    ids_copy.wait()
-    _, first, second = choice_table(ids_ref[...], n_targets)
-    tokens_copy.wait()
-    out[...] = pick_rows(as_bf16(first), as_bf16(second), tokens_ref)
-
-
-def send_tokens(n_targets, ids, tokens):
-    return pl.pallas_call(
-        functools.partial(send_tokens_kernel, n_targets),
-        out_shape=struct((n_targets * BLOCK, tokens.shape[1] // 2)),
-        in_specs=[HBM] * 2,
-        out_specs=VMEM,
-        scratch_shapes=[pltpu.VMEM(a.shape, a.dtype) for a in (ids, tokens)]
-        + [pltpu.SemaphoreType.DMA((2,))],
-        compiler_params=pltpu.CompilerParams(vmem_limit_bytes=60 * MIB),
-        name="send_tokens",
-    )(ids, tokens)
-
-
-def send_grads_kernel(n_targets, ids_ref, gates_ref, grads_ref, out):
+def dispatch_kernel(n_targets, *refs):
+    sources, (token_out, grad_out), targets, sems = refs[:4], refs[4:6], refs[6:10], refs[10]
+    ids_ref, tokens_ref, gates_ref, grads_ref = targets
+    copies = [
+        pltpu.make_async_copy(source, target, sems.at[i])
+        for i, (source, target) in enumerate(zip(sources, targets))
+    ]
+    for copy in copies:
+        copy.start()
+    copies[0].wait()
     matches, first, second = choice_table(ids_ref[...], n_targets)
+    copies[1].wait()
+    token_out[...] = pick_rows(as_bf16(first), as_bf16(second), tokens_ref)
+    copies[2].wait()
     gates = gates_ref[...].astype(jnp.float32)
     scale = jnp.zeros(first.shape, jnp.float32)
     for k, match in enumerate(matches):
         scale = scale + jnp.where(match, gates[k : k + 1, :], 0.0)
     first = jnp.where(first, scale, 0.0).astype(jnp.bfloat16)
     second = jnp.where(second, scale, 0.0).astype(jnp.bfloat16)
-    out[...] = pick_rows(first, second, grads_ref)
-
-
-def send_grads(n_targets, ids, gates, out_grad):
-    return pl.pallas_call(
-        functools.partial(send_grads_kernel, n_targets),
-        out_shape=struct((n_targets * BLOCK, out_grad.shape[1] // 2)),
-        in_specs=[VMEM] * 3,
-        out_specs=VMEM,
-        compiler_params=pltpu.CompilerParams(
-            vmem_limit_bytes=4 * MIB + 8 * n_targets * BLOCK * out_grad.shape[1]
-        ),
-        name="send_grads",
-    )(ids, gates, out_grad)
+    copies[3].wait()
+    grad_out[...] = pick_rows(first, second, grads_ref)
+
+
+def dispatch(n_targets, ids, tokens, gates, out_grad):
+    arrays = (ids, tokens, gates, out_grad)
+    return pl.pallas_call(
+        functools.partial(dispatch_kernel, n_targets),
+        out_shape=[struct((n_targets * BLOCK, tokens.shape[1] // 2))] * 2,
+        in_specs=[HBM] * 4,
+        out_specs=[VMEM] * 2,
+        scratch_shapes=[pltpu.VMEM(a.shape, a.dtype) for a in arrays]
+        + [pltpu.SemaphoreType.DMA((4,))],
+        compiler_params=pltpu.CompilerParams(vmem_limit_bytes=60 * MIB),
+        name="dispatch",
+    )(*arrays)
 
 
 def placement_kernel(n_targets, ids_ref, first_ref, second_ref, choice_ref):
@@ -187,15 +177,17 @@
     )(*pieces, gate_w, up_w)
 
 
-def row_grads(low, high, gate_w, up_w, received, parts, half):
-    units = gate_w.shape[0]
+def row_grads(low, high, gate_w, up_w, received, parts, start, size):
+    units, width = gate_w.shape
     block = parts[0].shape[0]
-    chunk = 512 if half % 512 == 0 else half
-
-    @pl.loop(0, half // chunk)
+    chunk = 512 if size % 512 == 0 else size
+
+    @pl.loop(0, size // chunk)
     def _(step):
-        near = pl.ds(pl.multiple_of(step * chunk, chunk), chunk)
-        far = pl.ds(pl.multiple_of(half + step * chunk, chunk), chunk)
+        offset = pl.multiple_of(step * chunk, chunk)
+        near = pl.ds(pl.multiple_of(start + offset, chunk), chunk)
+        far = pl.ds(pl.multiple_of(width // 2 + start + offset, chunk), chunk)
+        here = pl.ds(offset, chunk)
         total = None
         for rows, columns in ((low, near), (high, far)):
             for i, weight in enumerate((gate_w, up_w)):
@@ -206,17 +198,16 @@
                 )
                 total = term if total is None else total + term
         if received is not None:
-            total = total + received[:, near].astype(jnp.float32)
+            total = total + received[:, here].astype(jnp.float32)
         total = total.astype(jnp.bfloat16)
         for i, part in enumerate(parts):
-            part[:, near] = total[i * block : (i + 1) * block]
+            part[:, here] = total[i * block : (i + 1) * block]
 
 
 def backward_kernel(count, *refs):
     pieces = refs[:count]
     activated, slope, hidden, gate_w, up_w, down_w = refs[count : count + 6]
     part, halves, gate_out, up_out, low_out, high_out, gates_out = refs[count + 6 :]
-    half = halves.shape[1]
     rows = halves.shape[0]
     mine = rows // 2
     gather_pieces(pieces, halves)
@@ -228,11 +219,10 @@
     low = both.T.astype(jnp.bfloat16)
     high = pltpu.roll(both, CAP, 1).T.astype(jnp.bfloat16)
     gate_column = jnp.broadcast_to(gate_terms, (LANES, rows)).T.astype(jnp.bfloat16)
-    part[:, half:] = gate_column[mine:]
-    row_grads(low[mine:], high[mine:], gate_w, up_w, None, (part,), half)
-    low_out[...] = low[:mine]
-    high_out[...] = high[:mine]
-    gates_out[...] = gate_column[:mine]
+    row_grads(low[mine:], high[mine:], gate_w, up_w, None, (part,), 0, part.shape[1])
+    low_out[...] = low
+    high_out[...] = high
+    gates_out[...] = gate_column
     gate_out[...] = gate_pre.astype(jnp.bfloat16)
     up_out[...] = up_pre.astype(jnp.bfloat16)
 
@@ -243,13 +233,13 @@
     rows = count * pieces[0].shape[0]
     mine = rows // 2
     shapes = [
-        (mine, width // 2 + LANES),
+        (mine, width // 4),
         (rows, width // 2),
         (units, rows),
         (units, rows),
-        (mine, 2 * units),
-        (mine, 2 * units),
-        (mine, LANES),
+        (rows, 2 * units),
+        (rows, 2 * units),
+        (rows, LANES),
     ]
     return pl.pallas_call(
         functools.partial(backward_kernel, count),
@@ -262,7 +252,7 @@
             + 40 * rows * units
         ),
         cost_estimate=pl.CostEstimate(
-            flops=4 * rows * units * width,
+            flops=3 * rows * units * width,
             bytes_accessed=2 * units * width,
             transcendentals=0,
         ),
@@ -270,50 +260,80 @@
     )(*pieces, activated, slope, hidden, *weights)
 
 
-def own_kernel(low, high, gates, gate_w, up_w, received, *parts):
-    half = gate_w.shape[1] // 2
+def far_kernel(start, low, high, gates, gate_w, up_w, part):
+    span = pl.ds(part.shape[0], part.shape[0])
+    size = part.shape[1] - LANES
+    part[:, size:] = gates[span, :]
+    row_grads(low[span, :], high[span, :], gate_w, up_w, None, (part,), start, size)
+
+
+def far_rows(start, low, high, gates, gate_w, up_w):
+    rows, width = low.shape[0], gate_w.shape[1]
+    size = width // 2 - start
+    return pl.pallas_call(
+        functools.partial(far_kernel, start),
+        out_shape=struct((rows // 2, size + LANES)),
+        in_specs=[VMEM] * 5,
+        out_specs=VMEM,
+        compiler_params=pltpu.CompilerParams(vmem_limit_bytes=8 * MIB + 4 * rows * width),
+        cost_estimate=pl.CostEstimate(
+            flops=4 * rows * low.shape[1] * size, bytes_accessed=4 * rows * size, transcendentals=0
+        ),
+        name="far_rows",
+    )(low, high, gates, gate_w, up_w)
+
+
+def own_kernel(start, extra, low, high, gates, gate_w, up_w, received, *parts):
+    rows, size = received.shape
+    size -= extra
     block = parts[0].shape[0]
-    for i, part in enumerate(parts):
-        span = pl.ds(i * block, block)
-        part[:, half:] = (
-            gates[span, :].astype(jnp.float32) + received[span, half:].astype(jnp.float32)
-        ).astype(jnp.bfloat16)
-    row_grads(low[...], high[...], gate_w, up_w, received, parts, half)
-
-
-def own_rows(count, low, high, gates, gate_w, up_w, received):
+    if extra:
+        for i, part in enumerate(parts):
+            span = pl.ds(i * block, block)
+            part[:, size:] = (
+                gates[span, :].astype(jnp.float32) + received[span, size:].astype(jnp.float32)
+            ).astype(jnp.bfloat16)
+    row_grads(low[:rows, :], high[:rows, :], gate_w, up_w, received, parts, start, size)
+
+
+def own_rows(count, start, low, high, gates, gate_w, up_w, received):
     rows, width = received.shape
-    units = gate_w.shape[0]
-    return pl.pallas_call(
-        own_kernel,
+    return pl.pallas_call(
+        functools.partial(own_kernel, start, LANES if start else 0),
         out_shape=[struct((rows // count, width))] * count,
         in_specs=[VMEM] * 6,
         out_specs=[VMEM] * count,
-        compiler_params=pltpu.CompilerParams(vmem_limit_bytes=8 * MIB + 8 * rows * width),
+        compiler_params=pltpu.CompilerParams(vmem_limit_bytes=8 * MIB + 16 * rows * width),
         cost_estimate=pl.CostEstimate(
-            flops=4 * rows * units * gate_w.shape[1],
-            bytes_accessed=4 * units * gate_w.shape[1],
+            flops=4 * rows * low.shape[1] * width,
+            bytes_accessed=4 * rows * width,
             transcendentals=0,
         ),
         name="own_rows",
     )(low, high, gates, gate_w, up_w, received)
 
 
-def add_kernel(left, right, out):
-    out[...] = (left[...].astype(jnp.float32) + right[...].astype(jnp.float32)).astype(
-        jnp.bfloat16
-    )
-
-
-def add_rows(left, right):
-    return pl.pallas_call(
-        add_kernel,
-        out_shape=struct(right.shape),
-        in_specs=[VMEM] * 2,
+def add_kernel(count, *refs):
+    out = refs[-1]
+    base = 0
+    for left, right in zip(refs[:count], refs[count:-1]):
+        total = left[...].astype(jnp.float32) + right[...].astype(jnp.float32)
+        out[:, base : base + left.shape[1]] = total.astype(jnp.bfloat16)
+        base += left.shape[1]
+
+
+def add_rows(lefts, rights):
+    count = len(lefts)
+    rows = lefts[0].shape[0]
+    width = sum(left.shape[1] for left in lefts)
+    return pl.pallas_call(
+        functools.partial(add_kernel, count),
+        out_shape=struct((rows, width)),
+        in_specs=[VMEM] * 2 * count,
         out_specs=VMEM,
-        compiler_params=pltpu.CompilerParams(vmem_limit_bytes=4 * MIB + 16 * right.size),
+        compiler_params=pltpu.CompilerParams(vmem_limit_bytes=4 * MIB + 16 * rows * width),
         name="add_rows",
-    )(left, right)
+    )(*lefts, *rights)
 
 
 def weight_kernel(chunk, factor_ref, halves, out, stage, sems):
@@ -422,13 +442,11 @@
     weights = (w_gate[0], w_up[0], w_down[0])
     tie = lax.optimization_barrier
 
-    token_rows = send_tokens(n_targets, ids, tokens)
+    token_rows, grad_rows = dispatch(n_targets, ids, tokens, gates, out_grad)
     ids_after, token_rows = tie((ids, token_rows))
     token_rows = exchange(token_rows)
-    grad_rows = send_grads(n_targets, ids_after, gates, out_grad)
-    table_ids, token_rows = tie((ids_after, token_rows))
-    grad_rows, *table = tie((grad_rows, *placement(n_targets, table_ids)))
     grad_rows = exchange(grad_rows)
+    token_rows, *table = tie((token_rows, *placement(n_targets, ids_after)))
 
     token_held = cross(token_rows, far_bits)
     near = sorted(token_held)
@@ -441,27 +459,41 @@
     token_halves, activated, slope, hidden = forward(
         token_near + token_far, weights[0], weights[1]
     )
-    activated, slope, hidden, *grad_near = tie((activated, slope, hidden, *grad_near))
+    activated, slope, hidden, *grad_near[1:] = tie((activated, slope, hidden, *grad_near[1:]))
     grad_far = [flip(value, "dp", 1) for value in grad_near]
 
     part, grad_halves, gate_f, up_f, low, high, gate_column = backward(
         grad_near + grad_far, activated, slope, hidden, weights
     )
+    middle = width // 4
     received = flip(part, "dp", 1)
-    grad_gate = weight_grad(gate_f, token_halves)
-    received, grad_gate = tie((received, grad_gate))
-    totals = own_rows(len(near), low, high, gate_column, weights[0], weights[1], received)
-    sums = dict(zip(near, totals))
+    other = far_rows(middle, low, high, gate_column, weights[0], weights[1])
+    received, other = tie((received, other))
+    left = own_rows(len(near), 0, low, high, gate_column, weights[0], weights[1], received)
+    received = flip(other, "dp", 1)
+    received, left = tie((received, left))
+    right = own_rows(len(near), middle, low, high, gate_column, weights[0], weights[1], received)
+    lefts, rights = dict(zip(near, left)), dict(zip(near, right))
+    for bit in reversed(far_bits):
+        masks = [mask for mask in lefts if mask & bit]
+        moved_left = {mask: flip(lefts.pop(mask), "dp", bit) for mask in masks}
+        moved_right = {mask: flip(rights.pop(mask), "dp", bit) for mask in masks}
+        if bit == far_bits[-1]:
+            moved_left, rights, gate_f, up_f, hidden = tie(
+                (moved_left, rights, gate_f, up_f, hidden)
+            )
+            grad_gate = weight_grad(gate_f, token_halves)
+            moved_right, grad_gate = tie((moved_right, grad_gate))
+        for mask in masks:
+            terms = (lefts[mask ^ bit], rights[mask ^ bit]), (moved_left[mask], moved_right[mask])
+            if bit == far_bits[0]:
+                returned = exchange(add_rows(*terms))
+            else:
+                lefts[mask ^ bit] = add_rows(terms[0][:1], terms[1][:1])
+                rights[mask ^ bit] = add_rows(terms[0][1:], terms[1][1:])
     grad_up = weight_grad(up_f, token_halves)
-    for bit in reversed(far_bits):
-        moved = {mask: flip(sums.pop(mask), "dp", bit) for mask in list(sums) if mask & bit}
-        if bit == far_bits[0]:
-            moved, grad_up = tie((moved, grad_up))
-        for mask, value in moved.items():
-            sums[mask ^ bit] = add_rows(sums[mask ^ bit], value)
-    returned = exchange(sums[0])
     grad_down = weight_grad(hidden, grad_halves)
-    returned, grad_down = tie((returned, grad_down))
+    returned, grad_up, grad_down = tie((returned, grad_up, grad_down))
     token_grad, gate_grad = combine(table, gates, returned, width)
     return (token_grad, gate_grad.T, grad_gate[None], grad_up[None], grad_down[None])
 

time: 75.4 us -> 73.8 us (0.979)
  blocking collectives: 0 us -> 16.3 us
  waiting for transfers between devices: 28.5 us -> 18 us
  starting transfers between devices: 21.2 us -> 14.9 us
  local copies, waits for them, and re-layouts: 5.63 us -> 4.51 us
    all_to_all x0 -> x1, blocking collectives: none -> 16.3 us  [exchange(): lax.all_to_all(blocks, 'expert', split_axis=0, concat_axis=0, tiled=True)]
    ppermute x8 -> x10, waiting for transfers between devices: 15.2 us -> 8.14 us  [flip(): return lax.ppermute(value, axis, [(i, i ^ bit) for i in range(size)])]
    all_to_all x3 -> x2, starting transfers between devices: 15.9 us -> 9.31 us  [exchange(): lax.all_to_all(blocks, 'expert', split_axis=0, concat_axis=0, tiled=True)]
    all_to_all x3 -> x2, waiting for transfers between devices: 13.4 us -> 9.83 us  [exchange(): lax.all_to_all(blocks, 'expert', split_axis=0, concat_axis=0, tiled=True)]
    unnamed x28, local copies, waits for them, and re-layouts: 5.63 us -> 4.51 us
    pallas_call x4 -> x5, Pallas kernels: 4.97 us -> 5.82 us  [the longest x1 2.29 us: dispatch(): pl.pallas_call(functools.partial(dispatch_kernel, n_targets), out_shape=[...]
    pallas_call x1, Pallas kernels: 3.37 us -> 2.54 us  [backward(): pl.pallas_call(functools.partial(backward_kernel, count), out_shape=[stru...]
    ppermute x8 -> x10, starting transfers between devices: 5.26 us -> 5.63 us  [flip(): return lax.ppermute(value, axis, [(i, i ^ bit) for i in range(size)])]
  transfers between devices with their start and end apart: 11 -> 12, of which waited for: 9 -> 9; matrix products, arithmetic and copies ran while one was open for 0% -> 0% of each run, Pallas kernels for 13% -> 17%
where the time goes in v4:
time: 73.8 us; the launch traced here: 73.2 us
  Pallas kernels  18.7 us (25%)
  waiting for transfers between devices  18 us (24%)
  blocking collectives  16.3 us (22%)
  starting transfers between devices  14.9 us (20%)
  local copies, waits for them, and re-layouts  4.51 us (6%)
  between operations  0.83 us (1%)
    all_to_all x1, blocking collectives, exchange(): lax.all_to_all(blocks, 'expert', split_axis=0, concat_axis=0, tiled=True)  16.3 us
    all_to_all x2, waiting for transfers between devices, exchange(): lax.all_to_all(blocks, 'expert', split_axis=0, concat_axis=0, tiled=True)  9.83 us
    all_to_all x2, starting transfers between devices, exchange(): lax.all_to_all(blocks, 'expert', split_axis=0, concat_axis=0, tiled=True)  9.31 us
    ppermute x10, waiting for transfers between devices, flip(): return lax.ppermute(value, axis, [(i, i ^ bit) for i in range(size)])  8.14 us
    pallas_call x3, Pallas kernels, weight_grad(): pl.pallas_call(functools.partial(weight_kernel, chunk), out_shape=struct(...  5.97 us
    ppermute x10, starting transfers between devices, flip(): return lax.ppermute(value, axis, [(i, i ^ bit) for i in range(size)])  5.63 us
    unnamed x28, local copies, waits for them, and re-layouts  4.51 us
    pallas_call x1, Pallas kernels, forward(): pl.pallas_call(functools.partial(forward_kernel, count), out_shape=[struc...  3.21 us
  transfers between devices with their start and end apart: 12, of which 9 were waited for; matrix products, arithmetic and copies ran while one was open for 0% of the time, Pallas kernels for 17%

profile of v4, /device:TPU:0, one launch (start us, length us, event | category | flops | bytes accessed | tf_op | source)
XLA Modules:
  0.0 73.2 jit_solution(6907151377663048285)
XLA Ops:
  0.6 2.3 %dispatch.1 = (bf16[64,2048]{1,0:T(8,128)(2,1)}, bf16[64,2048]{1,0:T(8,128)(2,1)}) custom-call(s32[8,32]{1,0:T(8,128)} %bitcast.32, bf16[32,4096]{1,0:T(8,128)(2,1)} %refs_1_.1, bf16[8,32]{1,0:T(8,128)(2,1)} %bitcast.30, bf16[32,4096]{1,0:T(8,128)(2,1)} %refs_3_.1), custom_call_target="tpu_custom_call" | custom-call | tf_op jit(solution)/shard_map/dispatch/pallas_call | solution.py:84
  2.9 16.3 %all_to_all.15 = bf16[8,8,2048]{2,1,0:T(8,128)(2,1)} all-to-all(bf16[8,8,2048]{2,1,0:T(8,128)(2,1)} %bitcast.38), channel_id=1, replica_groups=mesh['expert'=8,'dp'=4] {'expert'}, dimensions={0} | all-to-all | bytes 524288 | tf_op jit(solution)/shard_map/all_to_all | solution.py:424
  19.2 3.6 %all-to-all-start.1 = ((bf16[8,8,2048]{2,1,0:T(8,128)(2,1)}), bf16[8,8,2048]{2,1,0:T(8,128)(2,1)S(1)}, u32[]{:S(2)}, u32[]{:S(2)}) async-start(bf16[8,8,2048]{2,1,0:T(8,128)(2,1)} %bitcast.37), calls=%async_computation.1 | async-start | bytes 524288 | tf_op jit(solution)/shard_map/all_to_all | solution.py:424
  23.7 1.6 %collective-permute-start = (bf16[64,2048]{1,0:T(8,128)(2,1)}, bf16[64,2048]{1,0:T(8,128)(2,1)}, u32[]{:S(2)}, u32[]{:S(2)}) collective-permute-start(bf16[64,2048]{1,0:T(8,128)(2,1)} %bitcast.3.refs_0_), channel_id=1, source_target_pairs={{0,2},{1,3},{2,0},{3,1},{4,6},{5,7},{6,4},{7,5},{8,10},{9,11},{10,... | collective-permute-start | bytes 786440 | tf_op jit(solution)/shard_map/ppermute | solution.py:417
  25.3 6.1 %all-to-all-done.1 = bf16[8,8,2048]{2,1,0:T(8,128)(2,1)S(1)} async-done(((bf16[8,8,2048]{2,1,0:T(8,128)(2,1)}), bf16[8,8,2048]{2,1,0:T(8,128)(2,1)S(1)}, u32[]{:S(2)}, u32[]{:S(2)}) %all-to-all-start.1) | async-done | bytes 262176 | tf_op jit(solution)/shard_map/all_to_all | solution.py:424
  31.5 1.5 %collective-permute-start.3 = (bf16[64,2048]{1,0:T(8,128)(2,1)S(1)}, bf16[64,2048]{1,0:T(8,128)(2,1)S(1)}, u32[]{:S(2)}, u32[]{:S(2)}) collective-permute-start(bf16[64,2048]{1,0:T(8,128)(2,1)S(1)} %bitcast.27), channel_id=1, source_target_pairs={{0,2},{1,3},{2,0},{3,1},{4,6},{5,7},{6,4},{7,5},{8,10},{9,11},{10,... | collective-permute-start | bytes 786440 | tf_op jit(solution)/shard_map/ppermute | solution.py:417
  33.2 1.9 %copy-done.1 = bf16[1,384,4096]{2,1,0:T(8,128)(2,1)S(1)} copy-done((bf16[1,384,4096]{2,1,0:T(8,128)(2,1)S(1)}, bf16[1,384,4096]{2,1,0:T(8,128)(2,1)}, u32[]{:S(2)}) %copy-start.1) | copy-done | bytes 3145752
  35.1 3.2 %forward.1 = (bf16[256,2048]{1,0:T(8,128)(2,1)S(1)}, f32[384,256]{1,0:T(8,128)S(1)}, f32[384,256]{1,0:T(8,128)S(1)}, bf16[384,256]{1,0:T(8,128)(2,1)S(1)}) custom-call(bf16[64,2048]{1,0:T(8,128)(2,1)} %bitcast.3.refs_0_, bf16[64,2048]{1,0:T(8,128)(2,1)} %collective-permute-done.refs_1_, bf16[64,2048]{1,0:T(8,128)(2,1)} %collective-permute-done.1.refs_2_, ...), custom_call_target="tpu_custom_call" | custom-call | flops 1610612736 | bytes 6291456 | tf_op jit(solution)/shard_map/forward/pallas_call | solution.py:158
  38.4 1.8 %collective-permute-done.3.refs_1_ = bf16[64,2048]{1,0:T(8,128)(2,1)S(1)} collective-permute-done((bf16[64,2048]{1,0:T(8,128)(2,1)S(1)}, bf16[64,2048]{1,0:T(8,128)(2,1)S(1)}, u32[]{:S(2)}, u32[]{:S(2)}) %collective-permute-start.3) | collective-permute-done | bytes 262176 | tf_op jit(solution)/shard_map/ppermute | solution.py:417
  40.2 1.5 %collective-permute-done.5.refs_3_ = bf16[64,2048]{1,0:T(8,128)(2,1)S(1)} collective-permute-done((bf16[64,2048]{1,0:T(8,128)(2,1)S(1)}, bf16[64,2048]{1,0:T(8,128)(2,1)S(1)}, u32[]{:S(2)}, u32[]{:S(2)}) %collective-permute-start.5) | collective-permute-done | bytes 262176 | tf_op jit(solution)/shard_map/ppermute | solution.py:417
  41.8 2.5 %backward.1 = (bf16[128,1024]{1,0:T(8,128)(2,1)S(1)}, bf16[256,2048]{1,0:T(8,128)(2,1)S(1)}, bf16[384,256]{1,0:T(8,128)(2,1)S(1)}, bf16[384,256]{1,0:T(8,128)(2,...) custom-call(bf16[64,2048]{1,0:T(8,128)(2,1)S(1)} %bitcast.29, ...), custom_call_target="tpu_custom_call" | custom-call | flops 1207959552 | bytes 3145728 | tf_op jit(solution)/shard_map/backward/pallas_call | solution.py:244
  45.1 0.9 %far_rows.1 = bf16[128,1152]{1,0:T(8,128)(2,1)S(1)} custom-call(bf16[256,768]{1,0:T(8,128)(2,1)S(1)} %get-tuple-element.75.low, bf16[256,768]{1,0:T(8,128)(2,1)S(1)} %get-tuple-element.76.high, bf16[256,128]{1,0:T(8,128)(2,1)S(1)} %get-tuple-element.77.gates, bf16[384,4096]{1,0:T(8,128)(2,1)S(1)} %bitcast.17, bf16[384,4096]{1,0:T(8,128)(2,1)S(1)} %bitcast.22), custom_call_target="tpu_custom_call" | custom-call | flops 805306368 | bytes 1048576 | tf_op jit(solution)/shard_map/far_rows/pallas_call | solution.py:273
  46.7 0.9 %own_rows.2 = (bf16[64,1024]{1,0:T(8,128)(2,1)S(1)}, bf16[64,1024]{1,0:T(8,128)(2,1)S(1)}) custom-call(bf16[256,768]{1,0:T(8,128)(2,1)S(1)} %get-tuple-element.75.low, bf16[256,768]{1,0:T(8,128)(2,1)S(1)} %get-tuple-element.76.high, bf16[256,128]{1,0:T(8,128)(2,1)S(1)} %get-tuple-element.77.gates, bf16[384,4096]{1,0:T(8,128)(2,1)S(1)} %bitcast.18, ...), custom_call_target="tpu_custom_call" | custom-call | flops 402653184 | bytes 524288 | tf_op jit(solution)/shard_map/own_rows/pallas_call | solution.py:301
  48.1 1.5 %collective-permute-start.8 = (bf16[64,1024]{1,0:T(8,128)(2,1)S(1)}, bf16[64,1024]{1,0:T(8,128)(2,1)S(1)}, u32[]{:S(2)}, u32[]{:S(2)}) collective-permute-start(bf16[64,1024]{1,0:T(8,128)(2,1)S(1)} %get-tuple-element.83), channel_id=1, source_target_pairs={{0,2},{1,3},{2,0},{3,1},{4,6},{5,7},{6,4},{7,5},{8,10},{9,11},{10,... | collective-permute-start | bytes 393224 | tf_op jit(solution)/shard_map/ppermute | solution.py:417
  49.6 0.9 %own_rows.3 = (bf16[64,1152]{1,0:T(8,128)(2,1)S(1)}, bf16[64,1152]{1,0:T(8,128)(2,1)S(1)}) custom-call(bf16[256,768]{1,0:T(8,128)(2,1)S(1)} %get-tuple-element.75.low, bf16[256,768]{1,0:T(8,128)(2,1)S(1)} %get-tuple-element.76.high, bf16[256,128]{1,0:T(8,128)(2,1)S(1)} %get-tuple-element.77.gates, bf16[384,4096]{1,0:T(8,128)(2,1)S(1)} %bitcast.19, ...), custom_call_target="tpu_custom_call" | custom-call | flops 452984832 | bytes 589824 | tf_op jit(solution)/shard_map/own_rows/pallas_call | solution.py:301
  51.2 3.0 %collective-permute-done.8.refs_2_ = bf16[64,1024]{1,0:T(8,128)(2,1)S(1)} collective-permute-done((bf16[64,1024]{1,0:T(8,128)(2,1)S(1)}, bf16[64,1024]{1,0:T(8,128)(2,1)S(1)}, u32[]{:S(2)}, u32[]{:S(2)}) %collective-permute-start.8) | collective-permute-done | bytes 131104 | tf_op jit(solution)/shard_map/ppermute | solution.py:417
  54.2 2.0 %weight_grad.3 = bf16[384,4096]{1,0:T(8,128)(2,1)} custom-call(bf16[384,256]{1,0:T(8,128)(2,1)S(1)} %get-tuple-element.91.factor_ref, bf16[256,2048]{1,0:T(8,128)(2,1)S(1)} %get-tuple-element.92.halves), custom_call_target="tpu_custom_call" | custom-call | flops 805306368 | bytes 3145728 | tf_op jit(solution)/shard_map/weight_grad/pallas_call | solution.py:364
  56.8 0.8 %add_rows.1 = bf16[64,2176]{1,0:T(8,128)(2,1)} custom-call(bf16[64,1024]{1,0:T(8,128)(2,1)S(1)} %get-tuple-element.82.refs_0_, bf16[64,1152]{1,0:T(8,128)(2,1)S(1)} %get-tuple-element.88.refs_1_, bf16[64,1024]{1,0:T(8,128)(2,1)S(1)} %collective-permute-done.8.refs_2_, bf16[64,1152]{1,0:T(8,128)(2,1)S(1)} %collective-permute-done.9.refs_3_), custom_call_target="tpu_custom_call" | custom-call | tf_op jit(solution)/shard_map/add_rows/pallas_call | solution.py:329
  57.6 5.7 %all-to-all-start.2 = ((bf16[8,8,2176]{2,1,0:T(8,128)(2,1)}), bf16[8,8,2176]{2,1,0:T(8,128)(2,1)S(1)}, u32[]{:S(2)}, u32[]{:S(2)}) async-start(bf16[8,8,2176]{2,1,0:T(8,128)(2,1)} %bitcast.9), calls=%async_computation.2 | async-start | bytes 557056 | tf_op jit(solution)/shard_map/all_to_all | solution.py:424
  63.3 1.2 %copy-done.4 = bf16[256,2048]{1,0:T(8,128)(2,1)S(1)} copy-done((bf16[256,2048]{1,0:T(8,128)(2,1)S(1)}, bf16[256,2048]{1,0:T(8,128)(2,1)}, u32[]{:S(2)}) %copy-start.4) | copy-done | bytes 1048600
  64.5 2.0 %weight_grad.4 = bf16[384,4096]{1,0:T(8,128)(2,1)} custom-call(bf16[384,256]{1,0:T(8,128)(2,1)S(1)} %copy-done.11, bf16[256,2048]{1,0:T(8,128)(2,1)S(1)} %copy-done.4), custom_call_target="tpu_custom_call" | custom-call | flops 805306368 | bytes 3145728 | tf_op jit(solution)/shard_map/weight_grad/pallas_call | solution.py:364
  66.6 2.0 %weight_grad.5 = bf16[384,4096]{1,0:T(8,128)(2,1)} custom-call(bf16[384,256]{1,0:T(8,128)(2,1)S(1)} %copy-done.9, bf16[256,2048]{1,0:T(8,128)(2,1)S(1)} %copy-done.7), custom_call_target="tpu_custom_call" | custom-call | flops 805306368 | bytes 3145728 | tf_op jit(solution)/shard_map/weight_grad/pallas_call | solution.py:364
  68.6 3.7 %all-to-all-done.2 = bf16[8,8,2176]{2,1,0:T(8,128)(2,1)S(1)} async-done(((bf16[8,8,2176]{2,1,0:T(8,128)(2,1)}), bf16[8,8,2176]{2,1,0:T(8,128)(2,1)S(1)}, u32[]{:S(2)}, u32[]{:S(2)}) %all-to-all-start.2) | async-done | bytes 278560 | tf_op jit(solution)/shard_map/all_to_all | solution.py:424
  72.3 1.0 %combine.1 = (bf16[32,4096]{1,0:T(8,128)(2,1)}, f32[8,32]{1,0:T(8,128)}) custom-call(bf16[64,32]{1,0:T(8,128)(2,1)S(1)} %get-tuple-element.60.first, bf16[64,32]{1,0:T(8,128)(2,1)S(1)} %get-tuple-element.61.second, s32[64,32]{1,0:T(8,128)S(1)} %get-tuple-element.62.choice_ref, bf16[8,32]{1,0:T(8,128)(2,1)S(1)} %bitcast.31, bf16[64,2176]{1,0:T(8,128)(2,1)S(1)} %bitcast.26), custom_call_target="tpu_custom_call" | custom-call | tf_op jit(solution)/shard_map/combine/pallas_call | solution.py:405
  (41 shorter events, 4.4 us)
Async XLA Ops:
  19.2 12.2 %all-to-all-start.1 = ((bf16[8,8,2048]{2,1,0:T(8,128)(2,1)}), bf16[8,8,2048]{2,1,0:T(8,128)(2,1)S(1)}, u32[]{:S(2)}, u32[]{:S(2)}) async-start(bf16[8,8,2048]{2,1,0:T(8,128)(2,1)} %bitcast.37), calls=%async_computation.1 | async-start | bytes 524288 | tf_op jit(solution)/shard_map/all_to_all | solution.py:424
  23.5 9.7 %copy-start = (bf16[1,384,4096]{2,1,0:T(8,128)(2,1)S(1)}, bf16[1,384,4096]{2,1,0:T(8,128)(2,1)}, u32[]{:S(2)}) copy-start(bf16[1,384,4096]{2,1,0:T(8,128)(2,1)} %param.11) | copy-start | bytes 9437188
  23.7 7.8 %collective-permute-start = (bf16[64,2048]{1,0:T(8,128)(2,1)}, bf16[64,2048]{1,0:T(8,128)(2,1)}, u32[]{:S(2)}, u32[]{:S(2)}) collective-permute-start(bf16[64,2048]{1,0:T(8,128)(2,1)} %bitcast.3.refs_0_), channel_id=1, source_target_pairs={{0,2},{1,3},{2,0},{3,1},{4,6},{5,7},{6,4},{7,5},{8,10},{9,11},{10,... | collective-permute-start | bytes 786440 | tf_op jit(solution)/shard_map/ppermute | solution.py:417
  25.2 8.0 %collective-permute-start.1 = (bf16[64,2048]{1,0:T(8,128)(2,1)}, bf16[64,2048]{1,0:T(8,128)(2,1)}, u32[]{:S(2)}, u32[]{:S(2)}) collective-permute-start(bf16[64,2048]{1,0:T(8,128)(2,1)} %bitcast.3.refs_0_), channel_id=1, source_target_pairs={{0,1},{1,0},{2,3},{3,2},{4,5},{5,4},{6,7},{7,6},{8,9},{9,8},{10,11... | collective-permute-start | bytes 786440 | tf_op jit(solution)/shard_map/ppermute | solution.py:417
  31.5 1.7 %collective-permute-start.2 = (bf16[64,2048]{1,0:T(8,128)(2,1)}, bf16[64,2048]{1,0:T(8,128)(2,1)S(1)}, u32[]{:S(2)}, u32[]{:S(2)}) collective-permute-start(bf16[64,2048]{1,0:T(8,128)(2,1)} %collective-permute-done.refs_1_), channel_id=1, source_target_pairs={{0,1},{1,0},{2,3},{3,2},{4,5},{5,4},{6,7},{7,6},{8,9},{9,8},{10,11... | collective-permute-start | bytes 786440 | tf_op jit(solution)/shard_map/ppermute | solution.py:417
  31.5 8.7 %collective-permute-start.3 = (bf16[64,2048]{1,0:T(8,128)(2,1)S(1)}, bf16[64,2048]{1,0:T(8,128)(2,1)S(1)}, u32[]{:S(2)}, u32[]{:S(2)}) collective-permute-start(bf16[64,2048]{1,0:T(8,128)(2,1)S(1)} %bitcast.27), channel_id=1, source_target_pairs={{0,2},{1,3},{2,0},{3,1},{4,6},{5,7},{6,4},{7,5},{8,10},{9,11},{10,... | collective-permute-start | bytes 786440 | tf_op jit(solution)/shard_map/ppermute | solution.py:417
  33.0 7.2 %collective-permute-start.4 = (bf16[64,2048]{1,0:T(8,128)(2,1)S(1)}, bf16[64,2048]{1,0:T(8,128)(2,1)S(1)}, u32[]{:S(2)}, u32[]{:S(2)}) collective-permute-start(bf16[64,2048]{1,0:T(8,128)(2,1)S(1)} %bitcast.28), channel_id=1, source_target_pairs={{0,1},{1,0},{2,3},{3,2},{4,5},{5,4},{6,7},{7,6},{8,9},{9,8},{10,11... | collective-permute-start | bytes 786440 | tf_op jit(solution)/shard_map/ppermute | solution.py:417
  33.2 1.9 %copy-start.1 = (bf16[1,384,4096]{2,1,0:T(8,128)(2,1)S(1)}, bf16[1,384,4096]{2,1,0:T(8,128)(2,1)}, u32[]{:S(2)}) copy-start(bf16[1,384,4096]{2,1,0:T(8,128)(2,1)} %param.12) | copy-start | bytes 9437188
  35.1 6.6 %copy-start.2 = (bf16[1,384,4096]{2,1,0:T(8,128)(2,1)S(1)}, bf16[1,384,4096]{2,1,0:T(8,128)(2,1)}, u32[]{:S(2)}) copy-start(bf16[1,384,4096]{2,1,0:T(8,128)(2,1)} %param.12) | copy-start | bytes 9437188
  35.1 6.6 %copy-start.5 = (bf16[1,384,4096]{2,1,0:T(8,128)(2,1)S(1)}, bf16[1,384,4096]{2,1,0:T(8,128)(2,1)}, u32[]{:S(2)}) copy-start(bf16[1,384,4096]{2,1,0:T(8,128)(2,1)} %param.13) | copy-start | bytes 9437188
  38.4 6.0 %copy-start.8 = (bf16[384,256]{1,0:T(8,128)(2,1)}, bf16[384,256]{1,0:T(8,128)(2,1)S(1)}, u32[]{:S(2)}) copy-start(bf16[384,256]{1,0:T(8,128)(2,1)S(1)} %get-tuple-element.95.refs_6_.factor_ref) | copy-start | bytes 589828
  38.4 15.8 %copy-start.3 = (bf16[256,2048]{1,0:T(8,128)(2,1)}, bf16[256,2048]{1,0:T(8,128)(2,1)S(1)}, u32[]{:S(2)}) copy-start(bf16[256,2048]{1,0:T(8,128)(2,1)S(1)} %get-tuple-element.92.halves) | copy-start | bytes 3145732
  40.2 1.5 %collective-permute-start.5 = (bf16[64,2048]{1,0:T(8,128)(2,1)S(1)}, bf16[64,2048]{1,0:T(8,128)(2,1)S(1)}, u32[]{:S(2)}, u32[]{:S(2)}) collective-permute-start(bf16[64,2048]{1,0:T(8,128)(2,1)S(1)} %collective-permute-done.3.refs_1_), channel_id=1, source_target_pairs={{0,1},{1,0},{2,3},{3,2},{4,5},{5,4},{6,7},{7,6},{8,9},{9,8},{10,11... | collective-permute-start | bytes 786440 | tf_op jit(solution)/shard_map/ppermute | solution.py:417
  45.0 1.1 %copy-start.6 = (bf16[256,2048]{1,0:T(8,128)(2,1)}, bf16[256,2048]{1,0:T(8,128)(2,1)S(1)}, u32[]{:S(2)}) copy-start(bf16[256,2048]{1,0:T(8,128)(2,1)S(1)} %get-tuple-element.96.halves) | copy-start | bytes 3145732
  45.0 1.5 %collective-permute-start.6 = (bf16[128,1024]{1,0:T(8,128)(2,1)S(1)}, bf16[128,1024]{1,0:T(8,128)(2,1)S(1)}, u32[]{:S(2)}, u32[]{:S(2)}) collective-permute-start(bf16[128,1024]{1,0:T(8,128)(2,1)S(1)} %get-tuple-element.74), channel_id=1, source_target_pairs={{0,1},{1,0},{2,3},{3,2},{4,5},{5,4},{6,7},{7,6},{8,9},{9,8},{10,11... | collective-permute-start | bytes 786440 | tf_op jit(solution)/shard_map/ppermute | solution.py:417
  46.5 1.6 %collective-permute-start.7 = (bf16[128,1152]{1,0:T(8,128)(2,1)S(1)}, bf16[128,1152]{1,0:T(8,128)(2,1)S(1)}, u32[]{:S(2)}, u32[]{:S(2)}) collective-permute-start(bf16[128,1152]{1,0:T(8,128)(2,1)S(1)} %far_rows.1), channel_id=1, source_target_pairs={{0,1},{1,0},{2,3},{3,2},{4,5},{5,4},{6,7},{7,6},{8,9},{9,8},{10,11... | collective-permute-start | bytes 884744 | tf_op jit(solution)/shard_map/ppermute | solution.py:417
  48.1 6.1 %collective-permute-start.8 = (bf16[64,1024]{1,0:T(8,128)(2,1)S(1)}, bf16[64,1024]{1,0:T(8,128)(2,1)S(1)}, u32[]{:S(2)}, u32[]{:S(2)}) collective-permute-start(bf16[64,1024]{1,0:T(8,128)(2,1)S(1)} %get-tuple-element.83), channel_id=1, source_target_pairs={{0,2},{1,3},{2,0},{3,1},{4,6},{5,7},{6,4},{7,5},{8,10},{9,11},{10,... | collective-permute-start | bytes 393224 | tf_op jit(solution)/shard_map/ppermute | solution.py:417
  50.5 12.8 %copy-start.11 = (bf16[384,256]{1,0:T(8,128)(2,1)S(1)}, bf16[384,256]{1,0:T(8,128)(2,1)}, u32[]{:S(2)}) copy-start(bf16[384,256]{1,0:T(8,128)(2,1)} %copy-done.10) | copy-start | bytes 589828
  50.5 6.3 %collective-permute-start.9 = (bf16[64,1152]{1,0:T(8,128)(2,1)S(1)}, bf16[64,1152]{1,0:T(8,128)(2,1)S(1)}, u32[]{:S(2)}, u32[]{:S(2)}) collective-permute-start(bf16[64,1152]{1,0:T(8,128)(2,1)S(1)} %get-tuple-element.90), channel_id=1, source_target_pairs={{0,2},{1,3},{2,0},{3,1},{4,6},{5,7},{6,4},{7,5},{8,10},{9,11},{10,... | collective-permute-start | bytes 442376 | tf_op jit(solution)/shard_map/ppermute | solution.py:417
  56.2 10.4 %copy-start.7 = (bf16[256,2048]{1,0:T(8,128)(2,1)S(1)}, bf16[256,2048]{1,0:T(8,128)(2,1)}, u32[]{:S(2)}) copy-start(bf16[256,2048]{1,0:T(8,128)(2,1)} %copy-done.6) | copy-start | bytes 3145732
  56.2 10.4 %copy-start.9 = (bf16[384,256]{1,0:T(8,128)(2,1)S(1)}, bf16[384,256]{1,0:T(8,128)(2,1)}, u32[]{:S(2)}) copy-start(bf16[384,256]{1,0:T(8,128)(2,1)} %copy-done.8) | copy-start | bytes 589828
  57.6 14.7 %all-to-all-start.2 = ((bf16[8,8,2176]{2,1,0:T(8,128)(2,1)}), bf16[8,8,2176]{2,1,0:T(8,128)(2,1)S(1)}, u32[]{:S(2)}, u32[]{:S(2)}) async-start(bf16[8,8,2176]{2,1,0:T(8,128)(2,1)} %bitcast.9), calls=%async_computation.2 | async-start | bytes 557056 | tf_op jit(solution)/shard_map/all_to_all | solution.py:424
  63.3 1.2 %copy-start.4 = (bf16[256,2048]{1,0:T(8,128)(2,1)S(1)}, bf16[256,2048]{1,0:T(8,128)(2,1)}, u32[]{:S(2)}) copy-start(bf16[256,2048]{1,0:T(8,128)(2,1)} %copy-done.3) | copy-start | bytes 3145732
  66.5 5.7 %copy-start.12 = (bf16[32,8]{0,1:T(8,128)(2,1)S(1)}, bf16[32,8]{0,1:T(8,128)(2,1)}, u32[]{:S(2)}) copy-start(bf16[32,8]{0,1:T(8,128)(2,1)} %param.9) | copy-start | bytes 1540
  (2 other events, 1.4 us)

commit v5 on v4

--- a/solution.py
+++ b/solution.py
@@ -34,7 +34,7 @@
     height = n_targets * BLOCK
     per_device = EXPERTS // n_targets
     row = lax.broadcasted_iota(jnp.int32, (height, 1), 0)
-    wanted = (row // BLOCK) * per_device
+    wanted = ((row // BLOCK) ^ lax.axis_index("expert")) * per_device
     slot = row % BLOCK
     matches = [ids[k : k + 1, :] == wanted for k in range(choices)]
     hit = functools.reduce(jnp.logical_or, matches)
@@ -56,7 +56,8 @@
 
 
 def dispatch_kernel(n_targets, *refs):
-    sources, (token_out, grad_out), targets, sems = refs[:4], refs[4:6], refs[6:10], refs[10]
+    sources, outs = refs[:4], refs[4 : 4 + n_targets]
+    targets, sems = refs[4 + n_targets : -1], refs[-1]
     ids_ref, tokens_ref, gates_ref, grads_ref = targets
     copies = [
         pltpu.make_async_copy(source, target, sems.at[i])
@@ -67,7 +68,10 @@
     copies[0].wait()
     matches, first, second = choice_table(ids_ref[...], n_targets)
     copies[1].wait()
-    token_out[...] = pick_rows(as_bf16(first), as_bf16(second), tokens_ref)
+    rows = pick_rows(as_bf16(first), as_bf16(second), tokens_ref)
+    half = rows.shape[1]
+    for k, out in enumerate(outs):
+        out[:, :half] = rows[k * BLOCK : (k + 1) * BLOCK]
     copies[2].wait()
     gates = gates_ref[...].astype(jnp.float32)
     scale = jnp.zeros(first.shape, jnp.float32)
@@ -76,16 +80,18 @@
     first = jnp.where(first, scale, 0.0).astype(jnp.bfloat16)
     second = jnp.where(second, scale, 0.0).astype(jnp.bfloat16)
     copies[3].wait()
-    grad_out[...] = pick_rows(first, second, grads_ref)
+    rows = pick_rows(first, second, grads_ref)
+    for k, out in enumerate(outs):
+        out[:, half:] = rows[k * BLOCK : (k + 1) * BLOCK]
 
 
 def dispatch(n_targets, ids, tokens, gates, out_grad):
     arrays = (ids, tokens, gates, out_grad)
     return pl.pallas_call(
         functools.partial(dispatch_kernel, n_targets),
-        out_shape=[struct((n_targets * BLOCK, tokens.shape[1] // 2))] * 2,
+        out_shape=[struct((BLOCK, tokens.shape[1]))] * n_targets,
         in_specs=[HBM] * 4,
-        out_specs=[VMEM] * 2,
+        out_specs=[VMEM] * n_targets,
         scratch_shapes=[pltpu.VMEM(a.shape, a.dtype) for a in arrays]
         + [pltpu.SemaphoreType.DMA((4,))],
         compiler_params=pltpu.CompilerParams(vmem_limit_bytes=60 * MIB),
@@ -116,6 +122,31 @@
         ),
         name="placement",
     )(ids)
+
+
+def pack_kernel(count, *refs):
+    blocks, (token_out, grad_out) = refs[:count], refs[count:]
+    half = token_out.shape[1]
+    for k in range(0, count, 2):
+        pair = jnp.concatenate([blocks[k][...], blocks[k + 1][...]], axis=0)
+        span = pl.ds(k * BLOCK, 2 * BLOCK)
+        token_out[span, :] = pair[:, :half]
+        grad_out[span, :] = pair[:, half:]
+
+
+def pack(blocks):
+    count = len(blocks)
+    shape = (count * BLOCK, blocks[0].shape[1] // 2)
+    return pl.pallas_call(
+        functools.partial(pack_kernel, count),
+        out_shape=[struct(shape)] * 2,
+        in_specs=[VMEM] * count,
+        out_specs=[VMEM] * 2,
+        compiler_params=pltpu.CompilerParams(
+            vmem_limit_bytes=4 * MIB + 16 * shape[0] * shape[1]
+        ),
+        name="pack",
+    )(*blocks)
 
 
 def gather_pieces(pieces, out):
@@ -314,75 +345,87 @@
 
 
 def add_kernel(count, *refs):
-    out = refs[-1]
+    lefts, rights, outs = refs[:count], refs[count : 2 * count], refs[2 * count :]
+    block = outs[0].shape[0]
     base = 0
-    for left, right in zip(refs[:count], refs[count:-1]):
-        total = left[...].astype(jnp.float32) + right[...].astype(jnp.float32)
-        out[:, base : base + left.shape[1]] = total.astype(jnp.bfloat16)
+    for left, right in zip(lefts, rights):
+        total = (left[...].astype(jnp.float32) + right[...].astype(jnp.float32)).astype(
+            jnp.bfloat16
+        )
+        for i, out in enumerate(outs):
+            out[:, base : base + left.shape[1]] = total[i * block : (i + 1) * block]
         base += left.shape[1]
 
 
-def add_rows(lefts, rights):
+def add_rows(lefts, rights, blocks=1):
     count = len(lefts)
     rows = lefts[0].shape[0]
     width = sum(left.shape[1] for left in lefts)
     return pl.pallas_call(
         functools.partial(add_kernel, count),
-        out_shape=struct((rows, width)),
+        out_shape=[struct((rows // blocks, width))] * blocks,
         in_specs=[VMEM] * 2 * count,
-        out_specs=VMEM,
+        out_specs=[VMEM] * blocks,
         compiler_params=pltpu.CompilerParams(vmem_limit_bytes=4 * MIB + 16 * rows * width),
         name="add_rows",
     )(*lefts, *rights)
 
 
-def weight_kernel(chunk, factor_ref, halves, out, stage, sems):
-    half = halves.shape[1]
-    low = factor_ref[...]
-    high = pltpu.roll(low.astype(jnp.float32), CAP, 1).astype(jnp.bfloat16)
+def weight_kernel(chunk, *refs):
+    gate_f, up_f, down_f, token_halves, grad_halves = refs[:5]
+    outs, stages, sems = refs[5:8], refs[8:11], refs[11]
+    half = token_halves.shape[1]
+    jobs = ((gate_f, token_halves), (up_f, token_halves), (down_f, grad_halves))
+    factors = []
+    for factor, _ in jobs:
+        low = factor[...]
+        high = pltpu.roll(low.astype(jnp.float32), CAP, 1).astype(jnp.bfloat16)
+        factors.append((low, high))
     copies = []
-    for factor, base in ((low, 0), (high, half)):
-        for start in range(0, half, chunk):
-            span = pl.ds(base + start, chunk)
-            stage[:, span] = jnp.dot(
-                factor, halves[:, pl.ds(start, chunk)], preferred_element_type=jnp.float32
-            ).astype(jnp.bfloat16)
-            copies.append(
-                pltpu.make_async_copy(
+    for start in range(0, half, chunk):
+        for (_, halves), pair, out, stage in zip(jobs, factors, outs, stages):
+            for factor, base in zip(pair, (0, half)):
+                span = pl.ds(base + start, chunk)
+                stage[:, span] = jnp.dot(
+                    factor, halves[:, pl.ds(start, chunk)], preferred_element_type=jnp.float32
+                ).astype(jnp.bfloat16)
+                copy = pltpu.make_async_copy(
                     stage.at[:, span], out.at[:, span], sems.at[len(copies)]
                 )
-            )
-            copies[-1].start()
+                copy.start()
+                copies.append(copy)
     for copy in copies:
         copy.wait()
 
 
-def weight_grad(factor, halves):
-    units, rows = factor.shape
-    half = halves.shape[1]
+def weight_grads(factors, token_halves, grad_halves):
+    units, rows = factors[0].shape
+    half = token_halves.shape[1]
     chunk = 512 if half % 512 == 0 else half
+    shape = (units, 2 * half)
     return pl.pallas_call(
         functools.partial(weight_kernel, chunk),
-        out_shape=struct((units, 2 * half)),
-        in_specs=[VMEM] * 2,
-        out_specs=HBM,
-        scratch_shapes=[
-            pltpu.VMEM((units, 2 * half), jnp.bfloat16),
-            pltpu.SemaphoreType.DMA((2 * half // chunk,)),
-        ],
+        out_shape=[struct(shape)] * 3,
+        in_specs=[VMEM] * 5,
+        out_specs=[HBM] * 3,
+        scratch_shapes=[pltpu.VMEM(shape, jnp.bfloat16)] * 3
+        + [pltpu.SemaphoreType.DMA((6 * half // chunk,))],
         compiler_params=pltpu.CompilerParams(
-            vmem_limit_bytes=8 * MIB + 4 * units * half + 8 * units * rows
+            vmem_limit_bytes=6 * MIB + 12 * units * half + 16 * units * rows
         ),
         cost_estimate=pl.CostEstimate(
-            flops=4 * rows * units * half,
-            bytes_accessed=4 * units * half,
+            flops=12 * rows * units * half,
+            bytes_accessed=12 * units * half,
             transcendentals=0,
         ),
-        name="weight_grad",
-    )(factor, halves)
-
-
-def combine_kernel(first, second, choice_ref, gates_ref, back, token_ref, gate_ref):
+        name="weight_grads",
+    )(*factors, token_halves, grad_halves)
+
+
+def combine_kernel(n_targets, first, second, choice_ref, gates_ref, *refs):
+    blocks, (token_ref, gate_ref) = refs[:n_targets], refs[n_targets:]
+    order = offsets(n_targets)
+    back = jnp.concatenate([blocks[order.index(k)][...] for k in range(n_targets)], axis=0)
     half = token_ref.shape[1] // 2
     choices, tokens = gates_ref.shape
     rows = back[:, :half]
@@ -400,16 +443,19 @@
         gate_ref[k : k + 1, :] = jnp.sum(chosen, axis=0, keepdims=True) / gate
 
 
-def combine(table, gates, returned, width):
+def combine(table, gates, blocks, width):
+    n_targets = len(blocks)
     choices, tokens = gates.shape
     return pl.pallas_call(
-        combine_kernel,
+        functools.partial(combine_kernel, n_targets),
         out_shape=[struct((tokens, width)), struct((choices, tokens), jnp.float32)],
-        in_specs=[VMEM] * 5,
+        in_specs=[VMEM] * (4 + n_targets),
         out_specs=[VMEM] * 2,
-        compiler_params=pltpu.CompilerParams(vmem_limit_bytes=4 * MIB + 16 * returned.size),
+        compiler_params=pltpu.CompilerParams(
+            vmem_limit_bytes=4 * MIB + 16 * n_targets * BLOCK * width
+        ),
         name="combine",
-    )(*table, gates, returned)
+    )(*table, gates, *blocks)
 
 
 def flip(value, axis, bit):
@@ -417,12 +463,14 @@
     return lax.ppermute(value, axis, [(i, i ^ bit) for i in range(size)])
 
 
-def exchange(value):
-    n_targets = lax.axis_size("expert")
-    rows, width = value.shape
-    blocks = value.reshape(n_targets, rows // n_targets, width)
-    blocks = lax.all_to_all(blocks, "expert", split_axis=0, concat_axis=0, tiled=True)
-    return blocks.reshape(rows, width)
+def offsets(count):
+    near, far = list(range(1, count // 2)), list(range(count // 2, count))
+    return [0] + near[:1] + far + near[1:]
+
+
+def exchange(blocks):
+    order = offsets(len(blocks))
+    return [flip(block, "expert", k) if k else block for k, block in zip(order, blocks)]
 
 
 def cross(block, far_bits):
@@ -442,19 +490,17 @@
     weights = (w_gate[0], w_up[0], w_down[0])
     tie = lax.optimization_barrier
 
-    token_rows, grad_rows = dispatch(n_targets, ids, tokens, gates, out_grad)
-    ids_after, token_rows = tie((ids, token_rows))
-    token_rows = exchange(token_rows)
-    grad_rows = exchange(grad_rows)
-    token_rows, *table = tie((token_rows, *placement(n_targets, ids_after)))
+    sent = dispatch(n_targets, ids, tokens, gates, out_grad)
+    ids_after, *sent = tie((ids, *sent))
+    arrived = exchange([sent[k] for k in offsets(n_targets)])
+    arrived[0], *table = tie((arrived[0], *placement(n_targets, ids_after)))
+    token_rows, grad_rows = pack(arrived)
 
     token_held = cross(token_rows, far_bits)
     near = sorted(token_held)
     token_near = [token_held[mask] for mask in near]
-    token_far = [flip(token_near[0], "dp", 1)]
-    grad_rows, *token_near[1:] = tie((grad_rows, *token_near[1:]))
+    token_far = [flip(value, "dp", 1) for value in token_near]
     grad_held = cross(grad_rows, far_bits)
-    token_far += [flip(value, "dp", 1) for value in token_near[1:]]
     grad_near = [grad_held[mask] for mask in near]
     token_halves, activated, slope, hidden = forward(
         token_near + token_far, weights[0], weights[1]
@@ -482,20 +528,17 @@
             moved_left, rights, gate_f, up_f, hidden = tie(
                 (moved_left, rights, gate_f, up_f, hidden)
             )
-            grad_gate = weight_grad(gate_f, token_halves)
-            moved_right, grad_gate = tie((moved_right, grad_gate))
+            grads = weight_grads((gate_f, up_f, hidden), token_halves, grad_halves)
+            moved_right, grads = tie((moved_right, grads))
         for mask in masks:
             terms = (lefts[mask ^ bit], rights[mask ^ bit]), (moved_left[mask], moved_right[mask])
             if bit == far_bits[0]:
-                returned = exchange(add_rows(*terms))
+                returned = exchange(add_rows(*terms, n_targets))
             else:
-                lefts[mask ^ bit] = add_rows(terms[0][:1], terms[1][:1])
-                rights[mask ^ bit] = add_rows(terms[0][1:], terms[1][1:])
-    grad_up = weight_grad(up_f, token_halves)
-    grad_down = weight_grad(hidden, grad_halves)
-    returned, grad_up, grad_down = tie((returned, grad_up, grad_down))
+                lefts[mask ^ bit] = add_rows(terms[0][:1], terms[1][:1])[0]
+                rights[mask ^ bit] = add_rows(terms[0][1:], terms[1][1:])[0]
     token_grad, gate_grad = combine(table, gates, returned, width)
-    return (token_grad, gate_grad.T, grad_gate[None], grad_up[None], grad_down[None])
+    return (token_grad, gate_grad.T, *(grad[None] for grad in grads))
 
 
 def solution(mesh):

time: 73.8 us -> 70.9 us (0.961)
  blocking collectives: 16.3 us -> 0 us
  starting transfers between devices: 14.9 us -> 30 us
  waiting for transfers between devices: 18 us -> 24.2 us
  local copies, waits for them, and re-layouts: 4.51 us -> 0.72 us
  Pallas kernels: 18.7 us -> 15 us
    ppermute x10 -> x24, starting transfers between devices: 5.63 us -> 30 us  [flip(): return lax.ppermute(value, axis, [(i, i ^ bit) for i in range(size)])]
    all_to_all x1 -> x0, blocking collectives: 16.3 us -> none  [exchange(): lax.all_to_all(blocks, 'expert', split_axis=0, concat_axis=0, tiled=True)]
    ppermute x10 -> x24, waiting for transfers between devices: 8.14 us -> 24.2 us  [flip(): return lax.ppermute(value, axis, [(i, i ^ bit) for i in range(size)])]
    all_to_all x2 -> x0, waiting for transfers between devices: 9.83 us -> none  [exchange(): lax.all_to_all(blocks, 'expert', split_axis=0, concat_axis=0, tiled=True)]
    all_to_all x2 -> x0, starting transfers between devices: 9.31 us -> none  [exchange(): lax.all_to_all(blocks, 'expert', split_axis=0, concat_axis=0, tiled=True)]
    unnamed x28 -> x12, local copies, waits for them, and re-layouts: 4.51 us -> 0.72 us
    pallas_call x5 -> x4, Pallas kernels: 7.71 us -> 5.18 us  [the longest x1 4.07 us: weight_grads(): pl.pallas_call(functools.partial(weight_kernel, chunk), out_shape=[struct...]
    pallas_call x1, Pallas kernels: 3.21 us -> 1.95 us  [forward(): pl.pallas_call(functools.partial(forward_kernel, count), out_shape=[struc...]
  transfers between devices with their start and end apart: 12 -> 24, of which waited for: 9 -> 12; matrix products, arithmetic and copies ran while one was open for 0% -> 0% of each run, Pallas kernels for 17% -> 13%
where the time goes in v5:
time: 70.9 us; the launch traced here: 70.6 us
  starting transfers between devices  30 us (42%)
  waiting for transfers between devices  24.2 us (34%)
  Pallas kernels  15 us (21%)
  between operations  0.78 us (1%)
  local copies, waits for them, and re-layouts  0.72 us (1%)
    ppermute x24, starting transfers between devices, flip(): return lax.ppermute(value, axis, [(i, i ^ bit) for i in range(size)])  30 us
    ppermute x24, waiting for transfers between devices, flip(): return lax.ppermute(value, axis, [(i, i ^ bit) for i in range(size)])  24.2 us
    pallas_call x1, Pallas kernels, weight_grads(): pl.pallas_call(functools.partial(weight_kernel, chunk), out_shape=[struct...  4.07 us
    pallas_call x1, Pallas kernels, backward(): pl.pallas_call(functools.partial(backward_kernel, count), out_shape=[stru...  2.54 us
    pallas_call x1, Pallas kernels, dispatch(): pl.pallas_call(functools.partial(dispatch_kernel, n_targets), out_shape=[...  2.34 us
    pallas_call x1, Pallas kernels, forward(): pl.pallas_call(functools.partial(forward_kernel, count), out_shape=[struc...  1.95 us
    pallas_call x2, Pallas kernels, own_rows(): pl.pallas_call(functools.partial(own_kernel, start, LANES if start else 0...  1.84 us
  transfers between devices with their start and end apart: 24, of which 12 were waited for; matrix products, arithmetic and copies ran while one was open for 0% of the time, Pallas kernels for 13%

profile of v5, /device:TPU:0, one launch (start us, length us, event | category | flops | bytes accessed | tf_op | source)
XLA Modules:
  0.0 70.6 jit_solution(11288001472616811225)
XLA Ops:
  0.6 2.3 %dispatch.1 = (bf16[8,4096]{1,0:T(8,128)(2,1)}, bf16[8,4096]{1,0:T(8,128)(2,1)}, bf16[8,4096]{1,0:T(8,128)(2,1)}, bf16[8,4096]{1,0:T(8,128)(2,1)}, bf16[8,4096]{...) custom-call(s32[8,32]{1,0:T(8,128)} %bitcast.22, ...), custom_call_target="tpu_custom_call" | custom-call | tf_op jit(solution)/shard_map/dispatch/pallas_call | solution.py:90
  3.0 3.0 %collective-permute-start = (bf16[8,4096]{1,0:T(8,128)(2,1)}, bf16[8,4096]{1,0:T(8,128)(2,1)S(1)}, u32[]{:S(2)}, u32[]{:S(2)}) collective-permute-start(bf16[8,4096]{1,0:T(8,128)(2,1)} %get-tuple-element.94), channel_id=1, source_target_pairs={{0,4},{4,0},{8,12},{12,8},{16,20},{20,16},{24,28},{28,24},{1,5},{5... | collective-permute-start | bytes 196616 | tf_op jit(solution)/shard_map/ppermute | solution.py:463
  6.1 2.6 %collective-permute-start.1 = (bf16[8,4096]{1,0:T(8,128)(2,1)}, bf16[8,4096]{1,0:T(8,128)(2,1)S(1)}, u32[]{:S(2)}, u32[]{:S(2)}) collective-permute-start(bf16[8,4096]{1,0:T(8,128)(2,1)} %get-tuple-element.95), channel_id=1, source_target_pairs={{0,16},{4,20},{8,24},{12,28},{16,0},{20,4},{24,8},{28,12},{1,17},{... | collective-permute-start | bytes 196616 | tf_op jit(solution)/shard_map/ppermute | solution.py:463
  8.6 3.9 %collective-permute-start.3 = (bf16[8,4096]{1,0:T(8,128)(2,1)}, bf16[8,4096]{1,0:T(8,128)(2,1)S(1)}, u32[]{:S(2)}, u32[]{:S(2)}) collective-permute-start(bf16[8,4096]{1,0:T(8,128)(2,1)} %get-tuple-element.97), channel_id=1, source_target_pairs={{0,24},{4,28},{8,16},{12,20},{16,8},{20,12},{24,0},{28,4},{1,25},{... | collective-permute-start | bytes 196616 | tf_op jit(solution)/shard_map/ppermute | solution.py:463
  12.5 1.2 %collective-permute-start.4 = (bf16[8,4096]{1,0:T(8,128)(2,1)}, bf16[8,4096]{1,0:T(8,128)(2,1)S(1)}, u32[]{:S(2)}, u32[]{:S(2)}) collective-permute-start(bf16[8,4096]{1,0:T(8,128)(2,1)} %get-tuple-element.98), channel_id=1, source_target_pairs={{0,28},{4,24},{8,20},{12,16},{16,12},{20,8},{24,4},{28,0},{1,29},{... | collective-permute-start | bytes 196616 | tf_op jit(solution)/shard_map/ppermute | solution.py:463
  14.0 1.5 %collective-permute-start.6 = (bf16[8,4096]{1,0:T(8,128)(2,1)}, bf16[8,4096]{1,0:T(8,128)(2,1)S(1)}, u32[]{:S(2)}, u32[]{:S(2)}) collective-permute-start(bf16[8,4096]{1,0:T(8,128)(2,1)} %get-tuple-element.100), channel_id=1, source_target_pairs={{0,12},{4,8},{8,4},{12,0},{16,28},{20,24},{24,20},{28,16},{1,13},{... | collective-permute-start | bytes 196616 | tf_op jit(solution)/shard_map/ppermute | solution.py:463
  16.4 2.2 %collective-permute-done.2.refs_3_ = bf16[8,4096]{1,0:T(8,128)(2,1)S(1)} collective-permute-done((bf16[8,4096]{1,0:T(8,128)(2,1)}, bf16[8,4096]{1,0:T(8,128)(2,1)S(1)}, u32[]{:S(2)}, u32[]{:S(2)}) %collective-permute-start.2) | collective-permute-done | bytes 65568 | tf_op jit(solution)/shard_map/ppermute | solution.py:463
  18.6 1.6 %collective-permute-done.4.refs_5_ = bf16[8,4096]{1,0:T(8,128)(2,1)S(1)} collective-permute-done((bf16[8,4096]{1,0:T(8,128)(2,1)}, bf16[8,4096]{1,0:T(8,128)(2,1)S(1)}, u32[]{:S(2)}, u32[]{:S(2)}) %collective-permute-start.4) | collective-permute-done | bytes 65568 | tf_op jit(solution)/shard_map/ppermute | solution.py:463
  20.9 1.6 %collective-permute-start.7 = (bf16[64,2048]{1,0:T(8,128)(2,1)S(1)}, bf16[64,2048]{1,0:T(8,128)(2,1)S(1)}, u32[]{:S(2)}, u32[]{:S(2)}) collective-permute-start(bf16[64,2048]{1,0:T(8,128)(2,1)S(1)} %get-tuple-element.102.refs_0_), channel_id=1, source_target_pairs={{0,2},{1,3},{2,0},{3,1},{4,6},{5,7},{6,4},{7,5},{8,10},{9,11},{10,... | collective-permute-start | bytes 786440 | tf_op jit(solution)/shard_map/ppermute | solution.py:463
  22.4 5.8 %collective-permute-done.7.refs_1_ = bf16[64,2048]{1,0:T(8,128)(2,1)S(1)} collective-permute-done((bf16[64,2048]{1,0:T(8,128)(2,1)S(1)}, bf16[64,2048]{1,0:T(8,128)(2,1)S(1)}, u32[]{:S(2)}, u32[]{:S(2)}) %collective-permute-start.7) | collective-permute-done | bytes 262176 | tf_op jit(solution)/shard_map/ppermute | solution.py:463
  28.2 1.5 %collective-permute-start.10 = (bf16[64,2048]{1,0:T(8,128)(2,1)S(1)}, bf16[64,2048]{1,0:T(8,128)(2,1)S(1)}, u32[]{:S(2)}, u32[]{:S(2)}) collective-permute-start(bf16[64,2048]{1,0:T(8,128)(2,1)S(1)} %get-tuple-element.101.refs_0_), channel_id=1, source_target_pairs={{0,2},{1,3},{2,0},{3,1},{4,6},{5,7},{6,4},{7,5},{8,10},{9,11},{10,... | collective-permute-start | bytes 786440 | tf_op jit(solution)/shard_map/ppermute | solution.py:463
  30.0 2.0 %forward.1 = (bf16[256,2048]{1,0:T(8,128)(2,1)S(1)}, f32[384,256]{1,0:T(8,128)S(1)}, f32[384,256]{1,0:T(8,128)S(1)}, bf16[384,256]{1,0:T(8,128)(2,1)S(1)}) custom-call(bf16[64,2048]{1,0:T(8,128)(2,1)S(1)} %get-tuple-element.102.refs_0_, bf16[64,2048]{1,0:T(8,128)(2,1)S(1)} %collective-permute-done.7.refs_1_, ...), custom_call_target="tpu_custom_call" | custom-call | flops 1610612736 | bytes 6291456 | tf_op jit(solution)/shard_map/forward/pallas_call | solution.py:189
  31.9 5.0 %collective-permute-done.10.refs_1_ = bf16[64,2048]{1,0:T(8,128)(2,1)S(1)} collective-permute-done((bf16[64,2048]{1,0:T(8,128)(2,1)S(1)}, bf16[64,2048]{1,0:T(8,128)(2,1)S(1)}, u32[]{:S(2)}, u32[]{:S(2)}) %collective-permute-start.10) | collective-permute-done | bytes 262176 | tf_op jit(solution)/shard_map/ppermute | solution.py:463
  36.9 1.5 %collective-permute-done.12.refs_3_ = bf16[64,2048]{1,0:T(8,128)(2,1)S(1)} collective-permute-done((bf16[64,2048]{1,0:T(8,128)(2,1)S(1)}, bf16[64,2048]{1,0:T(8,128)(2,1)S(1)}, u32[]{:S(2)}, u32[]{:S(2)}) %collective-permute-start.12) | collective-permute-done | bytes 262176 | tf_op jit(solution)/shard_map/ppermute | solution.py:463
  38.4 2.5 %backward.1 = (bf16[128,1024]{1,0:T(8,128)(2,1)S(1)}, bf16[256,2048]{1,0:T(8,128)(2,1)S(1)}, bf16[384,256]{1,0:T(8,128)(2,1)S(1)}, bf16[384,256]{1,0:T(8,128)(2,...) custom-call(bf16[64,2048]{1,0:T(8,128)(2,1)S(1)} %get-tuple-element.101.refs_0_, ...), custom_call_target="tpu_custom_call" | custom-call | flops 1207959552 | bytes 3145728 | tf_op jit(solution)/shard_map/backward/pallas_call | solution.py:275
  44.2 1.5 %collective-permute-start.15 = (bf16[64,1024]{1,0:T(8,128)(2,1)S(1)}, bf16[64,1024]{1,0:T(8,128)(2,1)S(1)}, u32[]{:S(2)}, u32[]{:S(2)}) collective-permute-start(bf16[64,1024]{1,0:T(8,128)(2,1)S(1)} %get-tuple-element.119), channel_id=1, source_target_pairs={{0,2},{1,3},{2,0},{3,1},{4,6},{5,7},{6,4},{7,5},{8,10},{9,11},{10,... | collective-permute-start | bytes 393224 | tf_op jit(solution)/shard_map/ppermute | solution.py:463
  47.2 3.0 %collective-permute-done.15.refs_2_ = bf16[64,1024]{1,0:T(8,128)(2,1)S(1)} collective-permute-done((bf16[64,1024]{1,0:T(8,128)(2,1)S(1)}, bf16[64,1024]{1,0:T(8,128)(2,1)S(1)}, u32[]{:S(2)}, u32[]{:S(2)}) %collective-permute-start.15) | collective-permute-done | bytes 131104 | tf_op jit(solution)/shard_map/ppermute | solution.py:463
  50.2 4.1 %weight_grads.1 = (bf16[384,4096]{1,0:T(8,128)(2,1)}, bf16[384,4096]{1,0:T(8,128)(2,1)}, bf16[384,4096]{1,0:T(8,128)(2,1)}) custom-call(bf16[384,256]{1,0:T(8,128)(2,1)S(1)} %get-tuple-element.127.refs_0_, bf16[384,256]{1,0:T(8,128)(2,1)S(1)} %get-tuple-element.128.refs_1_, bf16[384,256]{1,0:T(8,128)(2,1)S(1)} %get-tuple-element.129.refs_6_.refs_2_, ...), custom_call_target="tpu_custom_call" | custom-call | flops 2415919104 | bytes 9437184 | tf_op jit(solution)/shard_map/weight_grads/pallas_call | solution.py:406
  54.4 2.5 %collective-permute-start.17 = (bf16[8,2176]{1,0:T(8,128)(2,1)S(1)}, bf16[8,2176]{1,0:T(8,128)(2,1)S(1)}, u32[]{:S(2)}, u32[]{:S(2)}) collective-permute-start(bf16[8,2176]{1,0:T(8,128)(2,1)S(1)} %get-tuple-element.137), channel_id=1, source_target_pairs={{0,4},{4,0},{8,12},{12,8},{16,20},{20,16},{24,28},{28,24},{1,5},{5... | collective-permute-start | bytes 104456 | tf_op jit(solution)/shard_map/ppermute | solution.py:463
  56.9 2.8 %collective-permute-start.18 = (bf16[8,2176]{1,0:T(8,128)(2,1)S(1)}, bf16[8,2176]{1,0:T(8,128)(2,1)S(1)}, u32[]{:S(2)}, u32[]{:S(2)}) collective-permute-start(bf16[8,2176]{1,0:T(8,128)(2,1)S(1)} %get-tuple-element.138), channel_id=1, source_target_pairs={{0,16},{4,20},{8,24},{12,28},{16,0},{20,4},{24,8},{28,12},{1,17},{... | collective-permute-start | bytes 104456 | tf_op jit(solution)/shard_map/ppermute | solution.py:463
  59.7 3.0 %collective-permute-start.20 = (bf16[8,2176]{1,0:T(8,128)(2,1)S(1)}, bf16[8,2176]{1,0:T(8,128)(2,1)S(1)}, u32[]{:S(2)}, u32[]{:S(2)}) collective-permute-start(bf16[8,2176]{1,0:T(8,128)(2,1)S(1)} %get-tuple-element.140), channel_id=1, source_target_pairs={{0,24},{4,28},{8,16},{12,20},{16,8},{20,12},{24,0},{28,4},{1,25},{... | collective-permute-start | bytes 104456 | tf_op jit(solution)/shard_map/ppermute | solution.py:463
  62.7 1.8 %collective-permute-start.21 = (bf16[8,2176]{1,0:T(8,128)(2,1)S(1)}, bf16[8,2176]{1,0:T(8,128)(2,1)S(1)}, u32[]{:S(2)}, u32[]{:S(2)}) collective-permute-start(bf16[8,2176]{1,0:T(8,128)(2,1)S(1)} %get-tuple-element.141), channel_id=1, source_target_pairs={{0,28},{4,24},{8,20},{12,16},{16,12},{20,8},{24,4},{28,0},{1,29},{... | collective-permute-start | bytes 104456 | tf_op jit(solution)/shard_map/ppermute | solution.py:463
  64.5 1.9 %collective-permute-start.23 = (bf16[8,2176]{1,0:T(8,128)(2,1)S(1)}, bf16[8,2176]{1,0:T(8,128)(2,1)S(1)}, u32[]{:S(2)}, u32[]{:S(2)}) collective-permute-start(bf16[8,2176]{1,0:T(8,128)(2,1)S(1)} %get-tuple-element.143), channel_id=1, source_target_pairs={{0,12},{4,8},{8,4},{12,0},{16,28},{20,24},{24,20},{28,16},{1,13},{... | collective-permute-start | bytes 104456 | tf_op jit(solution)/shard_map/ppermute | solution.py:463
  66.5 2.9 %collective-permute-done.21.refs_5_ = bf16[8,2176]{1,0:T(8,128)(2,1)S(1)} collective-permute-done((bf16[8,2176]{1,0:T(8,128)(2,1)S(1)}, bf16[8,2176]{1,0:T(8,128)(2,1)S(1)}, u32[]{:S(2)}, u32[]{:S(2)}) %collective-permute-start.21) | collective-permute-done | bytes 34848 | tf_op jit(solution)/shard_map/ppermute | solution.py:463
  (47 shorter events, 8.2 us)
Async XLA Ops:
  3.0 10.7 %collective-permute-start = (bf16[8,4096]{1,0:T(8,128)(2,1)}, bf16[8,4096]{1,0:T(8,128)(2,1)S(1)}, u32[]{:S(2)}, u32[]{:S(2)}) collective-permute-start(bf16[8,4096]{1,0:T(8,128)(2,1)} %get-tuple-element.94), channel_id=1, source_target_pairs={{0,4},{4,0},{8,12},{12,8},{16,20},{20,16},{24,28},{28,24},{1,5},{5... | collective-permute-start | bytes 196616 | tf_op jit(solution)/shard_map/ppermute | solution.py:463
  6.1 8.0 %collective-permute-start.1 = (bf16[8,4096]{1,0:T(8,128)(2,1)}, bf16[8,4096]{1,0:T(8,128)(2,1)S(1)}, u32[]{:S(2)}, u32[]{:S(2)}) collective-permute-start(bf16[8,4096]{1,0:T(8,128)(2,1)} %get-tuple-element.95), channel_id=1, source_target_pairs={{0,16},{4,20},{8,24},{12,28},{16,0},{20,4},{24,8},{28,12},{1,17},{... | collective-permute-start | bytes 196616 | tf_op jit(solution)/shard_map/ppermute | solution.py:463
  8.6 9.9 %collective-permute-start.2 = (bf16[8,4096]{1,0:T(8,128)(2,1)}, bf16[8,4096]{1,0:T(8,128)(2,1)S(1)}, u32[]{:S(2)}, u32[]{:S(2)}) collective-permute-start(bf16[8,4096]{1,0:T(8,128)(2,1)} %get-tuple-element.96), channel_id=1, source_target_pairs={{0,20},{4,16},{8,28},{12,24},{16,4},{20,0},{24,12},{28,8},{1,21},{... | collective-permute-start | bytes 196616 | tf_op jit(solution)/shard_map/ppermute | solution.py:463
  8.6 9.9 %collective-permute-start.3 = (bf16[8,4096]{1,0:T(8,128)(2,1)}, bf16[8,4096]{1,0:T(8,128)(2,1)S(1)}, u32[]{:S(2)}, u32[]{:S(2)}) collective-permute-start(bf16[8,4096]{1,0:T(8,128)(2,1)} %get-tuple-element.97), channel_id=1, source_target_pairs={{0,24},{4,28},{8,16},{12,20},{16,8},{20,12},{24,0},{28,4},{1,25},{... | collective-permute-start | bytes 196616 | tf_op jit(solution)/shard_map/ppermute | solution.py:463
  12.5 7.7 %collective-permute-start.4 = (bf16[8,4096]{1,0:T(8,128)(2,1)}, bf16[8,4096]{1,0:T(8,128)(2,1)S(1)}, u32[]{:S(2)}, u32[]{:S(2)}) collective-permute-start(bf16[8,4096]{1,0:T(8,128)(2,1)} %get-tuple-element.98), channel_id=1, source_target_pairs={{0,28},{4,24},{8,20},{12,16},{16,12},{20,8},{24,4},{28,0},{1,29},{... | collective-permute-start | bytes 196616 | tf_op jit(solution)/shard_map/ppermute | solution.py:463
  13.7 6.5 %collective-permute-start.5 = (bf16[8,4096]{1,0:T(8,128)(2,1)}, bf16[8,4096]{1,0:T(8,128)(2,1)S(1)}, u32[]{:S(2)}, u32[]{:S(2)}) collective-permute-start(bf16[8,4096]{1,0:T(8,128)(2,1)} %get-tuple-element.99), channel_id=1, source_target_pairs={{0,8},{4,12},{8,0},{12,4},{16,24},{20,28},{24,16},{28,20},{1,9},{5... | collective-permute-start | bytes 196616 | tf_op jit(solution)/shard_map/ppermute | solution.py:463
  14.0 6.7 %collective-permute-start.6 = (bf16[8,4096]{1,0:T(8,128)(2,1)}, bf16[8,4096]{1,0:T(8,128)(2,1)S(1)}, u32[]{:S(2)}, u32[]{:S(2)}) collective-permute-start(bf16[8,4096]{1,0:T(8,128)(2,1)} %get-tuple-element.100), channel_id=1, source_target_pairs={{0,12},{4,8},{8,4},{12,0},{16,28},{20,24},{24,20},{28,16},{1,13},{... | collective-permute-start | bytes 196616 | tf_op jit(solution)/shard_map/ppermute | solution.py:463
  20.9 7.3 %collective-permute-start.7 = (bf16[64,2048]{1,0:T(8,128)(2,1)S(1)}, bf16[64,2048]{1,0:T(8,128)(2,1)S(1)}, u32[]{:S(2)}, u32[]{:S(2)}) collective-permute-start(bf16[64,2048]{1,0:T(8,128)(2,1)S(1)} %get-tuple-element.102.refs_0_), channel_id=1, source_target_pairs={{0,2},{1,3},{2,0},{3,1},{4,6},{5,7},{6,4},{7,5},{8,10},{9,11},{10,... | collective-permute-start | bytes 786440 | tf_op jit(solution)/shard_map/ppermute | solution.py:463
  22.4 7.5 %collective-permute-start.8 = (bf16[64,2048]{1,0:T(8,128)(2,1)S(1)}, bf16[64,2048]{1,0:T(8,128)(2,1)S(1)}, u32[]{:S(2)}, u32[]{:S(2)}) collective-permute-start(bf16[64,2048]{1,0:T(8,128)(2,1)S(1)} %get-tuple-element.102.refs_0_), channel_id=1, source_target_pairs={{0,1},{1,0},{2,3},{3,2},{4,5},{5,4},{6,7},{7,6},{8,9},{9,8},{10,11... | collective-permute-start | bytes 786440 | tf_op jit(solution)/shard_map/ppermute | solution.py:463
  28.2 1.8 %collective-permute-start.9 = (bf16[64,2048]{1,0:T(8,128)(2,1)S(1)}, bf16[64,2048]{1,0:T(8,128)(2,1)S(1)}, u32[]{:S(2)}, u32[]{:S(2)}) collective-permute-start(bf16[64,2048]{1,0:T(8,128)(2,1)S(1)} %collective-permute-done.7.refs_1_), channel_id=1, source_target_pairs={{0,1},{1,0},{2,3},{3,2},{4,5},{5,4},{6,7},{7,6},{8,9},{9,8},{10,11... | collective-permute-start | bytes 786440 | tf_op jit(solution)/shard_map/ppermute | solution.py:463
  28.2 8.7 %collective-permute-start.10 = (bf16[64,2048]{1,0:T(8,128)(2,1)S(1)}, bf16[64,2048]{1,0:T(8,128)(2,1)S(1)}, u32[]{:S(2)}, u32[]{:S(2)}) collective-permute-start(bf16[64,2048]{1,0:T(8,128)(2,1)S(1)} %get-tuple-element.101.refs_0_), channel_id=1, source_target_pairs={{0,2},{1,3},{2,0},{3,1},{4,6},{5,7},{6,4},{7,5},{8,10},{9,11},{10,... | collective-permute-start | bytes 786440 | tf_op jit(solution)/shard_map/ppermute | solution.py:463
  29.7 7.2 %collective-permute-start.11 = (bf16[64,2048]{1,0:T(8,128)(2,1)S(1)}, bf16[64,2048]{1,0:T(8,128)(2,1)S(1)}, u32[]{:S(2)}, u32[]{:S(2)}) collective-permute-start(bf16[64,2048]{1,0:T(8,128)(2,1)S(1)} %get-tuple-element.101.refs_0_), channel_id=1, source_target_pairs={{0,1},{1,0},{2,3},{3,2},{4,5},{5,4},{6,7},{7,6},{8,9},{9,8},{10,11... | collective-permute-start | bytes 786440 | tf_op jit(solution)/shard_map/ppermute | solution.py:463
  36.9 1.5 %collective-permute-start.12 = (bf16[64,2048]{1,0:T(8,128)(2,1)S(1)}, bf16[64,2048]{1,0:T(8,128)(2,1)S(1)}, u32[]{:S(2)}, u32[]{:S(2)}) collective-permute-start(bf16[64,2048]{1,0:T(8,128)(2,1)S(1)} %collective-permute-done.10.refs_1_), channel_id=1, source_target_pairs={{0,1},{1,0},{2,3},{3,2},{4,5},{5,4},{6,7},{7,6},{8,9},{9,8},{10,11... | collective-permute-start | bytes 786440 | tf_op jit(solution)/shard_map/ppermute | solution.py:463
  41.0 1.6 %collective-permute-start.13 = (bf16[128,1024]{1,0:T(8,128)(2,1)S(1)}, bf16[128,1024]{1,0:T(8,128)(2,1)S(1)}, u32[]{:S(2)}, u32[]{:S(2)}) collective-permute-start(bf16[128,1024]{1,0:T(8,128)(2,1)S(1)} %get-tuple-element.110), channel_id=1, source_target_pairs={{0,1},{1,0},{2,3},{3,2},{4,5},{5,4},{6,7},{7,6},{8,9},{9,8},{10,11... | collective-permute-start | bytes 786440 | tf_op jit(solution)/shard_map/ppermute | solution.py:463
  42.6 1.6 %collective-permute-start.14 = (bf16[128,1152]{1,0:T(8,128)(2,1)S(1)}, bf16[128,1152]{1,0:T(8,128)(2,1)S(1)}, u32[]{:S(2)}, u32[]{:S(2)}) collective-permute-start(bf16[128,1152]{1,0:T(8,128)(2,1)S(1)} %far_rows.1), channel_id=1, source_target_pairs={{0,1},{1,0},{2,3},{3,2},{4,5},{5,4},{6,7},{7,6},{8,9},{9,8},{10,11... | collective-permute-start | bytes 884744 | tf_op jit(solution)/shard_map/ppermute | solution.py:463
  44.2 6.0 %collective-permute-start.15 = (bf16[64,1024]{1,0:T(8,128)(2,1)S(1)}, bf16[64,1024]{1,0:T(8,128)(2,1)S(1)}, u32[]{:S(2)}, u32[]{:S(2)}) collective-permute-start(bf16[64,1024]{1,0:T(8,128)(2,1)S(1)} %get-tuple-element.119), channel_id=1, source_target_pairs={{0,2},{1,3},{2,0},{3,1},{4,6},{5,7},{6,4},{7,5},{8,10},{9,11},{10,... | collective-permute-start | bytes 393224 | tf_op jit(solution)/shard_map/ppermute | solution.py:463
  46.6 7.7 %collective-permute-start.16 = (bf16[64,1152]{1,0:T(8,128)(2,1)S(1)}, bf16[64,1152]{1,0:T(8,128)(2,1)S(1)}, u32[]{:S(2)}, u32[]{:S(2)}) collective-permute-start(bf16[64,1152]{1,0:T(8,128)(2,1)S(1)} %get-tuple-element.126), channel_id=1, source_target_pairs={{0,2},{1,3},{2,0},{3,1},{4,6},{5,7},{6,4},{7,5},{8,10},{9,11},{10,... | collective-permute-start | bytes 442376 | tf_op jit(solution)/shard_map/ppermute | solution.py:463
  54.4 10.1 %collective-permute-start.17 = (bf16[8,2176]{1,0:T(8,128)(2,1)S(1)}, bf16[8,2176]{1,0:T(8,128)(2,1)S(1)}, u32[]{:S(2)}, u32[]{:S(2)}) collective-permute-start(bf16[8,2176]{1,0:T(8,128)(2,1)S(1)} %get-tuple-element.137), channel_id=1, source_target_pairs={{0,4},{4,0},{8,12},{12,8},{16,20},{20,16},{24,28},{28,24},{1,5},{5... | collective-permute-start | bytes 104456 | tf_op jit(solution)/shard_map/ppermute | solution.py:463
  56.9 7.7 %collective-permute-start.18 = (bf16[8,2176]{1,0:T(8,128)(2,1)S(1)}, bf16[8,2176]{1,0:T(8,128)(2,1)S(1)}, u32[]{:S(2)}, u32[]{:S(2)}) collective-permute-start(bf16[8,2176]{1,0:T(8,128)(2,1)S(1)} %get-tuple-element.138), channel_id=1, source_target_pairs={{0,16},{4,20},{8,24},{12,28},{16,0},{20,4},{24,8},{28,12},{1,17},{... | collective-permute-start | bytes 104456 | tf_op jit(solution)/shard_map/ppermute | solution.py:463
  59.7 6.8 %collective-permute-start.19 = (bf16[8,2176]{1,0:T(8,128)(2,1)S(1)}, bf16[8,2176]{1,0:T(8,128)(2,1)S(1)}, u32[]{:S(2)}, u32[]{:S(2)}) collective-permute-start(bf16[8,2176]{1,0:T(8,128)(2,1)S(1)} %get-tuple-element.139), channel_id=1, source_target_pairs={{0,20},{4,16},{8,28},{12,24},{16,4},{20,0},{24,12},{28,8},{1,21},{... | collective-permute-start | bytes 104456 | tf_op jit(solution)/shard_map/ppermute | solution.py:463
  59.7 6.8 %collective-permute-start.20 = (bf16[8,2176]{1,0:T(8,128)(2,1)S(1)}, bf16[8,2176]{1,0:T(8,128)(2,1)S(1)}, u32[]{:S(2)}, u32[]{:S(2)}) collective-permute-start(bf16[8,2176]{1,0:T(8,128)(2,1)S(1)} %get-tuple-element.140), channel_id=1, source_target_pairs={{0,24},{4,28},{8,16},{12,20},{16,8},{20,12},{24,0},{28,4},{1,25},{... | collective-permute-start | bytes 104456 | tf_op jit(solution)/shard_map/ppermute | solution.py:463
  62.7 6.7 %collective-permute-start.21 = (bf16[8,2176]{1,0:T(8,128)(2,1)S(1)}, bf16[8,2176]{1,0:T(8,128)(2,1)S(1)}, u32[]{:S(2)}, u32[]{:S(2)}) collective-permute-start(bf16[8,2176]{1,0:T(8,128)(2,1)S(1)} %get-tuple-element.141), channel_id=1, source_target_pairs={{0,28},{4,24},{8,20},{12,16},{16,12},{20,8},{24,4},{28,0},{1,29},{... | collective-permute-start | bytes 104456 | tf_op jit(solution)/shard_map/ppermute | solution.py:463
  64.5 4.8 %collective-permute-start.22 = (bf16[8,2176]{1,0:T(8,128)(2,1)S(1)}, bf16[8,2176]{1,0:T(8,128)(2,1)S(1)}, u32[]{:S(2)}, u32[]{:S(2)}) collective-permute-start(bf16[8,2176]{1,0:T(8,128)(2,1)S(1)} %get-tuple-element.142), channel_id=1, source_target_pairs={{0,8},{4,12},{8,0},{12,4},{16,24},{20,28},{24,16},{28,20},{1,9},{5... | collective-permute-start | bytes 104456 | tf_op jit(solution)/shard_map/ppermute | solution.py:463
  64.5 5.2 %collective-permute-start.23 = (bf16[8,2176]{1,0:T(8,128)(2,1)S(1)}, bf16[8,2176]{1,0:T(8,128)(2,1)S(1)}, u32[]{:S(2)}, u32[]{:S(2)}) collective-permute-start(bf16[8,2176]{1,0:T(8,128)(2,1)S(1)} %get-tuple-element.143), channel_id=1, source_target_pairs={{0,12},{4,8},{8,4},{12,0},{16,28},{20,24},{24,20},{28,16},{1,13},{... | collective-permute-start | bytes 104456 | tf_op jit(solution)/shard_map/ppermute | solution.py:463
  (6 other events, 100.3 us)

commit v6 on v5

--- a/solution.py
+++ b/solution.py
@@ -19,6 +19,8 @@
 
 HBM = pl.BlockSpec(memory_space=pltpu.HBM)
 VMEM = pl.BlockSpec(memory_space=pltpu.VMEM)
+
+LIGHT = pl.CostEstimate(flops=10**6, bytes_accessed=10**4, transcendentals=0)
 
 
 def struct(shape, dtype=jnp.bfloat16):
@@ -125,34 +127,32 @@
 
 
 def pack_kernel(count, *refs):
-    blocks, (token_out, grad_out) = refs[:count], refs[count:]
-    half = token_out.shape[1]
+    blocks, out = refs[:count], refs[count]
     for k in range(0, count, 2):
-        pair = jnp.concatenate([blocks[k][...], blocks[k + 1][...]], axis=0)
-        span = pl.ds(k * BLOCK, 2 * BLOCK)
-        token_out[span, :] = pair[:, :half]
-        grad_out[span, :] = pair[:, half:]
+        out[pl.ds(k * BLOCK, 2 * BLOCK), :] = jnp.concatenate(
+            [blocks[k][...], blocks[k + 1][...]], axis=0
+        )
 
 
 def pack(blocks):
     count = len(blocks)
-    shape = (count * BLOCK, blocks[0].shape[1] // 2)
+    rows, width = count * BLOCK, blocks[0].shape[1]
     return pl.pallas_call(
         functools.partial(pack_kernel, count),
-        out_shape=[struct(shape)] * 2,
+        out_shape=struct((rows, width)),
         in_specs=[VMEM] * count,
-        out_specs=[VMEM] * 2,
-        compiler_params=pltpu.CompilerParams(
-            vmem_limit_bytes=4 * MIB + 16 * shape[0] * shape[1]
-        ),
+        out_specs=VMEM,
+        compiler_params=pltpu.CompilerParams(vmem_limit_bytes=4 * MIB + 8 * rows * width),
         name="pack",
     )(*blocks)
 
 
-def gather_pieces(pieces, out):
-    block = pieces[0].shape[0]
-    for i, piece in enumerate(pieces):
-        out[pl.ds(i * block, block), :] = piece[...]
+def gather_pieces(pieces, start, out):
+    base = 0
+    for piece in pieces:
+        rows = piece.shape[0]
+        out[pl.ds(base, rows), :] = piece[:, start : start + out.shape[1]]
+        base += rows
 
 
 def project(weight, halves):
@@ -170,7 +170,7 @@
 def forward_kernel(count, *refs):
     pieces = refs[:count]
     gate_w, up_w, halves, activated_out, slope_out, hidden_out = refs[count:]
-    gather_pieces(pieces, halves)
+    gather_pieces(pieces, 0, halves)
     pre_gate, pre_up = project(gate_w, halves), project(up_w, halves)
     is_slot = lax.broadcasted_iota(jnp.int32, (1, halves.shape[0]), 1) % BLOCK < CAP
     squash = 1.0 / (1.0 + jnp.exp(-pre_gate))
@@ -184,7 +184,7 @@
 def forward(pieces, gate_w, up_w):
     count = len(pieces)
     units, width = gate_w.shape
-    rows = count * pieces[0].shape[0]
+    rows = sum(piece.shape[0] for piece in pieces)
     kept = (units, rows)
     return pl.pallas_call(
         functools.partial(forward_kernel, count),
@@ -199,11 +199,7 @@
         compiler_params=pltpu.CompilerParams(
             vmem_limit_bytes=4 * MIB + rows * width + 40 * rows * units
         ),
-        cost_estimate=pl.CostEstimate(
-            flops=4 * rows * units * width,
-            bytes_accessed=4 * units * width,
-            transcendentals=rows * units,
-        ),
+        cost_estimate=LIGHT,
         name="forward",
     )(*pieces, gate_w, up_w)
 
@@ -241,7 +237,7 @@
     part, halves, gate_out, up_out, low_out, high_out, gates_out = refs[count + 6 :]
     rows = halves.shape[0]
     mine = rows // 2
-    gather_pieces(pieces, halves)
+    gather_pieces(pieces, halves.shape[1], halves)
     back = project(down_w, halves)
     gate_terms = jnp.sum(hidden[...].astype(jnp.float32) * back, axis=0, keepdims=True)
     up_pre = back * activated[...]
@@ -261,7 +257,7 @@
 def backward(pieces, activated, slope, hidden, weights):
     count = len(pieces)
     units, width = weights[0].shape
-    rows = count * pieces[0].shape[0]
+    rows = sum(piece.shape[0] for piece in pieces)
     mine = rows // 2
     shapes = [
         (mine, width // 4),
@@ -282,11 +278,7 @@
             + 2 * sum(height * across for height, across in shapes)
             + 40 * rows * units
         ),
-        cost_estimate=pl.CostEstimate(
-            flops=3 * rows * units * width,
-            bytes_accessed=2 * units * width,
-            transcendentals=0,
-        ),
+        cost_estimate=LIGHT,
         name="backward",
     )(*pieces, activated, slope, hidden, *weights)
 
@@ -307,9 +299,7 @@
         in_specs=[VMEM] * 5,
         out_specs=VMEM,
         compiler_params=pltpu.CompilerParams(vmem_limit_bytes=8 * MIB + 4 * rows * width),
-        cost_estimate=pl.CostEstimate(
-            flops=4 * rows * low.shape[1] * size, bytes_accessed=4 * rows * size, transcendentals=0
-        ),
+        cost_estimate=LIGHT,
         name="far_rows",
     )(low, high, gates, gate_w, up_w)
 
@@ -335,11 +325,7 @@
         in_specs=[VMEM] * 6,
         out_specs=[VMEM] * count,
         compiler_params=pltpu.CompilerParams(vmem_limit_bytes=8 * MIB + 16 * rows * width),
-        cost_estimate=pl.CostEstimate(
-            flops=4 * rows * low.shape[1] * width,
-            bytes_accessed=4 * rows * width,
-            transcendentals=0,
-        ),
+        cost_estimate=LIGHT,
         name="own_rows",
     )(low, high, gates, gate_w, up_w, received)
 
@@ -413,11 +399,7 @@
         compiler_params=pltpu.CompilerParams(
             vmem_limit_bytes=6 * MIB + 12 * units * half + 16 * units * rows
         ),
-        cost_estimate=pl.CostEstimate(
-            flops=12 * rows * units * half,
-            bytes_accessed=12 * units * half,
-            transcendentals=0,
-        ),
+        cost_estimate=LIGHT,
         name="weight_grads",
     )(*factors, token_halves, grad_halves)
 
@@ -465,7 +447,10 @@
 
 def offsets(count):
     near, far = list(range(1, count // 2)), list(range(count // 2, count))
-    return [0] + near[:1] + far + near[1:]
+    order = [0]
+    for i, k in enumerate(near):
+        order += [k, far[i]]
+    return order + far[len(near) :]
 
 
 def exchange(blocks):
@@ -491,25 +476,20 @@
     tie = lax.optimization_barrier
 
     sent = dispatch(n_targets, ids, tokens, gates, out_grad)
-    ids_after, *sent = tie((ids, *sent))
     arrived = exchange([sent[k] for k in offsets(n_targets)])
-    arrived[0], *table = tie((arrived[0], *placement(n_targets, ids_after)))
-    token_rows, grad_rows = pack(arrived)
-
-    token_held = cross(token_rows, far_bits)
-    near = sorted(token_held)
-    token_near = [token_held[mask] for mask in near]
-    token_far = [flip(value, "dp", 1) for value in token_near]
-    grad_held = cross(grad_rows, far_bits)
-    grad_near = [grad_held[mask] for mask in near]
-    token_halves, activated, slope, hidden = forward(
-        token_near + token_far, weights[0], weights[1]
-    )
-    activated, slope, hidden, *grad_near[1:] = tie((activated, slope, hidden, *grad_near[1:]))
-    grad_far = [flip(value, "dp", 1) for value in grad_near]
-
+    middle = n_targets // 2
+    early = pack(arrived[:middle])
+    ids_after, _ = tie((ids, early))
+    table, late = tie((placement(n_targets, ids_after), arrived[middle:]))
+    held = [cross(group, far_bits) for group in (early, pack(late))]
+    near = sorted(held[0])
+    others = [{mask: flip(held[0][mask], "dp", 1) for mask in near}]
+    others[0], held[1] = tie((others[0], held[1]))
+    others.append({mask: flip(held[1][mask], "dp", 1) for mask in near})
+    pieces = [group[mask] for groups in (held, others) for mask in near for group in groups]
+    token_halves, activated, slope, hidden = forward(pieces, weights[0], weights[1])
     part, grad_halves, gate_f, up_f, low, high, gate_column = backward(
-        grad_near + grad_far, activated, slope, hidden, weights
+        pieces, activated, slope, hidden, weights
     )
     middle = width // 4
     received = flip(part, "dp", 1)
@@ -525,11 +505,9 @@
         moved_left = {mask: flip(lefts.pop(mask), "dp", bit) for mask in masks}
         moved_right = {mask: flip(rights.pop(mask), "dp", bit) for mask in masks}
         if bit == far_bits[-1]:
-            moved_left, rights, gate_f, up_f, hidden = tie(
-                (moved_left, rights, gate_f, up_f, hidden)
-            )
+            rights, gate_f, up_f, hidden = tie((rights, gate_f, up_f, hidden))
             grads = weight_grads((gate_f, up_f, hidden), token_halves, grad_halves)
-            moved_right, grads = tie((moved_right, grads))
+            moved_left, moved_right, grads = tie((moved_left, moved_right, grads))
         for mask in masks:
             terms = (lefts[mask ^ bit], rights[mask ^ bit]), (moved_left[mask], moved_right[mask])
             if bit == far_bits[0]:

time: 70.9 us -> 66.9 us (0.944)
  waiting for transfers between devices: 24.2 us -> 17.7 us
  starting transfers between devices: 30 us -> 31.4 us
  local copies, waits for them, and re-layouts: 0.72 us -> 1.83 us
    ppermute x24, waiting for transfers between devices: 24.2 us -> 17.7 us  [flip(): return lax.ppermute(value, axis, [(i, i ^ bit) for i in range(size)])]
    ppermute x24, starting transfers between devices: 30 us -> 31.4 us  [flip(): return lax.ppermute(value, axis, [(i, i ^ bit) for i in range(size)])]
    unnamed x12, local copies, waits for them, and re-layouts: 0.72 us -> 1.83 us
  transfers between devices with their start and end apart: 24 -> 24, of which waited for: 12 -> 10; matrix products, arithmetic and copies ran while one was open for 0% -> 0% of each run, Pallas kernels for 13% -> 9%
where the time goes in v6:
time: 66.9 us; the launch traced here: 66.7 us
  starting transfers between devices  31.4 us (47%)
  waiting for transfers between devices  17.7 us (26%)
  Pallas kernels  15 us (22%)
  local copies, waits for them, and re-layouts  1.83 us (3%)
  between operations  0.8 us (1%)
    ppermute x24, starting transfers between devices, flip(): return lax.ppermute(value, axis, [(i, i ^ bit) for i in range(size)])  31.4 us
    ppermute x24, waiting for transfers between devices, flip(): return lax.ppermute(value, axis, [(i, i ^ bit) for i in range(size)])  17.7 us
    pallas_call x1, Pallas kernels, weight_grads(): pl.pallas_call(functools.partial(weight_kernel, chunk), out_shape=[struct...  4.07 us
    pallas_call x1, Pallas kernels, backward(): pl.pallas_call(functools.partial(backward_kernel, count), out_shape=[stru...  2.55 us
    pallas_call x1, Pallas kernels, dispatch(): pl.pallas_call(functools.partial(dispatch_kernel, n_targets), out_shape=[...  2.36 us
    pallas_call x1, Pallas kernels, forward(): pl.pallas_call(functools.partial(forward_kernel, count), out_shape=[struc...  1.96 us
    pallas_call x2, Pallas kernels, own_rows(): pl.pallas_call(functools.partial(own_kernel, start, LANES if start else 0...  1.84 us
    unnamed x12, local copies, waits for them, and re-layouts  1.83 us
  transfers between devices with their start and end apart: 24, of which 10 were waited for; matrix products, arithmetic and copies ran while one was open for 0% of the time, Pallas kernels for 9%

profile of v6, /device:TPU:0, one launch (start us, length us, event | category | flops | bytes accessed | tf_op | source)
XLA Modules:
  0.0 66.7 jit_solution(11252268692936029589)
XLA Ops:
  0.6 2.4 %dispatch.1 = (bf16[8,4096]{1,0:T(8,128)(2,1)}, bf16[8,4096]{1,0:T(8,128)(2,1)}, bf16[8,4096]{1,0:T(8,128)(2,1)}, bf16[8,4096]{1,0:T(8,128)(2,1)}, bf16[8,4096]{...) custom-call(s32[8,32]{1,0:T(8,128)} %bitcast.22, ...), custom_call_target="tpu_custom_call" | custom-call | tf_op jit(solution)/shard_map/dispatch/pallas_call | solution.py:92
  3.0 3.0 %collective-permute-start = (bf16[8,4096]{1,0:T(8,128)(2,1)}, bf16[8,4096]{1,0:T(8,128)(2,1)S(1)}, u32[]{:S(2)}, u32[]{:S(2)}) collective-permute-start(bf16[8,4096]{1,0:T(8,128)(2,1)} %get-tuple-element.71), channel_id=1, source_target_pairs={{0,4},{4,0},{8,12},{12,8},{16,20},{20,16},{24,28},{28,24},{1,5},{5... | collective-permute-start | bytes 196616 | tf_op jit(solution)/shard_map/ppermute | solution.py:445
  6.0 2.6 %collective-permute-start.1 = (bf16[8,4096]{1,0:T(8,128)(2,1)}, bf16[8,4096]{1,0:T(8,128)(2,1)S(1)}, u32[]{:S(2)}, u32[]{:S(2)}) collective-permute-start(bf16[8,4096]{1,0:T(8,128)(2,1)} %get-tuple-element.72), channel_id=1, source_target_pairs={{0,16},{4,20},{8,24},{12,28},{16,0},{20,4},{24,8},{28,12},{1,17},{... | collective-permute-start | bytes 196616 | tf_op jit(solution)/shard_map/ppermute | solution.py:445
  8.6 1.6 %collective-permute-start.2 = (bf16[8,4096]{1,0:T(8,128)(2,1)}, bf16[8,4096]{1,0:T(8,128)(2,1)S(1)}, u32[]{:S(2)}, u32[]{:S(2)}) collective-permute-start(bf16[8,4096]{1,0:T(8,128)(2,1)} %get-tuple-element.73), channel_id=1, source_target_pairs={{0,8},{4,12},{8,0},{12,4},{16,24},{20,28},{24,16},{28,20},{1,9},{5... | collective-permute-start | bytes 196616 | tf_op jit(solution)/shard_map/ppermute | solution.py:445
  10.5 1.4 %collective-permute-start.4 = (bf16[8,4096]{1,0:T(8,128)(2,1)}, bf16[8,4096]{1,0:T(8,128)(2,1)S(1)}, u32[]{:S(2)}, u32[]{:S(2)}) collective-permute-start(bf16[8,4096]{1,0:T(8,128)(2,1)} %get-tuple-element.79), channel_id=1, source_target_pairs={{0,12},{4,8},{8,4},{12,0},{16,28},{20,24},{24,20},{28,16},{1,13},{... | collective-permute-start | bytes 196616 | tf_op jit(solution)/shard_map/ppermute | solution.py:445
  11.9 3.6 %collective-permute-start.5 = (bf16[8,4096]{1,0:T(8,128)(2,1)}, bf16[8,4096]{1,0:T(8,128)(2,1)S(1)}, u32[]{:S(2)}, u32[]{:S(2)}) collective-permute-start(bf16[8,4096]{1,0:T(8,128)(2,1)} %get-tuple-element.80), channel_id=1, source_target_pairs={{0,24},{4,28},{8,16},{12,20},{16,8},{20,12},{24,0},{28,4},{1,25},{... | collective-permute-start | bytes 196616 | tf_op jit(solution)/shard_map/ppermute | solution.py:445
  15.5 1.6 %collective-permute-start.6 = (bf16[8,4096]{1,0:T(8,128)(2,1)}, bf16[8,4096]{1,0:T(8,128)(2,1)S(1)}, u32[]{:S(2)}, u32[]{:S(2)}) collective-permute-start(bf16[8,4096]{1,0:T(8,128)(2,1)} %get-tuple-element.81), channel_id=1, source_target_pairs={{0,28},{4,24},{8,20},{12,16},{16,12},{20,8},{24,4},{28,0},{1,29},{... | collective-permute-start | bytes 196616 | tf_op jit(solution)/shard_map/ppermute | solution.py:445
  18.0 1.6 %collective-permute-start.8 = (bf16[32,4096]{1,0:T(8,128)(2,1)S(1)}, bf16[32,4096]{1,0:T(8,128)(2,1)S(1)}, u32[]{:S(2)}, u32[]{:S(2)}) collective-permute-start(bf16[32,4096]{1,0:T(8,128)(2,1)S(1)} %pack.2.refs_0_), channel_id=1, source_target_pairs={{0,2},{1,3},{2,0},{3,1},{4,6},{5,7},{6,4},{7,5},{8,10},{9,11},{10,... | collective-permute-start | bytes 786440 | tf_op jit(solution)/shard_map/ppermute | solution.py:445
  20.8 1.9 %collective-permute-done.6.refs_3_ = bf16[8,4096]{1,0:T(8,128)(2,1)S(1)} collective-permute-done((bf16[8,4096]{1,0:T(8,128)(2,1)}, bf16[8,4096]{1,0:T(8,128)(2,1)S(1)}, u32[]{:S(2)}, u32[]{:S(2)}) %collective-permute-start.6) | collective-permute-done | bytes 65568 | tf_op jit(solution)/shard_map/ppermute | solution.py:445
  22.7 1.6 %collective-permute-start.10 = (bf16[32,4096]{1,0:T(8,128)(2,1)S(1)}, bf16[32,4096]{1,0:T(8,128)(2,1)S(1)}, u32[]{:S(2)}, u32[]{:S(2)}) collective-permute-start(bf16[32,4096]{1,0:T(8,128)(2,1)S(1)} %pack.3.refs_1_), channel_id=1, source_target_pairs={{0,2},{1,3},{2,0},{3,1},{4,6},{5,7},{6,4},{7,5},{8,10},{9,11},{10,... | collective-permute-start | bytes 786440 | tf_op jit(solution)/shard_map/ppermute | solution.py:445
  24.8 5.3 %collective-permute-done.10.refs_3_ = bf16[32,4096]{1,0:T(8,128)(2,1)S(1)} collective-permute-done((bf16[32,4096]{1,0:T(8,128)(2,1)S(1)}, bf16[32,4096]{1,0:T(8,128)(2,1)S(1)}, u32[]{:S(2)}, u32[]{:S(2)}) %collective-permute-start.10) | collective-permute-done | bytes 262176 | tf_op jit(solution)/shard_map/ppermute | solution.py:445
  30.5 1.0 %collective-permute-done.11.refs_5_ = bf16[32,4096]{1,0:T(8,128)(2,1)S(1)} collective-permute-done((bf16[32,4096]{1,0:T(8,128)(2,1)S(1)}, bf16[32,4096]{1,0:T(8,128)(2,1)S(1)}, u32[]{:S(2)}, u32[]{:S(2)}) %collective-permute-start.11) | collective-permute-done | bytes 262176 | tf_op jit(solution)/shard_map/ppermute | solution.py:445
  31.9 2.0 %forward.1 = (bf16[256,2048]{1,0:T(8,128)(2,1)S(1)}, f32[384,256]{1,0:T(8,128)S(1)}, f32[384,256]{1,0:T(8,128)S(1)}, bf16[384,256]{1,0:T(8,128)(2,1)S(1)}) custom-call(bf16[32,4096]{1,0:T(8,128)(2,1)S(1)} %pack.2.refs_0_, bf16[32,4096]{1,0:T(8,128)(2,1)S(1)} %pack.3.refs_1_, bf16[32,4096]{1,0:T(8,128)(2,1)S(1)} %collective-permute-done.8.refs_2_, ...), custom_call_target="tpu_custom_call" | custom-call | flops 1000000 | bytes 10000 | tf_op jit(solution)/shard_map/forward/pallas_call | solution.py:189
  33.9 2.6 %backward.1 = (bf16[128,1024]{1,0:T(8,128)(2,1)S(1)}, bf16[256,2048]{1,0:T(8,128)(2,1)S(1)}, bf16[384,256]{1,0:T(8,128)(2,1)S(1)}, bf16[384,256]{1,0:T(8,128)(2,...) custom-call(bf16[32,4096]{1,0:T(8,128)(2,1)S(1)} %pack.2.refs_0_, ...), custom_call_target="tpu_custom_call" | custom-call | flops 1000000 | bytes 10000 | tf_op jit(solution)/shard_map/backward/pallas_call | solution.py:271
  40.6 1.5 %collective-permute-start.16 = (bf16[64,1152]{1,0:T(8,128)(2,1)S(1)}, bf16[64,1152]{1,0:T(8,128)(2,1)S(1)}, u32[]{:S(2)}, u32[]{:S(2)}) collective-permute-start(bf16[64,1152]{1,0:T(8,128)(2,1)S(1)} %get-tuple-element.111), channel_id=1, source_target_pairs={{0,2},{1,3},{2,0},{3,1},{4,6},{5,7},{6,4},{7,5},{8,10},{9,11},{10,... | collective-permute-start | bytes 442376 | tf_op jit(solution)/shard_map/ppermute | solution.py:445
  42.7 4.1 %weight_grads.1 = (bf16[384,4096]{1,0:T(8,128)(2,1)}, bf16[384,4096]{1,0:T(8,128)(2,1)}, bf16[384,4096]{1,0:T(8,128)(2,1)}) custom-call(bf16[384,256]{1,0:T(8,128)(2,1)S(1)} %get-tuple-element.112.refs_0_, bf16[384,256]{1,0:T(8,128)(2,1)S(1)} %get-tuple-element.113.refs_1_, bf16[384,256]{1,0:T(8,128)(2,1)S(1)} %get-tuple-element.114.refs_10_.refs_2_, ...), custom_call_target="tpu_custom_call" | custom-call | flops 1000000 | bytes 10000 | tf_op jit(solution)/shard_map/weight_grads/pallas_call | solution.py:392
  46.8 2.6 %collective-permute-done.15.refs_2_ = bf16[64,1024]{1,0:T(8,128)(2,1)S(1)} collective-permute-done((bf16[64,1024]{1,0:T(8,128)(2,1)S(1)}, bf16[64,1024]{1,0:T(8,128)(2,1)S(1)}, u32[]{:S(2)}, u32[]{:S(2)}) %collective-permute-start.15) | collective-permute-done | bytes 131104 | tf_op jit(solution)/shard_map/ppermute | solution.py:445
  49.5 1.6 %collective-permute-start.17 = (bf16[8,2176]{1,0:T(8,128)(2,1)S(1)}, bf16[8,2176]{1,0:T(8,128)(2,1)S(1)}, u32[]{:S(2)}, u32[]{:S(2)}) collective-permute-start(bf16[8,2176]{1,0:T(8,128)(2,1)S(1)} %get-tuple-element.123), channel_id=1, source_target_pairs={{0,4},{4,0},{8,12},{12,8},{16,20},{20,16},{24,28},{28,24},{1,5},{5... | collective-permute-start | bytes 104456 | tf_op jit(solution)/shard_map/ppermute | solution.py:445
  51.0 2.8 %collective-permute-start.19 = (bf16[8,2176]{1,0:T(8,128)(2,1)S(1)}, bf16[8,2176]{1,0:T(8,128)(2,1)S(1)}, u32[]{:S(2)}, u32[]{:S(2)}) collective-permute-start(bf16[8,2176]{1,0:T(8,128)(2,1)S(1)} %get-tuple-element.125), channel_id=1, source_target_pairs={{0,8},{4,12},{8,0},{12,4},{16,24},{20,28},{24,16},{28,20},{1,9},{5... | collective-permute-start | bytes 104456 | tf_op jit(solution)/shard_map/ppermute | solution.py:445
  53.9 3.0 %collective-permute-start.21 = (bf16[8,2176]{1,0:T(8,128)(2,1)S(1)}, bf16[8,2176]{1,0:T(8,128)(2,1)S(1)}, u32[]{:S(2)}, u32[]{:S(2)}) collective-permute-start(bf16[8,2176]{1,0:T(8,128)(2,1)S(1)} %get-tuple-element.127), channel_id=1, source_target_pairs={{0,12},{4,8},{8,4},{12,0},{16,28},{20,24},{24,20},{28,16},{1,13},{... | collective-permute-start | bytes 104456 | tf_op jit(solution)/shard_map/ppermute | solution.py:445
  56.9 2.2 %collective-permute-start.22 = (bf16[8,2176]{1,0:T(8,128)(2,1)S(1)}, bf16[8,2176]{1,0:T(8,128)(2,1)S(1)}, u32[]{:S(2)}, u32[]{:S(2)}) collective-permute-start(bf16[8,2176]{1,0:T(8,128)(2,1)S(1)} %get-tuple-element.128), channel_id=1, source_target_pairs={{0,24},{4,28},{8,16},{12,20},{16,8},{20,12},{24,0},{28,4},{1,25},{... | collective-permute-start | bytes 104456 | tf_op jit(solution)/shard_map/ppermute | solution.py:445
  59.1 1.6 %collective-permute-start.23 = (bf16[8,2176]{1,0:T(8,128)(2,1)S(1)}, bf16[8,2176]{1,0:T(8,128)(2,1)S(1)}, u32[]{:S(2)}, u32[]{:S(2)}) collective-permute-start(bf16[8,2176]{1,0:T(8,128)(2,1)S(1)} %get-tuple-element.129), channel_id=1, source_target_pairs={{0,28},{4,24},{8,20},{12,16},{16,12},{20,8},{24,4},{28,0},{1,29},{... | collective-permute-start | bytes 104456 | tf_op jit(solution)/shard_map/ppermute | solution.py:445
  60.7 1.9 %collective-permute-done.22.refs_6_ = bf16[8,2176]{1,0:T(8,128)(2,1)S(1)} collective-permute-done((bf16[8,2176]{1,0:T(8,128)(2,1)S(1)}, bf16[8,2176]{1,0:T(8,128)(2,1)S(1)}, u32[]{:S(2)}, u32[]{:S(2)}) %collective-permute-start.22) | collective-permute-done | bytes 34848 | tf_op jit(solution)/shard_map/ppermute | solution.py:445
  62.6 3.1 %collective-permute-done.23.refs_7_ = bf16[8,2176]{1,0:T(8,128)(2,1)S(1)} collective-permute-done((bf16[8,2176]{1,0:T(8,128)(2,1)S(1)}, bf16[8,2176]{1,0:T(8,128)(2,1)S(1)}, u32[]{:S(2)}, u32[]{:S(2)}) %collective-permute-start.23) | collective-permute-done | bytes 34848 | tf_op jit(solution)/shard_map/ppermute | solution.py:445
  (48 shorter events, 9.6 us)
Async XLA Ops:
  3.0 8.9 %collective-permute-start = (bf16[8,4096]{1,0:T(8,128)(2,1)}, bf16[8,4096]{1,0:T(8,128)(2,1)S(1)}, u32[]{:S(2)}, u32[]{:S(2)}) collective-permute-start(bf16[8,4096]{1,0:T(8,128)(2,1)} %get-tuple-element.71), channel_id=1, source_target_pairs={{0,4},{4,0},{8,12},{12,8},{16,20},{20,16},{24,28},{28,24},{1,5},{5... | collective-permute-start | bytes 196616 | tf_op jit(solution)/shard_map/ppermute | solution.py:445
  6.0 9.5 %collective-permute-start.1 = (bf16[8,4096]{1,0:T(8,128)(2,1)}, bf16[8,4096]{1,0:T(8,128)(2,1)S(1)}, u32[]{:S(2)}, u32[]{:S(2)}) collective-permute-start(bf16[8,4096]{1,0:T(8,128)(2,1)} %get-tuple-element.72), channel_id=1, source_target_pairs={{0,16},{4,20},{8,24},{12,28},{16,0},{20,4},{24,8},{28,12},{1,17},{... | collective-permute-start | bytes 196616 | tf_op jit(solution)/shard_map/ppermute | solution.py:445
  8.6 8.4 %collective-permute-start.2 = (bf16[8,4096]{1,0:T(8,128)(2,1)}, bf16[8,4096]{1,0:T(8,128)(2,1)S(1)}, u32[]{:S(2)}, u32[]{:S(2)}) collective-permute-start(bf16[8,4096]{1,0:T(8,128)(2,1)} %get-tuple-element.73), channel_id=1, source_target_pairs={{0,8},{4,12},{8,0},{12,4},{16,24},{20,28},{24,16},{28,20},{1,9},{5... | collective-permute-start | bytes 196616 | tf_op jit(solution)/shard_map/ppermute | solution.py:445
  10.2 10.5 %collective-permute-start.3 = (bf16[8,4096]{1,0:T(8,128)(2,1)}, bf16[8,4096]{1,0:T(8,128)(2,1)S(1)}, u32[]{:S(2)}, u32[]{:S(2)}) collective-permute-start(bf16[8,4096]{1,0:T(8,128)(2,1)} %get-tuple-element.78), channel_id=1, source_target_pairs={{0,20},{4,16},{8,28},{12,24},{16,4},{20,0},{24,12},{28,8},{1,21},{... | collective-permute-start | bytes 196616 | tf_op jit(solution)/shard_map/ppermute | solution.py:445
  10.5 10.3 %collective-permute-start.4 = (bf16[8,4096]{1,0:T(8,128)(2,1)}, bf16[8,4096]{1,0:T(8,128)(2,1)S(1)}, u32[]{:S(2)}, u32[]{:S(2)}) collective-permute-start(bf16[8,4096]{1,0:T(8,128)(2,1)} %get-tuple-element.79), channel_id=1, source_target_pairs={{0,12},{4,8},{8,4},{12,0},{16,28},{20,24},{24,20},{28,16},{1,13},{... | collective-permute-start | bytes 196616 | tf_op jit(solution)/shard_map/ppermute | solution.py:445
  11.9 8.9 %collective-permute-start.5 = (bf16[8,4096]{1,0:T(8,128)(2,1)}, bf16[8,4096]{1,0:T(8,128)(2,1)S(1)}, u32[]{:S(2)}, u32[]{:S(2)}) collective-permute-start(bf16[8,4096]{1,0:T(8,128)(2,1)} %get-tuple-element.80), channel_id=1, source_target_pairs={{0,24},{4,28},{8,16},{12,20},{16,8},{20,12},{24,0},{28,4},{1,25},{... | collective-permute-start | bytes 196616 | tf_op jit(solution)/shard_map/ppermute | solution.py:445
  15.5 7.2 %collective-permute-start.6 = (bf16[8,4096]{1,0:T(8,128)(2,1)}, bf16[8,4096]{1,0:T(8,128)(2,1)S(1)}, u32[]{:S(2)}, u32[]{:S(2)}) collective-permute-start(bf16[8,4096]{1,0:T(8,128)(2,1)} %get-tuple-element.81), channel_id=1, source_target_pairs={{0,28},{4,24},{8,20},{12,16},{16,12},{20,8},{24,4},{28,0},{1,29},{... | collective-permute-start | bytes 196616 | tf_op jit(solution)/shard_map/ppermute | solution.py:445
  18.0 6.8 %collective-permute-start.8 = (bf16[32,4096]{1,0:T(8,128)(2,1)S(1)}, bf16[32,4096]{1,0:T(8,128)(2,1)S(1)}, u32[]{:S(2)}, u32[]{:S(2)}) collective-permute-start(bf16[32,4096]{1,0:T(8,128)(2,1)S(1)} %pack.2.refs_0_), channel_id=1, source_target_pairs={{0,2},{1,3},{2,0},{3,1},{4,6},{5,7},{6,4},{7,5},{8,10},{9,11},{10,... | collective-permute-start | bytes 786440 | tf_op jit(solution)/shard_map/ppermute | solution.py:445
  20.7 9.3 %collective-permute-start.7 = (bf16[32,4096]{1,0:T(8,128)(2,1)S(1)}, bf16[32,4096]{1,0:T(8,128)(2,1)S(1)}, u32[]{:S(2)}, u32[]{:S(2)}) collective-permute-start(bf16[32,4096]{1,0:T(8,128)(2,1)S(1)} %pack.2.refs_0_), channel_id=1, source_target_pairs={{0,1},{1,0},{2,3},{3,2},{4,5},{5,4},{6,7},{7,6},{8,9},{9,8},{10,11... | collective-permute-start | bytes 786440 | tf_op jit(solution)/shard_map/ppermute | solution.py:445
  22.7 7.3 %collective-permute-start.10 = (bf16[32,4096]{1,0:T(8,128)(2,1)S(1)}, bf16[32,4096]{1,0:T(8,128)(2,1)S(1)}, u32[]{:S(2)}, u32[]{:S(2)}) collective-permute-start(bf16[32,4096]{1,0:T(8,128)(2,1)S(1)} %pack.3.refs_1_), channel_id=1, source_target_pairs={{0,2},{1,3},{2,0},{3,1},{4,6},{5,7},{6,4},{7,5},{8,10},{9,11},{10,... | collective-permute-start | bytes 786440 | tf_op jit(solution)/shard_map/ppermute | solution.py:445
  24.8 5.3 %collective-permute-start.9 = (bf16[32,4096]{1,0:T(8,128)(2,1)S(1)}, bf16[32,4096]{1,0:T(8,128)(2,1)S(1)}, u32[]{:S(2)}, u32[]{:S(2)}) collective-permute-start(bf16[32,4096]{1,0:T(8,128)(2,1)S(1)} %collective-permute-done.8.refs_2_), channel_id=1, source_target_pairs={{0,1},{1,0},{2,3},{3,2},{4,5},{5,4},{6,7},{7,6},{8,9},{9,8},{10,11... | collective-permute-start | bytes 786440 | tf_op jit(solution)/shard_map/ppermute | solution.py:445
  30.0 1.5 %collective-permute-start.11 = (bf16[32,4096]{1,0:T(8,128)(2,1)S(1)}, bf16[32,4096]{1,0:T(8,128)(2,1)S(1)}, u32[]{:S(2)}, u32[]{:S(2)}) collective-permute-start(bf16[32,4096]{1,0:T(8,128)(2,1)S(1)} %pack.3.refs_1_), channel_id=1, source_target_pairs={{0,1},{1,0},{2,3},{3,2},{4,5},{5,4},{6,7},{7,6},{8,9},{9,8},{10,11... | collective-permute-start | bytes 786440 | tf_op jit(solution)/shard_map/ppermute | solution.py:445
  30.0 1.9 %collective-permute-start.12 = (bf16[32,4096]{1,0:T(8,128)(2,1)S(1)}, bf16[32,4096]{1,0:T(8,128)(2,1)S(1)}, u32[]{:S(2)}, u32[]{:S(2)}) collective-permute-start(bf16[32,4096]{1,0:T(8,128)(2,1)S(1)} %collective-permute-done.10.refs_3_), channel_id=1, source_target_pairs={{0,1},{1,0},{2,3},{3,2},{4,5},{5,4},{6,7},{7,6},{8,9},{9,8},{10,11... | collective-permute-start | bytes 786440 | tf_op jit(solution)/shard_map/ppermute | solution.py:445
  36.5 1.6 %collective-permute-start.13 = (bf16[128,1024]{1,0:T(8,128)(2,1)S(1)}, bf16[128,1024]{1,0:T(8,128)(2,1)S(1)}, u32[]{:S(2)}, u32[]{:S(2)}) collective-permute-start(bf16[128,1024]{1,0:T(8,128)(2,1)S(1)} %get-tuple-element.96), channel_id=1, source_target_pairs={{0,1},{1,0},{2,3},{3,2},{4,5},{5,4},{6,7},{7,6},{8,9},{9,8},{10,11... | collective-permute-start | bytes 786440 | tf_op jit(solution)/shard_map/ppermute | solution.py:445
  38.1 1.6 %collective-permute-start.14 = (bf16[128,1152]{1,0:T(8,128)(2,1)S(1)}, bf16[128,1152]{1,0:T(8,128)(2,1)S(1)}, u32[]{:S(2)}, u32[]{:S(2)}) collective-permute-start(bf16[128,1152]{1,0:T(8,128)(2,1)S(1)} %far_rows.1), channel_id=1, source_target_pairs={{0,1},{1,0},{2,3},{3,2},{4,5},{5,4},{6,7},{7,6},{8,9},{9,8},{10,11... | collective-permute-start | bytes 884744 | tf_op jit(solution)/shard_map/ppermute | solution.py:445
  40.6 8.8 %collective-permute-start.16 = (bf16[64,1152]{1,0:T(8,128)(2,1)S(1)}, bf16[64,1152]{1,0:T(8,128)(2,1)S(1)}, u32[]{:S(2)}, u32[]{:S(2)}) collective-permute-start(bf16[64,1152]{1,0:T(8,128)(2,1)S(1)} %get-tuple-element.111), channel_id=1, source_target_pairs={{0,2},{1,3},{2,0},{3,1},{4,6},{5,7},{6,4},{7,5},{8,10},{9,11},{10,... | collective-permute-start | bytes 442376 | tf_op jit(solution)/shard_map/ppermute | solution.py:445
  42.2 7.2 %collective-permute-start.15 = (bf16[64,1024]{1,0:T(8,128)(2,1)S(1)}, bf16[64,1024]{1,0:T(8,128)(2,1)S(1)}, u32[]{:S(2)}, u32[]{:S(2)}) collective-permute-start(bf16[64,1024]{1,0:T(8,128)(2,1)S(1)} %get-tuple-element.110), channel_id=1, source_target_pairs={{0,2},{1,3},{2,0},{3,1},{4,6},{5,7},{6,4},{7,5},{8,10},{9,11},{10,... | collective-permute-start | bytes 393224 | tf_op jit(solution)/shard_map/ppermute | solution.py:445
  49.5 7.4 %collective-permute-start.17 = (bf16[8,2176]{1,0:T(8,128)(2,1)S(1)}, bf16[8,2176]{1,0:T(8,128)(2,1)S(1)}, u32[]{:S(2)}, u32[]{:S(2)}) collective-permute-start(bf16[8,2176]{1,0:T(8,128)(2,1)S(1)} %get-tuple-element.123), channel_id=1, source_target_pairs={{0,4},{4,0},{8,12},{12,8},{16,20},{20,16},{24,28},{28,24},{1,5},{5... | collective-permute-start | bytes 104456 | tf_op jit(solution)/shard_map/ppermute | solution.py:445
  51.0 8.1 %collective-permute-start.18 = (bf16[8,2176]{1,0:T(8,128)(2,1)S(1)}, bf16[8,2176]{1,0:T(8,128)(2,1)S(1)}, u32[]{:S(2)}, u32[]{:S(2)}) collective-permute-start(bf16[8,2176]{1,0:T(8,128)(2,1)S(1)} %get-tuple-element.124), channel_id=1, source_target_pairs={{0,16},{4,20},{8,24},{12,28},{16,0},{20,4},{24,8},{28,12},{1,17},{... | collective-permute-start | bytes 104456 | tf_op jit(solution)/shard_map/ppermute | solution.py:445
  51.0 9.6 %collective-permute-start.19 = (bf16[8,2176]{1,0:T(8,128)(2,1)S(1)}, bf16[8,2176]{1,0:T(8,128)(2,1)S(1)}, u32[]{:S(2)}, u32[]{:S(2)}) collective-permute-start(bf16[8,2176]{1,0:T(8,128)(2,1)S(1)} %get-tuple-element.125), channel_id=1, source_target_pairs={{0,8},{4,12},{8,0},{12,4},{16,24},{20,28},{24,16},{28,20},{1,9},{5... | collective-permute-start | bytes 104456 | tf_op jit(solution)/shard_map/ppermute | solution.py:445
  53.8 6.9 %collective-permute-start.20 = (bf16[8,2176]{1,0:T(8,128)(2,1)S(1)}, bf16[8,2176]{1,0:T(8,128)(2,1)S(1)}, u32[]{:S(2)}, u32[]{:S(2)}) collective-permute-start(bf16[8,2176]{1,0:T(8,128)(2,1)S(1)} %get-tuple-element.126), channel_id=1, source_target_pairs={{0,20},{4,16},{8,28},{12,24},{16,4},{20,0},{24,12},{28,8},{1,21},{... | collective-permute-start | bytes 104456 | tf_op jit(solution)/shard_map/ppermute | solution.py:445
  53.9 6.8 %collective-permute-start.21 = (bf16[8,2176]{1,0:T(8,128)(2,1)S(1)}, bf16[8,2176]{1,0:T(8,128)(2,1)S(1)}, u32[]{:S(2)}, u32[]{:S(2)}) collective-permute-start(bf16[8,2176]{1,0:T(8,128)(2,1)S(1)} %get-tuple-element.127), channel_id=1, source_target_pairs={{0,12},{4,8},{8,4},{12,0},{16,28},{20,24},{24,20},{28,16},{1,13},{... | collective-permute-start | bytes 104456 | tf_op jit(solution)/shard_map/ppermute | solution.py:445
  56.9 5.7 %collective-permute-start.22 = (bf16[8,2176]{1,0:T(8,128)(2,1)S(1)}, bf16[8,2176]{1,0:T(8,128)(2,1)S(1)}, u32[]{:S(2)}, u32[]{:S(2)}) collective-permute-start(bf16[8,2176]{1,0:T(8,128)(2,1)S(1)} %get-tuple-element.128), channel_id=1, source_target_pairs={{0,24},{4,28},{8,16},{12,20},{16,8},{20,12},{24,0},{28,4},{1,25},{... | collective-permute-start | bytes 104456 | tf_op jit(solution)/shard_map/ppermute | solution.py:445
  59.1 6.6 %collective-permute-start.23 = (bf16[8,2176]{1,0:T(8,128)(2,1)S(1)}, bf16[8,2176]{1,0:T(8,128)(2,1)S(1)}, u32[]{:S(2)}, u32[]{:S(2)}) collective-permute-start(bf16[8,2176]{1,0:T(8,128)(2,1)S(1)} %get-tuple-element.129), channel_id=1, source_target_pairs={{0,28},{4,24},{8,20},{12,16},{16,12},{20,8},{24,4},{28,0},{1,29},{... | collective-permute-start | bytes 104456 | tf_op jit(solution)/shard_map/ppermute | solution.py:445
  (6 other events, 56.9 us)

commit v7 on v6

--- a/solution.py
+++ b/solution.py
@@ -21,6 +21,7 @@
 VMEM = pl.BlockSpec(memory_space=pltpu.VMEM)
 
 LIGHT = pl.CostEstimate(flops=10**6, bytes_accessed=10**4, transcendentals=0)
+SOME = pl.CostEstimate(flops=10**9, bytes_accessed=6 * 10**6, transcendentals=0)
 
 
 def struct(shape, dtype=jnp.bfloat16):
@@ -304,72 +305,66 @@
     )(low, high, gates, gate_w, up_w)
 
 
-def own_kernel(start, extra, low, high, gates, gate_w, up_w, received, *parts):
-    rows, size = received.shape
-    size -= extra
+def own_kernel(low, high, gates, gate_w, up_w, left, right, *parts):
+    rows, size = left.shape
+    extra = right.shape[1] - LANES
     block = parts[0].shape[0]
-    if extra:
-        for i, part in enumerate(parts):
-            span = pl.ds(i * block, block)
-            part[:, size:] = (
-                gates[span, :].astype(jnp.float32) + received[span, size:].astype(jnp.float32)
-            ).astype(jnp.bfloat16)
-    row_grads(low[:rows, :], high[:rows, :], gate_w, up_w, received, parts, start, size)
-
-
-def own_rows(count, start, low, high, gates, gate_w, up_w, received):
-    rows, width = received.shape
-    return pl.pallas_call(
-        functools.partial(own_kernel, start, LANES if start else 0),
+    for i, part in enumerate(parts):
+        span = pl.ds(i * block, block)
+        part[:, size + extra :] = (
+            gates[span, :].astype(jnp.float32) + right[span, extra:].astype(jnp.float32)
+        ).astype(jnp.bfloat16)
+    low, high = low[:rows, :], high[:rows, :]
+    row_grads(low, high, gate_w, up_w, left, parts, 0, size)
+    views = [part.at[:, pl.ds(size, extra)] for part in parts]
+    row_grads(low, high, gate_w, up_w, right, views, size, extra)
+
+
+def own_rows(count, low, high, gates, gate_w, up_w, left, right):
+    rows = left.shape[0]
+    width = left.shape[1] + right.shape[1]
+    return pl.pallas_call(
+        own_kernel,
         out_shape=[struct((rows // count, width))] * count,
-        in_specs=[VMEM] * 6,
+        in_specs=[VMEM] * 7,
         out_specs=[VMEM] * count,
         compiler_params=pltpu.CompilerParams(vmem_limit_bytes=8 * MIB + 16 * rows * width),
         cost_estimate=LIGHT,
         name="own_rows",
-    )(low, high, gates, gate_w, up_w, received)
-
-
-def add_kernel(count, *refs):
-    lefts, rights, outs = refs[:count], refs[count : 2 * count], refs[2 * count :]
+    )(low, high, gates, gate_w, up_w, left, right)
+
+
+def add_kernel(left, right, *outs):
+    total = (left[...].astype(jnp.float32) + right[...].astype(jnp.float32)).astype(jnp.bfloat16)
     block = outs[0].shape[0]
-    base = 0
-    for left, right in zip(lefts, rights):
-        total = (left[...].astype(jnp.float32) + right[...].astype(jnp.float32)).astype(
-            jnp.bfloat16
-        )
-        for i, out in enumerate(outs):
-            out[:, base : base + left.shape[1]] = total[i * block : (i + 1) * block]
-        base += left.shape[1]
-
-
-def add_rows(lefts, rights, blocks=1):
-    count = len(lefts)
-    rows = lefts[0].shape[0]
-    width = sum(left.shape[1] for left in lefts)
-    return pl.pallas_call(
-        functools.partial(add_kernel, count),
+    for i, out in enumerate(outs):
+        out[...] = total[i * block : (i + 1) * block]
+
+
+def add_rows(left, right, blocks):
+    rows, width = left.shape
+    return pl.pallas_call(
+        add_kernel,
         out_shape=[struct((rows // blocks, width))] * blocks,
-        in_specs=[VMEM] * 2 * count,
+        in_specs=[VMEM] * 2,
         out_specs=[VMEM] * blocks,
         compiler_params=pltpu.CompilerParams(vmem_limit_bytes=4 * MIB + 16 * rows * width),
         name="add_rows",
-    )(*lefts, *rights)
-
-
-def weight_kernel(chunk, *refs):
-    gate_f, up_f, down_f, token_halves, grad_halves = refs[:5]
-    outs, stages, sems = refs[5:8], refs[8:11], refs[11]
-    half = token_halves.shape[1]
-    jobs = ((gate_f, token_halves), (up_f, token_halves), (down_f, grad_halves))
-    factors = []
-    for factor, _ in jobs:
+    )(left, right)
+
+
+def weight_kernel(chunk, count, *refs):
+    factors, halves = refs[:count], refs[count]
+    outs, stages, sems = refs[count + 1 : 2 * count + 1], refs[2 * count + 1 : -1], refs[-1]
+    half = halves.shape[1]
+    pairs = []
+    for factor in factors:
         low = factor[...]
         high = pltpu.roll(low.astype(jnp.float32), CAP, 1).astype(jnp.bfloat16)
-        factors.append((low, high))
+        pairs.append((low, high))
     copies = []
     for start in range(0, half, chunk):
-        for (_, halves), pair, out, stage in zip(jobs, factors, outs, stages):
+        for pair, out, stage in zip(pairs, outs, stages):
             for factor, base in zip(pair, (0, half)):
                 span = pl.ds(base + start, chunk)
                 stage[:, span] = jnp.dot(
@@ -384,24 +379,25 @@
         copy.wait()
 
 
-def weight_grads(factors, token_halves, grad_halves):
+def weight_grads(factors, halves, cost):
+    count = len(factors)
     units, rows = factors[0].shape
-    half = token_halves.shape[1]
+    half = halves.shape[1]
     chunk = 512 if half % 512 == 0 else half
     shape = (units, 2 * half)
     return pl.pallas_call(
-        functools.partial(weight_kernel, chunk),
-        out_shape=[struct(shape)] * 3,
-        in_specs=[VMEM] * 5,
-        out_specs=[HBM] * 3,
-        scratch_shapes=[pltpu.VMEM(shape, jnp.bfloat16)] * 3
-        + [pltpu.SemaphoreType.DMA((6 * half // chunk,))],
+        functools.partial(weight_kernel, chunk, count),
+        out_shape=[struct(shape)] * count,
+        in_specs=[VMEM] * (count + 1),
+        out_specs=[HBM] * count,
+        scratch_shapes=[pltpu.VMEM(shape, jnp.bfloat16)] * count
+        + [pltpu.SemaphoreType.DMA((2 * count * half // chunk,))],
         compiler_params=pltpu.CompilerParams(
-            vmem_limit_bytes=6 * MIB + 12 * units * half + 16 * units * rows
+            vmem_limit_bytes=6 * MIB + 4 * count * units * half + 8 * count * units * rows
         ),
-        cost_estimate=LIGHT,
+        cost_estimate=cost,
         name="weight_grads",
-    )(*factors, token_halves, grad_halves)
+    )(*factors, halves)
 
 
 def combine_kernel(n_targets, first, second, choice_ref, gates_ref, *refs):
@@ -447,14 +443,13 @@
 
 def offsets(count):
     near, far = list(range(1, count // 2)), list(range(count // 2, count))
-    order = [0]
+    order = []
     for i, k in enumerate(near):
         order += [k, far[i]]
-    return order + far[len(near) :]
-
-
-def exchange(blocks):
-    order = offsets(len(blocks))
+    return order + far[len(near) :] + [0]
+
+
+def exchange(blocks, order):
     return [flip(block, "expert", k) if k else block for k, block in zip(order, blocks)]
 
 
@@ -475,47 +470,54 @@
     weights = (w_gate[0], w_up[0], w_down[0])
     tie = lax.optimization_barrier
 
+    order = offsets(n_targets)
+    middle = n_targets // 2
     sent = dispatch(n_targets, ids, tokens, gates, out_grad)
-    arrived = exchange([sent[k] for k in offsets(n_targets)])
-    middle = n_targets // 2
+    arrived = exchange([sent[k] for k in order], order)
     early = pack(arrived[:middle])
     ids_after, _ = tie((ids, early))
     table, late = tie((placement(n_targets, ids_after), arrived[middle:]))
     held = [cross(group, far_bits) for group in (early, pack(late))]
     near = sorted(held[0])
     others = [{mask: flip(held[0][mask], "dp", 1) for mask in near}]
-    others[0], held[1] = tie((others[0], held[1]))
-    others.append({mask: flip(held[1][mask], "dp", 1) for mask in near})
+    others.append({0: flip(held[1][0], "dp", 1)})
+    far_late = {mask: held[1][mask] for mask in near[1:]}
+    others, far_late = tie((others, far_late))
+    for mask in far_late:
+        others[1][mask] = flip(far_late[mask], "dp", 1)
     pieces = [group[mask] for groups in (held, others) for mask in near for group in groups]
     token_halves, activated, slope, hidden = forward(pieces, weights[0], weights[1])
     part, grad_halves, gate_f, up_f, low, high, gate_column = backward(
         pieces, activated, slope, hidden, weights
     )
-    middle = width // 4
+
     received = flip(part, "dp", 1)
-    other = far_rows(middle, low, high, gate_column, weights[0], weights[1])
+    other = far_rows(width // 4, low, high, gate_column, weights[0], weights[1])
     received, other = tie((received, other))
-    left = own_rows(len(near), 0, low, high, gate_column, weights[0], weights[1], received)
-    received = flip(other, "dp", 1)
-    received, left = tie((received, left))
-    right = own_rows(len(near), middle, low, high, gate_column, weights[0], weights[1], received)
-    lefts, rights = dict(zip(near, left)), dict(zip(near, right))
-    for bit in reversed(far_bits):
-        masks = [mask for mask in lefts if mask & bit]
-        moved_left = {mask: flip(lefts.pop(mask), "dp", bit) for mask in masks}
-        moved_right = {mask: flip(rights.pop(mask), "dp", bit) for mask in masks}
-        if bit == far_bits[-1]:
-            rights, gate_f, up_f, hidden = tie((rights, gate_f, up_f, hidden))
-            grads = weight_grads((gate_f, up_f, hidden), token_halves, grad_halves)
-            moved_left, moved_right, grads = tie((moved_left, moved_right, grads))
-        for mask in masks:
-            terms = (lefts[mask ^ bit], rights[mask ^ bit]), (moved_left[mask], moved_right[mask])
-            if bit == far_bits[0]:
-                returned = exchange(add_rows(*terms, n_targets))
-            else:
-                lefts[mask ^ bit] = add_rows(terms[0][:1], terms[1][:1])[0]
-                rights[mask ^ bit] = add_rows(terms[0][1:], terms[1][1:])[0]
+    parts = own_rows(
+        2 * len(near), low, high, gate_column, weights[0], weights[1], received, flip(other, "dp", 1)
+    )
+    sums = [dict(zip(near, parts[i::2])) for i in range(2)]
+    gate_f, up_f, _ = tie((gate_f, up_f, parts))
+    grad_gate, grad_up = weight_grads((gate_f, up_f), token_halves, LIGHT)
+    returned = []
+    for group in sums:
+        for bit in reversed(far_bits):
+            masks = [mask for mask in group if mask & bit]
+            moved = {mask: flip(group.pop(mask), "dp", bit) for mask in masks}
+            if group is sums[0] and bit == far_bits[-1]:
+                moved, grad_gate, grad_up = tie((moved, grad_gate, grad_up))
+            for mask in masks:
+                blocks = middle if bit == far_bits[0] else 1
+                total = add_rows(group[mask ^ bit], moved[mask], blocks)
+                group[mask ^ bit] = total if blocks > 1 else total[0]
+        returned += list(group[0])
+    hidden, _ = tie((hidden, returned[middle:]))
+    (grad_down,) = weight_grads((hidden,), grad_halves, SOME)
+    returned = exchange(returned, order)
+    returned, grad_down = tie((returned, grad_down))
     token_grad, gate_grad = combine(table, gates, returned, width)
+    grads = (grad_gate, grad_up, grad_down)
     return (token_grad, gate_grad.T, *(grad[None] for grad in grads))
 
 

time: 66.9 us -> 64.5 us (0.964)
  starting transfers between devices: 31.4 us -> 28.8 us
  Pallas kernels: 15 us -> 16 us
  local copies, waits for them, and re-layouts: 1.83 us -> 0.99 us
    ppermute x24, starting transfers between devices: 31.4 us -> 28.8 us  [flip(): return lax.ppermute(value, axis, [(i, i ^ bit) for i in range(size)])]
    pallas_call x4 -> x5, Pallas kernels: 5.98 us -> 6.95 us  [the longest x2 5.05 us: weight_grads(): pl.pallas_call(functools.partial(weight_kernel, chunk, count), out_shape=...]
    unnamed x12, local copies, waits for them, and re-layouts: 1.83 us -> 0.99 us
  transfers between devices with their start and end apart: 24 -> 24, of which waited for: 10 -> 8; matrix products, arithmetic and copies ran while one was open for 0% -> 0% of each run, Pallas kernels for 9% -> 10%
where the time goes in v7:
time: 64.5 us; the launch traced here: 64.3 us
  starting transfers between devices  28.8 us (45%)
  waiting for transfers between devices  17.7 us (27%)
  Pallas kernels  16 us (25%)
  local copies, waits for them, and re-layouts  0.99 us (2%)
  between operations  0.84 us (1%)
    ppermute x24, starting transfers between devices, flip(): return lax.ppermute(value, axis, [(i, i ^ bit) for i in range(size)])  28.8 us
    ppermute x24, waiting for transfers between devices, flip(): return lax.ppermute(value, axis, [(i, i ^ bit) for i in range(size)])  17.7 us
    pallas_call x2, Pallas kernels, weight_grads(): pl.pallas_call(functools.partial(weight_kernel, chunk, count), out_shape=...  5.05 us
    pallas_call x1, Pallas kernels, backward(): pl.pallas_call(functools.partial(backward_kernel, count), out_shape=[stru...  2.55 us
    pallas_call x1, Pallas kernels, dispatch(): pl.pallas_call(functools.partial(dispatch_kernel, n_targets), out_shape=[...  2.36 us
    pallas_call x1, Pallas kernels, forward(): pl.pallas_call(functools.partial(forward_kernel, count), out_shape=[struc...  1.95 us
    pallas_call x1, Pallas kernels, own_rows(): pl.pallas_call(own_kernel, out_shape=[struct((rows // count, width))] * c...  1.82 us
  transfers between devices with their start and end apart: 24, of which 8 were waited for; matrix products, arithmetic and copies ran while one was open for 0% of the time, Pallas kernels for 10%

profile of v7, /device:TPU:0, one launch (start us, length us, event | category | flops | bytes accessed | tf_op | source)
XLA Modules:
  0.0 64.3 jit_solution(6269467860423901820)
XLA Ops:
  0.6 2.4 %dispatch.1 = (bf16[8,4096]{1,0:T(8,128)(2,1)}, bf16[8,4096]{1,0:T(8,128)(2,1)}, bf16[8,4096]{1,0:T(8,128)(2,1)}, bf16[8,4096]{1,0:T(8,128)(2,1)}, bf16[8,4096]{...) custom-call(s32[8,32]{1,0:T(8,128)} %bitcast.20, ...), custom_call_target="tpu_custom_call" | custom-call | tf_op jit(solution)/shard_map/dispatch/pallas_call | solution.py:93
  3.0 3.0 %collective-permute-start = (bf16[8,4096]{1,0:T(8,128)(2,1)}, bf16[8,4096]{1,0:T(8,128)(2,1)S(1)}, u32[]{:S(2)}, u32[]{:S(2)}) collective-permute-start(bf16[8,4096]{1,0:T(8,128)(2,1)} %get-tuple-element.72), channel_id=1, source_target_pairs={{0,4},{4,0},{8,12},{12,8},{16,20},{20,16},{24,28},{28,24},{1,5},{5... | collective-permute-start | bytes 196616 | tf_op jit(solution)/shard_map/ppermute | solution.py:441
  6.0 2.6 %collective-permute-start.1 = (bf16[8,4096]{1,0:T(8,128)(2,1)}, bf16[8,4096]{1,0:T(8,128)(2,1)S(1)}, u32[]{:S(2)}, u32[]{:S(2)}) collective-permute-start(bf16[8,4096]{1,0:T(8,128)(2,1)} %get-tuple-element.73), channel_id=1, source_target_pairs={{0,16},{4,20},{8,24},{12,28},{16,0},{20,4},{24,8},{28,12},{1,17},{... | collective-permute-start | bytes 196616 | tf_op jit(solution)/shard_map/ppermute | solution.py:441
  8.6 1.6 %collective-permute-start.2 = (bf16[8,4096]{1,0:T(8,128)(2,1)}, bf16[8,4096]{1,0:T(8,128)(2,1)S(1)}, u32[]{:S(2)}, u32[]{:S(2)}) collective-permute-start(bf16[8,4096]{1,0:T(8,128)(2,1)} %get-tuple-element.74), channel_id=1, source_target_pairs={{0,8},{4,12},{8,0},{12,4},{16,24},{20,28},{24,16},{28,20},{1,9},{5... | collective-permute-start | bytes 196616 | tf_op jit(solution)/shard_map/ppermute | solution.py:441
  10.5 1.4 %collective-permute-start.4 = (bf16[8,4096]{1,0:T(8,128)(2,1)}, bf16[8,4096]{1,0:T(8,128)(2,1)S(1)}, u32[]{:S(2)}, u32[]{:S(2)}) collective-permute-start(bf16[8,4096]{1,0:T(8,128)(2,1)} %get-tuple-element.80), channel_id=1, source_target_pairs={{0,12},{4,8},{8,4},{12,0},{16,28},{20,24},{24,20},{28,16},{1,13},{... | collective-permute-start | bytes 196616 | tf_op jit(solution)/shard_map/ppermute | solution.py:441
  11.9 3.6 %collective-permute-start.5 = (bf16[8,4096]{1,0:T(8,128)(2,1)}, bf16[8,4096]{1,0:T(8,128)(2,1)S(1)}, u32[]{:S(2)}, u32[]{:S(2)}) collective-permute-start(bf16[8,4096]{1,0:T(8,128)(2,1)} %get-tuple-element.81), channel_id=1, source_target_pairs={{0,24},{4,28},{8,16},{12,20},{16,8},{20,12},{24,0},{28,4},{1,25},{... | collective-permute-start | bytes 196616 | tf_op jit(solution)/shard_map/ppermute | solution.py:441
  15.5 1.6 %collective-permute-start.6 = (bf16[8,4096]{1,0:T(8,128)(2,1)}, bf16[8,4096]{1,0:T(8,128)(2,1)S(1)}, u32[]{:S(2)}, u32[]{:S(2)}) collective-permute-start(bf16[8,4096]{1,0:T(8,128)(2,1)} %get-tuple-element.82), channel_id=1, source_target_pairs={{0,28},{4,24},{8,20},{12,16},{16,12},{20,8},{24,4},{28,0},{1,29},{... | collective-permute-start | bytes 196616 | tf_op jit(solution)/shard_map/ppermute | solution.py:441
  17.1 2.9 %collective-permute-done.3.refs_3_ = bf16[8,4096]{1,0:T(8,128)(2,1)S(1)} collective-permute-done((bf16[8,4096]{1,0:T(8,128)(2,1)}, bf16[8,4096]{1,0:T(8,128)(2,1)S(1)}, u32[]{:S(2)}, u32[]{:S(2)}) %collective-permute-start.3) | collective-permute-done | bytes 65568 | tf_op jit(solution)/shard_map/ppermute | solution.py:441
  20.1 1.6 %collective-permute-start.7 = (bf16[32,4096]{1,0:T(8,128)(2,1)S(1)}, bf16[32,4096]{1,0:T(8,128)(2,1)S(1)}, u32[]{:S(2)}, u32[]{:S(2)}) collective-permute-start(bf16[32,4096]{1,0:T(8,128)(2,1)S(1)} %pack.2.refs_0_), channel_id=1, source_target_pairs={{0,2},{1,3},{2,0},{3,1},{4,6},{5,7},{6,4},{7,5},{8,10},{9,11},{10,... | collective-permute-start | bytes 786440 | tf_op jit(solution)/shard_map/ppermute | solution.py:441
  24.3 3.0 %collective-permute-done.7.refs_2_ = bf16[32,4096]{1,0:T(8,128)(2,1)S(1)} collective-permute-done((bf16[32,4096]{1,0:T(8,128)(2,1)S(1)}, bf16[32,4096]{1,0:T(8,128)(2,1)S(1)}, u32[]{:S(2)}, u32[]{:S(2)}) %collective-permute-start.7) | collective-permute-done | bytes 262176 | tf_op jit(solution)/shard_map/ppermute | solution.py:441
  27.2 4.9 %collective-permute-done.8.refs_3_ = bf16[32,4096]{1,0:T(8,128)(2,1)S(1)} collective-permute-done((bf16[32,4096]{1,0:T(8,128)(2,1)S(1)}, bf16[32,4096]{1,0:T(8,128)(2,1)S(1)}, u32[]{:S(2)}, u32[]{:S(2)}) %collective-permute-start.8) | collective-permute-done | bytes 262176 | tf_op jit(solution)/shard_map/ppermute | solution.py:441
  32.2 1.5 %collective-permute-done.12.refs_7_ = bf16[32,4096]{1,0:T(8,128)(2,1)S(1)} collective-permute-done((bf16[32,4096]{1,0:T(8,128)(2,1)S(1)}, bf16[32,4096]{1,0:T(8,128)(2,1)S(1)}, u32[]{:S(2)}, u32[]{:S(2)}) %collective-permute-start.12) | collective-permute-done | bytes 262176 | tf_op jit(solution)/shard_map/ppermute | solution.py:441
  33.7 2.0 %forward.1 = (bf16[256,2048]{1,0:T(8,128)(2,1)S(1)}, f32[384,256]{1,0:T(8,128)S(1)}, f32[384,256]{1,0:T(8,128)S(1)}, bf16[384,256]{1,0:T(8,128)(2,1)S(1)}) custom-call(bf16[32,4096]{1,0:T(8,128)(2,1)S(1)} %pack.2.refs_0_, bf16[32,4096]{1,0:T(8,128)(2,1)S(1)} %pack.3.refs_1_, bf16[32,4096]{1,0:T(8,128)(2,1)S(1)} %collective-permute-done.7.refs_2_, ...), custom_call_target="tpu_custom_call" | custom-call | flops 1000000 | bytes 10000 | tf_op jit(solution)/shard_map/forward/pallas_call | solution.py:190
  35.7 2.6 %backward.1 = (bf16[128,1024]{1,0:T(8,128)(2,1)S(1)}, bf16[256,2048]{1,0:T(8,128)(2,1)S(1)}, bf16[384,256]{1,0:T(8,128)(2,1)S(1)}, bf16[384,256]{1,0:T(8,128)(2,...) custom-call(bf16[32,4096]{1,0:T(8,128)(2,1)S(1)} %pack.2.refs_0_, ...), custom_call_target="tpu_custom_call" | custom-call | flops 1000000 | bytes 10000 | tf_op jit(solution)/shard_map/backward/pallas_call | solution.py:272
  40.0 1.4 %collective-permute-done.14.right = bf16[128,1152]{1,0:T(8,128)(2,1)S(1)} collective-permute-done((bf16[128,1152]{1,0:T(8,128)(2,1)S(1)}, bf16[128,1152]{1,0:T(8,128)(2,1)S(1)}, u32[]{:S(2)}, u32[]{:S(2)}) %collective-permute-start.14) | collective-permute-done | bytes 294944 | tf_op jit(solution)/shard_map/ppermute | solution.py:441
  41.4 1.8 %own_rows.1 = (bf16[32,2176]{1,0:T(8,128)(2,1)S(1)}, bf16[32,2176]{1,0:T(8,128)(2,1)S(1)}, bf16[32,2176]{1,0:T(8,128)(2,1)S(1)}, bf16[32,2176]{1,0:T(8,128)(2,1)S(1)}) custom-call(bf16[256,768]{1,0:T(8,128)(2,1)S(1)} %get-tuple-element.98.low, bf16[256,768]{1,0:T(8,128)(2,1)S(1)} %get-tuple-element.99.high, bf16[256,128]{1,0:T(8,128)(2,1)S(1)} %get-tuple-element.100.gates, ...), custom_call_target="tpu_custom_call" | custom-call | flops 1000000 | bytes 10000 | tf_op jit(solution)/shard_map/own_rows/pallas_call | solution.py:326
  43.3 1.6 %collective-permute-start.15 = (bf16[32,2176]{1,0:T(8,128)(2,1)S(1)}, bf16[32,2176]{1,0:T(8,128)(2,1)S(1)}, u32[]{:S(2)}, u32[]{:S(2)}) collective-permute-start(bf16[32,2176]{1,0:T(8,128)(2,1)S(1)} %get-tuple-element.105), channel_id=1, source_target_pairs={{0,2},{1,3},{2,0},{3,1},{4,6},{5,7},{6,4},{7,5},{8,10},{9,11},{10,... | collective-permute-start | bytes 417800 | tf_op jit(solution)/shard_map/ppermute | solution.py:441
  45.4 3.1 %weight_grads.2 = (bf16[384,4096]{1,0:T(8,128)(2,1)}, bf16[384,4096]{1,0:T(8,128)(2,1)}) custom-call(bf16[384,256]{1,0:T(8,128)(2,1)S(1)} %get-tuple-element.110.refs_0_, bf16[384,256]{1,0:T(8,128)(2,1)S(1)} %get-tuple-element.111.refs_1_, bf16[256,2048]{1,0:T(8,128)(2,1)S(1)} %get-tuple-element.112.refs_2_), custom_call_target="tpu_custom_call" | custom-call | flops 1000000 | bytes 10000 | tf_op jit(solution)/shard_map/weight_grads/pallas_call | solution.py:388
  48.4 1.4 %collective-permute-done.15.right = bf16[32,2176]{1,0:T(8,128)(2,1)S(1)} collective-permute-done((bf16[32,2176]{1,0:T(8,128)(2,1)S(1)}, bf16[32,2176]{1,0:T(8,128)(2,1)S(1)}, u32[]{:S(2)}, u32[]{:S(2)}) %collective-permute-start.15) | collective-permute-done | bytes 139296 | tf_op jit(solution)/shard_map/ppermute | solution.py:441
  50.1 2.0 %collective-permute-done.20.right = bf16[32,2176]{1,0:T(8,128)(2,1)S(1)} collective-permute-done((bf16[32,2176]{1,0:T(8,128)(2,1)S(1)}, bf16[32,2176]{1,0:T(8,128)(2,1)S(1)}, u32[]{:S(2)}, u32[]{:S(2)}) %collective-permute-start.20) | collective-permute-done | bytes 139296 | tf_op jit(solution)/shard_map/ppermute | solution.py:441
  52.7 3.2 %collective-permute-start.22 = (bf16[8,2176]{1,0:T(8,128)(2,1)S(1)}, bf16[8,2176]{1,0:T(8,128)(2,1)S(1)}, u32[]{:S(2)}, u32[]{:S(2)}) collective-permute-start(bf16[8,2176]{1,0:T(8,128)(2,1)S(1)} %get-tuple-element.121), channel_id=1, source_target_pairs={{0,24},{4,28},{8,16},{12,20},{16,8},{20,12},{24,0},{28,4},{1,25},{... | collective-permute-start | bytes 104456 | tf_op jit(solution)/shard_map/ppermute | solution.py:441
  55.9 1.5 %collective-permute-start.23 = (bf16[8,2176]{1,0:T(8,128)(2,1)S(1)}, bf16[8,2176]{1,0:T(8,128)(2,1)S(1)}, u32[]{:S(2)}, u32[]{:S(2)}) collective-permute-start(bf16[8,2176]{1,0:T(8,128)(2,1)S(1)} %get-tuple-element.122), channel_id=1, source_target_pairs={{0,28},{4,24},{8,20},{12,16},{16,12},{20,8},{24,4},{28,0},{1,29},{... | collective-permute-start | bytes 104456 | tf_op jit(solution)/shard_map/ppermute | solution.py:441
  57.5 3.7 %collective-permute-start.19 = (bf16[8,2176]{1,0:T(8,128)(2,1)S(1)}, bf16[8,2176]{1,0:T(8,128)(2,1)S(1)}, u32[]{:S(2)}, u32[]{:S(2)}) collective-permute-start(bf16[8,2176]{1,0:T(8,128)(2,1)S(1)} %get-tuple-element.119), channel_id=1, source_target_pairs={{0,20},{4,16},{8,28},{12,24},{16,4},{20,0},{24,12},{28,8},{1,21},{... | collective-permute-start | bytes 104456 | tf_op jit(solution)/shard_map/ppermute | solution.py:441
  61.2 2.0 %weight_grads.3 = bf16[384,4096]{1,0:T(8,128)(2,1)} custom-call(bf16[384,256]{1,0:T(8,128)(2,1)S(1)} %get-tuple-element.124.refs_10_.refs_0_, bf16[256,2048]{1,0:T(8,128)(2,1)S(1)} %get-tuple-element.125.refs_1_), custom_call_target="tpu_custom_call" | custom-call | flops 1000000000 | bytes 6000000 | tf_op jit(solution)/shard_map/weight_grads/pallas_call | solution.py:388
  (49 shorter events, 7.1 us)
Async XLA Ops:
  3.0 8.9 %collective-permute-start = (bf16[8,4096]{1,0:T(8,128)(2,1)}, bf16[8,4096]{1,0:T(8,128)(2,1)S(1)}, u32[]{:S(2)}, u32[]{:S(2)}) collective-permute-start(bf16[8,4096]{1,0:T(8,128)(2,1)} %get-tuple-element.72), channel_id=1, source_target_pairs={{0,4},{4,0},{8,12},{12,8},{16,20},{20,16},{24,28},{28,24},{1,5},{5... | collective-permute-start | bytes 196616 | tf_op jit(solution)/shard_map/ppermute | solution.py:441
  6.0 9.5 %collective-permute-start.1 = (bf16[8,4096]{1,0:T(8,128)(2,1)}, bf16[8,4096]{1,0:T(8,128)(2,1)S(1)}, u32[]{:S(2)}, u32[]{:S(2)}) collective-permute-start(bf16[8,4096]{1,0:T(8,128)(2,1)} %get-tuple-element.73), channel_id=1, source_target_pairs={{0,16},{4,20},{8,24},{12,28},{16,0},{20,4},{24,8},{28,12},{1,17},{... | collective-permute-start | bytes 196616 | tf_op jit(solution)/shard_map/ppermute | solution.py:441
  8.6 8.4 %collective-permute-start.2 = (bf16[8,4096]{1,0:T(8,128)(2,1)}, bf16[8,4096]{1,0:T(8,128)(2,1)S(1)}, u32[]{:S(2)}, u32[]{:S(2)}) collective-permute-start(bf16[8,4096]{1,0:T(8,128)(2,1)} %get-tuple-element.74), channel_id=1, source_target_pairs={{0,8},{4,12},{8,0},{12,4},{16,24},{20,28},{24,16},{28,20},{1,9},{5... | collective-permute-start | bytes 196616 | tf_op jit(solution)/shard_map/ppermute | solution.py:441
  10.2 9.8 %collective-permute-start.3 = (bf16[8,4096]{1,0:T(8,128)(2,1)}, bf16[8,4096]{1,0:T(8,128)(2,1)S(1)}, u32[]{:S(2)}, u32[]{:S(2)}) collective-permute-start(bf16[8,4096]{1,0:T(8,128)(2,1)} %get-tuple-element.75), channel_id=1, source_target_pairs={{0,20},{4,16},{8,28},{12,24},{16,4},{20,0},{24,12},{28,8},{1,21},{... | collective-permute-start | bytes 196616 | tf_op jit(solution)/shard_map/ppermute | solution.py:441
  10.5 12.3 %collective-permute-start.4 = (bf16[8,4096]{1,0:T(8,128)(2,1)}, bf16[8,4096]{1,0:T(8,128)(2,1)S(1)}, u32[]{:S(2)}, u32[]{:S(2)}) collective-permute-start(bf16[8,4096]{1,0:T(8,128)(2,1)} %get-tuple-element.80), channel_id=1, source_target_pairs={{0,12},{4,8},{8,4},{12,0},{16,28},{20,24},{24,20},{28,16},{1,13},{... | collective-permute-start | bytes 196616 | tf_op jit(solution)/shard_map/ppermute | solution.py:441
  11.9 10.9 %collective-permute-start.5 = (bf16[8,4096]{1,0:T(8,128)(2,1)}, bf16[8,4096]{1,0:T(8,128)(2,1)S(1)}, u32[]{:S(2)}, u32[]{:S(2)}) collective-permute-start(bf16[8,4096]{1,0:T(8,128)(2,1)} %get-tuple-element.81), channel_id=1, source_target_pairs={{0,24},{4,28},{8,16},{12,20},{16,8},{20,12},{24,0},{28,4},{1,25},{... | collective-permute-start | bytes 196616 | tf_op jit(solution)/shard_map/ppermute | solution.py:441
  15.5 7.3 %collective-permute-start.6 = (bf16[8,4096]{1,0:T(8,128)(2,1)}, bf16[8,4096]{1,0:T(8,128)(2,1)S(1)}, u32[]{:S(2)}, u32[]{:S(2)}) collective-permute-start(bf16[8,4096]{1,0:T(8,128)(2,1)} %get-tuple-element.82), channel_id=1, source_target_pairs={{0,28},{4,24},{8,20},{12,16},{16,12},{20,8},{24,4},{28,0},{1,29},{... | collective-permute-start | bytes 196616 | tf_op jit(solution)/shard_map/ppermute | solution.py:441
  20.1 7.2 %collective-permute-start.7 = (bf16[32,4096]{1,0:T(8,128)(2,1)S(1)}, bf16[32,4096]{1,0:T(8,128)(2,1)S(1)}, u32[]{:S(2)}, u32[]{:S(2)}) collective-permute-start(bf16[32,4096]{1,0:T(8,128)(2,1)S(1)} %pack.2.refs_0_), channel_id=1, source_target_pairs={{0,2},{1,3},{2,0},{3,1},{4,6},{5,7},{6,4},{7,5},{8,10},{9,11},{10,... | collective-permute-start | bytes 786440 | tf_op jit(solution)/shard_map/ppermute | solution.py:441
  21.6 10.5 %collective-permute-start.9 = (bf16[32,4096]{1,0:T(8,128)(2,1)S(1)}, bf16[32,4096]{1,0:T(8,128)(2,1)S(1)}, u32[]{:S(2)}, u32[]{:S(2)}) collective-permute-start(bf16[32,4096]{1,0:T(8,128)(2,1)S(1)} %pack.2.refs_0_), channel_id=1, source_target_pairs={{0,1},{1,0},{2,3},{3,2},{4,5},{5,4},{6,7},{7,6},{8,9},{9,8},{10,11... | collective-permute-start | bytes 786440 | tf_op jit(solution)/shard_map/ppermute | solution.py:441
  22.9 9.2 %collective-permute-start.8 = (bf16[32,4096]{1,0:T(8,128)(2,1)S(1)}, bf16[32,4096]{1,0:T(8,128)(2,1)S(1)}, u32[]{:S(2)}, u32[]{:S(2)}) collective-permute-start(bf16[32,4096]{1,0:T(8,128)(2,1)S(1)} %pack.3.refs_1_), channel_id=1, source_target_pairs={{0,2},{1,3},{2,0},{3,1},{4,6},{5,7},{6,4},{7,5},{8,10},{9,11},{10,... | collective-permute-start | bytes 786440 | tf_op jit(solution)/shard_map/ppermute | solution.py:441
  24.3 7.9 %collective-permute-start.11 = (bf16[32,4096]{1,0:T(8,128)(2,1)S(1)}, bf16[32,4096]{1,0:T(8,128)(2,1)S(1)}, u32[]{:S(2)}, u32[]{:S(2)}) collective-permute-start(bf16[32,4096]{1,0:T(8,128)(2,1)S(1)} %pack.3.refs_1_), channel_id=1, source_target_pairs={{0,1},{1,0},{2,3},{3,2},{4,5},{5,4},{6,7},{7,6},{8,9},{9,8},{10,11... | collective-permute-start | bytes 786440 | tf_op jit(solution)/shard_map/ppermute | solution.py:441
  27.2 4.9 %collective-permute-start.10 = (bf16[32,4096]{1,0:T(8,128)(2,1)S(1)}, bf16[32,4096]{1,0:T(8,128)(2,1)S(1)}, u32[]{:S(2)}, u32[]{:S(2)}) collective-permute-start(bf16[32,4096]{1,0:T(8,128)(2,1)S(1)} %collective-permute-done.7.refs_2_), channel_id=1, source_target_pairs={{0,1},{1,0},{2,3},{3,2},{4,5},{5,4},{6,7},{7,6},{8,9},{9,8},{10,11... | collective-permute-start | bytes 786440 | tf_op jit(solution)/shard_map/ppermute | solution.py:441
  32.1 1.6 %collective-permute-start.12 = (bf16[32,4096]{1,0:T(8,128)(2,1)S(1)}, bf16[32,4096]{1,0:T(8,128)(2,1)S(1)}, u32[]{:S(2)}, u32[]{:S(2)}) collective-permute-start(bf16[32,4096]{1,0:T(8,128)(2,1)S(1)} %collective-permute-done.8.refs_3_), channel_id=1, source_target_pairs={{0,1},{1,0},{2,3},{3,2},{4,5},{5,4},{6,7},{7,6},{8,9},{9,8},{10,11... | collective-permute-start | bytes 786440 | tf_op jit(solution)/shard_map/ppermute | solution.py:441
  38.3 1.6 %collective-permute-start.13 = (bf16[128,1024]{1,0:T(8,128)(2,1)S(1)}, bf16[128,1024]{1,0:T(8,128)(2,1)S(1)}, u32[]{:S(2)}, u32[]{:S(2)}) collective-permute-start(bf16[128,1024]{1,0:T(8,128)(2,1)S(1)} %get-tuple-element.101), channel_id=1, source_target_pairs={{0,1},{1,0},{2,3},{3,2},{4,5},{5,4},{6,7},{7,6},{8,9},{9,8},{10,11... | collective-permute-start | bytes 786440 | tf_op jit(solution)/shard_map/ppermute | solution.py:441
  39.9 1.6 %collective-permute-start.14 = (bf16[128,1152]{1,0:T(8,128)(2,1)S(1)}, bf16[128,1152]{1,0:T(8,128)(2,1)S(1)}, u32[]{:S(2)}, u32[]{:S(2)}) collective-permute-start(bf16[128,1152]{1,0:T(8,128)(2,1)S(1)} %far_rows.1), channel_id=1, source_target_pairs={{0,1},{1,0},{2,3},{3,2},{4,5},{5,4},{6,7},{7,6},{8,9},{9,8},{10,11... | collective-permute-start | bytes 884744 | tf_op jit(solution)/shard_map/ppermute | solution.py:441
  43.3 6.6 %collective-permute-start.15 = (bf16[32,2176]{1,0:T(8,128)(2,1)S(1)}, bf16[32,2176]{1,0:T(8,128)(2,1)S(1)}, u32[]{:S(2)}, u32[]{:S(2)}) collective-permute-start(bf16[32,2176]{1,0:T(8,128)(2,1)S(1)} %get-tuple-element.105), channel_id=1, source_target_pairs={{0,2},{1,3},{2,0},{3,1},{4,6},{5,7},{6,4},{7,5},{8,10},{9,11},{10,... | collective-permute-start | bytes 417800 | tf_op jit(solution)/shard_map/ppermute | solution.py:441
  44.9 7.2 %collective-permute-start.20 = (bf16[32,2176]{1,0:T(8,128)(2,1)S(1)}, bf16[32,2176]{1,0:T(8,128)(2,1)S(1)}, u32[]{:S(2)}, u32[]{:S(2)}) collective-permute-start(bf16[32,2176]{1,0:T(8,128)(2,1)S(1)} %get-tuple-element.109), channel_id=1, source_target_pairs={{0,2},{1,3},{2,0},{3,1},{4,6},{5,7},{6,4},{7,5},{8,10},{9,11},{10,... | collective-permute-start | bytes 417800 | tf_op jit(solution)/shard_map/ppermute | solution.py:441
  49.9 7.6 %collective-permute-start.16 = (bf16[8,2176]{1,0:T(8,128)(2,1)S(1)}, bf16[8,2176]{1,0:T(8,128)(2,1)S(1)}, u32[]{:S(2)}, u32[]{:S(2)}) collective-permute-start(bf16[8,2176]{1,0:T(8,128)(2,1)S(1)} %get-tuple-element.116), channel_id=1, source_target_pairs={{0,4},{4,0},{8,12},{12,8},{16,20},{20,16},{24,28},{28,24},{1,5},{5... | collective-permute-start | bytes 104456 | tf_op jit(solution)/shard_map/ppermute | solution.py:441
  50.0 7.5 %collective-permute-start.17 = (bf16[8,2176]{1,0:T(8,128)(2,1)S(1)}, bf16[8,2176]{1,0:T(8,128)(2,1)S(1)}, u32[]{:S(2)}, u32[]{:S(2)}) collective-permute-start(bf16[8,2176]{1,0:T(8,128)(2,1)S(1)} %get-tuple-element.117), channel_id=1, source_target_pairs={{0,16},{4,20},{8,24},{12,28},{16,0},{20,4},{24,8},{28,12},{1,17},{... | collective-permute-start | bytes 104456 | tf_op jit(solution)/shard_map/ppermute | solution.py:441
  52.1 11.2 %collective-permute-start.21 = (bf16[8,2176]{1,0:T(8,128)(2,1)S(1)}, bf16[8,2176]{1,0:T(8,128)(2,1)S(1)}, u32[]{:S(2)}, u32[]{:S(2)}) collective-permute-start(bf16[8,2176]{1,0:T(8,128)(2,1)S(1)} %get-tuple-element.120), channel_id=1, source_target_pairs={{0,12},{4,8},{8,4},{12,0},{16,28},{20,24},{24,20},{28,16},{1,13},{... | collective-permute-start | bytes 104456 | tf_op jit(solution)/shard_map/ppermute | solution.py:441
  52.7 10.6 %collective-permute-start.22 = (bf16[8,2176]{1,0:T(8,128)(2,1)S(1)}, bf16[8,2176]{1,0:T(8,128)(2,1)S(1)}, u32[]{:S(2)}, u32[]{:S(2)}) collective-permute-start(bf16[8,2176]{1,0:T(8,128)(2,1)S(1)} %get-tuple-element.121), channel_id=1, source_target_pairs={{0,24},{4,28},{8,16},{12,20},{16,8},{20,12},{24,0},{28,4},{1,25},{... | collective-permute-start | bytes 104456 | tf_op jit(solution)/shard_map/ppermute | solution.py:441
  55.9 7.4 %collective-permute-start.23 = (bf16[8,2176]{1,0:T(8,128)(2,1)S(1)}, bf16[8,2176]{1,0:T(8,128)(2,1)S(1)}, u32[]{:S(2)}, u32[]{:S(2)}) collective-permute-start(bf16[8,2176]{1,0:T(8,128)(2,1)S(1)} %get-tuple-element.122), channel_id=1, source_target_pairs={{0,28},{4,24},{8,20},{12,16},{16,12},{20,8},{24,4},{28,0},{1,29},{... | collective-permute-start | bytes 104456 | tf_op jit(solution)/shard_map/ppermute | solution.py:441
  57.5 5.8 %collective-permute-start.18 = (bf16[8,2176]{1,0:T(8,128)(2,1)S(1)}, bf16[8,2176]{1,0:T(8,128)(2,1)S(1)}, u32[]{:S(2)}, u32[]{:S(2)}) collective-permute-start(bf16[8,2176]{1,0:T(8,128)(2,1)S(1)} %get-tuple-element.118), channel_id=1, source_target_pairs={{0,8},{4,12},{8,0},{12,4},{16,24},{20,28},{24,16},{28,20},{1,9},{5... | collective-permute-start | bytes 104456 | tf_op jit(solution)/shard_map/ppermute | solution.py:441
  57.5 5.8 %collective-permute-start.19 = (bf16[8,2176]{1,0:T(8,128)(2,1)S(1)}, bf16[8,2176]{1,0:T(8,128)(2,1)S(1)}, u32[]{:S(2)}, u32[]{:S(2)}) collective-permute-start(bf16[8,2176]{1,0:T(8,128)(2,1)S(1)} %get-tuple-element.119), channel_id=1, source_target_pairs={{0,20},{4,16},{8,28},{12,24},{16,4},{20,0},{24,12},{28,8},{1,21},{... | collective-permute-start | bytes 104456 | tf_op jit(solution)/shard_map/ppermute | solution.py:441
  (6 other events, 51.0 us)

commit v8 on v7

--- a/solution.py
+++ b/solution.py
@@ -21,7 +21,6 @@
 VMEM = pl.BlockSpec(memory_space=pltpu.VMEM)
 
 LIGHT = pl.CostEstimate(flops=10**6, bytes_accessed=10**4, transcendentals=0)
-SOME = pl.CostEstimate(flops=10**9, bytes_accessed=6 * 10**6, transcendentals=0)
 
 
 def struct(shape, dtype=jnp.bfloat16):
@@ -305,26 +304,42 @@
     )(low, high, gates, gate_w, up_w)
 
 
-def own_kernel(low, high, gates, gate_w, up_w, left, right, *parts):
+def own_first_kernel(low, high, gate_w, up_w, left, out):
+    rows, size = left.shape
+    row_grads(low[:rows, :], high[:rows, :], gate_w, up_w, left, (out,), 0, size)
+
+
+def own_first(low, high, gate_w, up_w, left):
+    return pl.pallas_call(
+        own_first_kernel,
+        out_shape=struct(left.shape),
+        in_specs=[VMEM] * 5,
+        out_specs=VMEM,
+        compiler_params=pltpu.CompilerParams(vmem_limit_bytes=8 * MIB + 16 * left.size),
+        cost_estimate=LIGHT,
+        name="own_first",
+    )(low, high, gate_w, up_w, left)
+
+
+def own_rows_kernel(low, high, gates, gate_w, up_w, left, right, *parts):
     rows, size = left.shape
     extra = right.shape[1] - LANES
     block = parts[0].shape[0]
     for i, part in enumerate(parts):
         span = pl.ds(i * block, block)
+        part[:, :size] = left[span, :]
         part[:, size + extra :] = (
             gates[span, :].astype(jnp.float32) + right[span, extra:].astype(jnp.float32)
         ).astype(jnp.bfloat16)
-    low, high = low[:rows, :], high[:rows, :]
-    row_grads(low, high, gate_w, up_w, left, parts, 0, size)
     views = [part.at[:, pl.ds(size, extra)] for part in parts]
-    row_grads(low, high, gate_w, up_w, right, views, size, extra)
+    row_grads(low[:rows, :], high[:rows, :], gate_w, up_w, right, views, size, extra)
 
 
 def own_rows(count, low, high, gates, gate_w, up_w, left, right):
     rows = left.shape[0]
     width = left.shape[1] + right.shape[1]
     return pl.pallas_call(
-        own_kernel,
+        own_rows_kernel,
         out_shape=[struct((rows // count, width))] * count,
         in_specs=[VMEM] * 7,
         out_specs=[VMEM] * count,
@@ -334,23 +349,39 @@
     )(low, high, gates, gate_w, up_w, left, right)
 
 
-def add_kernel(left, right, *outs):
-    total = (left[...].astype(jnp.float32) + right[...].astype(jnp.float32)).astype(jnp.bfloat16)
-    block = outs[0].shape[0]
-    for i, out in enumerate(outs):
-        out[...] = total[i * block : (i + 1) * block]
-
-
-def add_rows(left, right, blocks):
-    rows, width = left.shape
+def add_kernel(left, right, out):
+    total = left[...].astype(jnp.float32) + right[...].astype(jnp.float32)
+    out[...] = total.astype(jnp.bfloat16)
+
+
+def add_rows(left, right):
     return pl.pallas_call(
         add_kernel,
-        out_shape=[struct((rows // blocks, width))] * blocks,
+        out_shape=struct(left.shape),
         in_specs=[VMEM] * 2,
-        out_specs=[VMEM] * blocks,
-        compiler_params=pltpu.CompilerParams(vmem_limit_bytes=4 * MIB + 16 * rows * width),
+        out_specs=VMEM,
+        compiler_params=pltpu.CompilerParams(vmem_limit_bytes=4 * MIB + 16 * left.size),
         name="add_rows",
     )(left, right)
+
+
+def merge_kernel(kept, passed, *outs):
+    for i, out in enumerate(outs):
+        span = slice(i * BLOCK, (i + 1) * BLOCK)
+        out[...] = jnp.concatenate([kept[span, :], passed[span, :]], axis=0)
+
+
+def merge_rows(kept, passed):
+    rows, width = kept.shape
+    count = rows // BLOCK
+    return pl.pallas_call(
+        merge_kernel,
+        out_shape=[struct((2 * BLOCK, width))] * count,
+        in_specs=[VMEM] * 2,
+        out_specs=[VMEM] * count,
+        compiler_params=pltpu.CompilerParams(vmem_limit_bytes=4 * MIB + 24 * rows * width),
+        name="merge_rows",
+    )(kept, passed)
 
 
 def weight_kernel(chunk, count, *refs):
@@ -379,7 +410,7 @@
         copy.wait()
 
 
-def weight_grads(factors, halves, cost):
+def weight_grads(factors, halves):
     count = len(factors)
     units, rows = factors[0].shape
     half = halves.shape[1]
@@ -395,15 +426,15 @@
         compiler_params=pltpu.CompilerParams(
             vmem_limit_bytes=6 * MIB + 4 * count * units * half + 8 * count * units * rows
         ),
-        cost_estimate=cost,
+        cost_estimate=LIGHT,
         name="weight_grads",
     )(*factors, halves)
 
 
 def combine_kernel(n_targets, first, second, choice_ref, gates_ref, *refs):
-    blocks, (token_ref, gate_ref) = refs[:n_targets], refs[n_targets:]
-    order = offsets(n_targets)
-    back = jnp.concatenate([blocks[order.index(k)][...] for k in range(n_targets)], axis=0)
+    blocks, (token_ref, gate_ref) = refs[: n_targets // 2], refs[n_targets // 2 :]
+    even = offsets(n_targets)[1]
+    back = jnp.concatenate([blocks[even.index(k)][...] for k in range(0, n_targets, 2)], axis=0)
     half = token_ref.shape[1] // 2
     choices, tokens = gates_ref.shape
     rows = back[:, :half]
@@ -422,12 +453,12 @@
 
 
 def combine(table, gates, blocks, width):
-    n_targets = len(blocks)
+    n_targets = 2 * len(blocks)
     choices, tokens = gates.shape
     return pl.pallas_call(
         functools.partial(combine_kernel, n_targets),
         out_shape=[struct((tokens, width)), struct((choices, tokens), jnp.float32)],
-        in_specs=[VMEM] * (4 + n_targets),
+        in_specs=[VMEM] * (4 + len(blocks)),
         out_specs=[VMEM] * 2,
         compiler_params=pltpu.CompilerParams(
             vmem_limit_bytes=4 * MIB + 16 * n_targets * BLOCK * width
@@ -442,11 +473,8 @@
 
 
 def offsets(count):
-    near, far = list(range(1, count // 2)), list(range(count // 2, count))
-    order = []
-    for i, k in enumerate(near):
-        order += [k, far[i]]
-    return order + far[len(near) :] + [0]
+    even = list(range(count // 2, count, 2)) + list(range(count // 2 - 2, -1, -2))
+    return [k ^ 1 for k in even], even
 
 
 def exchange(blocks, order):
@@ -470,10 +498,10 @@
     weights = (w_gate[0], w_up[0], w_down[0])
     tie = lax.optimization_barrier
 
-    order = offsets(n_targets)
+    odd, even = offsets(n_targets)
     middle = n_targets // 2
     sent = dispatch(n_targets, ids, tokens, gates, out_grad)
-    arrived = exchange([sent[k] for k in order], order)
+    arrived = exchange([sent[k] for k in odd + even], odd + even)
     early = pack(arrived[:middle])
     ids_after, _ = tie((ids, early))
     table, late = tie((placement(n_targets, ids_after), arrived[middle:]))
@@ -494,28 +522,31 @@
     received = flip(part, "dp", 1)
     other = far_rows(width // 4, low, high, gate_column, weights[0], weights[1])
     received, other = tie((received, other))
+    left = own_first(low, high, weights[0], weights[1], received)
+    right, left = tie((flip(other, "dp", 1), left))
     parts = own_rows(
-        2 * len(near), low, high, gate_column, weights[0], weights[1], received, flip(other, "dp", 1)
-    )
-    sums = [dict(zip(near, parts[i::2])) for i in range(2)]
+        2 * len(near), low, high, gate_column, weights[0], weights[1], left, right
+    )
     gate_f, up_f, _ = tie((gate_f, up_f, parts))
-    grad_gate, grad_up = weight_grads((gate_f, up_f), token_halves, LIGHT)
-    returned = []
-    for group in sums:
+    grad_gate, grad_up = weight_grads((gate_f, up_f), token_halves)
+    sums = []
+    for group in range(2):
+        held = dict(zip(near, parts[group::2]))
         for bit in reversed(far_bits):
-            masks = [mask for mask in group if mask & bit]
-            moved = {mask: flip(group.pop(mask), "dp", bit) for mask in masks}
-            if group is sums[0] and bit == far_bits[-1]:
+            masks = [mask for mask in held if mask & bit]
+            moved = {mask: flip(held.pop(mask), "dp", bit) for mask in masks}
+            if group == 0 and bit == far_bits[-1]:
                 moved, grad_gate, grad_up = tie((moved, grad_gate, grad_up))
-            for mask in masks:
-                blocks = middle if bit == far_bits[0] else 1
-                total = add_rows(group[mask ^ bit], moved[mask], blocks)
-                group[mask ^ bit] = total if blocks > 1 else total[0]
-        returned += list(group[0])
-    hidden, _ = tie((hidden, returned[middle:]))
-    (grad_down,) = weight_grads((hidden,), grad_halves, SOME)
-    returned = exchange(returned, order)
-    returned, grad_down = tie((returned, grad_down))
+            if bit == far_bits[0]:
+                sums.append((held[0], moved[bit]))
+            else:
+                for mask in masks:
+                    held[mask ^ bit] = add_rows(held[mask ^ bit], moved[mask])
+    passed = add_rows(*sums[0])
+    hidden, _ = tie((hidden, passed))
+    (grad_down,) = weight_grads((hidden,), grad_halves)
+    kept, passed, grad_down = tie((add_rows(*sums[1]), flip(passed, "expert", 1), grad_down))
+    returned = exchange(merge_rows(kept, passed), even)
     token_grad, gate_grad = combine(table, gates, returned, width)
     grads = (grad_gate, grad_up, grad_down)
     return (token_grad, gate_grad.T, *(grad[None] for grad in grads))

time: 64.5 us -> 62 us (0.961)
  starting transfers between devices: 28.8 us -> 25.1 us
  waiting for transfers between devices: 17.7 us -> 18.8 us
    ppermute x24 -> x21, starting transfers between devices: 28.8 us -> 25.1 us  [flip(): return lax.ppermute(value, axis, [(i, i ^ bit) for i in range(size)])]
    ppermute x24 -> x21, waiting for transfers between devices: 17.7 us -> 18.8 us  [flip(): return lax.ppermute(value, axis, [(i, i ^ bit) for i in range(size)])]
    pallas_call x3 -> x5, Pallas kernels: 1.89 us -> 1.97 us  [the longest x1 0.94 us: own_rows(): pl.pallas_call(own_rows_kernel, out_shape=[struct((rows // count, width))...]
  transfers between devices with their start and end apart: 24 -> 21, of which waited for: 8 -> 13; matrix products, arithmetic and copies ran while one was open for 0% -> 0% of each run, Pallas kernels for 10% -> 12%
where the time goes in v8:
time: 62 us; the launch traced here: 61.8 us
  starting transfers between devices  25.1 us (40%)
  waiting for transfers between devices  18.8 us (30%)
  Pallas kernels  16 us (26%)
  local copies, waits for them, and re-layouts  1.01 us (2%)
  between operations  0.81 us (1%)
    ppermute x21, starting transfers between devices, flip(): return lax.ppermute(value, axis, [(i, i ^ bit) for i in range(size)])  25.1 us
    ppermute x21, waiting for transfers between devices, flip(): return lax.ppermute(value, axis, [(i, i ^ bit) for i in range(size)])  18.8 us
    pallas_call x2, Pallas kernels, weight_grads(): pl.pallas_call(functools.partial(weight_kernel, chunk, count), out_shape=...  5.06 us
    pallas_call x1, Pallas kernels, backward(): pl.pallas_call(functools.partial(backward_kernel, count), out_shape=[stru...  2.55 us
    pallas_call x1, Pallas kernels, dispatch(): pl.pallas_call(functools.partial(dispatch_kernel, n_targets), out_shape=[...  2.34 us
    pallas_call x1, Pallas kernels, forward(): pl.pallas_call(functools.partial(forward_kernel, count), out_shape=[struc...  1.95 us
  transfers between devices with their start and end apart: 21, of which 13 were waited for; matrix products, arithmetic and copies ran while one was open for 0% of the time, Pallas kernels for 12%

profile of v8, /device:TPU:0, one launch (start us, length us, event | category | flops | bytes accessed | tf_op | source)
XLA Modules:
  0.0 61.8 jit_solution(13504912286052279092)
XLA Ops:
  0.6 2.3 %dispatch.1 = (bf16[8,4096]{1,0:T(8,128)(2,1)}, bf16[8,4096]{1,0:T(8,128)(2,1)}, bf16[8,4096]{1,0:T(8,128)(2,1)}, bf16[8,4096]{1,0:T(8,128)(2,1)}, bf16[8,4096]{...) custom-call(s32[8,32]{1,0:T(8,128)} %bitcast.22, ...), custom_call_target="tpu_custom_call" | custom-call | tf_op jit(solution)/shard_map/dispatch/pallas_call | solution.py:92
  3.0 5.1 %collective-permute-start = (bf16[8,4096]{1,0:T(8,128)(2,1)}, bf16[8,4096]{1,0:T(8,128)(2,1)S(1)}, u32[]{:S(2)}, u32[]{:S(2)}) collective-permute-start(bf16[8,4096]{1,0:T(8,128)(2,1)} %get-tuple-element.64), channel_id=1, source_target_pairs={{0,20},{4,16},{8,28},{12,24},{16,4},{20,0},{24,12},{28,8},{1,21},{... | collective-permute-start | bytes 196616 | tf_op jit(solution)/shard_map/ppermute | solution.py:472
  8.0 1.3 %collective-permute-start.1 = (bf16[8,4096]{1,0:T(8,128)(2,1)}, bf16[8,4096]{1,0:T(8,128)(2,1)S(1)}, u32[]{:S(2)}, u32[]{:S(2)}) collective-permute-start(bf16[8,4096]{1,0:T(8,128)(2,1)} %get-tuple-element.65), channel_id=1, source_target_pairs={{0,28},{4,24},{8,20},{12,16},{16,12},{20,8},{24,4},{28,0},{1,29},{... | collective-permute-start | bytes 196616 | tf_op jit(solution)/shard_map/ppermute | solution.py:472
  9.8 1.2 %collective-permute-start.3 = (bf16[8,4096]{1,0:T(8,128)(2,1)}, bf16[8,4096]{1,0:T(8,128)(2,1)S(1)}, u32[]{:S(2)}, u32[]{:S(2)}) collective-permute-start(bf16[8,4096]{1,0:T(8,128)(2,1)} %get-tuple-element.67), channel_id=1, source_target_pairs={{0,4},{4,0},{8,12},{12,8},{16,20},{20,16},{24,28},{28,24},{1,5},{5... | collective-permute-start | bytes 196616 | tf_op jit(solution)/shard_map/ppermute | solution.py:472
  11.1 2.8 %collective-permute-start.4 = (bf16[8,4096]{1,0:T(8,128)(2,1)}, bf16[8,4096]{1,0:T(8,128)(2,1)S(1)}, u32[]{:S(2)}, u32[]{:S(2)}) collective-permute-start(bf16[8,4096]{1,0:T(8,128)(2,1)} %get-tuple-element.72), channel_id=1, source_target_pairs={{0,16},{4,20},{8,24},{12,28},{16,0},{20,4},{24,8},{28,12},{1,17},{... | collective-permute-start | bytes 196616 | tf_op jit(solution)/shard_map/ppermute | solution.py:472
  13.8 3.3 %collective-permute-start.5 = (bf16[8,4096]{1,0:T(8,128)(2,1)}, bf16[8,4096]{1,0:T(8,128)(2,1)S(1)}, u32[]{:S(2)}, u32[]{:S(2)}) collective-permute-start(bf16[8,4096]{1,0:T(8,128)(2,1)} %get-tuple-element.73), channel_id=1, source_target_pairs={{0,24},{4,28},{8,16},{12,20},{16,8},{20,12},{24,0},{28,4},{1,25},{... | collective-permute-start | bytes 196616 | tf_op jit(solution)/shard_map/ppermute | solution.py:472
  17.3 1.6 %collective-permute-start.7 = (bf16[32,4096]{1,0:T(8,128)(2,1)S(1)}, bf16[32,4096]{1,0:T(8,128)(2,1)S(1)}, u32[]{:S(2)}, u32[]{:S(2)}) collective-permute-start(bf16[32,4096]{1,0:T(8,128)(2,1)S(1)} %pack.2.refs_0_), channel_id=1, source_target_pairs={{0,2},{1,3},{2,0},{3,1},{4,6},{5,7},{6,4},{7,5},{8,10},{9,11},{10,... | collective-permute-start | bytes 786440 | tf_op jit(solution)/shard_map/ppermute | solution.py:472
  18.8 1.0 %copy-done.5 = s32[32,8]{0,1:T(8,128)S(1)} copy-done((s32[32,8]{0,1:T(8,128)S(1)}, s32[32,8]{0,1:T(8,128)}, u32[]{:S(2)}) %copy-start.5) | copy-done | bytes 1048
  20.6 1.1 %collective-permute-done.6.refs_2_ = bf16[8,4096]{1,0:T(8,128)(2,1)S(1)} collective-permute-done((bf16[8,4096]{1,0:T(8,128)(2,1)}, bf16[8,4096]{1,0:T(8,128)(2,1)S(1)}, u32[]{:S(2)}, u32[]{:S(2)}) %collective-permute-start.6) | collective-permute-done | bytes 65568 | tf_op jit(solution)/shard_map/ppermute | solution.py:472
  21.8 1.6 %collective-permute-start.8 = (bf16[32,4096]{1,0:T(8,128)(2,1)S(1)}, bf16[32,4096]{1,0:T(8,128)(2,1)S(1)}, u32[]{:S(2)}, u32[]{:S(2)}) collective-permute-start(bf16[32,4096]{1,0:T(8,128)(2,1)S(1)} %pack.3.refs_1_), channel_id=1, source_target_pairs={{0,2},{1,3},{2,0},{3,1},{4,6},{5,7},{6,4},{7,5},{8,10},{9,11},{10,... | collective-permute-start | bytes 786440 | tf_op jit(solution)/shard_map/ppermute | solution.py:472
  23.8 6.7 %collective-permute-done.8.refs_3_ = bf16[32,4096]{1,0:T(8,128)(2,1)S(1)} collective-permute-done((bf16[32,4096]{1,0:T(8,128)(2,1)S(1)}, bf16[32,4096]{1,0:T(8,128)(2,1)S(1)}, u32[]{:S(2)}, u32[]{:S(2)}) %collective-permute-start.8) | collective-permute-done | bytes 262176 | tf_op jit(solution)/shard_map/ppermute | solution.py:472
  30.5 1.5 %collective-permute-done.12.refs_7_ = bf16[32,4096]{1,0:T(8,128)(2,1)S(1)} collective-permute-done((bf16[32,4096]{1,0:T(8,128)(2,1)S(1)}, bf16[32,4096]{1,0:T(8,128)(2,1)S(1)}, u32[]{:S(2)}, u32[]{:S(2)}) %collective-permute-start.12) | collective-permute-done | bytes 262176 | tf_op jit(solution)/shard_map/ppermute | solution.py:472
  32.0 2.0 %forward.1 = (bf16[256,2048]{1,0:T(8,128)(2,1)S(1)}, f32[384,256]{1,0:T(8,128)S(1)}, f32[384,256]{1,0:T(8,128)S(1)}, bf16[384,256]{1,0:T(8,128)(2,1)S(1)}) custom-call(bf16[32,4096]{1,0:T(8,128)(2,1)S(1)} %pack.2.refs_0_, bf16[32,4096]{1,0:T(8,128)(2,1)S(1)} %pack.3.refs_1_, bf16[32,4096]{1,0:T(8,128)(2,1)S(1)} %collective-permute-done.7.refs_2_, ...), custom_call_target="tpu_custom_call" | custom-call | flops 1000000 | bytes 10000 | tf_op jit(solution)/shard_map/forward/pallas_call | solution.py:189
  34.0 2.5 %backward.1 = (bf16[128,1024]{1,0:T(8,128)(2,1)S(1)}, bf16[256,2048]{1,0:T(8,128)(2,1)S(1)}, bf16[384,256]{1,0:T(8,128)(2,1)S(1)}, bf16[384,256]{1,0:T(8,128)(2,...) custom-call(bf16[32,4096]{1,0:T(8,128)(2,1)S(1)} %pack.2.refs_0_, ...), custom_call_target="tpu_custom_call" | custom-call | flops 1000000 | bytes 10000 | tf_op jit(solution)/shard_map/backward/pallas_call | solution.py:271
  40.7 1.6 %collective-permute-start.16 = (bf16[32,2176]{1,0:T(8,128)(2,1)S(1)}, bf16[32,2176]{1,0:T(8,128)(2,1)S(1)}, u32[]{:S(2)}, u32[]{:S(2)}) collective-permute-start(bf16[32,2176]{1,0:T(8,128)(2,1)S(1)} %get-tuple-element.101), channel_id=1, source_target_pairs={{0,2},{1,3},{2,0},{3,1},{4,6},{5,7},{6,4},{7,5},{8,10},{9,11},{10,... | collective-permute-start | bytes 417800 | tf_op jit(solution)/shard_map/ppermute | solution.py:472
  42.8 3.1 %weight_grads.2 = (bf16[384,4096]{1,0:T(8,128)(2,1)}, bf16[384,4096]{1,0:T(8,128)(2,1)}) custom-call(bf16[384,256]{1,0:T(8,128)(2,1)S(1)} %get-tuple-element.104.refs_0_, bf16[384,256]{1,0:T(8,128)(2,1)S(1)} %get-tuple-element.105.refs_1_, bf16[256,2048]{1,0:T(8,128)(2,1)S(1)} %get-tuple-element.106.refs_2_), custom_call_target="tpu_custom_call" | custom-call | flops 1000000 | bytes 10000 | tf_op jit(solution)/shard_map/weight_grads/pallas_call | solution.py:419
  45.8 1.4 %collective-permute-done.16.right = bf16[32,2176]{1,0:T(8,128)(2,1)S(1)} collective-permute-done((bf16[32,2176]{1,0:T(8,128)(2,1)S(1)}, bf16[32,2176]{1,0:T(8,128)(2,1)S(1)}, u32[]{:S(2)}, u32[]{:S(2)}) %collective-permute-start.16) | collective-permute-done | bytes 139296 | tf_op jit(solution)/shard_map/ppermute | solution.py:472
  47.3 1.6 %collective-permute-start.17 = (bf16[32,2176]{1,0:T(8,128)(2,1)S(1)}, bf16[32,2176]{1,0:T(8,128)(2,1)S(1)}, u32[]{:S(2)}, u32[]{:S(2)}) collective-permute-start(bf16[32,2176]{1,0:T(8,128)(2,1)S(1)} %add_rows.3), channel_id=1, source_target_pairs={{0,4},{4,0},{8,12},{12,8},{16,20},{20,16},{24,28},{28,24},{1,5},{5... | collective-permute-start | bytes 417800 | tf_op jit(solution)/shard_map/ppermute | solution.py:472
  49.5 2.0 %weight_grads.3 = bf16[384,4096]{1,0:T(8,128)(2,1)} custom-call(bf16[384,256]{1,0:T(8,128)(2,1)S(1)} %get-tuple-element.110.refs_10_.refs_0_, bf16[256,2048]{1,0:T(8,128)(2,1)S(1)} %get-tuple-element.111.refs_1_), custom_call_target="tpu_custom_call" | custom-call | flops 1000000 | bytes 10000 | tf_op jit(solution)/shard_map/weight_grads/pallas_call | solution.py:419
  52.5 1.6 %collective-permute-start.18 = (bf16[16,2176]{1,0:T(8,128)(2,1)S(1)}, bf16[16,2176]{1,0:T(8,128)(2,1)S(1)}, u32[]{:S(2)}, u32[]{:S(2)}) collective-permute-start(bf16[16,2176]{1,0:T(8,128)(2,1)S(1)} %get-tuple-element.114), channel_id=1, source_target_pairs={{0,16},{4,20},{8,24},{12,28},{16,0},{20,4},{24,8},{28,12},{1,17},{... | collective-permute-start | bytes 208904 | tf_op jit(solution)/shard_map/ppermute | solution.py:472
  54.1 1.7 %collective-permute-start.19 = (bf16[16,2176]{1,0:T(8,128)(2,1)S(1)}, bf16[16,2176]{1,0:T(8,128)(2,1)S(1)}, u32[]{:S(2)}, u32[]{:S(2)}) collective-permute-start(bf16[16,2176]{1,0:T(8,128)(2,1)S(1)} %get-tuple-element.115), channel_id=1, source_target_pairs={{0,24},{4,28},{8,16},{12,20},{16,8},{20,12},{24,0},{28,4},{1,25},{... | collective-permute-start | bytes 208904 | tf_op jit(solution)/shard_map/ppermute | solution.py:472
  56.0 3.1 %collective-permute-done.18.refs_0_ = bf16[16,2176]{1,0:T(8,128)(2,1)S(1)} collective-permute-done((bf16[16,2176]{1,0:T(8,128)(2,1)S(1)}, bf16[16,2176]{1,0:T(8,128)(2,1)S(1)}, u32[]{:S(2)}, u32[]{:S(2)}) %collective-permute-start.18) | collective-permute-done | bytes 69664 | tf_op jit(solution)/shard_map/ppermute | solution.py:472
  59.2 1.2 %collective-permute-done.19.refs_1_ = bf16[16,2176]{1,0:T(8,128)(2,1)S(1)} collective-permute-done((bf16[16,2176]{1,0:T(8,128)(2,1)S(1)}, bf16[16,2176]{1,0:T(8,128)(2,1)S(1)}, u32[]{:S(2)}, u32[]{:S(2)}) %collective-permute-start.19) | collective-permute-done | bytes 69664 | tf_op jit(solution)/shard_map/ppermute | solution.py:472
  60.8 1.0 %combine.1 = (bf16[32,4096]{1,0:T(8,128)(2,1)}, f32[8,32]{1,0:T(8,128)}) custom-call(bf16[64,32]{1,0:T(8,128)(2,1)S(1)} %get-tuple-element.76.first, bf16[64,32]{1,0:T(8,128)(2,1)S(1)} %get-tuple-element.77.second, s32[64,32]{1,0:T(8,128)S(1)} %get-tuple-element.78.choice_ref, bf16[8,32]{1,0:T(8,128)(2,1)S(1)} %bitcast.21, ...), custom_call_target="tpu_custom_call" | custom-call | tf_op jit(solution)/shard_map/combine/pallas_call | solution.py:458
  (45 shorter events, 9.0 us)
Async XLA Ops:
  3.0 10.9 %collective-permute-start = (bf16[8,4096]{1,0:T(8,128)(2,1)}, bf16[8,4096]{1,0:T(8,128)(2,1)S(1)}, u32[]{:S(2)}, u32[]{:S(2)}) collective-permute-start(bf16[8,4096]{1,0:T(8,128)(2,1)} %get-tuple-element.64), channel_id=1, source_target_pairs={{0,20},{4,16},{8,28},{12,24},{16,4},{20,0},{24,12},{28,8},{1,21},{... | collective-permute-start | bytes 196616 | tf_op jit(solution)/shard_map/ppermute | solution.py:472
  8.0 9.1 %collective-permute-start.1 = (bf16[8,4096]{1,0:T(8,128)(2,1)}, bf16[8,4096]{1,0:T(8,128)(2,1)S(1)}, u32[]{:S(2)}, u32[]{:S(2)}) collective-permute-start(bf16[8,4096]{1,0:T(8,128)(2,1)} %get-tuple-element.65), channel_id=1, source_target_pairs={{0,28},{4,24},{8,20},{12,16},{16,12},{20,8},{24,4},{28,0},{1,29},{... | collective-permute-start | bytes 196616 | tf_op jit(solution)/shard_map/ppermute | solution.py:472
  9.3 7.8 %collective-permute-start.2 = (bf16[8,4096]{1,0:T(8,128)(2,1)}, bf16[8,4096]{1,0:T(8,128)(2,1)S(1)}, u32[]{:S(2)}, u32[]{:S(2)}) collective-permute-start(bf16[8,4096]{1,0:T(8,128)(2,1)} %get-tuple-element.66), channel_id=1, source_target_pairs={{0,12},{4,8},{8,4},{12,0},{16,28},{20,24},{24,20},{28,16},{1,13},{... | collective-permute-start | bytes 196616 | tf_op jit(solution)/shard_map/ppermute | solution.py:472
  9.8 7.3 %collective-permute-start.3 = (bf16[8,4096]{1,0:T(8,128)(2,1)}, bf16[8,4096]{1,0:T(8,128)(2,1)S(1)}, u32[]{:S(2)}, u32[]{:S(2)}) collective-permute-start(bf16[8,4096]{1,0:T(8,128)(2,1)} %get-tuple-element.67), channel_id=1, source_target_pairs={{0,4},{4,0},{8,12},{12,8},{16,20},{20,16},{24,28},{28,24},{1,5},{5... | collective-permute-start | bytes 196616 | tf_op jit(solution)/shard_map/ppermute | solution.py:472
  11.1 8.9 %collective-permute-start.4 = (bf16[8,4096]{1,0:T(8,128)(2,1)}, bf16[8,4096]{1,0:T(8,128)(2,1)S(1)}, u32[]{:S(2)}, u32[]{:S(2)}) collective-permute-start(bf16[8,4096]{1,0:T(8,128)(2,1)} %get-tuple-element.72), channel_id=1, source_target_pairs={{0,16},{4,20},{8,24},{12,28},{16,0},{20,4},{24,8},{28,12},{1,17},{... | collective-permute-start | bytes 196616 | tf_op jit(solution)/shard_map/ppermute | solution.py:472
  13.8 6.7 %collective-permute-start.5 = (bf16[8,4096]{1,0:T(8,128)(2,1)}, bf16[8,4096]{1,0:T(8,128)(2,1)S(1)}, u32[]{:S(2)}, u32[]{:S(2)}) collective-permute-start(bf16[8,4096]{1,0:T(8,128)(2,1)} %get-tuple-element.73), channel_id=1, source_target_pairs={{0,24},{4,28},{8,16},{12,20},{16,8},{20,12},{24,0},{28,4},{1,25},{... | collective-permute-start | bytes 196616 | tf_op jit(solution)/shard_map/ppermute | solution.py:472
  17.1 4.5 %collective-permute-start.6 = (bf16[8,4096]{1,0:T(8,128)(2,1)}, bf16[8,4096]{1,0:T(8,128)(2,1)S(1)}, u32[]{:S(2)}, u32[]{:S(2)}) collective-permute-start(bf16[8,4096]{1,0:T(8,128)(2,1)} %get-tuple-element.74), channel_id=1, source_target_pairs={{0,8},{4,12},{8,0},{12,4},{16,24},{20,28},{24,16},{28,20},{1,9},{5... | collective-permute-start | bytes 196616 | tf_op jit(solution)/shard_map/ppermute | solution.py:472
  17.2 14.8 %copy-start = (bf16[1,384,4096]{2,1,0:T(8,128)(2,1)S(1)}, bf16[1,384,4096]{2,1,0:T(8,128)(2,1)}, u32[]{:S(2)}) copy-start(bf16[1,384,4096]{2,1,0:T(8,128)(2,1)} %param.11) | copy-start | bytes 9437188
  17.2 14.8 %copy-start.1 = (bf16[1,384,4096]{2,1,0:T(8,128)(2,1)S(1)}, bf16[1,384,4096]{2,1,0:T(8,128)(2,1)}, u32[]{:S(2)}) copy-start(bf16[1,384,4096]{2,1,0:T(8,128)(2,1)} %param.12) | copy-start | bytes 9437188
  17.3 6.5 %collective-permute-start.7 = (bf16[32,4096]{1,0:T(8,128)(2,1)S(1)}, bf16[32,4096]{1,0:T(8,128)(2,1)S(1)}, u32[]{:S(2)}, u32[]{:S(2)}) collective-permute-start(bf16[32,4096]{1,0:T(8,128)(2,1)S(1)} %pack.2.refs_0_), channel_id=1, source_target_pairs={{0,2},{1,3},{2,0},{3,1},{4,6},{5,7},{6,4},{7,5},{8,10},{9,11},{10,... | collective-permute-start | bytes 786440 | tf_op jit(solution)/shard_map/ppermute | solution.py:472
  21.7 2.1 %collective-permute-start.11 = (bf16[32,4096]{1,0:T(8,128)(2,1)S(1)}, bf16[32,4096]{1,0:T(8,128)(2,1)S(1)}, u32[]{:S(2)}, u32[]{:S(2)}) collective-permute-start(bf16[32,4096]{1,0:T(8,128)(2,1)S(1)} %pack.3.refs_1_), channel_id=1, source_target_pairs={{0,1},{1,0},{2,3},{3,2},{4,5},{5,4},{6,7},{7,6},{8,9},{9,8},{10,11... | collective-permute-start | bytes 786440 | tf_op jit(solution)/shard_map/ppermute | solution.py:472
  21.8 8.7 %collective-permute-start.8 = (bf16[32,4096]{1,0:T(8,128)(2,1)S(1)}, bf16[32,4096]{1,0:T(8,128)(2,1)S(1)}, u32[]{:S(2)}, u32[]{:S(2)}) collective-permute-start(bf16[32,4096]{1,0:T(8,128)(2,1)S(1)} %pack.3.refs_1_), channel_id=1, source_target_pairs={{0,2},{1,3},{2,0},{3,1},{4,6},{5,7},{6,4},{7,5},{8,10},{9,11},{10,... | collective-permute-start | bytes 786440 | tf_op jit(solution)/shard_map/ppermute | solution.py:472
  23.3 7.2 %collective-permute-start.9 = (bf16[32,4096]{1,0:T(8,128)(2,1)S(1)}, bf16[32,4096]{1,0:T(8,128)(2,1)S(1)}, u32[]{:S(2)}, u32[]{:S(2)}) collective-permute-start(bf16[32,4096]{1,0:T(8,128)(2,1)S(1)} %pack.2.refs_0_), channel_id=1, source_target_pairs={{0,1},{1,0},{2,3},{3,2},{4,5},{5,4},{6,7},{7,6},{8,9},{9,8},{10,11... | collective-permute-start | bytes 786440 | tf_op jit(solution)/shard_map/ppermute | solution.py:472
  23.8 6.7 %collective-permute-start.10 = (bf16[32,4096]{1,0:T(8,128)(2,1)S(1)}, bf16[32,4096]{1,0:T(8,128)(2,1)S(1)}, u32[]{:S(2)}, u32[]{:S(2)}) collective-permute-start(bf16[32,4096]{1,0:T(8,128)(2,1)S(1)} %collective-permute-done.7.refs_2_), channel_id=1, source_target_pairs={{0,1},{1,0},{2,3},{3,2},{4,5},{5,4},{6,7},{7,6},{8,9},{9,8},{10,11... | collective-permute-start | bytes 786440 | tf_op jit(solution)/shard_map/ppermute | solution.py:472
  30.5 1.5 %collective-permute-start.12 = (bf16[32,4096]{1,0:T(8,128)(2,1)S(1)}, bf16[32,4096]{1,0:T(8,128)(2,1)S(1)}, u32[]{:S(2)}, u32[]{:S(2)}) collective-permute-start(bf16[32,4096]{1,0:T(8,128)(2,1)S(1)} %collective-permute-done.8.refs_3_), channel_id=1, source_target_pairs={{0,1},{1,0},{2,3},{3,2},{4,5},{5,4},{6,7},{7,6},{8,9},{9,8},{10,11... | collective-permute-start | bytes 786440 | tf_op jit(solution)/shard_map/ppermute | solution.py:472
  36.6 1.6 %collective-permute-start.13 = (bf16[128,1024]{1,0:T(8,128)(2,1)S(1)}, bf16[128,1024]{1,0:T(8,128)(2,1)S(1)}, u32[]{:S(2)}, u32[]{:S(2)}) collective-permute-start(bf16[128,1024]{1,0:T(8,128)(2,1)S(1)} %get-tuple-element.93), channel_id=1, source_target_pairs={{0,1},{1,0},{2,3},{3,2},{4,5},{5,4},{6,7},{7,6},{8,9},{9,8},{10,11... | collective-permute-start | bytes 786440 | tf_op jit(solution)/shard_map/ppermute | solution.py:472
  38.2 1.6 %collective-permute-start.14 = (bf16[128,1152]{1,0:T(8,128)(2,1)S(1)}, bf16[128,1152]{1,0:T(8,128)(2,1)S(1)}, u32[]{:S(2)}, u32[]{:S(2)}) collective-permute-start(bf16[128,1152]{1,0:T(8,128)(2,1)S(1)} %far_rows.1), channel_id=1, source_target_pairs={{0,1},{1,0},{2,3},{3,2},{4,5},{5,4},{6,7},{7,6},{8,9},{9,8},{10,11... | collective-permute-start | bytes 884744 | tf_op jit(solution)/shard_map/ppermute | solution.py:472
  40.7 6.6 %collective-permute-start.16 = (bf16[32,2176]{1,0:T(8,128)(2,1)S(1)}, bf16[32,2176]{1,0:T(8,128)(2,1)S(1)}, u32[]{:S(2)}, u32[]{:S(2)}) collective-permute-start(bf16[32,2176]{1,0:T(8,128)(2,1)S(1)} %get-tuple-element.101), channel_id=1, source_target_pairs={{0,2},{1,3},{2,0},{3,1},{4,6},{5,7},{6,4},{7,5},{8,10},{9,11},{10,... | collective-permute-start | bytes 417800 | tf_op jit(solution)/shard_map/ppermute | solution.py:472
  42.3 7.2 %collective-permute-start.15 = (bf16[32,2176]{1,0:T(8,128)(2,1)S(1)}, bf16[32,2176]{1,0:T(8,128)(2,1)S(1)}, u32[]{:S(2)}, u32[]{:S(2)}) collective-permute-start(bf16[32,2176]{1,0:T(8,128)(2,1)S(1)} %get-tuple-element.99), channel_id=1, source_target_pairs={{0,2},{1,3},{2,0},{3,1},{4,6},{5,7},{6,4},{7,5},{8,10},{9,11},{10,... | collective-permute-start | bytes 417800 | tf_op jit(solution)/shard_map/ppermute | solution.py:472
  42.8 18.0 %copy-start.4 = (bf16[32,8]{0,1:T(8,128)(2,1)S(1)}, bf16[32,8]{0,1:T(8,128)(2,1)}, u32[]{:S(2)}) copy-start(bf16[32,8]{0,1:T(8,128)(2,1)} %param.9) | copy-start | bytes 1540
  47.3 5.1 %collective-permute-start.17 = (bf16[32,2176]{1,0:T(8,128)(2,1)S(1)}, bf16[32,2176]{1,0:T(8,128)(2,1)S(1)}, u32[]{:S(2)}, u32[]{:S(2)}) collective-permute-start(bf16[32,2176]{1,0:T(8,128)(2,1)S(1)} %add_rows.3), channel_id=1, source_target_pairs={{0,4},{4,0},{8,12},{12,8},{16,20},{20,16},{24,28},{28,24},{1,5},{5... | collective-permute-start | bytes 417800 | tf_op jit(solution)/shard_map/ppermute | solution.py:472
  52.5 6.7 %collective-permute-start.18 = (bf16[16,2176]{1,0:T(8,128)(2,1)S(1)}, bf16[16,2176]{1,0:T(8,128)(2,1)S(1)}, u32[]{:S(2)}, u32[]{:S(2)}) collective-permute-start(bf16[16,2176]{1,0:T(8,128)(2,1)S(1)} %get-tuple-element.114), channel_id=1, source_target_pairs={{0,16},{4,20},{8,24},{12,28},{16,0},{20,4},{24,8},{28,12},{1,17},{... | collective-permute-start | bytes 208904 | tf_op jit(solution)/shard_map/ppermute | solution.py:472
  54.1 6.3 %collective-permute-start.19 = (bf16[16,2176]{1,0:T(8,128)(2,1)S(1)}, bf16[16,2176]{1,0:T(8,128)(2,1)S(1)}, u32[]{:S(2)}, u32[]{:S(2)}) collective-permute-start(bf16[16,2176]{1,0:T(8,128)(2,1)S(1)} %get-tuple-element.115), channel_id=1, source_target_pairs={{0,24},{4,28},{8,16},{12,20},{16,8},{20,12},{24,0},{28,4},{1,25},{... | collective-permute-start | bytes 208904 | tf_op jit(solution)/shard_map/ppermute | solution.py:472
  55.7 5.1 %collective-permute-start.20 = (bf16[16,2176]{1,0:T(8,128)(2,1)S(1)}, bf16[16,2176]{1,0:T(8,128)(2,1)S(1)}, u32[]{:S(2)}, u32[]{:S(2)}) collective-permute-start(bf16[16,2176]{1,0:T(8,128)(2,1)S(1)} %get-tuple-element.116), channel_id=1, source_target_pairs={{0,8},{4,12},{8,0},{12,4},{16,24},{20,28},{24,16},{28,20},{1,9},{5... | collective-permute-start | bytes 208904 | tf_op jit(solution)/shard_map/ppermute | solution.py:472
  (3 other events, 7.4 us)

commit v9 on v8

--- a/solution.py
+++ b/solution.py
@@ -473,7 +473,9 @@
 
 
 def offsets(count):
-    even = list(range(count // 2, count, 2)) + list(range(count // 2 - 2, -1, -2))
+    even = []
+    for k in range(0, count // 2, 2):
+        even += [k, k + count // 2]
     return [k ^ 1 for k in even], even
 
 
@@ -505,15 +507,25 @@
     early = pack(arrived[:middle])
     ids_after, _ = tie((ids, early))
     table, late = tie((placement(n_targets, ids_after), arrived[middle:]))
-    held = [cross(group, far_bits) for group in (early, pack(late))]
-    near = sorted(held[0])
-    others = [{mask: flip(held[0][mask], "dp", 1) for mask in near}]
-    others.append({0: flip(held[1][0], "dp", 1)})
-    far_late = {mask: held[1][mask] for mask in near[1:]}
-    others, far_late = tie((others, far_late))
-    for mask in far_late:
-        others[1][mask] = flip(far_late[mask], "dp", 1)
-    pieces = [group[mask] for groups in (held, others) for mask in near for group in groups]
+    late = pack(late)
+    early_near, late_near = (cross(value, far_bits) for value in (early, late))
+    near = sorted(early_near)
+    crossed = {mask: early_near[mask] for mask in near[1:]}
+    early, late, crossed = tie((early, late, crossed))
+    early_far = {0: flip(early, "dp", 1)}
+    for mask, value in crossed.items():
+        early_far[mask] = flip(value, "dp", 1)
+    late_far = {0: flip(late, "dp", 1)}
+    crossed = {mask: late_near[mask] for mask in near[1:]}
+    early_far, late_far, crossed = tie((early_far, late_far, crossed))
+    for mask, value in crossed.items():
+        late_far[mask] = flip(value, "dp", 1)
+    pieces = [
+        group[mask]
+        for groups in ((early_near, late_near), (early_far, late_far))
+        for mask in near
+        for group in groups
+    ]
     token_halves, activated, slope, hidden = forward(pieces, weights[0], weights[1])
     part, grad_halves, gate_f, up_f, low, high, gate_column = backward(
         pieces, activated, slope, hidden, weights
@@ -545,7 +557,9 @@
     passed = add_rows(*sums[0])
     hidden, _ = tie((hidden, passed))
     (grad_down,) = weight_grads((hidden,), grad_halves)
-    kept, passed, grad_down = tie((add_rows(*sums[1]), flip(passed, "expert", 1), grad_down))
+    passed = flip(passed, "expert", 1)
+    kept, moved, grad_down = tie((*sums[1], grad_down))
+    kept, passed = tie((add_rows(kept, moved), passed))
     returned = exchange(merge_rows(kept, passed), even)
     token_grad, gate_grad = combine(table, gates, returned, width)
     grads = (grad_gate, grad_up, grad_down)

time: 62 us -> 62.3 us (level)
  starting transfers between devices: 25.1 us -> 27.5 us
  waiting for transfers between devices: 18.8 us -> 16.7 us
    ppermute x21, starting transfers between devices: 25.1 us -> 27.5 us  [flip(): return lax.ppermute(value, axis, [(i, i ^ bit) for i in range(size)])]
    ppermute x21, waiting for transfers between devices: 18.8 us -> 16.7 us  [flip(): return lax.ppermute(value, axis, [(i, i ^ bit) for i in range(size)])]
  transfers between devices with their start and end apart: 21 -> 21, of which waited for: 13 -> 10; matrix products, arithmetic and copies ran while one was open for 0% -> 0% of each run, Pallas kernels for 12% -> 12%
where the time goes in v9:
time: 62.3 us; the launch traced here: 62 us
  starting transfers between devices  27.5 us (44%)
  waiting for transfers between devices  16.7 us (27%)
  Pallas kernels  16 us (26%)
  local copies, waits for them, and re-layouts  1.01 us (2%)
  between operations  0.83 us (1%)
    ppermute x21, starting transfers between devices, flip(): return lax.ppermute(value, axis, [(i, i ^ bit) for i in range(size)])  27.5 us
    ppermute x21, waiting for transfers between devices, flip(): return lax.ppermute(value, axis, [(i, i ^ bit) for i in range(size)])  16.7 us
    pallas_call x2, Pallas kernels, weight_grads(): pl.pallas_call(functools.partial(weight_kernel, chunk, count), out_shape=...  5.05 us
    pallas_call x1, Pallas kernels, backward(): pl.pallas_call(functools.partial(backward_kernel, count), out_shape=[stru...  2.55 us
    pallas_call x1, Pallas kernels, dispatch(): pl.pallas_call(functools.partial(dispatch_kernel, n_targets), out_shape=[...  2.34 us
    pallas_call x1, Pallas kernels, forward(): pl.pallas_call(functools.partial(forward_kernel, count), out_shape=[struc...  1.95 us
  transfers between devices with their start and end apart: 21, of which 10 were waited for; matrix products, arithmetic and copies ran while one was open for 0% of the time, Pallas kernels for 12%

profile of v9, /device:TPU:0, one launch (start us, length us, event | category | flops | bytes accessed | tf_op | source)
XLA Modules:
  0.0 62.0 jit_solution(9722869140104397169)
XLA Ops:
  0.6 2.3 %dispatch.1 = (bf16[8,4096]{1,0:T(8,128)(2,1)}, bf16[8,4096]{1,0:T(8,128)(2,1)}, bf16[8,4096]{1,0:T(8,128)(2,1)}, bf16[8,4096]{1,0:T(8,128)(2,1)}, bf16[8,4096]{...) custom-call(s32[8,32]{1,0:T(8,128)} %bitcast.22, ...), custom_call_target="tpu_custom_call" | custom-call | tf_op jit(solution)/shard_map/dispatch/pallas_call | solution.py:92
  3.0 3.0 %collective-permute-start = (bf16[8,4096]{1,0:T(8,128)(2,1)}, bf16[8,4096]{1,0:T(8,128)(2,1)S(1)}, u32[]{:S(2)}, u32[]{:S(2)}) collective-permute-start(bf16[8,4096]{1,0:T(8,128)(2,1)} %get-tuple-element.69), channel_id=1, source_target_pairs={{0,4},{4,0},{8,12},{12,8},{16,20},{20,16},{24,28},{28,24},{1,5},{5... | collective-permute-start | bytes 196616 | tf_op jit(solution)/shard_map/ppermute | solution.py:472
  6.0 2.5 %collective-permute-start.1 = (bf16[8,4096]{1,0:T(8,128)(2,1)}, bf16[8,4096]{1,0:T(8,128)(2,1)S(1)}, u32[]{:S(2)}, u32[]{:S(2)}) collective-permute-start(bf16[8,4096]{1,0:T(8,128)(2,1)} %get-tuple-element.70), channel_id=1, source_target_pairs={{0,20},{4,16},{8,28},{12,24},{16,4},{20,0},{24,12},{28,8},{1,21},{... | collective-permute-start | bytes 196616 | tf_op jit(solution)/shard_map/ppermute | solution.py:472
  8.5 2.5 %collective-permute-start.2 = (bf16[8,4096]{1,0:T(8,128)(2,1)}, bf16[8,4096]{1,0:T(8,128)(2,1)S(1)}, u32[]{:S(2)}, u32[]{:S(2)}) collective-permute-start(bf16[8,4096]{1,0:T(8,128)(2,1)} %get-tuple-element.71), channel_id=1, source_target_pairs={{0,12},{4,8},{8,4},{12,0},{16,28},{20,24},{24,20},{28,16},{1,13},{... | collective-permute-start | bytes 196616 | tf_op jit(solution)/shard_map/ppermute | solution.py:472
  11.1 1.9 %collective-permute-start.4 = (bf16[8,4096]{1,0:T(8,128)(2,1)}, bf16[8,4096]{1,0:T(8,128)(2,1)S(1)}, u32[]{:S(2)}, u32[]{:S(2)}) collective-permute-start(bf16[8,4096]{1,0:T(8,128)(2,1)} %get-tuple-element.78), channel_id=1, source_target_pairs={{0,16},{4,20},{8,24},{12,28},{16,0},{20,4},{24,8},{28,12},{1,17},{... | collective-permute-start | bytes 196616 | tf_op jit(solution)/shard_map/ppermute | solution.py:472
  12.9 2.5 %collective-permute-start.5 = (bf16[8,4096]{1,0:T(8,128)(2,1)}, bf16[8,4096]{1,0:T(8,128)(2,1)S(1)}, u32[]{:S(2)}, u32[]{:S(2)}) collective-permute-start(bf16[8,4096]{1,0:T(8,128)(2,1)} %get-tuple-element.79), channel_id=1, source_target_pairs={{0,8},{4,12},{8,0},{12,4},{16,24},{20,28},{24,16},{28,20},{1,9},{5... | collective-permute-start | bytes 196616 | tf_op jit(solution)/shard_map/ppermute | solution.py:472
  15.4 4.0 %collective-permute-start.6 = (bf16[8,4096]{1,0:T(8,128)(2,1)}, bf16[8,4096]{1,0:T(8,128)(2,1)S(1)}, u32[]{:S(2)}, u32[]{:S(2)}) collective-permute-start(bf16[8,4096]{1,0:T(8,128)(2,1)} %get-tuple-element.80), channel_id=1, source_target_pairs={{0,24},{4,28},{8,16},{12,20},{16,8},{20,12},{24,0},{28,4},{1,25},{... | collective-permute-start | bytes 196616 | tf_op jit(solution)/shard_map/ppermute | solution.py:472
  19.5 1.6 %collective-permute-start.7 = (bf16[32,4096]{1,0:T(8,128)(2,1)S(1)}, bf16[32,4096]{1,0:T(8,128)(2,1)S(1)}, u32[]{:S(2)}, u32[]{:S(2)}) collective-permute-start(bf16[32,4096]{1,0:T(8,128)(2,1)S(1)} %pack.2.refs_0_), channel_id=1, source_target_pairs={{0,2},{1,3},{2,0},{3,1},{4,6},{5,7},{6,4},{7,5},{8,10},{9,11},{10,... | collective-permute-start | bytes 786440 | tf_op jit(solution)/shard_map/ppermute | solution.py:472
  21.0 1.0 %copy-done.5 = s32[32,8]{0,1:T(8,128)S(1)} copy-done((s32[32,8]{0,1:T(8,128)S(1)}, s32[32,8]{0,1:T(8,128)}, u32[]{:S(2)}) %copy-start.5) | copy-done | bytes 1048
  22.3 1.1 %collective-permute-start.8 = (bf16[32,4096]{1,0:T(8,128)(2,1)S(1)}, bf16[32,4096]{1,0:T(8,128)(2,1)S(1)}, u32[]{:S(2)}, u32[]{:S(2)}) collective-permute-start(bf16[32,4096]{1,0:T(8,128)(2,1)S(1)} %pack.3.refs_1_), channel_id=1, source_target_pairs={{0,2},{1,3},{2,0},{3,1},{4,6},{5,7},{6,4},{7,5},{8,10},{9,11},{10,... | collective-permute-start | bytes 786440 | tf_op jit(solution)/shard_map/ppermute | solution.py:472
  23.5 4.3 %collective-permute-done.7.refs_2_ = bf16[32,4096]{1,0:T(8,128)(2,1)S(1)} collective-permute-done((bf16[32,4096]{1,0:T(8,128)(2,1)S(1)}, bf16[32,4096]{1,0:T(8,128)(2,1)S(1)}, u32[]{:S(2)}, u32[]{:S(2)}) %collective-permute-start.7) | collective-permute-done | bytes 262176 | tf_op jit(solution)/shard_map/ppermute | solution.py:472
  28.2 2.3 %collective-permute-done.8.refs_3_ = bf16[32,4096]{1,0:T(8,128)(2,1)S(1)} collective-permute-done((bf16[32,4096]{1,0:T(8,128)(2,1)S(1)}, bf16[32,4096]{1,0:T(8,128)(2,1)S(1)}, u32[]{:S(2)}, u32[]{:S(2)}) %collective-permute-start.8) | collective-permute-done | bytes 262176 | tf_op jit(solution)/shard_map/ppermute | solution.py:472
  30.6 1.5 %collective-permute-done.12.refs_7_ = bf16[32,4096]{1,0:T(8,128)(2,1)S(1)} collective-permute-done((bf16[32,4096]{1,0:T(8,128)(2,1)S(1)}, bf16[32,4096]{1,0:T(8,128)(2,1)S(1)}, u32[]{:S(2)}, u32[]{:S(2)}) %collective-permute-start.12) | collective-permute-done | bytes 262176 | tf_op jit(solution)/shard_map/ppermute | solution.py:472
  32.1 2.0 %forward.1 = (bf16[256,2048]{1,0:T(8,128)(2,1)S(1)}, f32[384,256]{1,0:T(8,128)S(1)}, f32[384,256]{1,0:T(8,128)S(1)}, bf16[384,256]{1,0:T(8,128)(2,1)S(1)}) custom-call(bf16[32,4096]{1,0:T(8,128)(2,1)S(1)} %pack.2.refs_0_, bf16[32,4096]{1,0:T(8,128)(2,1)S(1)} %pack.3.refs_1_, bf16[32,4096]{1,0:T(8,128)(2,1)S(1)} %collective-permute-done.7.refs_2_, ...), custom_call_target="tpu_custom_call" | custom-call | flops 1000000 | bytes 10000 | tf_op jit(solution)/shard_map/forward/pallas_call | solution.py:189
  34.1 2.5 %backward.1 = (bf16[128,1024]{1,0:T(8,128)(2,1)S(1)}, bf16[256,2048]{1,0:T(8,128)(2,1)S(1)}, bf16[384,256]{1,0:T(8,128)(2,1)S(1)}, bf16[384,256]{1,0:T(8,128)(2,...) custom-call(bf16[32,4096]{1,0:T(8,128)(2,1)S(1)} %pack.2.refs_0_, ...), custom_call_target="tpu_custom_call" | custom-call | flops 1000000 | bytes 10000 | tf_op jit(solution)/shard_map/backward/pallas_call | solution.py:271
  40.8 1.6 %collective-permute-start.16 = (bf16[32,2176]{1,0:T(8,128)(2,1)S(1)}, bf16[32,2176]{1,0:T(8,128)(2,1)S(1)}, u32[]{:S(2)}, u32[]{:S(2)}) collective-permute-start(bf16[32,2176]{1,0:T(8,128)(2,1)S(1)} %get-tuple-element.109), channel_id=1, source_target_pairs={{0,2},{1,3},{2,0},{3,1},{4,6},{5,7},{6,4},{7,5},{8,10},{9,11},{10,... | collective-permute-start | bytes 417800 | tf_op jit(solution)/shard_map/ppermute | solution.py:472
  42.9 3.1 %weight_grads.2 = (bf16[384,4096]{1,0:T(8,128)(2,1)}, bf16[384,4096]{1,0:T(8,128)(2,1)}) custom-call(bf16[384,256]{1,0:T(8,128)(2,1)S(1)} %get-tuple-element.112.refs_0_, bf16[384,256]{1,0:T(8,128)(2,1)S(1)} %get-tuple-element.113.refs_1_, bf16[256,2048]{1,0:T(8,128)(2,1)S(1)} %get-tuple-element.114.refs_2_), custom_call_target="tpu_custom_call" | custom-call | flops 1000000 | bytes 10000 | tf_op jit(solution)/shard_map/weight_grads/pallas_call | solution.py:419
  46.0 1.4 %collective-permute-done.16.right = bf16[32,2176]{1,0:T(8,128)(2,1)S(1)} collective-permute-done((bf16[32,2176]{1,0:T(8,128)(2,1)S(1)}, bf16[32,2176]{1,0:T(8,128)(2,1)S(1)}, u32[]{:S(2)}, u32[]{:S(2)}) %collective-permute-start.16) | collective-permute-done | bytes 139296 | tf_op jit(solution)/shard_map/ppermute | solution.py:472
  48.4 2.0 %weight_grads.3 = bf16[384,4096]{1,0:T(8,128)(2,1)} custom-call(bf16[384,256]{1,0:T(8,128)(2,1)S(1)} %get-tuple-element.118.refs_10_.refs_0_, bf16[256,2048]{1,0:T(8,128)(2,1)S(1)} %get-tuple-element.119.refs_1_), custom_call_target="tpu_custom_call" | custom-call | flops 1000000 | bytes 10000 | tf_op jit(solution)/shard_map/weight_grads/pallas_call | solution.py:419
  50.4 2.1 %collective-permute-done.17.passed = bf16[32,2176]{1,0:T(8,128)(2,1)S(1)} collective-permute-done((bf16[32,2176]{1,0:T(8,128)(2,1)S(1)}, bf16[32,2176]{1,0:T(8,128)(2,1)S(1)}, u32[]{:S(2)}, u32[]{:S(2)}) %collective-permute-start.17) | collective-permute-done | bytes 139296 | tf_op jit(solution)/shard_map/ppermute | solution.py:472
  52.6 2.1 %collective-permute-start.18 = (bf16[16,2176]{1,0:T(8,128)(2,1)S(1)}, bf16[16,2176]{1,0:T(8,128)(2,1)S(1)}, u32[]{:S(2)}, u32[]{:S(2)}) collective-permute-start(bf16[16,2176]{1,0:T(8,128)(2,1)S(1)} %get-tuple-element.125), channel_id=1, source_target_pairs={{0,16},{4,20},{8,24},{12,28},{16,0},{20,4},{24,8},{28,12},{1,17},{... | collective-permute-start | bytes 208904 | tf_op jit(solution)/shard_map/ppermute | solution.py:472
  54.9 2.2 %collective-permute-start.20 = (bf16[16,2176]{1,0:T(8,128)(2,1)S(1)}, bf16[16,2176]{1,0:T(8,128)(2,1)S(1)}, u32[]{:S(2)}, u32[]{:S(2)}) collective-permute-start(bf16[16,2176]{1,0:T(8,128)(2,1)S(1)} %get-tuple-element.127), channel_id=1, source_target_pairs={{0,24},{4,28},{8,16},{12,20},{16,8},{20,12},{24,0},{28,4},{1,25},{... | collective-permute-start | bytes 208904 | tf_op jit(solution)/shard_map/ppermute | solution.py:472
  57.0 1.7 %collective-permute-done.18.refs_1_ = bf16[16,2176]{1,0:T(8,128)(2,1)S(1)} collective-permute-done((bf16[16,2176]{1,0:T(8,128)(2,1)S(1)}, bf16[16,2176]{1,0:T(8,128)(2,1)S(1)}, u32[]{:S(2)}, u32[]{:S(2)}) %collective-permute-start.18) | collective-permute-done | bytes 69664 | tf_op jit(solution)/shard_map/ppermute | solution.py:472
  59.3 1.8 %collective-permute-done.20.refs_3_ = bf16[16,2176]{1,0:T(8,128)(2,1)S(1)} collective-permute-done((bf16[16,2176]{1,0:T(8,128)(2,1)S(1)}, bf16[16,2176]{1,0:T(8,128)(2,1)S(1)}, u32[]{:S(2)}, u32[]{:S(2)}) %collective-permute-start.20) | collective-permute-done | bytes 69664 | tf_op jit(solution)/shard_map/ppermute | solution.py:472
  (45 shorter events, 8.3 us)
Async XLA Ops:
  3.0 10.0 %collective-permute-start = (bf16[8,4096]{1,0:T(8,128)(2,1)}, bf16[8,4096]{1,0:T(8,128)(2,1)S(1)}, u32[]{:S(2)}, u32[]{:S(2)}) collective-permute-start(bf16[8,4096]{1,0:T(8,128)(2,1)} %get-tuple-element.69), channel_id=1, source_target_pairs={{0,4},{4,0},{8,12},{12,8},{16,20},{20,16},{24,28},{28,24},{1,5},{5... | collective-permute-start | bytes 196616 | tf_op jit(solution)/shard_map/ppermute | solution.py:472
  6.0 9.4 %collective-permute-start.1 = (bf16[8,4096]{1,0:T(8,128)(2,1)}, bf16[8,4096]{1,0:T(8,128)(2,1)S(1)}, u32[]{:S(2)}, u32[]{:S(2)}) collective-permute-start(bf16[8,4096]{1,0:T(8,128)(2,1)} %get-tuple-element.70), channel_id=1, source_target_pairs={{0,20},{4,16},{8,28},{12,24},{16,4},{20,0},{24,12},{28,8},{1,21},{... | collective-permute-start | bytes 196616 | tf_op jit(solution)/shard_map/ppermute | solution.py:472
  8.5 10.9 %collective-permute-start.2 = (bf16[8,4096]{1,0:T(8,128)(2,1)}, bf16[8,4096]{1,0:T(8,128)(2,1)S(1)}, u32[]{:S(2)}, u32[]{:S(2)}) collective-permute-start(bf16[8,4096]{1,0:T(8,128)(2,1)} %get-tuple-element.71), channel_id=1, source_target_pairs={{0,12},{4,8},{8,4},{12,0},{16,28},{20,24},{24,20},{28,16},{1,13},{... | collective-permute-start | bytes 196616 | tf_op jit(solution)/shard_map/ppermute | solution.py:472
  11.1 8.3 %collective-permute-start.3 = (bf16[8,4096]{1,0:T(8,128)(2,1)}, bf16[8,4096]{1,0:T(8,128)(2,1)S(1)}, u32[]{:S(2)}, u32[]{:S(2)}) collective-permute-start(bf16[8,4096]{1,0:T(8,128)(2,1)} %get-tuple-element.72), channel_id=1, source_target_pairs={{0,28},{4,24},{8,20},{12,16},{16,12},{20,8},{24,4},{28,0},{1,29},{... | collective-permute-start | bytes 196616 | tf_op jit(solution)/shard_map/ppermute | solution.py:472
  11.1 11.1 %collective-permute-start.4 = (bf16[8,4096]{1,0:T(8,128)(2,1)}, bf16[8,4096]{1,0:T(8,128)(2,1)S(1)}, u32[]{:S(2)}, u32[]{:S(2)}) collective-permute-start(bf16[8,4096]{1,0:T(8,128)(2,1)} %get-tuple-element.78), channel_id=1, source_target_pairs={{0,16},{4,20},{8,24},{12,28},{16,0},{20,4},{24,8},{28,12},{1,17},{... | collective-permute-start | bytes 196616 | tf_op jit(solution)/shard_map/ppermute | solution.py:472
  12.9 9.3 %collective-permute-start.5 = (bf16[8,4096]{1,0:T(8,128)(2,1)}, bf16[8,4096]{1,0:T(8,128)(2,1)S(1)}, u32[]{:S(2)}, u32[]{:S(2)}) collective-permute-start(bf16[8,4096]{1,0:T(8,128)(2,1)} %get-tuple-element.79), channel_id=1, source_target_pairs={{0,8},{4,12},{8,0},{12,4},{16,24},{20,28},{24,16},{28,20},{1,9},{5... | collective-permute-start | bytes 196616 | tf_op jit(solution)/shard_map/ppermute | solution.py:472
  15.4 6.8 %collective-permute-start.6 = (bf16[8,4096]{1,0:T(8,128)(2,1)}, bf16[8,4096]{1,0:T(8,128)(2,1)S(1)}, u32[]{:S(2)}, u32[]{:S(2)}) collective-permute-start(bf16[8,4096]{1,0:T(8,128)(2,1)} %get-tuple-element.80), channel_id=1, source_target_pairs={{0,24},{4,28},{8,16},{12,20},{16,8},{20,12},{24,0},{28,4},{1,25},{... | collective-permute-start | bytes 196616 | tf_op jit(solution)/shard_map/ppermute | solution.py:472
  19.5 12.7 %copy-start = (bf16[1,384,4096]{2,1,0:T(8,128)(2,1)S(1)}, bf16[1,384,4096]{2,1,0:T(8,128)(2,1)}, u32[]{:S(2)}) copy-start(bf16[1,384,4096]{2,1,0:T(8,128)(2,1)} %param.11) | copy-start | bytes 9437188
  19.5 12.7 %copy-start.1 = (bf16[1,384,4096]{2,1,0:T(8,128)(2,1)S(1)}, bf16[1,384,4096]{2,1,0:T(8,128)(2,1)}, u32[]{:S(2)}) copy-start(bf16[1,384,4096]{2,1,0:T(8,128)(2,1)} %param.12) | copy-start | bytes 9437188
  19.5 8.2 %collective-permute-start.7 = (bf16[32,4096]{1,0:T(8,128)(2,1)S(1)}, bf16[32,4096]{1,0:T(8,128)(2,1)S(1)}, u32[]{:S(2)}, u32[]{:S(2)}) collective-permute-start(bf16[32,4096]{1,0:T(8,128)(2,1)S(1)} %pack.2.refs_0_), channel_id=1, source_target_pairs={{0,2},{1,3},{2,0},{3,1},{4,6},{5,7},{6,4},{7,5},{8,10},{9,11},{10,... | collective-permute-start | bytes 786440 | tf_op jit(solution)/shard_map/ppermute | solution.py:472
  22.3 8.2 %collective-permute-start.8 = (bf16[32,4096]{1,0:T(8,128)(2,1)S(1)}, bf16[32,4096]{1,0:T(8,128)(2,1)S(1)}, u32[]{:S(2)}, u32[]{:S(2)}) collective-permute-start(bf16[32,4096]{1,0:T(8,128)(2,1)S(1)} %pack.3.refs_1_), channel_id=1, source_target_pairs={{0,2},{1,3},{2,0},{3,1},{4,6},{5,7},{6,4},{7,5},{8,10},{9,11},{10,... | collective-permute-start | bytes 786440 | tf_op jit(solution)/shard_map/ppermute | solution.py:472
  27.7 2.8 %collective-permute-start.9 = (bf16[32,4096]{1,0:T(8,128)(2,1)S(1)}, bf16[32,4096]{1,0:T(8,128)(2,1)S(1)}, u32[]{:S(2)}, u32[]{:S(2)}) collective-permute-start(bf16[32,4096]{1,0:T(8,128)(2,1)S(1)} %pack.2.refs_0_), channel_id=1, source_target_pairs={{0,1},{1,0},{2,3},{3,2},{4,5},{5,4},{6,7},{7,6},{8,9},{9,8},{10,11... | collective-permute-start | bytes 786440 | tf_op jit(solution)/shard_map/ppermute | solution.py:472
  27.7 2.8 %collective-permute-start.10 = (bf16[32,4096]{1,0:T(8,128)(2,1)S(1)}, bf16[32,4096]{1,0:T(8,128)(2,1)S(1)}, u32[]{:S(2)}, u32[]{:S(2)}) collective-permute-start(bf16[32,4096]{1,0:T(8,128)(2,1)S(1)} %collective-permute-done.7.refs_2_), channel_id=1, source_target_pairs={{0,1},{1,0},{2,3},{3,2},{4,5},{5,4},{6,7},{7,6},{8,9},{9,8},{10,11... | collective-permute-start | bytes 786440 | tf_op jit(solution)/shard_map/ppermute | solution.py:472
  28.2 2.3 %collective-permute-start.11 = (bf16[32,4096]{1,0:T(8,128)(2,1)S(1)}, bf16[32,4096]{1,0:T(8,128)(2,1)S(1)}, u32[]{:S(2)}, u32[]{:S(2)}) collective-permute-start(bf16[32,4096]{1,0:T(8,128)(2,1)S(1)} %pack.3.refs_1_), channel_id=1, source_target_pairs={{0,1},{1,0},{2,3},{3,2},{4,5},{5,4},{6,7},{7,6},{8,9},{9,8},{10,11... | collective-permute-start | bytes 786440 | tf_op jit(solution)/shard_map/ppermute | solution.py:472
  30.5 1.6 %collective-permute-start.12 = (bf16[32,4096]{1,0:T(8,128)(2,1)S(1)}, bf16[32,4096]{1,0:T(8,128)(2,1)S(1)}, u32[]{:S(2)}, u32[]{:S(2)}) collective-permute-start(bf16[32,4096]{1,0:T(8,128)(2,1)S(1)} %collective-permute-done.8.refs_3_), channel_id=1, source_target_pairs={{0,1},{1,0},{2,3},{3,2},{4,5},{5,4},{6,7},{7,6},{8,9},{9,8},{10,11... | collective-permute-start | bytes 786440 | tf_op jit(solution)/shard_map/ppermute | solution.py:472
  36.7 1.6 %collective-permute-start.13 = (bf16[128,1024]{1,0:T(8,128)(2,1)S(1)}, bf16[128,1024]{1,0:T(8,128)(2,1)S(1)}, u32[]{:S(2)}, u32[]{:S(2)}) collective-permute-start(bf16[128,1024]{1,0:T(8,128)(2,1)S(1)} %get-tuple-element.101), channel_id=1, source_target_pairs={{0,1},{1,0},{2,3},{3,2},{4,5},{5,4},{6,7},{7,6},{8,9},{9,8},{10,11... | collective-permute-start | bytes 786440 | tf_op jit(solution)/shard_map/ppermute | solution.py:472
  38.3 1.6 %collective-permute-start.14 = (bf16[128,1152]{1,0:T(8,128)(2,1)S(1)}, bf16[128,1152]{1,0:T(8,128)(2,1)S(1)}, u32[]{:S(2)}, u32[]{:S(2)}) collective-permute-start(bf16[128,1152]{1,0:T(8,128)(2,1)S(1)} %far_rows.1), channel_id=1, source_target_pairs={{0,1},{1,0},{2,3},{3,2},{4,5},{5,4},{6,7},{7,6},{8,9},{9,8},{10,11... | collective-permute-start | bytes 884744 | tf_op jit(solution)/shard_map/ppermute | solution.py:472
  40.8 6.6 %collective-permute-start.16 = (bf16[32,2176]{1,0:T(8,128)(2,1)S(1)}, bf16[32,2176]{1,0:T(8,128)(2,1)S(1)}, u32[]{:S(2)}, u32[]{:S(2)}) collective-permute-start(bf16[32,2176]{1,0:T(8,128)(2,1)S(1)} %get-tuple-element.109), channel_id=1, source_target_pairs={{0,2},{1,3},{2,0},{3,1},{4,6},{5,7},{6,4},{7,5},{8,10},{9,11},{10,... | collective-permute-start | bytes 417800 | tf_op jit(solution)/shard_map/ppermute | solution.py:472
  42.4 8.0 %collective-permute-start.15 = (bf16[32,2176]{1,0:T(8,128)(2,1)S(1)}, bf16[32,2176]{1,0:T(8,128)(2,1)S(1)}, u32[]{:S(2)}, u32[]{:S(2)}) collective-permute-start(bf16[32,2176]{1,0:T(8,128)(2,1)S(1)} %get-tuple-element.107), channel_id=1, source_target_pairs={{0,2},{1,3},{2,0},{3,1},{4,6},{5,7},{6,4},{7,5},{8,10},{9,11},{10,... | collective-permute-start | bytes 417800 | tf_op jit(solution)/shard_map/ppermute | solution.py:472
  42.9 18.2 %copy-start.4 = (bf16[32,8]{0,1:T(8,128)(2,1)S(1)}, bf16[32,8]{0,1:T(8,128)(2,1)}, u32[]{:S(2)}) copy-start(bf16[32,8]{0,1:T(8,128)(2,1)} %param.9) | copy-start | bytes 1540
  47.4 5.1 %collective-permute-start.17 = (bf16[32,2176]{1,0:T(8,128)(2,1)S(1)}, bf16[32,2176]{1,0:T(8,128)(2,1)S(1)}, u32[]{:S(2)}, u32[]{:S(2)}) collective-permute-start(bf16[32,2176]{1,0:T(8,128)(2,1)S(1)} %add_rows.2), channel_id=1, source_target_pairs={{0,4},{4,0},{8,12},{12,8},{16,20},{20,16},{24,28},{28,24},{1,5},{5... | collective-permute-start | bytes 417800 | tf_op jit(solution)/shard_map/ppermute | solution.py:472
  52.6 6.1 %collective-permute-start.18 = (bf16[16,2176]{1,0:T(8,128)(2,1)S(1)}, bf16[16,2176]{1,0:T(8,128)(2,1)S(1)}, u32[]{:S(2)}, u32[]{:S(2)}) collective-permute-start(bf16[16,2176]{1,0:T(8,128)(2,1)S(1)} %get-tuple-element.125), channel_id=1, source_target_pairs={{0,16},{4,20},{8,24},{12,28},{16,0},{20,4},{24,8},{28,12},{1,17},{... | collective-permute-start | bytes 208904 | tf_op jit(solution)/shard_map/ppermute | solution.py:472
  54.7 4.6 %collective-permute-start.19 = (bf16[16,2176]{1,0:T(8,128)(2,1)S(1)}, bf16[16,2176]{1,0:T(8,128)(2,1)S(1)}, u32[]{:S(2)}, u32[]{:S(2)}) collective-permute-start(bf16[16,2176]{1,0:T(8,128)(2,1)S(1)} %get-tuple-element.126), channel_id=1, source_target_pairs={{0,8},{4,12},{8,0},{12,4},{16,24},{20,28},{24,16},{28,20},{1,9},{5... | collective-permute-start | bytes 208904 | tf_op jit(solution)/shard_map/ppermute | solution.py:472
  54.9 6.2 %collective-permute-start.20 = (bf16[16,2176]{1,0:T(8,128)(2,1)S(1)}, bf16[16,2176]{1,0:T(8,128)(2,1)S(1)}, u32[]{:S(2)}, u32[]{:S(2)}) collective-permute-start(bf16[16,2176]{1,0:T(8,128)(2,1)S(1)} %get-tuple-element.127), channel_id=1, source_target_pairs={{0,24},{4,28},{8,16},{12,20},{16,8},{20,12},{24,0},{28,4},{1,25},{... | collective-permute-start | bytes 208904 | tf_op jit(solution)/shard_map/ppermute | solution.py:472
  (3 other events, 5.7 us)

commit v10 on v9

--- a/solution.py
+++ b/solution.py
@@ -204,17 +204,16 @@
     )(*pieces, gate_w, up_w)
 
 
-def row_grads(low, high, gate_w, up_w, received, parts, start, size):
+def row_grads(low, high, gate_w, up_w, parts, start):
     units, width = gate_w.shape
-    block = parts[0].shape[0]
-    chunk = 512 if size % 512 == 0 else size
+    block, size = parts[0].shape
+    chunk = 256 if size % 256 == 0 else size
 
     @pl.loop(0, size // chunk)
     def _(step):
         offset = pl.multiple_of(step * chunk, chunk)
         near = pl.ds(pl.multiple_of(start + offset, chunk), chunk)
         far = pl.ds(pl.multiple_of(width // 2 + start + offset, chunk), chunk)
-        here = pl.ds(offset, chunk)
         total = None
         for rows, columns in ((low, near), (high, far)):
             for i, weight in enumerate((gate_w, up_w)):
@@ -224,43 +223,39 @@
                     preferred_element_type=jnp.float32,
                 )
                 total = term if total is None else total + term
-        if received is not None:
-            total = total + received[:, here].astype(jnp.float32)
         total = total.astype(jnp.bfloat16)
         for i, part in enumerate(parts):
-            part[:, here] = total[i * block : (i + 1) * block]
+            part[:, pl.ds(offset, chunk)] = total[i * block : (i + 1) * block]
 
 
 def backward_kernel(count, *refs):
     pieces = refs[:count]
     activated, slope, hidden, gate_w, up_w, down_w = refs[count : count + 6]
-    part, halves, gate_out, up_out, low_out, high_out, gates_out = refs[count + 6 :]
+    own, far, halves, gate_out, up_out, low_out, high_out, gates_out = refs[count + 6 :]
     rows = halves.shape[0]
-    mine = rows // 2
     gather_pieces(pieces, halves.shape[1], halves)
     back = project(down_w, halves)
     gate_terms = jnp.sum(hidden[...].astype(jnp.float32) * back, axis=0, keepdims=True)
     up_pre = back * activated[...]
     gate_pre = back * slope[...]
     both = jnp.concatenate([gate_pre, up_pre], axis=0)
-    low = both.T.astype(jnp.bfloat16)
-    high = pltpu.roll(both, CAP, 1).T.astype(jnp.bfloat16)
+    low_out[...] = both.T.astype(jnp.bfloat16)
+    high_out[...] = pltpu.roll(both, CAP, 1).T.astype(jnp.bfloat16)
     gate_column = jnp.broadcast_to(gate_terms, (LANES, rows)).T.astype(jnp.bfloat16)
-    row_grads(low[mine:], high[mine:], gate_w, up_w, None, (part,), 0, part.shape[1])
-    low_out[...] = low
-    high_out[...] = high
+    row_grads(low_out, high_out, gate_w, up_w, (own, far), 0)
     gates_out[...] = gate_column
     gate_out[...] = gate_pre.astype(jnp.bfloat16)
     up_out[...] = up_pre.astype(jnp.bfloat16)
 
 
-def backward(pieces, activated, slope, hidden, weights):
+def backward(pieces, activated, slope, hidden, weights, size):
     count = len(pieces)
     units, width = weights[0].shape
     rows = sum(piece.shape[0] for piece in pieces)
     mine = rows // 2
     shapes = [
-        (mine, width // 4),
+        (mine, size),
+        (mine, size),
         (rows, width // 2),
         (units, rows),
         (units, rows),
@@ -274,79 +269,63 @@
         in_specs=[VMEM] * (count + 6),
         out_specs=[VMEM] * len(shapes),
         compiler_params=pltpu.CompilerParams(
-            vmem_limit_bytes=4 * MIB
+            vmem_limit_bytes=6 * MIB
             + 2 * sum(height * across for height, across in shapes)
-            + 40 * rows * units
+            + 56 * rows * units
         ),
         cost_estimate=LIGHT,
         name="backward",
     )(*pieces, activated, slope, hidden, *weights)
 
 
-def far_kernel(start, low, high, gates, gate_w, up_w, part):
-    span = pl.ds(part.shape[0], part.shape[0])
-    size = part.shape[1] - LANES
-    part[:, size:] = gates[span, :]
-    row_grads(low[span, :], high[span, :], gate_w, up_w, None, (part,), start, size)
-
-
-def far_rows(start, low, high, gates, gate_w, up_w):
+def rest_kernel(start, low, high, gates, gate_w, up_w, own, far):
+    mine, size = own.shape
+    size -= LANES
+    own[:, size:] = gates[:mine, :]
+    far[:, size:] = gates[mine:, :]
+    views = [part.at[:, pl.ds(0, size)] for part in (own, far)]
+    row_grads(low, high, gate_w, up_w, views, start)
+
+
+def rest_rows(start, low, high, gates, gate_w, up_w):
     rows, width = low.shape[0], gate_w.shape[1]
-    size = width // 2 - start
-    return pl.pallas_call(
-        functools.partial(far_kernel, start),
-        out_shape=struct((rows // 2, size + LANES)),
+    size = width // 2 - start + LANES
+    return pl.pallas_call(
+        functools.partial(rest_kernel, start),
+        out_shape=[struct((rows // 2, size))] * 2,
         in_specs=[VMEM] * 5,
-        out_specs=VMEM,
+        out_specs=[VMEM] * 2,
         compiler_params=pltpu.CompilerParams(vmem_limit_bytes=8 * MIB + 4 * rows * width),
         cost_estimate=LIGHT,
-        name="far_rows",
+        name="rest_rows",
     )(low, high, gates, gate_w, up_w)
 
 
-def own_first_kernel(low, high, gate_w, up_w, left, out):
-    rows, size = left.shape
-    row_grads(low[:rows, :], high[:rows, :], gate_w, up_w, left, (out,), 0, size)
-
-
-def own_first(low, high, gate_w, up_w, left):
-    return pl.pallas_call(
-        own_first_kernel,
-        out_shape=struct(left.shape),
-        in_specs=[VMEM] * 5,
-        out_specs=VMEM,
-        compiler_params=pltpu.CompilerParams(vmem_limit_bytes=8 * MIB + 16 * left.size),
-        cost_estimate=LIGHT,
-        name="own_first",
-    )(low, high, gate_w, up_w, left)
-
-
-def own_rows_kernel(low, high, gates, gate_w, up_w, left, right, *parts):
-    rows, size = left.shape
-    extra = right.shape[1] - LANES
-    block = parts[0].shape[0]
-    for i, part in enumerate(parts):
-        span = pl.ds(i * block, block)
-        part[:, :size] = left[span, :]
-        part[:, size + extra :] = (
-            gates[span, :].astype(jnp.float32) + right[span, extra:].astype(jnp.float32)
-        ).astype(jnp.bfloat16)
-    views = [part.at[:, pl.ds(size, extra)] for part in parts]
-    row_grads(low[:rows, :], high[:rows, :], gate_w, up_w, right, views, size, extra)
-
-
-def own_rows(count, low, high, gates, gate_w, up_w, left, right):
-    rows = left.shape[0]
-    width = left.shape[1] + right.shape[1]
-    return pl.pallas_call(
-        own_rows_kernel,
+def sum_kernel(targets, own_left, own_right, left, right, *outs):
+    base = 0
+    for own, other in ((own_left, left), (own_right, right)):
+        span = pl.ds(base, own.shape[1])
+        base += own.shape[1]
+        total = (own[...].astype(jnp.float32) + other[...].astype(jnp.float32)).astype(
+            jnp.bfloat16
+        )
+        for i, (out, slot) in enumerate(targets):
+            outs[out][pl.ds(slot * BLOCK, BLOCK), span] = total[i * BLOCK : (i + 1) * BLOCK]
+
+
+def sum_rows(targets, own, other):
+    rows = own[0].shape[0]
+    width = sum(part.shape[1] for part in own)
+    count = 1 + max(out for out, _ in targets)
+    return pl.pallas_call(
+        functools.partial(sum_kernel, targets),
         out_shape=[struct((rows // count, width))] * count,
-        in_specs=[VMEM] * 7,
+        in_specs=[VMEM] * 4,
         out_specs=[VMEM] * count,
         compiler_params=pltpu.CompilerParams(vmem_limit_bytes=8 * MIB + 16 * rows * width),
         cost_estimate=LIGHT,
-        name="own_rows",
-    )(low, high, gates, gate_w, up_w, left, right)
+        name="sum_rows",
+    )(*own, *other)
 
 
 def add_kernel(left, right, out):
@@ -433,7 +412,7 @@
 
 def combine_kernel(n_targets, first, second, choice_ref, gates_ref, *refs):
     blocks, (token_ref, gate_ref) = refs[: n_targets // 2], refs[n_targets // 2 :]
-    even = offsets(n_targets)[1]
+    even = return_offsets(n_targets)[1]
     back = jnp.concatenate([blocks[even.index(k)][...] for k in range(0, n_targets, 2)], axis=0)
     half = token_ref.shape[1] // 2
     choices, tokens = gates_ref.shape
@@ -473,9 +452,15 @@
 
 
 def offsets(count):
-    even = []
-    for k in range(0, count // 2, 2):
-        even += [k, k + count // 2]
+    near, far = list(range(1, count // 2)), list(range(count // 2, count))
+    order = []
+    for i, k in enumerate(near):
+        order += [k, far[i]]
+    return order + far[len(near) :] + [0]
+
+
+def return_offsets(count):
+    even = list(range(count // 2, count, 2)) + list(range(count // 2 - 2, -1, -2))
     return [k ^ 1 for k in even], even
 
 
@@ -500,10 +485,11 @@
     weights = (w_gate[0], w_up[0], w_down[0])
     tie = lax.optimization_barrier
 
-    odd, even = offsets(n_targets)
+    order = offsets(n_targets)
+    odd, even = return_offsets(n_targets)
     middle = n_targets // 2
     sent = dispatch(n_targets, ids, tokens, gates, out_grad)
-    arrived = exchange([sent[k] for k in odd + even], odd + even)
+    arrived = exchange([sent[k] for k in order], order)
     early = pack(arrived[:middle])
     ids_after, _ = tie((ids, early))
     table, late = tie((placement(n_targets, ids_after), arrived[middle:]))
@@ -527,18 +513,21 @@
         for group in groups
     ]
     token_halves, activated, slope, hidden = forward(pieces, weights[0], weights[1])
-    part, grad_halves, gate_f, up_f, low, high, gate_column = backward(
-        pieces, activated, slope, hidden, weights
+    size = width // 16 * 5
+    own_left, far_left, grad_halves, gate_f, up_f, low, high, gate_column = backward(
+        pieces, activated, slope, hidden, weights, size
     )
 
-    received = flip(part, "dp", 1)
-    other = far_rows(width // 4, low, high, gate_column, weights[0], weights[1])
-    received, other = tie((received, other))
-    left = own_first(low, high, weights[0], weights[1], received)
-    right, left = tie((flip(other, "dp", 1), left))
-    parts = own_rows(
-        2 * len(near), low, high, gate_column, weights[0], weights[1], left, right
-    )
+    left = flip(far_left, "dp", 1)
+    own_right, far_right = rest_rows(size, low, high, gate_column, weights[0], weights[1])
+    left, own_right = tie((left, own_right))
+    right = flip(far_right, "dp", 1)
+    targets = [
+        (2 * i, odd.index(k)) if k % 2 else (2 * i + 1, even.index(k))
+        for i in range(len(near))
+        for k in order
+    ]
+    parts = sum_rows(targets, (own_left, own_right), (left, right))
     gate_f, up_f, _ = tie((gate_f, up_f, parts))
     grad_gate, grad_up = weight_grads((gate_f, up_f), token_halves)
     sums = []

time: 62.3 us -> 61.1 us (0.981)
  starting transfers between devices: 27.5 us -> 24.3 us
  waiting for transfers between devices: 16.7 us -> 18.9 us
    ppermute x21, starting transfers between devices: 27.5 us -> 24.3 us  [flip(): return lax.ppermute(value, axis, [(i, i ^ bit) for i in range(size)])]
    ppermute x21, waiting for transfers between devices: 16.7 us -> 18.9 us  [flip(): return lax.ppermute(value, axis, [(i, i ^ bit) for i in range(size)])]
    pallas_call x3 -> x2, Pallas kernels: 2.77 us -> 1.44 us  [the longest x1 1.31 us: rest_rows(): pl.pallas_call(functools.partial(rest_kernel, start), out_shape=[struct((...]
    pallas_call x1, Pallas kernels: 2.55 us -> 3.73 us  [backward(): pl.pallas_call(functools.partial(backward_kernel, count), out_shape=[stru...]
  transfers between devices with their start and end apart: 21 -> 21, of which waited for: 10 -> 10; matrix products, arithmetic and copies ran while one was open for 0% -> 0% of each run, Pallas kernels for 12% -> 11%
where the time goes in v10:
time: 61.1 us; the launch traced here: 60.9 us
  starting transfers between devices  24.3 us (40%)
  waiting for transfers between devices  18.9 us (31%)
  Pallas kernels  15.9 us (26%)
  local copies, waits for them, and re-layouts  0.99 us (2%)
  between operations  0.82 us (1%)
    ppermute x21, starting transfers between devices, flip(): return lax.ppermute(value, axis, [(i, i ^ bit) for i in range(size)])  24.3 us
    ppermute x21, waiting for transfers between devices, flip(): return lax.ppermute(value, axis, [(i, i ^ bit) for i in range(size)])  18.9 us
    pallas_call x2, Pallas kernels, weight_grads(): pl.pallas_call(functools.partial(weight_kernel, chunk, count), out_shape=...  5.05 us
    pallas_call x1, Pallas kernels, backward(): pl.pallas_call(functools.partial(backward_kernel, count), out_shape=[stru...  3.73 us
    pallas_call x1, Pallas kernels, dispatch(): pl.pallas_call(functools.partial(dispatch_kernel, n_targets), out_shape=[...  2.34 us
    pallas_call x1, Pallas kernels, forward(): pl.pallas_call(functools.partial(forward_kernel, count), out_shape=[struc...  1.96 us
    pallas_call x1, Pallas kernels, rest_rows(): pl.pallas_call(functools.partial(rest_kernel, start), out_shape=[struct((...  1.31 us
  transfers between devices with their start and end apart: 21, of which 10 were waited for; matrix products, arithmetic and copies ran while one was open for 0% of the time, Pallas kernels for 11%

profile of v10, /device:TPU:0, one launch (start us, length us, event | category | flops | bytes accessed | tf_op | source)
XLA Modules:
  0.0 60.9 jit_solution(10958061052466378660)
XLA Ops:
  0.6 2.3 %dispatch.1 = (bf16[8,4096]{1,0:T(8,128)(2,1)}, bf16[8,4096]{1,0:T(8,128)(2,1)}, bf16[8,4096]{1,0:T(8,128)(2,1)}, bf16[8,4096]{1,0:T(8,128)(2,1)}, bf16[8,4096]{...) custom-call(s32[8,32]{1,0:T(8,128)} %bitcast.18, ...), custom_call_target="tpu_custom_call" | custom-call | tf_op jit(solution)/shard_map/dispatch/pallas_call | solution.py:92
  3.0 3.0 %collective-permute-start = (bf16[8,4096]{1,0:T(8,128)(2,1)}, bf16[8,4096]{1,0:T(8,128)(2,1)S(1)}, u32[]{:S(2)}, u32[]{:S(2)}) collective-permute-start(bf16[8,4096]{1,0:T(8,128)(2,1)} %get-tuple-element.70), channel_id=1, source_target_pairs={{0,4},{4,0},{8,12},{12,8},{16,20},{20,16},{24,28},{28,24},{1,5},{5... | collective-permute-start | bytes 196616 | tf_op jit(solution)/shard_map/ppermute | solution.py:451
  6.0 2.6 %collective-permute-start.1 = (bf16[8,4096]{1,0:T(8,128)(2,1)}, bf16[8,4096]{1,0:T(8,128)(2,1)S(1)}, u32[]{:S(2)}, u32[]{:S(2)}) collective-permute-start(bf16[8,4096]{1,0:T(8,128)(2,1)} %get-tuple-element.71), channel_id=1, source_target_pairs={{0,16},{4,20},{8,24},{12,28},{16,0},{20,4},{24,8},{28,12},{1,17},{... | collective-permute-start | bytes 196616 | tf_op jit(solution)/shard_map/ppermute | solution.py:451
  8.6 1.6 %collective-permute-start.2 = (bf16[8,4096]{1,0:T(8,128)(2,1)}, bf16[8,4096]{1,0:T(8,128)(2,1)S(1)}, u32[]{:S(2)}, u32[]{:S(2)}) collective-permute-start(bf16[8,4096]{1,0:T(8,128)(2,1)} %get-tuple-element.72), channel_id=1, source_target_pairs={{0,8},{4,12},{8,0},{12,4},{16,24},{20,28},{24,16},{28,20},{1,9},{5... | collective-permute-start | bytes 196616 | tf_op jit(solution)/shard_map/ppermute | solution.py:451
  10.5 1.4 %collective-permute-start.4 = (bf16[8,4096]{1,0:T(8,128)(2,1)}, bf16[8,4096]{1,0:T(8,128)(2,1)S(1)}, u32[]{:S(2)}, u32[]{:S(2)}) collective-permute-start(bf16[8,4096]{1,0:T(8,128)(2,1)} %get-tuple-element.78), channel_id=1, source_target_pairs={{0,12},{4,8},{8,4},{12,0},{16,28},{20,24},{24,20},{28,16},{1,13},{... | collective-permute-start | bytes 196616 | tf_op jit(solution)/shard_map/ppermute | solution.py:451
  11.9 3.6 %collective-permute-start.5 = (bf16[8,4096]{1,0:T(8,128)(2,1)}, bf16[8,4096]{1,0:T(8,128)(2,1)S(1)}, u32[]{:S(2)}, u32[]{:S(2)}) collective-permute-start(bf16[8,4096]{1,0:T(8,128)(2,1)} %get-tuple-element.79), channel_id=1, source_target_pairs={{0,24},{4,28},{8,16},{12,20},{16,8},{20,12},{24,0},{28,4},{1,25},{... | collective-permute-start | bytes 196616 | tf_op jit(solution)/shard_map/ppermute | solution.py:451
  15.5 1.6 %collective-permute-start.6 = (bf16[8,4096]{1,0:T(8,128)(2,1)}, bf16[8,4096]{1,0:T(8,128)(2,1)S(1)}, u32[]{:S(2)}, u32[]{:S(2)}) collective-permute-start(bf16[8,4096]{1,0:T(8,128)(2,1)} %get-tuple-element.80), channel_id=1, source_target_pairs={{0,28},{4,24},{8,20},{12,16},{16,12},{20,8},{24,4},{28,0},{1,29},{... | collective-permute-start | bytes 196616 | tf_op jit(solution)/shard_map/ppermute | solution.py:451
  17.0 2.9 %collective-permute-done.3.refs_3_ = bf16[8,4096]{1,0:T(8,128)(2,1)S(1)} collective-permute-done((bf16[8,4096]{1,0:T(8,128)(2,1)}, bf16[8,4096]{1,0:T(8,128)(2,1)S(1)}, u32[]{:S(2)}, u32[]{:S(2)}) %collective-permute-start.3) | collective-permute-done | bytes 65568 | tf_op jit(solution)/shard_map/ppermute | solution.py:451
  20.0 1.6 %collective-permute-start.7 = (bf16[32,4096]{1,0:T(8,128)(2,1)S(1)}, bf16[32,4096]{1,0:T(8,128)(2,1)S(1)}, u32[]{:S(2)}, u32[]{:S(2)}) collective-permute-start(bf16[32,4096]{1,0:T(8,128)(2,1)S(1)} %pack.2.refs_0_), channel_id=1, source_target_pairs={{0,2},{1,3},{2,0},{3,1},{4,6},{5,7},{6,4},{7,5},{8,10},{9,11},{10,... | collective-permute-start | bytes 786440 | tf_op jit(solution)/shard_map/ppermute | solution.py:451
  22.9 1.4 %collective-permute-start.8 = (bf16[32,4096]{1,0:T(8,128)(2,1)S(1)}, bf16[32,4096]{1,0:T(8,128)(2,1)S(1)}, u32[]{:S(2)}, u32[]{:S(2)}) collective-permute-start(bf16[32,4096]{1,0:T(8,128)(2,1)S(1)} %pack.3.refs_1_), channel_id=1, source_target_pairs={{0,2},{1,3},{2,0},{3,1},{4,6},{5,7},{6,4},{7,5},{8,10},{9,11},{10,... | collective-permute-start | bytes 786440 | tf_op jit(solution)/shard_map/ppermute | solution.py:451
  24.2 3.8 %collective-permute-done.7.refs_2_ = bf16[32,4096]{1,0:T(8,128)(2,1)S(1)} collective-permute-done((bf16[32,4096]{1,0:T(8,128)(2,1)S(1)}, bf16[32,4096]{1,0:T(8,128)(2,1)S(1)}, u32[]{:S(2)}, u32[]{:S(2)}) %collective-permute-start.7) | collective-permute-done | bytes 262176 | tf_op jit(solution)/shard_map/ppermute | solution.py:451
  28.6 2.3 %collective-permute-done.8.refs_3_ = bf16[32,4096]{1,0:T(8,128)(2,1)S(1)} collective-permute-done((bf16[32,4096]{1,0:T(8,128)(2,1)S(1)}, bf16[32,4096]{1,0:T(8,128)(2,1)S(1)}, u32[]{:S(2)}, u32[]{:S(2)}) %collective-permute-start.8) | collective-permute-done | bytes 262176 | tf_op jit(solution)/shard_map/ppermute | solution.py:451
  31.0 1.5 %collective-permute-done.12.refs_7_ = bf16[32,4096]{1,0:T(8,128)(2,1)S(1)} collective-permute-done((bf16[32,4096]{1,0:T(8,128)(2,1)S(1)}, bf16[32,4096]{1,0:T(8,128)(2,1)S(1)}, u32[]{:S(2)}, u32[]{:S(2)}) %collective-permute-start.12) | collective-permute-done | bytes 262176 | tf_op jit(solution)/shard_map/ppermute | solution.py:451
  32.5 2.0 %forward.1 = (bf16[256,2048]{1,0:T(8,128)(2,1)S(1)}, f32[384,256]{1,0:T(8,128)S(1)}, f32[384,256]{1,0:T(8,128)S(1)}, bf16[384,256]{1,0:T(8,128)(2,1)S(1)}) custom-call(bf16[32,4096]{1,0:T(8,128)(2,1)S(1)} %pack.2.refs_0_, bf16[32,4096]{1,0:T(8,128)(2,1)S(1)} %pack.3.refs_1_, bf16[32,4096]{1,0:T(8,128)(2,1)S(1)} %collective-permute-done.7.refs_2_, ...), custom_call_target="tpu_custom_call" | custom-call | flops 1000000 | bytes 10000 | tf_op jit(solution)/shard_map/forward/pallas_call | solution.py:189
  34.5 3.7 %backward.1 = (bf16[128,1280]{1,0:T(8,128)(2,1)S(1)}, bf16[128,1280]{1,0:T(8,128)(2,1)S(1)}, bf16[256,2048]{1,0:T(8,128)(2,1)S(1)}, bf16[384,256]{1,0:T(8,128)(2...) custom-call(bf16[32,4096]{1,0:T(8,128)(2,1)S(1)} %pack.2.refs_0_, ...), custom_call_target="tpu_custom_call" | custom-call | flops 1000000 | bytes 10000 | tf_op jit(solution)/shard_map/backward/pallas_call | solution.py:266
  38.4 1.3 %rest_rows.1 = (bf16[128,896]{1,0:T(8,128)(2,1)S(1)}, bf16[128,896]{1,0:T(8,128)(2,1)S(1)}) custom-call(bf16[256,768]{1,0:T(8,128)(2,1)S(1)} %get-tuple-element.101.low, bf16[256,768]{1,0:T(8,128)(2,1)S(1)} %get-tuple-element.102.high, bf16[256,128]{1,0:T(8,128)(2,1)S(1)} %get-tuple-element.103.gates, bf16[384,4096]{1,0:T(8,128)(2,1)S(1)} %bitcast.11, ...), custom_call_target="tpu_custom_call" | custom-call | flops 1000000 | bytes 10000 | tf_op jit(solution)/shard_map/rest_rows/pallas_call | solution.py:293
  41.4 1.6 %collective-permute-start.16 = (bf16[32,2176]{1,0:T(8,128)(2,1)S(1)}, bf16[32,2176]{1,0:T(8,128)(2,1)S(1)}, u32[]{:S(2)}, u32[]{:S(2)}) collective-permute-start(bf16[32,2176]{1,0:T(8,128)(2,1)S(1)} %get-tuple-element.111), channel_id=1, source_target_pairs={{0,2},{1,3},{2,0},{3,1},{4,6},{5,7},{6,4},{7,5},{8,10},{9,11},{10,... | collective-permute-start | bytes 417800 | tf_op jit(solution)/shard_map/ppermute | solution.py:451
  43.5 3.1 %weight_grads.2 = (bf16[384,4096]{1,0:T(8,128)(2,1)}, bf16[384,4096]{1,0:T(8,128)(2,1)}) custom-call(bf16[384,256]{1,0:T(8,128)(2,1)S(1)} %get-tuple-element.114.refs_0_, bf16[384,256]{1,0:T(8,128)(2,1)S(1)} %get-tuple-element.115.refs_1_, bf16[256,2048]{1,0:T(8,128)(2,1)S(1)} %get-tuple-element.116.refs_2_), custom_call_target="tpu_custom_call" | custom-call | flops 1000000 | bytes 10000 | tf_op jit(solution)/shard_map/weight_grads/pallas_call | solution.py:398
  46.6 1.4 %collective-permute-done.16.right = bf16[32,2176]{1,0:T(8,128)(2,1)S(1)} collective-permute-done((bf16[32,2176]{1,0:T(8,128)(2,1)S(1)}, bf16[32,2176]{1,0:T(8,128)(2,1)S(1)}, u32[]{:S(2)}, u32[]{:S(2)}) %collective-permute-start.16) | collective-permute-done | bytes 139296 | tf_op jit(solution)/shard_map/ppermute | solution.py:451
  48.4 2.0 %weight_grads.3 = bf16[384,4096]{1,0:T(8,128)(2,1)} custom-call(bf16[384,256]{1,0:T(8,128)(2,1)S(1)} %get-tuple-element.120.refs_10_.refs_0_, bf16[256,2048]{1,0:T(8,128)(2,1)S(1)} %get-tuple-element.121.refs_1_), custom_call_target="tpu_custom_call" | custom-call | flops 1000000 | bytes 10000 | tf_op jit(solution)/shard_map/weight_grads/pallas_call | solution.py:398
  50.5 2.7 %collective-permute-done.17.passed = bf16[32,2176]{1,0:T(8,128)(2,1)S(1)} collective-permute-done((bf16[32,2176]{1,0:T(8,128)(2,1)S(1)}, bf16[32,2176]{1,0:T(8,128)(2,1)S(1)}, u32[]{:S(2)}, u32[]{:S(2)}) %collective-permute-start.17) | collective-permute-done | bytes 139296 | tf_op jit(solution)/shard_map/ppermute | solution.py:451
  53.3 1.3 %collective-permute-start.19 = (bf16[16,2176]{1,0:T(8,128)(2,1)S(1)}, bf16[16,2176]{1,0:T(8,128)(2,1)S(1)}, u32[]{:S(2)}, u32[]{:S(2)}) collective-permute-start(bf16[16,2176]{1,0:T(8,128)(2,1)S(1)} %get-tuple-element.127), channel_id=1, source_target_pairs={{0,24},{4,28},{8,16},{12,20},{16,8},{20,12},{24,0},{28,4},{1,25},{... | collective-permute-start | bytes 208904 | tf_op jit(solution)/shard_map/ppermute | solution.py:451
  54.6 2.1 %collective-permute-start.20 = (bf16[16,2176]{1,0:T(8,128)(2,1)S(1)}, bf16[16,2176]{1,0:T(8,128)(2,1)S(1)}, u32[]{:S(2)}, u32[]{:S(2)}) collective-permute-start(bf16[16,2176]{1,0:T(8,128)(2,1)S(1)} %get-tuple-element.128), channel_id=1, source_target_pairs={{0,8},{4,12},{8,0},{12,4},{16,24},{20,28},{24,16},{28,20},{1,9},{5... | collective-permute-start | bytes 208904 | tf_op jit(solution)/shard_map/ppermute | solution.py:451
  56.7 1.7 %collective-permute-done.18.refs_0_ = bf16[16,2176]{1,0:T(8,128)(2,1)S(1)} collective-permute-done((bf16[16,2176]{1,0:T(8,128)(2,1)S(1)}, bf16[16,2176]{1,0:T(8,128)(2,1)S(1)}, u32[]{:S(2)}, u32[]{:S(2)}) %collective-permute-start.18) | collective-permute-done | bytes 69664 | tf_op jit(solution)/shard_map/ppermute | solution.py:451
  (44 shorter events, 7.6 us)
Async XLA Ops:
  3.0 8.9 %collective-permute-start = (bf16[8,4096]{1,0:T(8,128)(2,1)}, bf16[8,4096]{1,0:T(8,128)(2,1)S(1)}, u32[]{:S(2)}, u32[]{:S(2)}) collective-permute-start(bf16[8,4096]{1,0:T(8,128)(2,1)} %get-tuple-element.70), channel_id=1, source_target_pairs={{0,4},{4,0},{8,12},{12,8},{16,20},{20,16},{24,28},{28,24},{1,5},{5... | collective-permute-start | bytes 196616 | tf_op jit(solution)/shard_map/ppermute | solution.py:451
  6.0 9.5 %collective-permute-start.1 = (bf16[8,4096]{1,0:T(8,128)(2,1)}, bf16[8,4096]{1,0:T(8,128)(2,1)S(1)}, u32[]{:S(2)}, u32[]{:S(2)}) collective-permute-start(bf16[8,4096]{1,0:T(8,128)(2,1)} %get-tuple-element.71), channel_id=1, source_target_pairs={{0,16},{4,20},{8,24},{12,28},{16,0},{20,4},{24,8},{28,12},{1,17},{... | collective-permute-start | bytes 196616 | tf_op jit(solution)/shard_map/ppermute | solution.py:451
  8.6 8.4 %collective-permute-start.2 = (bf16[8,4096]{1,0:T(8,128)(2,1)}, bf16[8,4096]{1,0:T(8,128)(2,1)S(1)}, u32[]{:S(2)}, u32[]{:S(2)}) collective-permute-start(bf16[8,4096]{1,0:T(8,128)(2,1)} %get-tuple-element.72), channel_id=1, source_target_pairs={{0,8},{4,12},{8,0},{12,4},{16,24},{20,28},{24,16},{28,20},{1,9},{5... | collective-permute-start | bytes 196616 | tf_op jit(solution)/shard_map/ppermute | solution.py:451
  10.2 9.8 %collective-permute-start.3 = (bf16[8,4096]{1,0:T(8,128)(2,1)}, bf16[8,4096]{1,0:T(8,128)(2,1)S(1)}, u32[]{:S(2)}, u32[]{:S(2)}) collective-permute-start(bf16[8,4096]{1,0:T(8,128)(2,1)} %get-tuple-element.73), channel_id=1, source_target_pairs={{0,20},{4,16},{8,28},{12,24},{16,4},{20,0},{24,12},{28,8},{1,21},{... | collective-permute-start | bytes 196616 | tf_op jit(solution)/shard_map/ppermute | solution.py:451
  10.5 12.3 %collective-permute-start.4 = (bf16[8,4096]{1,0:T(8,128)(2,1)}, bf16[8,4096]{1,0:T(8,128)(2,1)S(1)}, u32[]{:S(2)}, u32[]{:S(2)}) collective-permute-start(bf16[8,4096]{1,0:T(8,128)(2,1)} %get-tuple-element.78), channel_id=1, source_target_pairs={{0,12},{4,8},{8,4},{12,0},{16,28},{20,24},{24,20},{28,16},{1,13},{... | collective-permute-start | bytes 196616 | tf_op jit(solution)/shard_map/ppermute | solution.py:451
  11.9 10.9 %collective-permute-start.5 = (bf16[8,4096]{1,0:T(8,128)(2,1)}, bf16[8,4096]{1,0:T(8,128)(2,1)S(1)}, u32[]{:S(2)}, u32[]{:S(2)}) collective-permute-start(bf16[8,4096]{1,0:T(8,128)(2,1)} %get-tuple-element.79), channel_id=1, source_target_pairs={{0,24},{4,28},{8,16},{12,20},{16,8},{20,12},{24,0},{28,4},{1,25},{... | collective-permute-start | bytes 196616 | tf_op jit(solution)/shard_map/ppermute | solution.py:451
  15.5 7.3 %collective-permute-start.6 = (bf16[8,4096]{1,0:T(8,128)(2,1)}, bf16[8,4096]{1,0:T(8,128)(2,1)S(1)}, u32[]{:S(2)}, u32[]{:S(2)}) collective-permute-start(bf16[8,4096]{1,0:T(8,128)(2,1)} %get-tuple-element.80), channel_id=1, source_target_pairs={{0,28},{4,24},{8,20},{12,16},{16,12},{20,8},{24,4},{28,0},{1,29},{... | collective-permute-start | bytes 196616 | tf_op jit(solution)/shard_map/ppermute | solution.py:451
  20.0 12.5 %copy-start = (bf16[1,384,4096]{2,1,0:T(8,128)(2,1)S(1)}, bf16[1,384,4096]{2,1,0:T(8,128)(2,1)}, u32[]{:S(2)}) copy-start(bf16[1,384,4096]{2,1,0:T(8,128)(2,1)} %param.11) | copy-start | bytes 9437188
  20.0 12.5 %copy-start.1 = (bf16[1,384,4096]{2,1,0:T(8,128)(2,1)S(1)}, bf16[1,384,4096]{2,1,0:T(8,128)(2,1)}, u32[]{:S(2)}) copy-start(bf16[1,384,4096]{2,1,0:T(8,128)(2,1)} %param.12) | copy-start | bytes 9437188
  20.0 8.0 %collective-permute-start.7 = (bf16[32,4096]{1,0:T(8,128)(2,1)S(1)}, bf16[32,4096]{1,0:T(8,128)(2,1)S(1)}, u32[]{:S(2)}, u32[]{:S(2)}) collective-permute-start(bf16[32,4096]{1,0:T(8,128)(2,1)S(1)} %pack.2.refs_0_), channel_id=1, source_target_pairs={{0,2},{1,3},{2,0},{3,1},{4,6},{5,7},{6,4},{7,5},{8,10},{9,11},{10,... | collective-permute-start | bytes 786440 | tf_op jit(solution)/shard_map/ppermute | solution.py:451
  22.9 8.0 %collective-permute-start.8 = (bf16[32,4096]{1,0:T(8,128)(2,1)S(1)}, bf16[32,4096]{1,0:T(8,128)(2,1)S(1)}, u32[]{:S(2)}, u32[]{:S(2)}) collective-permute-start(bf16[32,4096]{1,0:T(8,128)(2,1)S(1)} %pack.3.refs_1_), channel_id=1, source_target_pairs={{0,2},{1,3},{2,0},{3,1},{4,6},{5,7},{6,4},{7,5},{8,10},{9,11},{10,... | collective-permute-start | bytes 786440 | tf_op jit(solution)/shard_map/ppermute | solution.py:451
  28.1 2.8 %collective-permute-start.9 = (bf16[32,4096]{1,0:T(8,128)(2,1)S(1)}, bf16[32,4096]{1,0:T(8,128)(2,1)S(1)}, u32[]{:S(2)}, u32[]{:S(2)}) collective-permute-start(bf16[32,4096]{1,0:T(8,128)(2,1)S(1)} %pack.2.refs_0_), channel_id=1, source_target_pairs={{0,1},{1,0},{2,3},{3,2},{4,5},{5,4},{6,7},{7,6},{8,9},{9,8},{10,11... | collective-permute-start | bytes 786440 | tf_op jit(solution)/shard_map/ppermute | solution.py:451
  28.1 2.8 %collective-permute-start.10 = (bf16[32,4096]{1,0:T(8,128)(2,1)S(1)}, bf16[32,4096]{1,0:T(8,128)(2,1)S(1)}, u32[]{:S(2)}, u32[]{:S(2)}) collective-permute-start(bf16[32,4096]{1,0:T(8,128)(2,1)S(1)} %collective-permute-done.7.refs_2_), channel_id=1, source_target_pairs={{0,1},{1,0},{2,3},{3,2},{4,5},{5,4},{6,7},{7,6},{8,9},{9,8},{10,11... | collective-permute-start | bytes 786440 | tf_op jit(solution)/shard_map/ppermute | solution.py:451
  28.6 2.3 %collective-permute-start.11 = (bf16[32,4096]{1,0:T(8,128)(2,1)S(1)}, bf16[32,4096]{1,0:T(8,128)(2,1)S(1)}, u32[]{:S(2)}, u32[]{:S(2)}) collective-permute-start(bf16[32,4096]{1,0:T(8,128)(2,1)S(1)} %pack.3.refs_1_), channel_id=1, source_target_pairs={{0,1},{1,0},{2,3},{3,2},{4,5},{5,4},{6,7},{7,6},{8,9},{9,8},{10,11... | collective-permute-start | bytes 786440 | tf_op jit(solution)/shard_map/ppermute | solution.py:451
  30.9 1.6 %collective-permute-start.12 = (bf16[32,4096]{1,0:T(8,128)(2,1)S(1)}, bf16[32,4096]{1,0:T(8,128)(2,1)S(1)}, u32[]{:S(2)}, u32[]{:S(2)}) collective-permute-start(bf16[32,4096]{1,0:T(8,128)(2,1)S(1)} %collective-permute-done.8.refs_3_), channel_id=1, source_target_pairs={{0,1},{1,0},{2,3},{3,2},{4,5},{5,4},{6,7},{7,6},{8,9},{9,8},{10,11... | collective-permute-start | bytes 786440 | tf_op jit(solution)/shard_map/ppermute | solution.py:451
  38.2 2.0 %collective-permute-start.13 = (bf16[128,1280]{1,0:T(8,128)(2,1)S(1)}, bf16[128,1280]{1,0:T(8,128)(2,1)S(1)}, u32[]{:S(2)}, u32[]{:S(2)}) collective-permute-start(bf16[128,1280]{1,0:T(8,128)(2,1)S(1)} %get-tuple-element.100), channel_id=1, source_target_pairs={{0,1},{1,0},{2,3},{3,2},{4,5},{5,4},{6,7},{7,6},{8,9},{9,8},{10,11... | collective-permute-start | bytes 983048 | tf_op jit(solution)/shard_map/ppermute | solution.py:451
  39.7 1.6 %collective-permute-start.14 = (bf16[128,896]{1,0:T(8,128)(2,1)S(1)}, bf16[128,896]{1,0:T(8,128)(2,1)S(1)}, u32[]{:S(2)}, u32[]{:S(2)}) collective-permute-start(bf16[128,896]{1,0:T(8,128)(2,1)S(1)} %get-tuple-element.107), channel_id=1, source_target_pairs={{0,1},{1,0},{2,3},{3,2},{4,5},{5,4},{6,7},{7,6},{8,9},{9,8},{10,11... | collective-permute-start | bytes 688136 | tf_op jit(solution)/shard_map/ppermute | solution.py:451
  41.4 6.6 %collective-permute-start.16 = (bf16[32,2176]{1,0:T(8,128)(2,1)S(1)}, bf16[32,2176]{1,0:T(8,128)(2,1)S(1)}, u32[]{:S(2)}, u32[]{:S(2)}) collective-permute-start(bf16[32,2176]{1,0:T(8,128)(2,1)S(1)} %get-tuple-element.111), channel_id=1, source_target_pairs={{0,2},{1,3},{2,0},{3,1},{4,6},{5,7},{6,4},{7,5},{8,10},{9,11},{10,... | collective-permute-start | bytes 417800 | tf_op jit(solution)/shard_map/ppermute | solution.py:451
  43.0 7.4 %collective-permute-start.15 = (bf16[32,2176]{1,0:T(8,128)(2,1)S(1)}, bf16[32,2176]{1,0:T(8,128)(2,1)S(1)}, u32[]{:S(2)}, u32[]{:S(2)}) collective-permute-start(bf16[32,2176]{1,0:T(8,128)(2,1)S(1)} %get-tuple-element.109), channel_id=1, source_target_pairs={{0,2},{1,3},{2,0},{3,1},{4,6},{5,7},{6,4},{7,5},{8,10},{9,11},{10,... | collective-permute-start | bytes 417800 | tf_op jit(solution)/shard_map/ppermute | solution.py:451
  43.5 16.4 %copy-start.4 = (bf16[32,8]{0,1:T(8,128)(2,1)S(1)}, bf16[32,8]{0,1:T(8,128)(2,1)}, u32[]{:S(2)}) copy-start(bf16[32,8]{0,1:T(8,128)(2,1)} %param.9) | copy-start | bytes 1540
  48.0 5.1 %collective-permute-start.17 = (bf16[32,2176]{1,0:T(8,128)(2,1)S(1)}, bf16[32,2176]{1,0:T(8,128)(2,1)S(1)}, u32[]{:S(2)}, u32[]{:S(2)}) collective-permute-start(bf16[32,2176]{1,0:T(8,128)(2,1)S(1)} %add_rows.2), channel_id=1, source_target_pairs={{0,4},{4,0},{8,12},{12,8},{16,20},{20,16},{24,28},{28,24},{1,5},{5... | collective-permute-start | bytes 417800 | tf_op jit(solution)/shard_map/ppermute | solution.py:451
  53.2 5.3 %collective-permute-start.18 = (bf16[16,2176]{1,0:T(8,128)(2,1)S(1)}, bf16[16,2176]{1,0:T(8,128)(2,1)S(1)}, u32[]{:S(2)}, u32[]{:S(2)}) collective-permute-start(bf16[16,2176]{1,0:T(8,128)(2,1)S(1)} %get-tuple-element.126), channel_id=1, source_target_pairs={{0,16},{4,20},{8,24},{12,28},{16,0},{20,4},{24,8},{28,12},{1,17},{... | collective-permute-start | bytes 208904 | tf_op jit(solution)/shard_map/ppermute | solution.py:451
  53.3 6.3 %collective-permute-start.19 = (bf16[16,2176]{1,0:T(8,128)(2,1)S(1)}, bf16[16,2176]{1,0:T(8,128)(2,1)S(1)}, u32[]{:S(2)}, u32[]{:S(2)}) collective-permute-start(bf16[16,2176]{1,0:T(8,128)(2,1)S(1)} %get-tuple-element.127), channel_id=1, source_target_pairs={{0,24},{4,28},{8,16},{12,20},{16,8},{20,12},{24,0},{28,4},{1,25},{... | collective-permute-start | bytes 208904 | tf_op jit(solution)/shard_map/ppermute | solution.py:451
  54.6 5.3 %collective-permute-start.20 = (bf16[16,2176]{1,0:T(8,128)(2,1)S(1)}, bf16[16,2176]{1,0:T(8,128)(2,1)S(1)}, u32[]{:S(2)}, u32[]{:S(2)}) collective-permute-start(bf16[16,2176]{1,0:T(8,128)(2,1)S(1)} %get-tuple-element.128), channel_id=1, source_target_pairs={{0,8},{4,12},{8,0},{12,4},{16,24},{20,28},{24,16},{28,20},{1,9},{5... | collective-permute-start | bytes 208904 | tf_op jit(solution)/shard_map/ppermute | solution.py:451
  (3 other events, 5.7 us)

commit v11 on v10

--- a/solution.py
+++ b/solution.py
@@ -204,26 +204,28 @@
     )(*pieces, gate_w, up_w)
 
 
-def row_grads(low, high, gate_w, up_w, parts, start):
+def row_grads(factors, gate_w, up_w, parts, start):
     units, width = gate_w.shape
     block, size = parts[0].shape
+    slots = factors.shape[0]
     chunk = 256 if size % 256 == 0 else size
+
+    def product(columns):
+        return jnp.dot(
+            factors[:, :units], gate_w[:, columns], preferred_element_type=jnp.float32
+        ) + jnp.dot(factors[:, units:], up_w[:, columns], preferred_element_type=jnp.float32)
 
     @pl.loop(0, size // chunk)
     def _(step):
         offset = pl.multiple_of(step * chunk, chunk)
-        near = pl.ds(pl.multiple_of(start + offset, chunk), chunk)
-        far = pl.ds(pl.multiple_of(width // 2 + start + offset, chunk), chunk)
-        total = None
-        for rows, columns in ((low, near), (high, far)):
-            for i, weight in enumerate((gate_w, up_w)):
-                term = jnp.dot(
-                    rows[:, i * units : (i + 1) * units],
-                    weight[:, columns],
-                    preferred_element_type=jnp.float32,
-                )
-                total = term if total is None else total + term
-        total = total.astype(jnp.bfloat16)
+        low = product(pl.ds(pl.multiple_of(start + offset, chunk), chunk))
+        high = product(pl.ds(pl.multiple_of(width // 2 + start + offset, chunk), chunk))
+        is_low = lax.broadcasted_iota(jnp.int32, (slots, 1), 0) % BLOCK < CAP
+        even = jnp.where(is_low, low, pltpu.roll(high, CAP, 0))
+        odd = jnp.where(is_low, pltpu.roll(low, slots - CAP, 0), high)
+        tiles = (slots // BLOCK, BLOCK, chunk)
+        total = jnp.stack([even.reshape(tiles), odd.reshape(tiles)], axis=1)
+        total = total.reshape(2 * slots, chunk).astype(jnp.bfloat16)
         for i, part in enumerate(parts):
             part[:, pl.ds(offset, chunk)] = total[i * block : (i + 1) * block]
 
@@ -231,7 +233,7 @@
 def backward_kernel(count, *refs):
     pieces = refs[:count]
     activated, slope, hidden, gate_w, up_w, down_w = refs[count : count + 6]
-    own, far, halves, gate_out, up_out, low_out, high_out, gates_out = refs[count + 6 :]
+    own, far, halves, gate_out, up_out, factors, gates_out = refs[count + 6 :]
     rows = halves.shape[0]
     gather_pieces(pieces, halves.shape[1], halves)
     back = project(down_w, halves)
@@ -239,10 +241,13 @@
     up_pre = back * activated[...]
     gate_pre = back * slope[...]
     both = jnp.concatenate([gate_pre, up_pre], axis=0)
-    low_out[...] = both.T.astype(jnp.bfloat16)
-    high_out[...] = pltpu.roll(both, CAP, 1).T.astype(jnp.bfloat16)
+    both = both.T
+    tiles = (rows // (2 * BLOCK), 2, BLOCK, both.shape[1])
+    even = both.reshape(tiles)[:, 0]
+    odd = pltpu.roll(both, CAP, 0).reshape(tiles)[:, 1]
+    factors[...] = (even + odd).reshape(factors.shape).astype(jnp.bfloat16)
     gate_column = jnp.broadcast_to(gate_terms, (LANES, rows)).T.astype(jnp.bfloat16)
-    row_grads(low_out, high_out, gate_w, up_w, (own, far), 0)
+    row_grads(factors, gate_w, up_w, (own, far), 0)
     gates_out[...] = gate_column
     gate_out[...] = gate_pre.astype(jnp.bfloat16)
     up_out[...] = up_pre.astype(jnp.bfloat16)
@@ -259,8 +264,7 @@
         (rows, width // 2),
         (units, rows),
         (units, rows),
-        (rows, 2 * units),
-        (rows, 2 * units),
+        (mine, 2 * units),
         (rows, LANES),
     ]
     return pl.pallas_call(
@@ -278,27 +282,27 @@
     )(*pieces, activated, slope, hidden, *weights)
 
 
-def rest_kernel(start, low, high, gates, gate_w, up_w, own, far):
+def rest_kernel(start, factors, gates, gate_w, up_w, own, far):
     mine, size = own.shape
     size -= LANES
     own[:, size:] = gates[:mine, :]
     far[:, size:] = gates[mine:, :]
     views = [part.at[:, pl.ds(0, size)] for part in (own, far)]
-    row_grads(low, high, gate_w, up_w, views, start)
-
-
-def rest_rows(start, low, high, gates, gate_w, up_w):
-    rows, width = low.shape[0], gate_w.shape[1]
+    row_grads(factors, gate_w, up_w, views, start)
+
+
+def rest_rows(start, factors, gates, gate_w, up_w):
+    rows, width = gates.shape[0], gate_w.shape[1]
     size = width // 2 - start + LANES
     return pl.pallas_call(
         functools.partial(rest_kernel, start),
         out_shape=[struct((rows // 2, size))] * 2,
-        in_specs=[VMEM] * 5,
+        in_specs=[VMEM] * 4,
         out_specs=[VMEM] * 2,
         compiler_params=pltpu.CompilerParams(vmem_limit_bytes=8 * MIB + 4 * rows * width),
         cost_estimate=LIGHT,
         name="rest_rows",
-    )(low, high, gates, gate_w, up_w)
+    )(factors, gates, gate_w, up_w)
 
 
 def sum_kernel(targets, own_left, own_right, left, right, *outs):
@@ -514,12 +518,12 @@
     ]
     token_halves, activated, slope, hidden = forward(pieces, weights[0], weights[1])
     size = width // 16 * 5
-    own_left, far_left, grad_halves, gate_f, up_f, low, high, gate_column = backward(
+    own_left, far_left, grad_halves, gate_f, up_f, factors, gate_column = backward(
         pieces, activated, slope, hidden, weights, size
     )
 
     left = flip(far_left, "dp", 1)
-    own_right, far_right = rest_rows(size, low, high, gate_column, weights[0], weights[1])
+    own_right, far_right = rest_rows(size, factors, gate_column, weights[0], weights[1])
     left, own_right = tie((left, own_right))
     right = flip(far_right, "dp", 1)
     targets = [

time: 61.1 us -> 60.1 us (0.984)
  Pallas kernels: 15.9 us -> 14.8 us
    pallas_call x1, Pallas kernels: 3.73 us -> 2.98 us  [backward(): pl.pallas_call(functools.partial(backward_kernel, count), out_shape=[stru...]
  transfers between devices with their start and end apart: 21 -> 21, of which waited for: 10 -> 11; matrix products, arithmetic and copies ran while one was open for 0% -> 0% of each run, Pallas kernels for 11% -> 11%
where the time goes in v11:
time: 60.1 us; the launch traced here: 59.8 us
  starting transfers between devices  24.3 us (40%)
  waiting for transfers between devices  18.9 us (31%)
  Pallas kernels  14.8 us (25%)
  local copies, waits for them, and re-layouts  0.99 us (2%)
  between operations  0.82 us (1%)
    ppermute x21, starting transfers between devices, flip(): return lax.ppermute(value, axis, [(i, i ^ bit) for i in range(size)])  24.3 us
    ppermute x21, waiting for transfers between devices, flip(): return lax.ppermute(value, axis, [(i, i ^ bit) for i in range(size)])  18.9 us
    pallas_call x2, Pallas kernels, weight_grads(): pl.pallas_call(functools.partial(weight_kernel, chunk, count), out_shape=...  5.05 us
    pallas_call x1, Pallas kernels, backward(): pl.pallas_call(functools.partial(backward_kernel, count), out_shape=[stru...  2.98 us
    pallas_call x1, Pallas kernels, dispatch(): pl.pallas_call(functools.partial(dispatch_kernel, n_targets), out_shape=[...  2.34 us
    pallas_call x1, Pallas kernels, forward(): pl.pallas_call(functools.partial(forward_kernel, count), out_shape=[struc...  1.96 us
  transfers between devices with their start and end apart: 21, of which 11 were waited for; matrix products, arithmetic and copies ran while one was open for 0% of the time, Pallas kernels for 11%

profile of v11, /device:TPU:0, one launch (start us, length us, event | category | flops | bytes accessed | tf_op | source)
XLA Modules:
  0.0 59.8 jit_solution(372501701543703854)
XLA Ops:
  0.6 2.3 %dispatch.1 = (bf16[8,4096]{1,0:T(8,128)(2,1)}, bf16[8,4096]{1,0:T(8,128)(2,1)}, bf16[8,4096]{1,0:T(8,128)(2,1)}, bf16[8,4096]{1,0:T(8,128)(2,1)}, bf16[8,4096]{...) custom-call(s32[8,32]{1,0:T(8,128)} %bitcast.18, ...), custom_call_target="tpu_custom_call" | custom-call | tf_op jit(solution)/shard_map/dispatch/pallas_call | solution.py:92
  3.0 3.0 %collective-permute-start = (bf16[8,4096]{1,0:T(8,128)(2,1)}, bf16[8,4096]{1,0:T(8,128)(2,1)S(1)}, u32[]{:S(2)}, u32[]{:S(2)}) collective-permute-start(bf16[8,4096]{1,0:T(8,128)(2,1)} %get-tuple-element.69), channel_id=1, source_target_pairs={{0,4},{4,0},{8,12},{12,8},{16,20},{20,16},{24,28},{28,24},{1,5},{5... | collective-permute-start | bytes 196616 | tf_op jit(solution)/shard_map/ppermute | solution.py:455
  6.0 2.6 %collective-permute-start.1 = (bf16[8,4096]{1,0:T(8,128)(2,1)}, bf16[8,4096]{1,0:T(8,128)(2,1)S(1)}, u32[]{:S(2)}, u32[]{:S(2)}) collective-permute-start(bf16[8,4096]{1,0:T(8,128)(2,1)} %get-tuple-element.70), channel_id=1, source_target_pairs={{0,16},{4,20},{8,24},{12,28},{16,0},{20,4},{24,8},{28,12},{1,17},{... | collective-permute-start | bytes 196616 | tf_op jit(solution)/shard_map/ppermute | solution.py:455
  8.6 1.6 %collective-permute-start.2 = (bf16[8,4096]{1,0:T(8,128)(2,1)}, bf16[8,4096]{1,0:T(8,128)(2,1)S(1)}, u32[]{:S(2)}, u32[]{:S(2)}) collective-permute-start(bf16[8,4096]{1,0:T(8,128)(2,1)} %get-tuple-element.71), channel_id=1, source_target_pairs={{0,8},{4,12},{8,0},{12,4},{16,24},{20,28},{24,16},{28,20},{1,9},{5... | collective-permute-start | bytes 196616 | tf_op jit(solution)/shard_map/ppermute | solution.py:455
  10.5 1.4 %collective-permute-start.4 = (bf16[8,4096]{1,0:T(8,128)(2,1)}, bf16[8,4096]{1,0:T(8,128)(2,1)S(1)}, u32[]{:S(2)}, u32[]{:S(2)}) collective-permute-start(bf16[8,4096]{1,0:T(8,128)(2,1)} %get-tuple-element.77), channel_id=1, source_target_pairs={{0,12},{4,8},{8,4},{12,0},{16,28},{20,24},{24,20},{28,16},{1,13},{... | collective-permute-start | bytes 196616 | tf_op jit(solution)/shard_map/ppermute | solution.py:455
  11.9 3.6 %collective-permute-start.5 = (bf16[8,4096]{1,0:T(8,128)(2,1)}, bf16[8,4096]{1,0:T(8,128)(2,1)S(1)}, u32[]{:S(2)}, u32[]{:S(2)}) collective-permute-start(bf16[8,4096]{1,0:T(8,128)(2,1)} %get-tuple-element.78), channel_id=1, source_target_pairs={{0,24},{4,28},{8,16},{12,20},{16,8},{20,12},{24,0},{28,4},{1,25},{... | collective-permute-start | bytes 196616 | tf_op jit(solution)/shard_map/ppermute | solution.py:455
  15.5 1.6 %collective-permute-start.6 = (bf16[8,4096]{1,0:T(8,128)(2,1)}, bf16[8,4096]{1,0:T(8,128)(2,1)S(1)}, u32[]{:S(2)}, u32[]{:S(2)}) collective-permute-start(bf16[8,4096]{1,0:T(8,128)(2,1)} %get-tuple-element.79), channel_id=1, source_target_pairs={{0,28},{4,24},{8,20},{12,16},{16,12},{20,8},{24,4},{28,0},{1,29},{... | collective-permute-start | bytes 196616 | tf_op jit(solution)/shard_map/ppermute | solution.py:455
  17.0 2.9 %collective-permute-done.3.refs_3_ = bf16[8,4096]{1,0:T(8,128)(2,1)S(1)} collective-permute-done((bf16[8,4096]{1,0:T(8,128)(2,1)}, bf16[8,4096]{1,0:T(8,128)(2,1)S(1)}, u32[]{:S(2)}, u32[]{:S(2)}) %collective-permute-start.3) | collective-permute-done | bytes 65568 | tf_op jit(solution)/shard_map/ppermute | solution.py:455
  20.0 1.6 %collective-permute-start.7 = (bf16[32,4096]{1,0:T(8,128)(2,1)S(1)}, bf16[32,4096]{1,0:T(8,128)(2,1)S(1)}, u32[]{:S(2)}, u32[]{:S(2)}) collective-permute-start(bf16[32,4096]{1,0:T(8,128)(2,1)S(1)} %pack.2.refs_0_), channel_id=1, source_target_pairs={{0,2},{1,3},{2,0},{3,1},{4,6},{5,7},{6,4},{7,5},{8,10},{9,11},{10,... | collective-permute-start | bytes 786440 | tf_op jit(solution)/shard_map/ppermute | solution.py:455
  22.9 1.4 %collective-permute-start.8 = (bf16[32,4096]{1,0:T(8,128)(2,1)S(1)}, bf16[32,4096]{1,0:T(8,128)(2,1)S(1)}, u32[]{:S(2)}, u32[]{:S(2)}) collective-permute-start(bf16[32,4096]{1,0:T(8,128)(2,1)S(1)} %pack.3.refs_1_), channel_id=1, source_target_pairs={{0,2},{1,3},{2,0},{3,1},{4,6},{5,7},{6,4},{7,5},{8,10},{9,11},{10,... | collective-permute-start | bytes 786440 | tf_op jit(solution)/shard_map/ppermute | solution.py:455
  24.2 3.8 %collective-permute-done.7.refs_2_ = bf16[32,4096]{1,0:T(8,128)(2,1)S(1)} collective-permute-done((bf16[32,4096]{1,0:T(8,128)(2,1)S(1)}, bf16[32,4096]{1,0:T(8,128)(2,1)S(1)}, u32[]{:S(2)}, u32[]{:S(2)}) %collective-permute-start.7) | collective-permute-done | bytes 262176 | tf_op jit(solution)/shard_map/ppermute | solution.py:455
  28.6 2.3 %collective-permute-done.8.refs_3_ = bf16[32,4096]{1,0:T(8,128)(2,1)S(1)} collective-permute-done((bf16[32,4096]{1,0:T(8,128)(2,1)S(1)}, bf16[32,4096]{1,0:T(8,128)(2,1)S(1)}, u32[]{:S(2)}, u32[]{:S(2)}) %collective-permute-start.8) | collective-permute-done | bytes 262176 | tf_op jit(solution)/shard_map/ppermute | solution.py:455
  31.0 1.5 %collective-permute-done.12.refs_7_ = bf16[32,4096]{1,0:T(8,128)(2,1)S(1)} collective-permute-done((bf16[32,4096]{1,0:T(8,128)(2,1)S(1)}, bf16[32,4096]{1,0:T(8,128)(2,1)S(1)}, u32[]{:S(2)}, u32[]{:S(2)}) %collective-permute-start.12) | collective-permute-done | bytes 262176 | tf_op jit(solution)/shard_map/ppermute | solution.py:455
  32.5 2.0 %forward.1 = (bf16[256,2048]{1,0:T(8,128)(2,1)S(1)}, f32[384,256]{1,0:T(8,128)S(1)}, f32[384,256]{1,0:T(8,128)S(1)}, bf16[384,256]{1,0:T(8,128)(2,1)S(1)}) custom-call(bf16[32,4096]{1,0:T(8,128)(2,1)S(1)} %pack.2.refs_0_, bf16[32,4096]{1,0:T(8,128)(2,1)S(1)} %pack.3.refs_1_, bf16[32,4096]{1,0:T(8,128)(2,1)S(1)} %collective-permute-done.7.refs_2_, ...), custom_call_target="tpu_custom_call" | custom-call | flops 1000000 | bytes 10000 | tf_op jit(solution)/shard_map/forward/pallas_call | solution.py:189
  34.5 3.0 %backward.1 = (bf16[128,1280]{1,0:T(8,128)(2,1)S(1)}, bf16[128,1280]{1,0:T(8,128)(2,1)S(1)}, bf16[256,2048]{1,0:T(8,128)(2,1)S(1)}, bf16[384,256]{1,0:T(8,128)(2...) custom-call(bf16[32,4096]{1,0:T(8,128)(2,1)S(1)} %pack.2.refs_0_, ...), custom_call_target="tpu_custom_call" | custom-call | flops 1000000 | bytes 10000 | tf_op jit(solution)/shard_map/backward/pallas_call | solution.py:270
  40.3 1.6 %collective-permute-start.16 = (bf16[32,2176]{1,0:T(8,128)(2,1)S(1)}, bf16[32,2176]{1,0:T(8,128)(2,1)S(1)}, u32[]{:S(2)}, u32[]{:S(2)}) collective-permute-start(bf16[32,2176]{1,0:T(8,128)(2,1)S(1)} %get-tuple-element.109), channel_id=1, source_target_pairs={{0,2},{1,3},{2,0},{3,1},{4,6},{5,7},{6,4},{7,5},{8,10},{9,11},{10,... | collective-permute-start | bytes 417800 | tf_op jit(solution)/shard_map/ppermute | solution.py:455
  42.4 3.1 %weight_grads.2 = (bf16[384,4096]{1,0:T(8,128)(2,1)}, bf16[384,4096]{1,0:T(8,128)(2,1)}) custom-call(bf16[384,256]{1,0:T(8,128)(2,1)S(1)} %get-tuple-element.112.refs_0_, bf16[384,256]{1,0:T(8,128)(2,1)S(1)} %get-tuple-element.113.refs_1_, bf16[256,2048]{1,0:T(8,128)(2,1)S(1)} %get-tuple-element.114.refs_2_), custom_call_target="tpu_custom_call" | custom-call | flops 1000000 | bytes 10000 | tf_op jit(solution)/shard_map/weight_grads/pallas_call | solution.py:402
  45.5 1.4 %collective-permute-done.16.right = bf16[32,2176]{1,0:T(8,128)(2,1)S(1)} collective-permute-done((bf16[32,2176]{1,0:T(8,128)(2,1)S(1)}, bf16[32,2176]{1,0:T(8,128)(2,1)S(1)}, u32[]{:S(2)}, u32[]{:S(2)}) %collective-permute-start.16) | collective-permute-done | bytes 139296 | tf_op jit(solution)/shard_map/ppermute | solution.py:455
  47.3 2.0 %weight_grads.3 = bf16[384,4096]{1,0:T(8,128)(2,1)} custom-call(bf16[384,256]{1,0:T(8,128)(2,1)S(1)} %get-tuple-element.118.refs_10_.refs_0_, bf16[256,2048]{1,0:T(8,128)(2,1)S(1)} %get-tuple-element.119.refs_1_), custom_call_target="tpu_custom_call" | custom-call | flops 1000000 | bytes 10000 | tf_op jit(solution)/shard_map/weight_grads/pallas_call | solution.py:402
  49.4 2.7 %collective-permute-done.17.passed = bf16[32,2176]{1,0:T(8,128)(2,1)S(1)} collective-permute-done((bf16[32,2176]{1,0:T(8,128)(2,1)S(1)}, bf16[32,2176]{1,0:T(8,128)(2,1)S(1)}, u32[]{:S(2)}, u32[]{:S(2)}) %collective-permute-start.17) | collective-permute-done | bytes 139296 | tf_op jit(solution)/shard_map/ppermute | solution.py:455
  52.2 1.3 %collective-permute-start.19 = (bf16[16,2176]{1,0:T(8,128)(2,1)S(1)}, bf16[16,2176]{1,0:T(8,128)(2,1)S(1)}, u32[]{:S(2)}, u32[]{:S(2)}) collective-permute-start(bf16[16,2176]{1,0:T(8,128)(2,1)S(1)} %get-tuple-element.125), channel_id=1, source_target_pairs={{0,24},{4,28},{8,16},{12,20},{16,8},{20,12},{24,0},{28,4},{1,25},{... | collective-permute-start | bytes 208904 | tf_op jit(solution)/shard_map/ppermute | solution.py:455
  53.5 2.1 %collective-permute-start.20 = (bf16[16,2176]{1,0:T(8,128)(2,1)S(1)}, bf16[16,2176]{1,0:T(8,128)(2,1)S(1)}, u32[]{:S(2)}, u32[]{:S(2)}) collective-permute-start(bf16[16,2176]{1,0:T(8,128)(2,1)S(1)} %get-tuple-element.126), channel_id=1, source_target_pairs={{0,8},{4,12},{8,0},{12,4},{16,24},{20,28},{24,16},{28,20},{1,9},{5... | collective-permute-start | bytes 208904 | tf_op jit(solution)/shard_map/ppermute | solution.py:455
  55.7 1.7 %collective-permute-done.18.refs_0_ = bf16[16,2176]{1,0:T(8,128)(2,1)S(1)} collective-permute-done((bf16[16,2176]{1,0:T(8,128)(2,1)S(1)}, bf16[16,2176]{1,0:T(8,128)(2,1)S(1)}, u32[]{:S(2)}, u32[]{:S(2)}) %collective-permute-start.18) | collective-permute-done | bytes 69664 | tf_op jit(solution)/shard_map/ppermute | solution.py:455
  57.4 1.1 %collective-permute-done.19.refs_1_ = bf16[16,2176]{1,0:T(8,128)(2,1)S(1)} collective-permute-done((bf16[16,2176]{1,0:T(8,128)(2,1)S(1)}, bf16[16,2176]{1,0:T(8,128)(2,1)S(1)}, u32[]{:S(2)}, u32[]{:S(2)}) %collective-permute-start.19) | collective-permute-done | bytes 69664 | tf_op jit(solution)/shard_map/ppermute | solution.py:455
  (44 shorter events, 7.4 us)
Async XLA Ops:
  3.0 8.9 %collective-permute-start = (bf16[8,4096]{1,0:T(8,128)(2,1)}, bf16[8,4096]{1,0:T(8,128)(2,1)S(1)}, u32[]{:S(2)}, u32[]{:S(2)}) collective-permute-start(bf16[8,4096]{1,0:T(8,128)(2,1)} %get-tuple-element.69), channel_id=1, source_target_pairs={{0,4},{4,0},{8,12},{12,8},{16,20},{20,16},{24,28},{28,24},{1,5},{5... | collective-permute-start | bytes 196616 | tf_op jit(solution)/shard_map/ppermute | solution.py:455
  6.0 9.5 %collective-permute-start.1 = (bf16[8,4096]{1,0:T(8,128)(2,1)}, bf16[8,4096]{1,0:T(8,128)(2,1)S(1)}, u32[]{:S(2)}, u32[]{:S(2)}) collective-permute-start(bf16[8,4096]{1,0:T(8,128)(2,1)} %get-tuple-element.70), channel_id=1, source_target_pairs={{0,16},{4,20},{8,24},{12,28},{16,0},{20,4},{24,8},{28,12},{1,17},{... | collective-permute-start | bytes 196616 | tf_op jit(solution)/shard_map/ppermute | solution.py:455
  8.6 8.4 %collective-permute-start.2 = (bf16[8,4096]{1,0:T(8,128)(2,1)}, bf16[8,4096]{1,0:T(8,128)(2,1)S(1)}, u32[]{:S(2)}, u32[]{:S(2)}) collective-permute-start(bf16[8,4096]{1,0:T(8,128)(2,1)} %get-tuple-element.71), channel_id=1, source_target_pairs={{0,8},{4,12},{8,0},{12,4},{16,24},{20,28},{24,16},{28,20},{1,9},{5... | collective-permute-start | bytes 196616 | tf_op jit(solution)/shard_map/ppermute | solution.py:455
  10.2 9.8 %collective-permute-start.3 = (bf16[8,4096]{1,0:T(8,128)(2,1)}, bf16[8,4096]{1,0:T(8,128)(2,1)S(1)}, u32[]{:S(2)}, u32[]{:S(2)}) collective-permute-start(bf16[8,4096]{1,0:T(8,128)(2,1)} %get-tuple-element.72), channel_id=1, source_target_pairs={{0,20},{4,16},{8,28},{12,24},{16,4},{20,0},{24,12},{28,8},{1,21},{... | collective-permute-start | bytes 196616 | tf_op jit(solution)/shard_map/ppermute | solution.py:455
  10.5 12.3 %collective-permute-start.4 = (bf16[8,4096]{1,0:T(8,128)(2,1)}, bf16[8,4096]{1,0:T(8,128)(2,1)S(1)}, u32[]{:S(2)}, u32[]{:S(2)}) collective-permute-start(bf16[8,4096]{1,0:T(8,128)(2,1)} %get-tuple-element.77), channel_id=1, source_target_pairs={{0,12},{4,8},{8,4},{12,0},{16,28},{20,24},{24,20},{28,16},{1,13},{... | collective-permute-start | bytes 196616 | tf_op jit(solution)/shard_map/ppermute | solution.py:455
  11.9 10.9 %collective-permute-start.5 = (bf16[8,4096]{1,0:T(8,128)(2,1)}, bf16[8,4096]{1,0:T(8,128)(2,1)S(1)}, u32[]{:S(2)}, u32[]{:S(2)}) collective-permute-start(bf16[8,4096]{1,0:T(8,128)(2,1)} %get-tuple-element.78), channel_id=1, source_target_pairs={{0,24},{4,28},{8,16},{12,20},{16,8},{20,12},{24,0},{28,4},{1,25},{... | collective-permute-start | bytes 196616 | tf_op jit(solution)/shard_map/ppermute | solution.py:455
  15.5 7.3 %collective-permute-start.6 = (bf16[8,4096]{1,0:T(8,128)(2,1)}, bf16[8,4096]{1,0:T(8,128)(2,1)S(1)}, u32[]{:S(2)}, u32[]{:S(2)}) collective-permute-start(bf16[8,4096]{1,0:T(8,128)(2,1)} %get-tuple-element.79), channel_id=1, source_target_pairs={{0,28},{4,24},{8,20},{12,16},{16,12},{20,8},{24,4},{28,0},{1,29},{... | collective-permute-start | bytes 196616 | tf_op jit(solution)/shard_map/ppermute | solution.py:455
  20.0 12.5 %copy-start = (bf16[1,384,4096]{2,1,0:T(8,128)(2,1)S(1)}, bf16[1,384,4096]{2,1,0:T(8,128)(2,1)}, u32[]{:S(2)}) copy-start(bf16[1,384,4096]{2,1,0:T(8,128)(2,1)} %param.11) | copy-start | bytes 9437188
  20.0 12.5 %copy-start.1 = (bf16[1,384,4096]{2,1,0:T(8,128)(2,1)S(1)}, bf16[1,384,4096]{2,1,0:T(8,128)(2,1)}, u32[]{:S(2)}) copy-start(bf16[1,384,4096]{2,1,0:T(8,128)(2,1)} %param.12) | copy-start | bytes 9437188
  20.0 8.0 %collective-permute-start.7 = (bf16[32,4096]{1,0:T(8,128)(2,1)S(1)}, bf16[32,4096]{1,0:T(8,128)(2,1)S(1)}, u32[]{:S(2)}, u32[]{:S(2)}) collective-permute-start(bf16[32,4096]{1,0:T(8,128)(2,1)S(1)} %pack.2.refs_0_), channel_id=1, source_target_pairs={{0,2},{1,3},{2,0},{3,1},{4,6},{5,7},{6,4},{7,5},{8,10},{9,11},{10,... | collective-permute-start | bytes 786440 | tf_op jit(solution)/shard_map/ppermute | solution.py:455
  22.9 8.0 %collective-permute-start.8 = (bf16[32,4096]{1,0:T(8,128)(2,1)S(1)}, bf16[32,4096]{1,0:T(8,128)(2,1)S(1)}, u32[]{:S(2)}, u32[]{:S(2)}) collective-permute-start(bf16[32,4096]{1,0:T(8,128)(2,1)S(1)} %pack.3.refs_1_), channel_id=1, source_target_pairs={{0,2},{1,3},{2,0},{3,1},{4,6},{5,7},{6,4},{7,5},{8,10},{9,11},{10,... | collective-permute-start | bytes 786440 | tf_op jit(solution)/shard_map/ppermute | solution.py:455
  28.1 2.8 %collective-permute-start.9 = (bf16[32,4096]{1,0:T(8,128)(2,1)S(1)}, bf16[32,4096]{1,0:T(8,128)(2,1)S(1)}, u32[]{:S(2)}, u32[]{:S(2)}) collective-permute-start(bf16[32,4096]{1,0:T(8,128)(2,1)S(1)} %pack.2.refs_0_), channel_id=1, source_target_pairs={{0,1},{1,0},{2,3},{3,2},{4,5},{5,4},{6,7},{7,6},{8,9},{9,8},{10,11... | collective-permute-start | bytes 786440 | tf_op jit(solution)/shard_map/ppermute | solution.py:455
  28.1 2.8 %collective-permute-start.10 = (bf16[32,4096]{1,0:T(8,128)(2,1)S(1)}, bf16[32,4096]{1,0:T(8,128)(2,1)S(1)}, u32[]{:S(2)}, u32[]{:S(2)}) collective-permute-start(bf16[32,4096]{1,0:T(8,128)(2,1)S(1)} %collective-permute-done.7.refs_2_), channel_id=1, source_target_pairs={{0,1},{1,0},{2,3},{3,2},{4,5},{5,4},{6,7},{7,6},{8,9},{9,8},{10,11... | collective-permute-start | bytes 786440 | tf_op jit(solution)/shard_map/ppermute | solution.py:455
  28.6 2.3 %collective-permute-start.11 = (bf16[32,4096]{1,0:T(8,128)(2,1)S(1)}, bf16[32,4096]{1,0:T(8,128)(2,1)S(1)}, u32[]{:S(2)}, u32[]{:S(2)}) collective-permute-start(bf16[32,4096]{1,0:T(8,128)(2,1)S(1)} %pack.3.refs_1_), channel_id=1, source_target_pairs={{0,1},{1,0},{2,3},{3,2},{4,5},{5,4},{6,7},{7,6},{8,9},{9,8},{10,11... | collective-permute-start | bytes 786440 | tf_op jit(solution)/shard_map/ppermute | solution.py:455
  30.9 1.6 %collective-permute-start.12 = (bf16[32,4096]{1,0:T(8,128)(2,1)S(1)}, bf16[32,4096]{1,0:T(8,128)(2,1)S(1)}, u32[]{:S(2)}, u32[]{:S(2)}) collective-permute-start(bf16[32,4096]{1,0:T(8,128)(2,1)S(1)} %collective-permute-done.8.refs_3_), channel_id=1, source_target_pairs={{0,1},{1,0},{2,3},{3,2},{4,5},{5,4},{6,7},{7,6},{8,9},{9,8},{10,11... | collective-permute-start | bytes 786440 | tf_op jit(solution)/shard_map/ppermute | solution.py:455
  37.5 1.7 %collective-permute-start.13 = (bf16[128,1280]{1,0:T(8,128)(2,1)S(1)}, bf16[128,1280]{1,0:T(8,128)(2,1)S(1)}, u32[]{:S(2)}, u32[]{:S(2)}) collective-permute-start(bf16[128,1280]{1,0:T(8,128)(2,1)S(1)} %get-tuple-element.99), channel_id=1, source_target_pairs={{0,1},{1,0},{2,3},{3,2},{4,5},{5,4},{6,7},{7,6},{8,9},{9,8},{10,11... | collective-permute-start | bytes 983048 | tf_op jit(solution)/shard_map/ppermute | solution.py:455
  38.6 1.6 %collective-permute-start.14 = (bf16[128,896]{1,0:T(8,128)(2,1)S(1)}, bf16[128,896]{1,0:T(8,128)(2,1)S(1)}, u32[]{:S(2)}, u32[]{:S(2)}) collective-permute-start(bf16[128,896]{1,0:T(8,128)(2,1)S(1)} %get-tuple-element.105), channel_id=1, source_target_pairs={{0,1},{1,0},{2,3},{3,2},{4,5},{5,4},{6,7},{7,6},{8,9},{9,8},{10,11... | collective-permute-start | bytes 688136 | tf_op jit(solution)/shard_map/ppermute | solution.py:455
  40.3 6.6 %collective-permute-start.16 = (bf16[32,2176]{1,0:T(8,128)(2,1)S(1)}, bf16[32,2176]{1,0:T(8,128)(2,1)S(1)}, u32[]{:S(2)}, u32[]{:S(2)}) collective-permute-start(bf16[32,2176]{1,0:T(8,128)(2,1)S(1)} %get-tuple-element.109), channel_id=1, source_target_pairs={{0,2},{1,3},{2,0},{3,1},{4,6},{5,7},{6,4},{7,5},{8,10},{9,11},{10,... | collective-permute-start | bytes 417800 | tf_op jit(solution)/shard_map/ppermute | solution.py:455
  41.9 7.4 %collective-permute-start.15 = (bf16[32,2176]{1,0:T(8,128)(2,1)S(1)}, bf16[32,2176]{1,0:T(8,128)(2,1)S(1)}, u32[]{:S(2)}, u32[]{:S(2)}) collective-permute-start(bf16[32,2176]{1,0:T(8,128)(2,1)S(1)} %get-tuple-element.107), channel_id=1, source_target_pairs={{0,2},{1,3},{2,0},{3,1},{4,6},{5,7},{6,4},{7,5},{8,10},{9,11},{10,... | collective-permute-start | bytes 417800 | tf_op jit(solution)/shard_map/ppermute | solution.py:455
  42.4 16.4 %copy-start.4 = (bf16[32,8]{0,1:T(8,128)(2,1)S(1)}, bf16[32,8]{0,1:T(8,128)(2,1)}, u32[]{:S(2)}) copy-start(bf16[32,8]{0,1:T(8,128)(2,1)} %param.9) | copy-start | bytes 1540
  46.9 5.1 %collective-permute-start.17 = (bf16[32,2176]{1,0:T(8,128)(2,1)S(1)}, bf16[32,2176]{1,0:T(8,128)(2,1)S(1)}, u32[]{:S(2)}, u32[]{:S(2)}) collective-permute-start(bf16[32,2176]{1,0:T(8,128)(2,1)S(1)} %add_rows.2), channel_id=1, source_target_pairs={{0,4},{4,0},{8,12},{12,8},{16,20},{20,16},{24,28},{28,24},{1,5},{5... | collective-permute-start | bytes 417800 | tf_op jit(solution)/shard_map/ppermute | solution.py:455
  52.1 5.3 %collective-permute-start.18 = (bf16[16,2176]{1,0:T(8,128)(2,1)S(1)}, bf16[16,2176]{1,0:T(8,128)(2,1)S(1)}, u32[]{:S(2)}, u32[]{:S(2)}) collective-permute-start(bf16[16,2176]{1,0:T(8,128)(2,1)S(1)} %get-tuple-element.124), channel_id=1, source_target_pairs={{0,16},{4,20},{8,24},{12,28},{16,0},{20,4},{24,8},{28,12},{1,17},{... | collective-permute-start | bytes 208904 | tf_op jit(solution)/shard_map/ppermute | solution.py:455
  52.2 6.3 %collective-permute-start.19 = (bf16[16,2176]{1,0:T(8,128)(2,1)S(1)}, bf16[16,2176]{1,0:T(8,128)(2,1)S(1)}, u32[]{:S(2)}, u32[]{:S(2)}) collective-permute-start(bf16[16,2176]{1,0:T(8,128)(2,1)S(1)} %get-tuple-element.125), channel_id=1, source_target_pairs={{0,24},{4,28},{8,16},{12,20},{16,8},{20,12},{24,0},{28,4},{1,25},{... | collective-permute-start | bytes 208904 | tf_op jit(solution)/shard_map/ppermute | solution.py:455
  53.5 5.3 %collective-permute-start.20 = (bf16[16,2176]{1,0:T(8,128)(2,1)S(1)}, bf16[16,2176]{1,0:T(8,128)(2,1)S(1)}, u32[]{:S(2)}, u32[]{:S(2)}) collective-permute-start(bf16[16,2176]{1,0:T(8,128)(2,1)S(1)} %get-tuple-element.126), channel_id=1, source_target_pairs={{0,8},{4,12},{8,0},{12,4},{16,24},{20,28},{24,16},{28,20},{1,9},{5... | collective-permute-start | bytes 208904 | tf_op jit(solution)/shard_map/ppermute | solution.py:455
  (3 other events, 5.7 us)

commit v12 on v11

--- a/solution.py
+++ b/solution.py
@@ -332,18 +332,22 @@
     )(*own, *other)
 
 
-def add_kernel(left, right, out):
-    total = left[...].astype(jnp.float32) + right[...].astype(jnp.float32)
-    out[...] = total.astype(jnp.bfloat16)
-
-
-def add_rows(left, right):
+def add_kernel(left, right, *outs):
+    total = (left[...].astype(jnp.float32) + right[...].astype(jnp.float32)).astype(jnp.bfloat16)
+    base = 0
+    for out in outs:
+        out[...] = total[base : base + out.shape[0]]
+        base += out.shape[0]
+
+
+def add_rows(left, right, pieces):
+    rows, width = left.shape
     return pl.pallas_call(
         add_kernel,
-        out_shape=struct(left.shape),
+        out_shape=[struct((piece, width)) for piece in pieces],
         in_specs=[VMEM] * 2,
-        out_specs=VMEM,
-        compiler_params=pltpu.CompilerParams(vmem_limit_bytes=4 * MIB + 16 * left.size),
+        out_specs=[VMEM] * len(pieces),
+        compiler_params=pltpu.CompilerParams(vmem_limit_bytes=4 * MIB + 16 * rows * width),
         name="add_rows",
     )(left, right)
 
@@ -415,9 +419,15 @@
 
 
 def combine_kernel(n_targets, first, second, choice_ref, gates_ref, *refs):
-    blocks, (token_ref, gate_ref) = refs[: n_targets // 2], refs[n_targets // 2 :]
-    even = return_offsets(n_targets)[1]
-    back = jnp.concatenate([blocks[even.index(k)][...] for k in range(0, n_targets, 2)], axis=0)
+    blocks, (token_ref, gate_ref) = refs[:-2], refs[-2:]
+    odd, even = return_offsets(n_targets)
+    far = n_targets // 4
+    placed = {}
+    for k, block in zip(odd[:far] + even[:far], blocks):
+        placed[k] = block[...]
+    for k, block in zip(even[far:], blocks[2 * far :]):
+        placed[k], placed[k ^ 1] = block[:BLOCK, :], block[BLOCK:, :]
+    back = jnp.concatenate([placed[k] for k in range(n_targets)], axis=0)
     half = token_ref.shape[1] // 2
     choices, tokens = gates_ref.shape
     rows = back[:, :half]
@@ -436,7 +446,7 @@
 
 
 def combine(table, gates, blocks, width):
-    n_targets = 2 * len(blocks)
+    n_targets = len(blocks) // 3 * 4
     choices, tokens = gates.shape
     return pl.pallas_call(
         functools.partial(combine_kernel, n_targets),
@@ -546,14 +556,20 @@
                 sums.append((held[0], moved[bit]))
             else:
                 for mask in masks:
-                    held[mask ^ bit] = add_rows(held[mask ^ bit], moved[mask])
-    passed = add_rows(*sums[0])
-    hidden, _ = tie((hidden, passed))
+                    both = (held[mask ^ bit], moved[mask])
+                    (held[mask ^ bit],) = add_rows(*both, both[0].shape[:1])
+    far = n_targets // 4
+    rows = [BLOCK] * far + [BLOCK * far]
+    *far_odd, passed = add_rows(*sums[0], rows)
+    passed = flip(passed, "expert", 1)
+    far_odd = exchange(far_odd, odd[:far])
+    far_odd[0], moved = tie((far_odd[0], sums[1][1]))
+    *far_even, kept = add_rows(sums[1][0], moved, rows)
+    merged = list(merge_rows(kept, passed))
+    hidden, _ = tie((hidden, merged))
     (grad_down,) = weight_grads((hidden,), grad_halves)
-    passed = flip(passed, "expert", 1)
-    kept, moved, grad_down = tie((*sums[1], grad_down))
-    kept, passed = tie((add_rows(kept, moved), passed))
-    returned = exchange(merge_rows(kept, passed), even)
+    returned = far_odd + exchange(far_even + merged, even)
+    returned, grad_down = tie((returned, grad_down))
     token_grad, gate_grad = combine(table, gates, returned, width)
     grads = (grad_gate, grad_up, grad_down)
     return (token_grad, gate_grad.T, *(grad[None] for grad in grads))

time: 60.1 us -> 64.8 us (1.078)
  waiting for transfers between devices: 18.9 us -> 22.1 us
  starting transfers between devices: 24.3 us -> 25.8 us
    ppermute x21 -> x23, waiting for transfers between devices: 18.9 us -> 22.1 us  [flip(): return lax.ppermute(value, axis, [(i, i ^ bit) for i in range(size)])]
    ppermute x21 -> x23, starting transfers between devices: 24.3 us -> 25.8 us  [flip(): return lax.ppermute(value, axis, [(i, i ^ bit) for i in range(size)])]
  transfers between devices with their start and end apart: 21 -> 23, of which waited for: 11 -> 11; matrix products, arithmetic and copies ran while one was open for 0% -> 0% of each run, Pallas kernels for 11% -> 10%
where the time goes in v12:
time: 64.8 us; the launch traced here: 64.5 us
  starting transfers between devices  25.8 us (40%)
  waiting for transfers between devices  22.1 us (34%)
  Pallas kernels  14.8 us (23%)
  local copies, waits for them, and re-layouts  0.99 us (2%)
  between operations  0.83 us (1%)
    ppermute x23, starting transfers between devices, flip(): return lax.ppermute(value, axis, [(i, i ^ bit) for i in range(size)])  25.8 us
    ppermute x23, waiting for transfers between devices, flip(): return lax.ppermute(value, axis, [(i, i ^ bit) for i in range(size)])  22.1 us
    pallas_call x2, Pallas kernels, weight_grads(): pl.pallas_call(functools.partial(weight_kernel, chunk, count), out_shape=...  5.05 us
    pallas_call x1, Pallas kernels, backward(): pl.pallas_call(functools.partial(backward_kernel, count), out_shape=[stru...  2.98 us
    pallas_call x1, Pallas kernels, dispatch(): pl.pallas_call(functools.partial(dispatch_kernel, n_targets), out_shape=[...  2.34 us
    pallas_call x1, Pallas kernels, forward(): pl.pallas_call(functools.partial(forward_kernel, count), out_shape=[struc...  1.96 us
  transfers between devices with their start and end apart: 23, of which 11 were waited for; matrix products, arithmetic and copies ran while one was open for 0% of the time, Pallas kernels for 10%

profile of v12, /device:TPU:0, one launch (start us, length us, event | category | flops | bytes accessed | tf_op | source)
XLA Modules:
  0.0 64.5 jit_solution(635995631415287532)
XLA Ops:
  0.6 2.3 %dispatch.1 = (bf16[8,4096]{1,0:T(8,128)(2,1)}, bf16[8,4096]{1,0:T(8,128)(2,1)}, bf16[8,4096]{1,0:T(8,128)(2,1)}, bf16[8,4096]{1,0:T(8,128)(2,1)}, bf16[8,4096]{...) custom-call(s32[8,32]{1,0:T(8,128)} %bitcast.18, ...), custom_call_target="tpu_custom_call" | custom-call | tf_op jit(solution)/shard_map/dispatch/pallas_call | solution.py:92
  3.0 3.0 %collective-permute-start = (bf16[8,4096]{1,0:T(8,128)(2,1)}, bf16[8,4096]{1,0:T(8,128)(2,1)S(1)}, u32[]{:S(2)}, u32[]{:S(2)}) collective-permute-start(bf16[8,4096]{1,0:T(8,128)(2,1)} %get-tuple-element.77), channel_id=1, source_target_pairs={{0,4},{4,0},{8,12},{12,8},{16,20},{20,16},{24,28},{28,24},{1,5},{5... | collective-permute-start | bytes 196616 | tf_op jit(solution)/shard_map/ppermute | solution.py:465
  6.0 2.6 %collective-permute-start.1 = (bf16[8,4096]{1,0:T(8,128)(2,1)}, bf16[8,4096]{1,0:T(8,128)(2,1)S(1)}, u32[]{:S(2)}, u32[]{:S(2)}) collective-permute-start(bf16[8,4096]{1,0:T(8,128)(2,1)} %get-tuple-element.78), channel_id=1, source_target_pairs={{0,16},{4,20},{8,24},{12,28},{16,0},{20,4},{24,8},{28,12},{1,17},{... | collective-permute-start | bytes 196616 | tf_op jit(solution)/shard_map/ppermute | solution.py:465
  8.6 1.6 %collective-permute-start.2 = (bf16[8,4096]{1,0:T(8,128)(2,1)}, bf16[8,4096]{1,0:T(8,128)(2,1)S(1)}, u32[]{:S(2)}, u32[]{:S(2)}) collective-permute-start(bf16[8,4096]{1,0:T(8,128)(2,1)} %get-tuple-element.79), channel_id=1, source_target_pairs={{0,8},{4,12},{8,0},{12,4},{16,24},{20,28},{24,16},{28,20},{1,9},{5... | collective-permute-start | bytes 196616 | tf_op jit(solution)/shard_map/ppermute | solution.py:465
  10.5 1.4 %collective-permute-start.4 = (bf16[8,4096]{1,0:T(8,128)(2,1)}, bf16[8,4096]{1,0:T(8,128)(2,1)S(1)}, u32[]{:S(2)}, u32[]{:S(2)}) collective-permute-start(bf16[8,4096]{1,0:T(8,128)(2,1)} %get-tuple-element.85), channel_id=1, source_target_pairs={{0,12},{4,8},{8,4},{12,0},{16,28},{20,24},{24,20},{28,16},{1,13},{... | collective-permute-start | bytes 196616 | tf_op jit(solution)/shard_map/ppermute | solution.py:465
  11.9 3.6 %collective-permute-start.5 = (bf16[8,4096]{1,0:T(8,128)(2,1)}, bf16[8,4096]{1,0:T(8,128)(2,1)S(1)}, u32[]{:S(2)}, u32[]{:S(2)}) collective-permute-start(bf16[8,4096]{1,0:T(8,128)(2,1)} %get-tuple-element.86), channel_id=1, source_target_pairs={{0,24},{4,28},{8,16},{12,20},{16,8},{20,12},{24,0},{28,4},{1,25},{... | collective-permute-start | bytes 196616 | tf_op jit(solution)/shard_map/ppermute | solution.py:465
  15.5 1.6 %collective-permute-start.6 = (bf16[8,4096]{1,0:T(8,128)(2,1)}, bf16[8,4096]{1,0:T(8,128)(2,1)S(1)}, u32[]{:S(2)}, u32[]{:S(2)}) collective-permute-start(bf16[8,4096]{1,0:T(8,128)(2,1)} %get-tuple-element.87), channel_id=1, source_target_pairs={{0,28},{4,24},{8,20},{12,16},{16,12},{20,8},{24,4},{28,0},{1,29},{... | collective-permute-start | bytes 196616 | tf_op jit(solution)/shard_map/ppermute | solution.py:465
  17.0 2.9 %collective-permute-done.3.refs_3_ = bf16[8,4096]{1,0:T(8,128)(2,1)S(1)} collective-permute-done((bf16[8,4096]{1,0:T(8,128)(2,1)}, bf16[8,4096]{1,0:T(8,128)(2,1)S(1)}, u32[]{:S(2)}, u32[]{:S(2)}) %collective-permute-start.3) | collective-permute-done | bytes 65568 | tf_op jit(solution)/shard_map/ppermute | solution.py:465
  20.0 1.6 %collective-permute-start.7 = (bf16[32,4096]{1,0:T(8,128)(2,1)S(1)}, bf16[32,4096]{1,0:T(8,128)(2,1)S(1)}, u32[]{:S(2)}, u32[]{:S(2)}) collective-permute-start(bf16[32,4096]{1,0:T(8,128)(2,1)S(1)} %pack.2.refs_0_), channel_id=1, source_target_pairs={{0,2},{1,3},{2,0},{3,1},{4,6},{5,7},{6,4},{7,5},{8,10},{9,11},{10,... | collective-permute-start | bytes 786440 | tf_op jit(solution)/shard_map/ppermute | solution.py:465
  22.9 1.4 %collective-permute-start.8 = (bf16[32,4096]{1,0:T(8,128)(2,1)S(1)}, bf16[32,4096]{1,0:T(8,128)(2,1)S(1)}, u32[]{:S(2)}, u32[]{:S(2)}) collective-permute-start(bf16[32,4096]{1,0:T(8,128)(2,1)S(1)} %pack.3.refs_1_), channel_id=1, source_target_pairs={{0,2},{1,3},{2,0},{3,1},{4,6},{5,7},{6,4},{7,5},{8,10},{9,11},{10,... | collective-permute-start | bytes 786440 | tf_op jit(solution)/shard_map/ppermute | solution.py:465
  24.3 3.8 %collective-permute-done.7.refs_2_ = bf16[32,4096]{1,0:T(8,128)(2,1)S(1)} collective-permute-done((bf16[32,4096]{1,0:T(8,128)(2,1)S(1)}, bf16[32,4096]{1,0:T(8,128)(2,1)S(1)}, u32[]{:S(2)}, u32[]{:S(2)}) %collective-permute-start.7) | collective-permute-done | bytes 262176 | tf_op jit(solution)/shard_map/ppermute | solution.py:465
  28.6 2.3 %collective-permute-done.8.refs_3_ = bf16[32,4096]{1,0:T(8,128)(2,1)S(1)} collective-permute-done((bf16[32,4096]{1,0:T(8,128)(2,1)S(1)}, bf16[32,4096]{1,0:T(8,128)(2,1)S(1)}, u32[]{:S(2)}, u32[]{:S(2)}) %collective-permute-start.8) | collective-permute-done | bytes 262176 | tf_op jit(solution)/shard_map/ppermute | solution.py:465
  31.0 1.5 %collective-permute-done.12.refs_7_ = bf16[32,4096]{1,0:T(8,128)(2,1)S(1)} collective-permute-done((bf16[32,4096]{1,0:T(8,128)(2,1)S(1)}, bf16[32,4096]{1,0:T(8,128)(2,1)S(1)}, u32[]{:S(2)}, u32[]{:S(2)}) %collective-permute-start.12) | collective-permute-done | bytes 262176 | tf_op jit(solution)/shard_map/ppermute | solution.py:465
  32.5 2.0 %forward.1 = (bf16[256,2048]{1,0:T(8,128)(2,1)S(1)}, f32[384,256]{1,0:T(8,128)S(1)}, f32[384,256]{1,0:T(8,128)S(1)}, bf16[384,256]{1,0:T(8,128)(2,1)S(1)}) custom-call(bf16[32,4096]{1,0:T(8,128)(2,1)S(1)} %pack.2.refs_0_, bf16[32,4096]{1,0:T(8,128)(2,1)S(1)} %pack.3.refs_1_, bf16[32,4096]{1,0:T(8,128)(2,1)S(1)} %collective-permute-done.7.refs_2_, ...), custom_call_target="tpu_custom_call" | custom-call | flops 1000000 | bytes 10000 | tf_op jit(solution)/shard_map/forward/pallas_call | solution.py:189
  34.5 3.0 %backward.1 = (bf16[128,1280]{1,0:T(8,128)(2,1)S(1)}, bf16[128,1280]{1,0:T(8,128)(2,1)S(1)}, bf16[256,2048]{1,0:T(8,128)(2,1)S(1)}, bf16[384,256]{1,0:T(8,128)(2...) custom-call(bf16[32,4096]{1,0:T(8,128)(2,1)S(1)} %pack.2.refs_0_, ...), custom_call_target="tpu_custom_call" | custom-call | flops 1000000 | bytes 10000 | tf_op jit(solution)/shard_map/backward/pallas_call | solution.py:270
  40.3 1.6 %collective-permute-start.15 = (bf16[32,2176]{1,0:T(8,128)(2,1)S(1)}, bf16[32,2176]{1,0:T(8,128)(2,1)S(1)}, u32[]{:S(2)}, u32[]{:S(2)}) collective-permute-start(bf16[32,2176]{1,0:T(8,128)(2,1)S(1)} %get-tuple-element.115), channel_id=1, source_target_pairs={{0,2},{1,3},{2,0},{3,1},{4,6},{5,7},{6,4},{7,5},{8,10},{9,11},{10,... | collective-permute-start | bytes 417800 | tf_op jit(solution)/shard_map/ppermute | solution.py:465
  42.4 3.1 %weight_grads.2 = (bf16[384,4096]{1,0:T(8,128)(2,1)}, bf16[384,4096]{1,0:T(8,128)(2,1)}) custom-call(bf16[384,256]{1,0:T(8,128)(2,1)S(1)} %get-tuple-element.120.refs_0_, bf16[384,256]{1,0:T(8,128)(2,1)S(1)} %get-tuple-element.121.refs_1_, bf16[256,2048]{1,0:T(8,128)(2,1)S(1)} %get-tuple-element.122.refs_2_), custom_call_target="tpu_custom_call" | custom-call | flops 1000000 | bytes 10000 | tf_op jit(solution)/shard_map/weight_grads/pallas_call | solution.py:406
  45.5 1.4 %collective-permute-done.15.right = bf16[32,2176]{1,0:T(8,128)(2,1)S(1)} collective-permute-done((bf16[32,2176]{1,0:T(8,128)(2,1)S(1)}, bf16[32,2176]{1,0:T(8,128)(2,1)S(1)}, u32[]{:S(2)}, u32[]{:S(2)}) %collective-permute-start.15) | collective-permute-done | bytes 139296 | tf_op jit(solution)/shard_map/ppermute | solution.py:465
  47.4 2.0 %collective-permute-done.17.right = bf16[32,2176]{1,0:T(8,128)(2,1)S(1)} collective-permute-done((bf16[32,2176]{1,0:T(8,128)(2,1)S(1)}, bf16[32,2176]{1,0:T(8,128)(2,1)S(1)}, u32[]{:S(2)}, u32[]{:S(2)}) %collective-permute-start.17) | collective-permute-done | bytes 139296 | tf_op jit(solution)/shard_map/ppermute | solution.py:465
  49.3 3.7 %collective-permute-done.16.refs_0_ = bf16[8,2176]{1,0:T(8,128)(2,1)S(1)} collective-permute-done((bf16[8,2176]{1,0:T(8,128)(2,1)S(1)}, bf16[8,2176]{1,0:T(8,128)(2,1)S(1)}, u32[]{:S(2)}, u32[]{:S(2)}) %collective-permute-start.16) | collective-permute-done | bytes 34848 | tf_op jit(solution)/shard_map/ppermute | solution.py:465
  53.2 1.6 %collective-permute-start.18 = (bf16[8,2176]{1,0:T(8,128)(2,1)S(1)}, bf16[8,2176]{1,0:T(8,128)(2,1)S(1)}, u32[]{:S(2)}, u32[]{:S(2)}) collective-permute-start(bf16[8,2176]{1,0:T(8,128)(2,1)S(1)} %get-tuple-element.128), channel_id=1, source_target_pairs={{0,28},{4,24},{8,20},{12,16},{16,12},{20,8},{24,4},{28,0},{1,29},{... | collective-permute-start | bytes 104456 | tf_op jit(solution)/shard_map/ppermute | solution.py:465
  54.8 3.0 %collective-permute-start.19 = (bf16[8,2176]{1,0:T(8,128)(2,1)S(1)}, bf16[8,2176]{1,0:T(8,128)(2,1)S(1)}, u32[]{:S(2)}, u32[]{:S(2)}) collective-permute-start(bf16[8,2176]{1,0:T(8,128)(2,1)S(1)} %get-tuple-element.130), channel_id=1, source_target_pairs={{0,16},{4,20},{8,24},{12,28},{16,0},{20,4},{24,8},{28,12},{1,17},{... | collective-permute-start | bytes 104456 | tf_op jit(solution)/shard_map/ppermute | solution.py:465
  58.3 2.0 %weight_grads.3 = bf16[384,4096]{1,0:T(8,128)(2,1)} custom-call(bf16[384,256]{1,0:T(8,128)(2,1)S(1)} %get-tuple-element.136.refs_10_.refs_0_, bf16[256,2048]{1,0:T(8,128)(2,1)S(1)} %get-tuple-element.137.refs_1_), custom_call_target="tpu_custom_call" | custom-call | flops 1000000 | bytes 10000 | tf_op jit(solution)/shard_map/weight_grads/pallas_call | solution.py:406
  60.9 2.7 %collective-permute-done.20.refs_3_ = bf16[8,2176]{1,0:T(8,128)(2,1)S(1)} collective-permute-done((bf16[8,2176]{1,0:T(8,128)(2,1)S(1)}, bf16[8,2176]{1,0:T(8,128)(2,1)S(1)}, u32[]{:S(2)}, u32[]{:S(2)}) %collective-permute-start.20) | collective-permute-done | bytes 34848 | tf_op jit(solution)/shard_map/ppermute | solution.py:465
  (48 shorter events, 8.1 us)
Async XLA Ops:
  3.0 8.9 %collective-permute-start = (bf16[8,4096]{1,0:T(8,128)(2,1)}, bf16[8,4096]{1,0:T(8,128)(2,1)S(1)}, u32[]{:S(2)}, u32[]{:S(2)}) collective-permute-start(bf16[8,4096]{1,0:T(8,128)(2,1)} %get-tuple-element.77), channel_id=1, source_target_pairs={{0,4},{4,0},{8,12},{12,8},{16,20},{20,16},{24,28},{28,24},{1,5},{5... | collective-permute-start | bytes 196616 | tf_op jit(solution)/shard_map/ppermute | solution.py:465
  6.0 9.5 %collective-permute-start.1 = (bf16[8,4096]{1,0:T(8,128)(2,1)}, bf16[8,4096]{1,0:T(8,128)(2,1)S(1)}, u32[]{:S(2)}, u32[]{:S(2)}) collective-permute-start(bf16[8,4096]{1,0:T(8,128)(2,1)} %get-tuple-element.78), channel_id=1, source_target_pairs={{0,16},{4,20},{8,24},{12,28},{16,0},{20,4},{24,8},{28,12},{1,17},{... | collective-permute-start | bytes 196616 | tf_op jit(solution)/shard_map/ppermute | solution.py:465
  8.6 8.4 %collective-permute-start.2 = (bf16[8,4096]{1,0:T(8,128)(2,1)}, bf16[8,4096]{1,0:T(8,128)(2,1)S(1)}, u32[]{:S(2)}, u32[]{:S(2)}) collective-permute-start(bf16[8,4096]{1,0:T(8,128)(2,1)} %get-tuple-element.79), channel_id=1, source_target_pairs={{0,8},{4,12},{8,0},{12,4},{16,24},{20,28},{24,16},{28,20},{1,9},{5... | collective-permute-start | bytes 196616 | tf_op jit(solution)/shard_map/ppermute | solution.py:465
  10.2 9.8 %collective-permute-start.3 = (bf16[8,4096]{1,0:T(8,128)(2,1)}, bf16[8,4096]{1,0:T(8,128)(2,1)S(1)}, u32[]{:S(2)}, u32[]{:S(2)}) collective-permute-start(bf16[8,4096]{1,0:T(8,128)(2,1)} %get-tuple-element.80), channel_id=1, source_target_pairs={{0,20},{4,16},{8,28},{12,24},{16,4},{20,0},{24,12},{28,8},{1,21},{... | collective-permute-start | bytes 196616 | tf_op jit(solution)/shard_map/ppermute | solution.py:465
  10.5 12.3 %collective-permute-start.4 = (bf16[8,4096]{1,0:T(8,128)(2,1)}, bf16[8,4096]{1,0:T(8,128)(2,1)S(1)}, u32[]{:S(2)}, u32[]{:S(2)}) collective-permute-start(bf16[8,4096]{1,0:T(8,128)(2,1)} %get-tuple-element.85), channel_id=1, source_target_pairs={{0,12},{4,8},{8,4},{12,0},{16,28},{20,24},{24,20},{28,16},{1,13},{... | collective-permute-start | bytes 196616 | tf_op jit(solution)/shard_map/ppermute | solution.py:465
  11.9 10.9 %collective-permute-start.5 = (bf16[8,4096]{1,0:T(8,128)(2,1)}, bf16[8,4096]{1,0:T(8,128)(2,1)S(1)}, u32[]{:S(2)}, u32[]{:S(2)}) collective-permute-start(bf16[8,4096]{1,0:T(8,128)(2,1)} %get-tuple-element.86), channel_id=1, source_target_pairs={{0,24},{4,28},{8,16},{12,20},{16,8},{20,12},{24,0},{28,4},{1,25},{... | collective-permute-start | bytes 196616 | tf_op jit(solution)/shard_map/ppermute | solution.py:465
  15.5 7.3 %collective-permute-start.6 = (bf16[8,4096]{1,0:T(8,128)(2,1)}, bf16[8,4096]{1,0:T(8,128)(2,1)S(1)}, u32[]{:S(2)}, u32[]{:S(2)}) collective-permute-start(bf16[8,4096]{1,0:T(8,128)(2,1)} %get-tuple-element.87), channel_id=1, source_target_pairs={{0,28},{4,24},{8,20},{12,16},{16,12},{20,8},{24,4},{28,0},{1,29},{... | collective-permute-start | bytes 196616 | tf_op jit(solution)/shard_map/ppermute | solution.py:465
  20.0 8.0 %collective-permute-start.7 = (bf16[32,4096]{1,0:T(8,128)(2,1)S(1)}, bf16[32,4096]{1,0:T(8,128)(2,1)S(1)}, u32[]{:S(2)}, u32[]{:S(2)}) collective-permute-start(bf16[32,4096]{1,0:T(8,128)(2,1)S(1)} %pack.2.refs_0_), channel_id=1, source_target_pairs={{0,2},{1,3},{2,0},{3,1},{4,6},{5,7},{6,4},{7,5},{8,10},{9,11},{10,... | collective-permute-start | bytes 786440 | tf_op jit(solution)/shard_map/ppermute | solution.py:465
  22.9 8.0 %collective-permute-start.8 = (bf16[32,4096]{1,0:T(8,128)(2,1)S(1)}, bf16[32,4096]{1,0:T(8,128)(2,1)S(1)}, u32[]{:S(2)}, u32[]{:S(2)}) collective-permute-start(bf16[32,4096]{1,0:T(8,128)(2,1)S(1)} %pack.3.refs_1_), channel_id=1, source_target_pairs={{0,2},{1,3},{2,0},{3,1},{4,6},{5,7},{6,4},{7,5},{8,10},{9,11},{10,... | collective-permute-start | bytes 786440 | tf_op jit(solution)/shard_map/ppermute | solution.py:465
  28.1 2.8 %collective-permute-start.9 = (bf16[32,4096]{1,0:T(8,128)(2,1)S(1)}, bf16[32,4096]{1,0:T(8,128)(2,1)S(1)}, u32[]{:S(2)}, u32[]{:S(2)}) collective-permute-start(bf16[32,4096]{1,0:T(8,128)(2,1)S(1)} %pack.2.refs_0_), channel_id=1, source_target_pairs={{0,1},{1,0},{2,3},{3,2},{4,5},{5,4},{6,7},{7,6},{8,9},{9,8},{10,11... | collective-permute-start | bytes 786440 | tf_op jit(solution)/shard_map/ppermute | solution.py:465
  28.1 2.8 %collective-permute-start.10 = (bf16[32,4096]{1,0:T(8,128)(2,1)S(1)}, bf16[32,4096]{1,0:T(8,128)(2,1)S(1)}, u32[]{:S(2)}, u32[]{:S(2)}) collective-permute-start(bf16[32,4096]{1,0:T(8,128)(2,1)S(1)} %collective-permute-done.7.refs_2_), channel_id=1, source_target_pairs={{0,1},{1,0},{2,3},{3,2},{4,5},{5,4},{6,7},{7,6},{8,9},{9,8},{10,11... | collective-permute-start | bytes 786440 | tf_op jit(solution)/shard_map/ppermute | solution.py:465
  28.6 2.3 %collective-permute-start.11 = (bf16[32,4096]{1,0:T(8,128)(2,1)S(1)}, bf16[32,4096]{1,0:T(8,128)(2,1)S(1)}, u32[]{:S(2)}, u32[]{:S(2)}) collective-permute-start(bf16[32,4096]{1,0:T(8,128)(2,1)S(1)} %pack.3.refs_1_), channel_id=1, source_target_pairs={{0,1},{1,0},{2,3},{3,2},{4,5},{5,4},{6,7},{7,6},{8,9},{9,8},{10,11... | collective-permute-start | bytes 786440 | tf_op jit(solution)/shard_map/ppermute | solution.py:465
  30.9 1.6 %collective-permute-start.12 = (bf16[32,4096]{1,0:T(8,128)(2,1)S(1)}, bf16[32,4096]{1,0:T(8,128)(2,1)S(1)}, u32[]{:S(2)}, u32[]{:S(2)}) collective-permute-start(bf16[32,4096]{1,0:T(8,128)(2,1)S(1)} %collective-permute-done.8.refs_3_), channel_id=1, source_target_pairs={{0,1},{1,0},{2,3},{3,2},{4,5},{5,4},{6,7},{7,6},{8,9},{9,8},{10,11... | collective-permute-start | bytes 786440 | tf_op jit(solution)/shard_map/ppermute | solution.py:465
  37.5 1.7 %collective-permute-start.13 = (bf16[128,1280]{1,0:T(8,128)(2,1)S(1)}, bf16[128,1280]{1,0:T(8,128)(2,1)S(1)}, u32[]{:S(2)}, u32[]{:S(2)}) collective-permute-start(bf16[128,1280]{1,0:T(8,128)(2,1)S(1)} %get-tuple-element.107), channel_id=1, source_target_pairs={{0,1},{1,0},{2,3},{3,2},{4,5},{5,4},{6,7},{7,6},{8,9},{9,8},{10,11... | collective-permute-start | bytes 983048 | tf_op jit(solution)/shard_map/ppermute | solution.py:465
  38.6 1.6 %collective-permute-start.14 = (bf16[128,896]{1,0:T(8,128)(2,1)S(1)}, bf16[128,896]{1,0:T(8,128)(2,1)S(1)}, u32[]{:S(2)}, u32[]{:S(2)}) collective-permute-start(bf16[128,896]{1,0:T(8,128)(2,1)S(1)} %get-tuple-element.113), channel_id=1, source_target_pairs={{0,1},{1,0},{2,3},{3,2},{4,5},{5,4},{6,7},{7,6},{8,9},{9,8},{10,11... | collective-permute-start | bytes 688136 | tf_op jit(solution)/shard_map/ppermute | solution.py:465
  40.3 6.6 %collective-permute-start.15 = (bf16[32,2176]{1,0:T(8,128)(2,1)S(1)}, bf16[32,2176]{1,0:T(8,128)(2,1)S(1)}, u32[]{:S(2)}, u32[]{:S(2)}) collective-permute-start(bf16[32,2176]{1,0:T(8,128)(2,1)S(1)} %get-tuple-element.115), channel_id=1, source_target_pairs={{0,2},{1,3},{2,0},{3,1},{4,6},{5,7},{6,4},{7,5},{8,10},{9,11},{10,... | collective-permute-start | bytes 417800 | tf_op jit(solution)/shard_map/ppermute | solution.py:465
  41.9 7.4 %collective-permute-start.17 = (bf16[32,2176]{1,0:T(8,128)(2,1)S(1)}, bf16[32,2176]{1,0:T(8,128)(2,1)S(1)}, u32[]{:S(2)}, u32[]{:S(2)}) collective-permute-start(bf16[32,2176]{1,0:T(8,128)(2,1)S(1)} %get-tuple-element.119), channel_id=1, source_target_pairs={{0,2},{1,3},{2,0},{3,1},{4,6},{5,7},{6,4},{7,5},{8,10},{9,11},{10,... | collective-permute-start | bytes 417800 | tf_op jit(solution)/shard_map/ppermute | solution.py:465
  42.4 21.1 %copy-start.4 = (bf16[32,8]{0,1:T(8,128)(2,1)S(1)}, bf16[32,8]{0,1:T(8,128)(2,1)}, u32[]{:S(2)}) copy-start(bf16[32,8]{0,1:T(8,128)(2,1)} %param.9) | copy-start | bytes 1540
  46.9 6.2 %collective-permute-start.21 = (bf16[16,2176]{1,0:T(8,128)(2,1)S(1)}, bf16[16,2176]{1,0:T(8,128)(2,1)S(1)}, u32[]{:S(2)}, u32[]{:S(2)}) collective-permute-start(bf16[16,2176]{1,0:T(8,128)(2,1)S(1)} %get-tuple-element.133), channel_id=1, source_target_pairs={{0,4},{4,0},{8,12},{12,8},{16,20},{20,16},{24,28},{28,24},{1,5},{5... | collective-permute-start | bytes 208904 | tf_op jit(solution)/shard_map/ppermute | solution.py:465
  47.3 5.7 %collective-permute-start.16 = (bf16[8,2176]{1,0:T(8,128)(2,1)S(1)}, bf16[8,2176]{1,0:T(8,128)(2,1)S(1)}, u32[]{:S(2)}, u32[]{:S(2)}) collective-permute-start(bf16[8,2176]{1,0:T(8,128)(2,1)S(1)} %get-tuple-element.126), channel_id=1, source_target_pairs={{0,20},{4,16},{8,28},{12,24},{16,4},{20,0},{24,12},{28,8},{1,21},{... | collective-permute-start | bytes 104456 | tf_op jit(solution)/shard_map/ppermute | solution.py:465
  53.2 10.4 %collective-permute-start.22 = (bf16[16,2176]{1,0:T(8,128)(2,1)S(1)}, bf16[16,2176]{1,0:T(8,128)(2,1)S(1)}, u32[]{:S(2)}, u32[]{:S(2)}) collective-permute-start(bf16[16,2176]{1,0:T(8,128)(2,1)S(1)} %get-tuple-element.134), channel_id=1, source_target_pairs={{0,8},{4,12},{8,0},{12,4},{16,24},{20,28},{24,16},{28,20},{1,9},{5... | collective-permute-start | bytes 208904 | tf_op jit(solution)/shard_map/ppermute | solution.py:465
  53.2 7.0 %collective-permute-start.18 = (bf16[8,2176]{1,0:T(8,128)(2,1)S(1)}, bf16[8,2176]{1,0:T(8,128)(2,1)S(1)}, u32[]{:S(2)}, u32[]{:S(2)}) collective-permute-start(bf16[8,2176]{1,0:T(8,128)(2,1)S(1)} %get-tuple-element.128), channel_id=1, source_target_pairs={{0,28},{4,24},{8,20},{12,16},{16,12},{20,8},{24,4},{28,0},{1,29},{... | collective-permute-start | bytes 104456 | tf_op jit(solution)/shard_map/ppermute | solution.py:465
  54.8 6.1 %collective-permute-start.19 = (bf16[8,2176]{1,0:T(8,128)(2,1)S(1)}, bf16[8,2176]{1,0:T(8,128)(2,1)S(1)}, u32[]{:S(2)}, u32[]{:S(2)}) collective-permute-start(bf16[8,2176]{1,0:T(8,128)(2,1)S(1)} %get-tuple-element.130), channel_id=1, source_target_pairs={{0,16},{4,20},{8,24},{12,28},{16,0},{20,4},{24,8},{28,12},{1,17},{... | collective-permute-start | bytes 104456 | tf_op jit(solution)/shard_map/ppermute | solution.py:465
  57.8 5.7 %collective-permute-start.20 = (bf16[8,2176]{1,0:T(8,128)(2,1)S(1)}, bf16[8,2176]{1,0:T(8,128)(2,1)S(1)}, u32[]{:S(2)}, u32[]{:S(2)}) collective-permute-start(bf16[8,2176]{1,0:T(8,128)(2,1)S(1)} %get-tuple-element.131), channel_id=1, source_target_pairs={{0,24},{4,28},{8,16},{12,20},{16,8},{20,12},{24,0},{28,4},{1,25},{... | collective-permute-start | bytes 104456 | tf_op jit(solution)/shard_map/ppermute | solution.py:465
  (5 other events, 30.7 us)

commit v13 on v11

--- a/solution.py
+++ b/solution.py
@@ -12,7 +12,6 @@
 BLOCK = 2 * CAP
 LANES = 128
 MIB = 2**20
-COVER = 40
 
 CONTRACT_LAST = (((1,), (1,)), ((), ()))
 CONTRACT_FIRST = (((0,), (0,)), ((), ()))
@@ -21,6 +20,7 @@
 VMEM = pl.BlockSpec(memory_space=pltpu.VMEM)
 
 LIGHT = pl.CostEstimate(flops=10**6, bytes_accessed=10**4, transcendentals=0)
+COVER = pl.CostEstimate(flops=4 * 10**10, bytes_accessed=4 * 10**7, transcendentals=0)
 
 
 def struct(shape, dtype=jnp.bfloat16):
@@ -119,9 +119,7 @@
         in_specs=[VMEM],
         out_specs=[VMEM] * 3,
         compiler_params=pltpu.CompilerParams(vmem_limit_bytes=4 * MIB),
-        cost_estimate=pl.CostEstimate(
-            flops=COVER * 10**9, bytes_accessed=COVER * 10**6, transcendentals=0
-        ),
+        cost_estimate=LIGHT,
         name="placement",
     )(ids)
 
@@ -143,15 +141,37 @@
         in_specs=[VMEM] * count,
         out_specs=VMEM,
         compiler_params=pltpu.CompilerParams(vmem_limit_bytes=4 * MIB + 8 * rows * width),
+        cost_estimate=LIGHT,
         name="pack",
     )(*blocks)
 
 
+def split_kernel(rows, token_out, grad_out):
+    half = token_out.shape[1]
+    token_out[...] = rows[:, :half]
+    grad_out[...] = rows[:, half:]
+
+
+def split(rows):
+    height, width = rows.shape
+    return pl.pallas_call(
+        split_kernel,
+        out_shape=[struct((height, width // 2))] * 2,
+        in_specs=[VMEM],
+        out_specs=[VMEM] * 2,
+        compiler_params=pltpu.CompilerParams(vmem_limit_bytes=4 * MIB + 8 * height * width),
+        cost_estimate=COVER,
+        name="split",
+    )(rows)
+
+
 def gather_pieces(pieces, start, out):
     base = 0
+    half = out.shape[1]
     for piece in pieces:
-        rows = piece.shape[0]
-        out[pl.ds(base, rows), :] = piece[:, start : start + out.shape[1]]
+        rows, width = piece.shape
+        first = min(start, width - half)
+        out[pl.ds(base, rows), :] = piece[:, first : first + half]
         base += rows
 
 
@@ -457,10 +477,10 @@
 
 def offsets(count):
     near, far = list(range(1, count // 2)), list(range(count // 2, count))
-    order = []
+    order = [0]
     for i, k in enumerate(near):
         order += [k, far[i]]
-    return order + far[len(near) :] + [0]
+    return order + far[len(near) :]
 
 
 def return_offsets(count):
@@ -495,9 +515,9 @@
     sent = dispatch(n_targets, ids, tokens, gates, out_grad)
     arrived = exchange([sent[k] for k in order], order)
     early = pack(arrived[:middle])
-    ids_after, _ = tie((ids, early))
-    table, late = tie((placement(n_targets, ids_after), arrived[middle:]))
+    (early_tokens, early_grads), late = tie((split(early), arrived[middle:]))
     late = pack(late)
+    ids_after, _ = tie((ids, late))
     early_near, late_near = (cross(value, far_bits) for value in (early, late))
     near = sorted(early_near)
     crossed = {mask: early_near[mask] for mask in near[1:]}
@@ -507,7 +527,8 @@
         early_far[mask] = flip(value, "dp", 1)
     late_far = {0: flip(late, "dp", 1)}
     crossed = {mask: late_near[mask] for mask in near[1:]}
-    early_far, late_far, crossed = tie((early_far, late_far, crossed))
+    table = placement(n_targets, ids_after)
+    table, early_far, late_far, crossed = tie((table, early_far, late_far, crossed))
     for mask, value in crossed.items():
         late_far[mask] = flip(value, "dp", 1)
     pieces = [
@@ -516,10 +537,12 @@
         for mask in near
         for group in groups
     ]
-    token_halves, activated, slope, hidden = forward(pieces, weights[0], weights[1])
+    token_halves, activated, slope, hidden = forward(
+        [early_tokens, *pieces[1:]], weights[0], weights[1]
+    )
     size = width // 16 * 5
     own_left, far_left, grad_halves, gate_f, up_f, factors, gate_column = backward(
-        pieces, activated, slope, hidden, weights, size
+        [early_grads, *pieces[1:]], activated, slope, hidden, weights, size
     )
 
     left = flip(far_left, "dp", 1)

time: 60.1 us -> 59.4 us (0.988)
  waiting for transfers between devices: 18.9 us -> 17.2 us
  starting transfers between devices: 24.3 us -> 25.6 us
    ppermute x21, waiting for transfers between devices: 18.9 us -> 17.2 us  [flip(): return lax.ppermute(value, axis, [(i, i ^ bit) for i in range(size)])]
    ppermute x21, starting transfers between devices: 24.3 us -> 25.6 us  [flip(): return lax.ppermute(value, axis, [(i, i ^ bit) for i in range(size)])]
  transfers between devices with their start and end apart: 21 -> 21, of which waited for: 11 -> 12; matrix products, arithmetic and copies ran while one was open for 0% -> 0% of each run, Pallas kernels for 11% -> 11%
where the time goes in v13:
time: 59.4 us; the launch traced here: 59.2 us
  starting transfers between devices  25.6 us (43%)
  waiting for transfers between devices  17.2 us (29%)
  Pallas kernels  14.8 us (25%)
  local copies, waits for them, and re-layouts  0.87 us (1%)
  between operations  0.79 us (1%)
    ppermute x21, starting transfers between devices, flip(): return lax.ppermute(value, axis, [(i, i ^ bit) for i in range(size)])  25.6 us
    ppermute x21, waiting for transfers between devices, flip(): return lax.ppermute(value, axis, [(i, i ^ bit) for i in range(size)])  17.2 us
    pallas_call x2, Pallas kernels, weight_grads(): pl.pallas_call(functools.partial(weight_kernel, chunk, count), out_shape=...  5.05 us
    pallas_call x1, Pallas kernels, backward(): pl.pallas_call(functools.partial(backward_kernel, count), out_shape=[stru...  2.98 us
    pallas_call x1, Pallas kernels, dispatch(): pl.pallas_call(functools.partial(dispatch_kernel, n_targets), out_shape=[...  2.35 us
    pallas_call x1, Pallas kernels, forward(): pl.pallas_call(functools.partial(forward_kernel, count), out_shape=[struc...  1.95 us
  transfers between devices with their start and end apart: 21, of which 12 were waited for; matrix products, arithmetic and copies ran while one was open for 0% of the time, Pallas kernels for 11%

profile of v13, /device:TPU:0, one launch (start us, length us, event | category | flops | bytes accessed | tf_op | source)
XLA Modules:
  0.0 59.2 jit_solution(8816345065942208251)
XLA Ops:
  0.6 2.4 %dispatch.1 = (bf16[8,4096]{1,0:T(8,128)(2,1)}, bf16[8,4096]{1,0:T(8,128)(2,1)}, bf16[8,4096]{1,0:T(8,128)(2,1)}, bf16[8,4096]{1,0:T(8,128)(2,1)}, bf16[8,4096]{...) custom-call(s32[8,32]{1,0:T(8,128)} %bitcast.16, ...), custom_call_target="tpu_custom_call" | custom-call | tf_op jit(solution)/shard_map/dispatch/pallas_call | solution.py:92
  3.0 3.0 %collective-permute-start = (bf16[8,4096]{1,0:T(8,128)(2,1)}, bf16[8,4096]{1,0:T(8,128)(2,1)S(1)}, u32[]{:S(2)}, u32[]{:S(2)}) collective-permute-start(bf16[8,4096]{1,0:T(8,128)(2,1)} %get-tuple-element.74), channel_id=1, source_target_pairs={{0,4},{4,0},{8,12},{12,8},{16,20},{20,16},{24,28},{28,24},{1,5},{5... | collective-permute-start | bytes 196616 | tf_op jit(solution)/shard_map/ppermute | solution.py:475
  6.0 2.6 %collective-permute-start.1 = (bf16[8,4096]{1,0:T(8,128)(2,1)}, bf16[8,4096]{1,0:T(8,128)(2,1)S(1)}, u32[]{:S(2)}, u32[]{:S(2)}) collective-permute-start(bf16[8,4096]{1,0:T(8,128)(2,1)} %get-tuple-element.75), channel_id=1, source_target_pairs={{0,16},{4,20},{8,24},{12,28},{16,0},{20,4},{24,8},{28,12},{1,17},{... | collective-permute-start | bytes 196616 | tf_op jit(solution)/shard_map/ppermute | solution.py:475
  8.6 1.6 %collective-permute-start.2 = (bf16[8,4096]{1,0:T(8,128)(2,1)}, bf16[8,4096]{1,0:T(8,128)(2,1)S(1)}, u32[]{:S(2)}, u32[]{:S(2)}) collective-permute-start(bf16[8,4096]{1,0:T(8,128)(2,1)} %get-tuple-element.76), channel_id=1, source_target_pairs={{0,8},{4,12},{8,0},{12,4},{16,24},{20,28},{24,16},{28,20},{1,9},{5... | collective-permute-start | bytes 196616 | tf_op jit(solution)/shard_map/ppermute | solution.py:475
  10.5 1.4 %collective-permute-start.4 = (bf16[8,4096]{1,0:T(8,128)(2,1)}, bf16[8,4096]{1,0:T(8,128)(2,1)S(1)}, u32[]{:S(2)}, u32[]{:S(2)}) collective-permute-start(bf16[8,4096]{1,0:T(8,128)(2,1)} %get-tuple-element.80), channel_id=1, source_target_pairs={{0,12},{4,8},{8,4},{12,0},{16,28},{20,24},{24,20},{28,16},{1,13},{... | collective-permute-start | bytes 196616 | tf_op jit(solution)/shard_map/ppermute | solution.py:475
  11.9 3.6 %collective-permute-start.5 = (bf16[8,4096]{1,0:T(8,128)(2,1)}, bf16[8,4096]{1,0:T(8,128)(2,1)S(1)}, u32[]{:S(2)}, u32[]{:S(2)}) collective-permute-start(bf16[8,4096]{1,0:T(8,128)(2,1)} %get-tuple-element.81), channel_id=1, source_target_pairs={{0,24},{4,28},{8,16},{12,20},{16,8},{20,12},{24,0},{28,4},{1,25},{... | collective-permute-start | bytes 196616 | tf_op jit(solution)/shard_map/ppermute | solution.py:475
  15.5 1.6 %collective-permute-start.6 = (bf16[8,4096]{1,0:T(8,128)(2,1)}, bf16[8,4096]{1,0:T(8,128)(2,1)S(1)}, u32[]{:S(2)}, u32[]{:S(2)}) collective-permute-start(bf16[8,4096]{1,0:T(8,128)(2,1)} %get-tuple-element.82), channel_id=1, source_target_pairs={{0,28},{4,24},{8,20},{12,16},{16,12},{20,8},{24,4},{28,0},{1,29},{... | collective-permute-start | bytes 196616 | tf_op jit(solution)/shard_map/ppermute | solution.py:475
  18.0 1.6 %collective-permute-start.7 = (bf16[32,4096]{1,0:T(8,128)(2,1)S(1)}, bf16[32,4096]{1,0:T(8,128)(2,1)S(1)}, u32[]{:S(2)}, u32[]{:S(2)}) collective-permute-start(bf16[32,4096]{1,0:T(8,128)(2,1)S(1)} %pack.2.rows), channel_id=1, source_target_pairs={{0,2},{1,3},{2,0},{3,1},{4,6},{5,7},{6,4},{7,5},{8,10},{9,11},{10,... | collective-permute-start | bytes 786440 | tf_op jit(solution)/shard_map/ppermute | solution.py:475
  20.0 2.7 %collective-permute-done.6.refs_3_ = bf16[8,4096]{1,0:T(8,128)(2,1)S(1)} collective-permute-done((bf16[8,4096]{1,0:T(8,128)(2,1)}, bf16[8,4096]{1,0:T(8,128)(2,1)S(1)}, u32[]{:S(2)}, u32[]{:S(2)}) %collective-permute-start.6) | collective-permute-done | bytes 65568 | tf_op jit(solution)/shard_map/ppermute | solution.py:475
  22.7 1.6 %collective-permute-start.11 = (bf16[32,4096]{1,0:T(8,128)(2,1)S(1)}, bf16[32,4096]{1,0:T(8,128)(2,1)S(1)}, u32[]{:S(2)}, u32[]{:S(2)}) collective-permute-start(bf16[32,4096]{1,0:T(8,128)(2,1)S(1)} %pack.3.refs_1_), channel_id=1, source_target_pairs={{0,2},{1,3},{2,0},{3,1},{4,6},{5,7},{6,4},{7,5},{8,10},{9,11},{10,... | collective-permute-start | bytes 786440 | tf_op jit(solution)/shard_map/ppermute | solution.py:475
  24.3 2.1 %collective-permute-done.7.refs_2_ = bf16[32,4096]{1,0:T(8,128)(2,1)S(1)} collective-permute-done((bf16[32,4096]{1,0:T(8,128)(2,1)S(1)}, bf16[32,4096]{1,0:T(8,128)(2,1)S(1)}, u32[]{:S(2)}, u32[]{:S(2)}) %collective-permute-start.7) | collective-permute-done | bytes 262176 | tf_op jit(solution)/shard_map/ppermute | solution.py:475
  27.1 2.9 %collective-permute-done.11.refs_3_ = bf16[32,4096]{1,0:T(8,128)(2,1)S(1)} collective-permute-done((bf16[32,4096]{1,0:T(8,128)(2,1)S(1)}, bf16[32,4096]{1,0:T(8,128)(2,1)S(1)}, u32[]{:S(2)}, u32[]{:S(2)}) %collective-permute-start.11) | collective-permute-done | bytes 262176 | tf_op jit(solution)/shard_map/ppermute | solution.py:475
  30.1 1.5 %collective-permute-done.12.refs_7_ = bf16[32,4096]{1,0:T(8,128)(2,1)S(1)} collective-permute-done((bf16[32,4096]{1,0:T(8,128)(2,1)S(1)}, bf16[32,4096]{1,0:T(8,128)(2,1)S(1)}, u32[]{:S(2)}, u32[]{:S(2)}) %collective-permute-start.12) | collective-permute-done | bytes 262176 | tf_op jit(solution)/shard_map/ppermute | solution.py:475
  31.7 2.0 %forward.1 = (bf16[256,2048]{1,0:T(8,128)(2,1)S(1)}, f32[384,256]{1,0:T(8,128)S(1)}, f32[384,256]{1,0:T(8,128)S(1)}, bf16[384,256]{1,0:T(8,128)(2,1)S(1)}) custom-call(bf16[32,2048]{1,0:T(8,128)(2,1)S(1)} %get-tuple-element.102.refs_0_, bf16[32,4096]{1,0:T(8,128)(2,1)S(1)} %pack.3.refs_1_, bf16[32,4096]{1,0:T(8,128)(2,1)S(1)} %collective-permute-done.7.refs_2_, ...), custom_call_target="tpu_custom_call" | custom-call | flops 1000000 | bytes 10000 | tf_op jit(solution)/shard_map/forward/pallas_call | solution.py:209
  33.6 3.0 %backward.1 = (bf16[128,1280]{1,0:T(8,128)(2,1)S(1)}, bf16[128,1280]{1,0:T(8,128)(2,1)S(1)}, bf16[256,2048]{1,0:T(8,128)(2,1)S(1)}, bf16[384,256]{1,0:T(8,128)(2...) custom-call(bf16[32,2048]{1,0:T(8,128)(2,1)S(1)} %get-tuple-element.97.refs_0_, ...), custom_call_target="tpu_custom_call" | custom-call | flops 1000000 | bytes 10000 | tf_op jit(solution)/shard_map/backward/pallas_call | solution.py:290
  39.5 1.6 %collective-permute-start.16 = (bf16[32,2176]{1,0:T(8,128)(2,1)S(1)}, bf16[32,2176]{1,0:T(8,128)(2,1)S(1)}, u32[]{:S(2)}, u32[]{:S(2)}) collective-permute-start(bf16[32,2176]{1,0:T(8,128)(2,1)S(1)} %get-tuple-element.117), channel_id=1, source_target_pairs={{0,2},{1,3},{2,0},{3,1},{4,6},{5,7},{6,4},{7,5},{8,10},{9,11},{10,... | collective-permute-start | bytes 417800 | tf_op jit(solution)/shard_map/ppermute | solution.py:475
  41.6 3.1 %weight_grads.2 = (bf16[384,4096]{1,0:T(8,128)(2,1)}, bf16[384,4096]{1,0:T(8,128)(2,1)}) custom-call(bf16[384,256]{1,0:T(8,128)(2,1)S(1)} %get-tuple-element.120.refs_0_, bf16[384,256]{1,0:T(8,128)(2,1)S(1)} %get-tuple-element.121.refs_1_, bf16[256,2048]{1,0:T(8,128)(2,1)S(1)} %get-tuple-element.122.refs_2_), custom_call_target="tpu_custom_call" | custom-call | flops 1000000 | bytes 10000 | tf_op jit(solution)/shard_map/weight_grads/pallas_call | solution.py:422
  44.7 1.4 %collective-permute-done.16.right = bf16[32,2176]{1,0:T(8,128)(2,1)S(1)} collective-permute-done((bf16[32,2176]{1,0:T(8,128)(2,1)S(1)}, bf16[32,2176]{1,0:T(8,128)(2,1)S(1)}, u32[]{:S(2)}, u32[]{:S(2)}) %collective-permute-start.16) | collective-permute-done | bytes 139296 | tf_op jit(solution)/shard_map/ppermute | solution.py:475
  46.1 1.6 %collective-permute-start.17 = (bf16[32,2176]{1,0:T(8,128)(2,1)S(1)}, bf16[32,2176]{1,0:T(8,128)(2,1)S(1)}, u32[]{:S(2)}, u32[]{:S(2)}) collective-permute-start(bf16[32,2176]{1,0:T(8,128)(2,1)S(1)} %add_rows.2), channel_id=1, source_target_pairs={{0,4},{4,0},{8,12},{12,8},{16,20},{20,16},{24,28},{28,24},{1,5},{5... | collective-permute-start | bytes 417800 | tf_op jit(solution)/shard_map/ppermute | solution.py:475
  47.7 2.0 %weight_grads.3 = bf16[384,4096]{1,0:T(8,128)(2,1)} custom-call(bf16[384,256]{1,0:T(8,128)(2,1)S(1)} %get-tuple-element.126.refs_10_.refs_0_, bf16[256,2048]{1,0:T(8,128)(2,1)S(1)} %get-tuple-element.127.refs_1_), custom_call_target="tpu_custom_call" | custom-call | flops 1000000 | bytes 10000 | tf_op jit(solution)/shard_map/weight_grads/pallas_call | solution.py:422
  49.7 1.5 %collective-permute-done.17.passed = bf16[32,2176]{1,0:T(8,128)(2,1)S(1)} collective-permute-done((bf16[32,2176]{1,0:T(8,128)(2,1)S(1)}, bf16[32,2176]{1,0:T(8,128)(2,1)S(1)}, u32[]{:S(2)}, u32[]{:S(2)}) %collective-permute-start.17) | collective-permute-done | bytes 139296 | tf_op jit(solution)/shard_map/ppermute | solution.py:475
  51.3 2.0 %collective-permute-start.19 = (bf16[16,2176]{1,0:T(8,128)(2,1)S(1)}, bf16[16,2176]{1,0:T(8,128)(2,1)S(1)}, u32[]{:S(2)}, u32[]{:S(2)}) collective-permute-start(bf16[16,2176]{1,0:T(8,128)(2,1)S(1)} %get-tuple-element.133), channel_id=1, source_target_pairs={{0,24},{4,28},{8,16},{12,20},{16,8},{20,12},{24,0},{28,4},{1,25},{... | collective-permute-start | bytes 208904 | tf_op jit(solution)/shard_map/ppermute | solution.py:475
  53.3 1.5 %collective-permute-start.20 = (bf16[16,2176]{1,0:T(8,128)(2,1)S(1)}, bf16[16,2176]{1,0:T(8,128)(2,1)S(1)}, u32[]{:S(2)}, u32[]{:S(2)}) collective-permute-start(bf16[16,2176]{1,0:T(8,128)(2,1)S(1)} %get-tuple-element.134), channel_id=1, source_target_pairs={{0,8},{4,12},{8,0},{12,4},{16,24},{20,28},{24,16},{28,20},{1,9},{5... | collective-permute-start | bytes 208904 | tf_op jit(solution)/shard_map/ppermute | solution.py:475
  54.8 2.0 %collective-permute-done.18.refs_0_ = bf16[16,2176]{1,0:T(8,128)(2,1)S(1)} collective-permute-done((bf16[16,2176]{1,0:T(8,128)(2,1)S(1)}, bf16[16,2176]{1,0:T(8,128)(2,1)S(1)}, u32[]{:S(2)}, u32[]{:S(2)}) %collective-permute-start.18) | collective-permute-done | bytes 69664 | tf_op jit(solution)/shard_map/ppermute | solution.py:475
  (45 shorter events, 8.5 us)
Async XLA Ops:
  3.0 8.9 %collective-permute-start = (bf16[8,4096]{1,0:T(8,128)(2,1)}, bf16[8,4096]{1,0:T(8,128)(2,1)S(1)}, u32[]{:S(2)}, u32[]{:S(2)}) collective-permute-start(bf16[8,4096]{1,0:T(8,128)(2,1)} %get-tuple-element.74), channel_id=1, source_target_pairs={{0,4},{4,0},{8,12},{12,8},{16,20},{20,16},{24,28},{28,24},{1,5},{5... | collective-permute-start | bytes 196616 | tf_op jit(solution)/shard_map/ppermute | solution.py:475
  6.0 9.5 %collective-permute-start.1 = (bf16[8,4096]{1,0:T(8,128)(2,1)}, bf16[8,4096]{1,0:T(8,128)(2,1)S(1)}, u32[]{:S(2)}, u32[]{:S(2)}) collective-permute-start(bf16[8,4096]{1,0:T(8,128)(2,1)} %get-tuple-element.75), channel_id=1, source_target_pairs={{0,16},{4,20},{8,24},{12,28},{16,0},{20,4},{24,8},{28,12},{1,17},{... | collective-permute-start | bytes 196616 | tf_op jit(solution)/shard_map/ppermute | solution.py:475
  8.6 8.4 %collective-permute-start.2 = (bf16[8,4096]{1,0:T(8,128)(2,1)}, bf16[8,4096]{1,0:T(8,128)(2,1)S(1)}, u32[]{:S(2)}, u32[]{:S(2)}) collective-permute-start(bf16[8,4096]{1,0:T(8,128)(2,1)} %get-tuple-element.76), channel_id=1, source_target_pairs={{0,8},{4,12},{8,0},{12,4},{16,24},{20,28},{24,16},{28,20},{1,9},{5... | collective-permute-start | bytes 196616 | tf_op jit(solution)/shard_map/ppermute | solution.py:475
  10.2 9.8 %collective-permute-start.3 = (bf16[8,4096]{1,0:T(8,128)(2,1)}, bf16[8,4096]{1,0:T(8,128)(2,1)S(1)}, u32[]{:S(2)}, u32[]{:S(2)}) collective-permute-start(bf16[8,4096]{1,0:T(8,128)(2,1)} %get-tuple-element.79), channel_id=1, source_target_pairs={{0,20},{4,16},{8,28},{12,24},{16,4},{20,0},{24,12},{28,8},{1,21},{... | collective-permute-start | bytes 196616 | tf_op jit(solution)/shard_map/ppermute | solution.py:475
  10.5 9.5 %collective-permute-start.4 = (bf16[8,4096]{1,0:T(8,128)(2,1)}, bf16[8,4096]{1,0:T(8,128)(2,1)S(1)}, u32[]{:S(2)}, u32[]{:S(2)}) collective-permute-start(bf16[8,4096]{1,0:T(8,128)(2,1)} %get-tuple-element.80), channel_id=1, source_target_pairs={{0,12},{4,8},{8,4},{12,0},{16,28},{20,24},{24,20},{28,16},{1,13},{... | collective-permute-start | bytes 196616 | tf_op jit(solution)/shard_map/ppermute | solution.py:475
  11.9 8.1 %collective-permute-start.5 = (bf16[8,4096]{1,0:T(8,128)(2,1)}, bf16[8,4096]{1,0:T(8,128)(2,1)S(1)}, u32[]{:S(2)}, u32[]{:S(2)}) collective-permute-start(bf16[8,4096]{1,0:T(8,128)(2,1)} %get-tuple-element.81), channel_id=1, source_target_pairs={{0,24},{4,28},{8,16},{12,20},{16,8},{20,12},{24,0},{28,4},{1,25},{... | collective-permute-start | bytes 196616 | tf_op jit(solution)/shard_map/ppermute | solution.py:475
  15.5 7.2 %collective-permute-start.6 = (bf16[8,4096]{1,0:T(8,128)(2,1)}, bf16[8,4096]{1,0:T(8,128)(2,1)S(1)}, u32[]{:S(2)}, u32[]{:S(2)}) collective-permute-start(bf16[8,4096]{1,0:T(8,128)(2,1)} %get-tuple-element.82), channel_id=1, source_target_pairs={{0,28},{4,24},{8,20},{12,16},{16,12},{20,8},{24,4},{28,0},{1,29},{... | collective-permute-start | bytes 196616 | tf_op jit(solution)/shard_map/ppermute | solution.py:475
  18.0 13.7 %copy-start = (bf16[1,384,4096]{2,1,0:T(8,128)(2,1)S(1)}, bf16[1,384,4096]{2,1,0:T(8,128)(2,1)}, u32[]{:S(2)}) copy-start(bf16[1,384,4096]{2,1,0:T(8,128)(2,1)} %param.11) | copy-start | bytes 9437188
  18.0 13.7 %copy-start.1 = (bf16[1,384,4096]{2,1,0:T(8,128)(2,1)S(1)}, bf16[1,384,4096]{2,1,0:T(8,128)(2,1)}, u32[]{:S(2)}) copy-start(bf16[1,384,4096]{2,1,0:T(8,128)(2,1)} %param.12) | copy-start | bytes 9437188
  18.0 8.4 %collective-permute-start.7 = (bf16[32,4096]{1,0:T(8,128)(2,1)S(1)}, bf16[32,4096]{1,0:T(8,128)(2,1)S(1)}, u32[]{:S(2)}, u32[]{:S(2)}) collective-permute-start(bf16[32,4096]{1,0:T(8,128)(2,1)S(1)} %pack.2.rows), channel_id=1, source_target_pairs={{0,2},{1,3},{2,0},{3,1},{4,6},{5,7},{6,4},{7,5},{8,10},{9,11},{10,... | collective-permute-start | bytes 786440 | tf_op jit(solution)/shard_map/ppermute | solution.py:475
  22.7 7.3 %collective-permute-start.11 = (bf16[32,4096]{1,0:T(8,128)(2,1)S(1)}, bf16[32,4096]{1,0:T(8,128)(2,1)S(1)}, u32[]{:S(2)}, u32[]{:S(2)}) collective-permute-start(bf16[32,4096]{1,0:T(8,128)(2,1)S(1)} %pack.3.refs_1_), channel_id=1, source_target_pairs={{0,2},{1,3},{2,0},{3,1},{4,6},{5,7},{6,4},{7,5},{8,10},{9,11},{10,... | collective-permute-start | bytes 786440 | tf_op jit(solution)/shard_map/ppermute | solution.py:475
  26.4 3.6 %collective-permute-start.8 = (bf16[32,4096]{1,0:T(8,128)(2,1)S(1)}, bf16[32,4096]{1,0:T(8,128)(2,1)S(1)}, u32[]{:S(2)}, u32[]{:S(2)}) collective-permute-start(bf16[32,4096]{1,0:T(8,128)(2,1)S(1)} %pack.2.rows), channel_id=1, source_target_pairs={{0,1},{1,0},{2,3},{3,2},{4,5},{5,4},{6,7},{7,6},{8,9},{9,8},{10,11... | collective-permute-start | bytes 786440 | tf_op jit(solution)/shard_map/ppermute | solution.py:475
  26.4 3.6 %collective-permute-start.9 = (bf16[32,4096]{1,0:T(8,128)(2,1)S(1)}, bf16[32,4096]{1,0:T(8,128)(2,1)S(1)}, u32[]{:S(2)}, u32[]{:S(2)}) collective-permute-start(bf16[32,4096]{1,0:T(8,128)(2,1)S(1)} %collective-permute-done.7.refs_2_), channel_id=1, source_target_pairs={{0,1},{1,0},{2,3},{3,2},{4,5},{5,4},{6,7},{7,6},{8,9},{9,8},{10,11... | collective-permute-start | bytes 786440 | tf_op jit(solution)/shard_map/ppermute | solution.py:475
  26.9 3.1 %collective-permute-start.10 = (bf16[32,4096]{1,0:T(8,128)(2,1)S(1)}, bf16[32,4096]{1,0:T(8,128)(2,1)S(1)}, u32[]{:S(2)}, u32[]{:S(2)}) collective-permute-start(bf16[32,4096]{1,0:T(8,128)(2,1)S(1)} %pack.3.refs_1_), channel_id=1, source_target_pairs={{0,1},{1,0},{2,3},{3,2},{4,5},{5,4},{6,7},{7,6},{8,9},{9,8},{10,11... | collective-permute-start | bytes 786440 | tf_op jit(solution)/shard_map/ppermute | solution.py:475
  30.0 1.6 %collective-permute-start.12 = (bf16[32,4096]{1,0:T(8,128)(2,1)S(1)}, bf16[32,4096]{1,0:T(8,128)(2,1)S(1)}, u32[]{:S(2)}, u32[]{:S(2)}) collective-permute-start(bf16[32,4096]{1,0:T(8,128)(2,1)S(1)} %collective-permute-done.11.refs_3_), channel_id=1, source_target_pairs={{0,1},{1,0},{2,3},{3,2},{4,5},{5,4},{6,7},{7,6},{8,9},{9,8},{10,11... | collective-permute-start | bytes 786440 | tf_op jit(solution)/shard_map/ppermute | solution.py:475
  36.6 1.7 %collective-permute-start.13 = (bf16[128,1280]{1,0:T(8,128)(2,1)S(1)}, bf16[128,1280]{1,0:T(8,128)(2,1)S(1)}, u32[]{:S(2)}, u32[]{:S(2)}) collective-permute-start(bf16[128,1280]{1,0:T(8,128)(2,1)S(1)} %get-tuple-element.107), channel_id=1, source_target_pairs={{0,1},{1,0},{2,3},{3,2},{4,5},{5,4},{6,7},{7,6},{8,9},{9,8},{10,11... | collective-permute-start | bytes 983048 | tf_op jit(solution)/shard_map/ppermute | solution.py:475
  37.8 1.6 %collective-permute-start.14 = (bf16[128,896]{1,0:T(8,128)(2,1)S(1)}, bf16[128,896]{1,0:T(8,128)(2,1)S(1)}, u32[]{:S(2)}, u32[]{:S(2)}) collective-permute-start(bf16[128,896]{1,0:T(8,128)(2,1)S(1)} %get-tuple-element.113), channel_id=1, source_target_pairs={{0,1},{1,0},{2,3},{3,2},{4,5},{5,4},{6,7},{7,6},{8,9},{9,8},{10,11... | collective-permute-start | bytes 688136 | tf_op jit(solution)/shard_map/ppermute | solution.py:475
  39.5 6.6 %collective-permute-start.16 = (bf16[32,2176]{1,0:T(8,128)(2,1)S(1)}, bf16[32,2176]{1,0:T(8,128)(2,1)S(1)}, u32[]{:S(2)}, u32[]{:S(2)}) collective-permute-start(bf16[32,2176]{1,0:T(8,128)(2,1)S(1)} %get-tuple-element.117), channel_id=1, source_target_pairs={{0,2},{1,3},{2,0},{3,1},{4,6},{5,7},{6,4},{7,5},{8,10},{9,11},{10,... | collective-permute-start | bytes 417800 | tf_op jit(solution)/shard_map/ppermute | solution.py:475
  41.1 8.6 %collective-permute-start.15 = (bf16[32,2176]{1,0:T(8,128)(2,1)S(1)}, bf16[32,2176]{1,0:T(8,128)(2,1)S(1)}, u32[]{:S(2)}, u32[]{:S(2)}) collective-permute-start(bf16[32,2176]{1,0:T(8,128)(2,1)S(1)} %get-tuple-element.115), channel_id=1, source_target_pairs={{0,2},{1,3},{2,0},{3,1},{4,6},{5,7},{6,4},{7,5},{8,10},{9,11},{10,... | collective-permute-start | bytes 417800 | tf_op jit(solution)/shard_map/ppermute | solution.py:475
  41.6 16.7 %copy-start.5 = (bf16[32,8]{0,1:T(8,128)(2,1)S(1)}, bf16[32,8]{0,1:T(8,128)(2,1)}, u32[]{:S(2)}) copy-start(bf16[32,8]{0,1:T(8,128)(2,1)} %param.9) | copy-start | bytes 1540
  46.1 5.1 %collective-permute-start.17 = (bf16[32,2176]{1,0:T(8,128)(2,1)S(1)}, bf16[32,2176]{1,0:T(8,128)(2,1)S(1)}, u32[]{:S(2)}, u32[]{:S(2)}) collective-permute-start(bf16[32,2176]{1,0:T(8,128)(2,1)S(1)} %add_rows.2), channel_id=1, source_target_pairs={{0,4},{4,0},{8,12},{12,8},{16,20},{20,16},{24,28},{28,24},{1,5},{5... | collective-permute-start | bytes 417800 | tf_op jit(solution)/shard_map/ppermute | solution.py:475
  51.3 5.5 %collective-permute-start.18 = (bf16[16,2176]{1,0:T(8,128)(2,1)S(1)}, bf16[16,2176]{1,0:T(8,128)(2,1)S(1)}, u32[]{:S(2)}, u32[]{:S(2)}) collective-permute-start(bf16[16,2176]{1,0:T(8,128)(2,1)S(1)} %get-tuple-element.132), channel_id=1, source_target_pairs={{0,16},{4,20},{8,24},{12,28},{16,0},{20,4},{24,8},{28,12},{1,17},{... | collective-permute-start | bytes 208904 | tf_op jit(solution)/shard_map/ppermute | solution.py:475
  51.3 6.3 %collective-permute-start.19 = (bf16[16,2176]{1,0:T(8,128)(2,1)S(1)}, bf16[16,2176]{1,0:T(8,128)(2,1)S(1)}, u32[]{:S(2)}, u32[]{:S(2)}) collective-permute-start(bf16[16,2176]{1,0:T(8,128)(2,1)S(1)} %get-tuple-element.133), channel_id=1, source_target_pairs={{0,24},{4,28},{8,16},{12,20},{16,8},{20,12},{24,0},{28,4},{1,25},{... | collective-permute-start | bytes 208904 | tf_op jit(solution)/shard_map/ppermute | solution.py:475
  53.3 5.0 %collective-permute-start.20 = (bf16[16,2176]{1,0:T(8,128)(2,1)S(1)}, bf16[16,2176]{1,0:T(8,128)(2,1)S(1)}, u32[]{:S(2)}, u32[]{:S(2)}) collective-permute-start(bf16[16,2176]{1,0:T(8,128)(2,1)S(1)} %get-tuple-element.134), channel_id=1, source_target_pairs={{0,8},{4,12},{8,0},{12,4},{16,24},{20,28},{24,16},{28,20},{1,9},{5... | collective-permute-start | bytes 208904 | tf_op jit(solution)/shard_map/ppermute | solution.py:475
  (3 other events, 11.8 us)

commit v14 on v13

--- a/solution.py
+++ b/solution.py
@@ -50,11 +50,10 @@
     return matches, first, second
 
 
-def pick_rows(first, second, rows_ref):
+def pick_rows(picks, rows_ref):
     half = rows_ref.shape[1] // 2
-    low = jnp.dot(first, rows_ref[:, :half], preferred_element_type=jnp.float32)
-    high = jnp.dot(second, rows_ref[:, half:], preferred_element_type=jnp.float32)
-    return (low + high).astype(jnp.bfloat16)
+    rows = jnp.concatenate([rows_ref[:, :half], rows_ref[:, half:]], axis=0)
+    return jnp.dot(picks, rows, preferred_element_type=jnp.float32).astype(jnp.bfloat16)
 
 
 def dispatch_kernel(n_targets, *refs):
@@ -69,8 +68,9 @@
         copy.start()
     copies[0].wait()
     matches, first, second = choice_table(ids_ref[...], n_targets)
+    picks = jnp.concatenate([first.astype(jnp.float32), second.astype(jnp.float32)], axis=1)
     copies[1].wait()
-    rows = pick_rows(as_bf16(first), as_bf16(second), tokens_ref)
+    rows = pick_rows(picks.astype(jnp.bfloat16), tokens_ref)
     half = rows.shape[1]
     for k, out in enumerate(outs):
         out[:, :half] = rows[k * BLOCK : (k + 1) * BLOCK]
@@ -79,10 +79,9 @@
     scale = jnp.zeros(first.shape, jnp.float32)
     for k, match in enumerate(matches):
         scale = scale + jnp.where(match, gates[k : k + 1, :], 0.0)
-    first = jnp.where(first, scale, 0.0).astype(jnp.bfloat16)
-    second = jnp.where(second, scale, 0.0).astype(jnp.bfloat16)
+    picks = (picks * jnp.concatenate([scale, scale], axis=1)).astype(jnp.bfloat16)
     copies[3].wait()
-    rows = pick_rows(first, second, grads_ref)
+    rows = pick_rows(picks, grads_ref)
     for k, out in enumerate(outs):
         out[:, half:] = rows[k * BLOCK : (k + 1) * BLOCK]
 
@@ -124,26 +123,25 @@
     )(ids)
 
 
-def pack_kernel(count, *refs):
-    blocks, out = refs[:count], refs[count]
-    for k in range(0, count, 2):
-        out[pl.ds(k * BLOCK, 2 * BLOCK), :] = jnp.concatenate(
-            [blocks[k][...], blocks[k + 1][...]], axis=0
-        )
-
-
-def pack(blocks):
-    count = len(blocks)
-    rows, width = count * BLOCK, blocks[0].shape[1]
-    return pl.pallas_call(
-        functools.partial(pack_kernel, count),
+def pack_kernel(refs, out):
+    blocks = [
+        ref[pl.ds(i, BLOCK), :] for ref in refs for i in range(0, ref.shape[0], BLOCK)
+    ]
+    for k in range(0, len(blocks), 2):
+        out[pl.ds(k * BLOCK, 2 * BLOCK), :] = jnp.concatenate(blocks[k : k + 2], axis=0)
+
+
+def pack(arrays, cost):
+    rows, width = sum(array.shape[0] for array in arrays), arrays[0].shape[1]
+    return pl.pallas_call(
+        lambda *refs: pack_kernel(refs[:-1], refs[-1]),
         out_shape=struct((rows, width)),
-        in_specs=[VMEM] * count,
+        in_specs=[VMEM] * len(arrays),
         out_specs=VMEM,
         compiler_params=pltpu.CompilerParams(vmem_limit_bytes=4 * MIB + 8 * rows * width),
-        cost_estimate=LIGHT,
+        cost_estimate=cost,
         name="pack",
-    )(*blocks)
+    )(*arrays)
 
 
 def split_kernel(rows, token_out, grad_out):
@@ -514,9 +512,10 @@
     middle = n_targets // 2
     sent = dispatch(n_targets, ids, tokens, gates, out_grad)
     arrived = exchange([sent[k] for k in order], order)
-    early = pack(arrived[:middle])
+    first = pack(arrived[1:3], COVER)
+    early = pack([arrived[0], first, *arrived[3:middle]], LIGHT)
     (early_tokens, early_grads), late = tie((split(early), arrived[middle:]))
-    late = pack(late)
+    late = pack(late, LIGHT)
     ids_after, _ = tie((ids, late))
     early_near, late_near = (cross(value, far_bits) for value in (early, late))
     near = sorted(early_near)
@@ -540,7 +539,7 @@
     token_halves, activated, slope, hidden = forward(
         [early_tokens, *pieces[1:]], weights[0], weights[1]
     )
-    size = width // 16 * 5
+    size = width // 8 * 3
     own_left, far_left, grad_halves, gate_f, up_f, factors, gate_column = backward(
         [early_grads, *pieces[1:]], activated, slope, hidden, weights, size
     )

time: 59.4 us -> 58.7 us (0.988)
  local copies, waits for them, and re-layouts: 0.87 us -> 0.03 us
    unnamed x12, local copies, waits for them, and re-layouts: 0.87 us -> 0.03 us
  transfers between devices with their start and end apart: 21 -> 21, of which waited for: 12 -> 12; matrix products, arithmetic and copies ran while one was open for 0% -> 0% of each run, Pallas kernels for 11% -> 10%
where the time goes in v14:
time: 58.7 us; the launch traced here: 58.5 us
  starting transfers between devices  25.6 us (44%)
  waiting for transfers between devices  17.3 us (29%)
  Pallas kernels  14.8 us (25%)
  between operations  0.81 us (1%)
    ppermute x21, starting transfers between devices, flip(): return lax.ppermute(value, axis, [(i, i ^ bit) for i in range(size)])  25.6 us
    ppermute x21, waiting for transfers between devices, flip(): return lax.ppermute(value, axis, [(i, i ^ bit) for i in range(size)])  17.3 us
    pallas_call x2, Pallas kernels, weight_grads(): pl.pallas_call(functools.partial(weight_kernel, chunk, count), out_shape=...  5.05 us
    pallas_call x1, Pallas kernels, backward(): pl.pallas_call(functools.partial(backward_kernel, count), out_shape=[stru...  3.3 us
    pallas_call x1, Pallas kernels, dispatch(): pl.pallas_call(functools.partial(dispatch_kernel, n_targets), out_shape=[...  2.28 us
    pallas_call x1, Pallas kernels, forward(): pl.pallas_call(functools.partial(forward_kernel, count), out_shape=[struc...  1.95 us
  transfers between devices with their start and end apart: 21, of which 12 were waited for; matrix products, arithmetic and copies ran while one was open for 0% of the time, Pallas kernels for 10%

profile of v14, /device:TPU:0, one launch (start us, length us, event | category | flops | bytes accessed | tf_op | source)
XLA Modules:
  0.0 58.5 jit_solution(13483919886974144234)
XLA Ops:
  0.6 2.3 %dispatch.1 = (bf16[8,4096]{1,0:T(8,128)(2,1)}, bf16[8,4096]{1,0:T(8,128)(2,1)}, bf16[8,4096]{1,0:T(8,128)(2,1)}, bf16[8,4096]{1,0:T(8,128)(2,1)}, bf16[8,4096]{...) custom-call(s32[8,32]{1,0:T(8,128)} %bitcast.16, ...), custom_call_target="tpu_custom_call" | custom-call | tf_op jit(solution)/shard_map/dispatch/pallas_call | solution.py:91
  2.9 3.0 %collective-permute-start = (bf16[8,4096]{1,0:T(8,128)(2,1)}, bf16[8,4096]{1,0:T(8,128)(2,1)S(1)}, u32[]{:S(2)}, u32[]{:S(2)}) collective-permute-start(bf16[8,4096]{1,0:T(8,128)(2,1)} %get-tuple-element.74), channel_id=1, source_target_pairs={{0,4},{4,0},{8,12},{12,8},{16,20},{20,16},{24,28},{28,24},{1,5},{5... | collective-permute-start | bytes 196616 | tf_op jit(solution)/shard_map/ppermute | solution.py:473
  6.0 2.6 %collective-permute-start.1 = (bf16[8,4096]{1,0:T(8,128)(2,1)}, bf16[8,4096]{1,0:T(8,128)(2,1)S(1)}, u32[]{:S(2)}, u32[]{:S(2)}) collective-permute-start(bf16[8,4096]{1,0:T(8,128)(2,1)} %get-tuple-element.75), channel_id=1, source_target_pairs={{0,16},{4,20},{8,24},{12,28},{16,0},{20,4},{24,8},{28,12},{1,17},{... | collective-permute-start | bytes 196616 | tf_op jit(solution)/shard_map/ppermute | solution.py:473
  8.5 1.6 %collective-permute-start.2 = (bf16[8,4096]{1,0:T(8,128)(2,1)}, bf16[8,4096]{1,0:T(8,128)(2,1)S(1)}, u32[]{:S(2)}, u32[]{:S(2)}) collective-permute-start(bf16[8,4096]{1,0:T(8,128)(2,1)} %get-tuple-element.76), channel_id=1, source_target_pairs={{0,8},{4,12},{8,0},{12,4},{16,24},{20,28},{24,16},{28,20},{1,9},{5... | collective-permute-start | bytes 196616 | tf_op jit(solution)/shard_map/ppermute | solution.py:473
  10.4 1.4 %collective-permute-start.4 = (bf16[8,4096]{1,0:T(8,128)(2,1)}, bf16[8,4096]{1,0:T(8,128)(2,1)S(1)}, u32[]{:S(2)}, u32[]{:S(2)}) collective-permute-start(bf16[8,4096]{1,0:T(8,128)(2,1)} %get-tuple-element.80), channel_id=1, source_target_pairs={{0,12},{4,8},{8,4},{12,0},{16,28},{20,24},{24,20},{28,16},{1,13},{... | collective-permute-start | bytes 196616 | tf_op jit(solution)/shard_map/ppermute | solution.py:473
  11.8 3.6 %collective-permute-start.5 = (bf16[8,4096]{1,0:T(8,128)(2,1)}, bf16[8,4096]{1,0:T(8,128)(2,1)S(1)}, u32[]{:S(2)}, u32[]{:S(2)}) collective-permute-start(bf16[8,4096]{1,0:T(8,128)(2,1)} %get-tuple-element.81), channel_id=1, source_target_pairs={{0,24},{4,28},{8,16},{12,20},{16,8},{20,12},{24,0},{28,4},{1,25},{... | collective-permute-start | bytes 196616 | tf_op jit(solution)/shard_map/ppermute | solution.py:473
  15.4 1.6 %collective-permute-start.6 = (bf16[8,4096]{1,0:T(8,128)(2,1)}, bf16[8,4096]{1,0:T(8,128)(2,1)S(1)}, u32[]{:S(2)}, u32[]{:S(2)}) collective-permute-start(bf16[8,4096]{1,0:T(8,128)(2,1)} %get-tuple-element.82), channel_id=1, source_target_pairs={{0,28},{4,24},{8,20},{12,16},{16,12},{20,8},{24,4},{28,0},{1,29},{... | collective-permute-start | bytes 196616 | tf_op jit(solution)/shard_map/ppermute | solution.py:473
  17.1 1.5 %collective-permute-start.7 = (bf16[32,4096]{1,0:T(8,128)(2,1)S(1)}, bf16[32,4096]{1,0:T(8,128)(2,1)S(1)}, u32[]{:S(2)}, u32[]{:S(2)}) collective-permute-start(bf16[32,4096]{1,0:T(8,128)(2,1)S(1)} %pack.4.rows), channel_id=1, source_target_pairs={{0,2},{1,3},{2,0},{3,1},{4,6},{5,7},{6,4},{7,5},{8,10},{9,11},{10,... | collective-permute-start | bytes 786440 | tf_op jit(solution)/shard_map/ppermute | solution.py:473
  18.7 1.2 %collective-permute-done.3.refs_0_ = bf16[8,4096]{1,0:T(8,128)(2,1)S(1)} collective-permute-done((bf16[8,4096]{1,0:T(8,128)(2,1)}, bf16[8,4096]{1,0:T(8,128)(2,1)S(1)}, u32[]{:S(2)}, u32[]{:S(2)}) %collective-permute-start.3) | collective-permute-done | bytes 65568 | tf_op jit(solution)/shard_map/ppermute | solution.py:473
  19.9 2.7 %collective-permute-done.6.refs_3_ = bf16[8,4096]{1,0:T(8,128)(2,1)S(1)} collective-permute-done((bf16[8,4096]{1,0:T(8,128)(2,1)}, bf16[8,4096]{1,0:T(8,128)(2,1)S(1)}, u32[]{:S(2)}, u32[]{:S(2)}) %collective-permute-start.6) | collective-permute-done | bytes 65568 | tf_op jit(solution)/shard_map/ppermute | solution.py:473
  22.6 1.6 %collective-permute-start.11 = (bf16[32,4096]{1,0:T(8,128)(2,1)S(1)}, bf16[32,4096]{1,0:T(8,128)(2,1)S(1)}, u32[]{:S(2)}, u32[]{:S(2)}) collective-permute-start(bf16[32,4096]{1,0:T(8,128)(2,1)S(1)} %pack.5.refs_1_), channel_id=1, source_target_pairs={{0,2},{1,3},{2,0},{3,1},{4,6},{5,7},{6,4},{7,5},{8,10},{9,11},{10,... | collective-permute-start | bytes 786440 | tf_op jit(solution)/shard_map/ppermute | solution.py:473
  25.3 3.8 %collective-permute-done.11.refs_3_ = bf16[32,4096]{1,0:T(8,128)(2,1)S(1)} collective-permute-done((bf16[32,4096]{1,0:T(8,128)(2,1)S(1)}, bf16[32,4096]{1,0:T(8,128)(2,1)S(1)}, u32[]{:S(2)}, u32[]{:S(2)}) %collective-permute-start.11) | collective-permute-done | bytes 262176 | tf_op jit(solution)/shard_map/ppermute | solution.py:473
  29.3 1.5 %collective-permute-done.12.refs_7_ = bf16[32,4096]{1,0:T(8,128)(2,1)S(1)} collective-permute-done((bf16[32,4096]{1,0:T(8,128)(2,1)S(1)}, bf16[32,4096]{1,0:T(8,128)(2,1)S(1)}, u32[]{:S(2)}, u32[]{:S(2)}) %collective-permute-start.12) | collective-permute-done | bytes 262176 | tf_op jit(solution)/shard_map/ppermute | solution.py:473
  30.8 2.0 %forward.1 = (bf16[256,2048]{1,0:T(8,128)(2,1)S(1)}, f32[384,256]{1,0:T(8,128)S(1)}, f32[384,256]{1,0:T(8,128)S(1)}, bf16[384,256]{1,0:T(8,128)(2,1)S(1)}) custom-call(bf16[32,2048]{1,0:T(8,128)(2,1)S(1)} %get-tuple-element.102.refs_0_, bf16[32,4096]{1,0:T(8,128)(2,1)S(1)} %pack.5.refs_1_, bf16[32,4096]{1,0:T(8,128)(2,1)S(1)} %collective-permute-done.7.refs_2_, ...), custom_call_target="tpu_custom_call" | custom-call | flops 1000000 | bytes 10000 | tf_op jit(solution)/shard_map/forward/pallas_call | solution.py:207
  32.8 3.3 %backward.1 = (bf16[128,1536]{1,0:T(8,128)(2,1)S(1)}, bf16[128,1536]{1,0:T(8,128)(2,1)S(1)}, bf16[256,2048]{1,0:T(8,128)(2,1)S(1)}, bf16[384,256]{1,0:T(8,128)(2...) custom-call(bf16[32,2048]{1,0:T(8,128)(2,1)S(1)} %get-tuple-element.97.refs_0_, ...), custom_call_target="tpu_custom_call" | custom-call | flops 1000000 | bytes 10000 | tf_op jit(solution)/shard_map/backward/pallas_call | solution.py:288
  38.5 1.6 %collective-permute-start.16 = (bf16[32,2176]{1,0:T(8,128)(2,1)S(1)}, bf16[32,2176]{1,0:T(8,128)(2,1)S(1)}, u32[]{:S(2)}, u32[]{:S(2)}) collective-permute-start(bf16[32,2176]{1,0:T(8,128)(2,1)S(1)} %get-tuple-element.117), channel_id=1, source_target_pairs={{0,2},{1,3},{2,0},{3,1},{4,6},{5,7},{6,4},{7,5},{8,10},{9,11},{10,... | collective-permute-start | bytes 417800 | tf_op jit(solution)/shard_map/ppermute | solution.py:473
  40.6 3.1 %weight_grads.2 = (bf16[384,4096]{1,0:T(8,128)(2,1)}, bf16[384,4096]{1,0:T(8,128)(2,1)}) custom-call(bf16[384,256]{1,0:T(8,128)(2,1)S(1)} %get-tuple-element.120.refs_0_, bf16[384,256]{1,0:T(8,128)(2,1)S(1)} %get-tuple-element.121.refs_1_, bf16[256,2048]{1,0:T(8,128)(2,1)S(1)} %get-tuple-element.122.refs_2_), custom_call_target="tpu_custom_call" | custom-call | flops 1000000 | bytes 10000 | tf_op jit(solution)/shard_map/weight_grads/pallas_call | solution.py:420
  43.7 1.4 %collective-permute-done.16.right = bf16[32,2176]{1,0:T(8,128)(2,1)S(1)} collective-permute-done((bf16[32,2176]{1,0:T(8,128)(2,1)S(1)}, bf16[32,2176]{1,0:T(8,128)(2,1)S(1)}, u32[]{:S(2)}, u32[]{:S(2)}) %collective-permute-start.16) | collective-permute-done | bytes 139296 | tf_op jit(solution)/shard_map/ppermute | solution.py:473
  45.1 1.6 %collective-permute-start.17 = (bf16[32,2176]{1,0:T(8,128)(2,1)S(1)}, bf16[32,2176]{1,0:T(8,128)(2,1)S(1)}, u32[]{:S(2)}, u32[]{:S(2)}) collective-permute-start(bf16[32,2176]{1,0:T(8,128)(2,1)S(1)} %add_rows.2), channel_id=1, source_target_pairs={{0,4},{4,0},{8,12},{12,8},{16,20},{20,16},{24,28},{28,24},{1,5},{5... | collective-permute-start | bytes 417800 | tf_op jit(solution)/shard_map/ppermute | solution.py:473
  46.7 2.0 %weight_grads.3 = bf16[384,4096]{1,0:T(8,128)(2,1)} custom-call(bf16[384,256]{1,0:T(8,128)(2,1)S(1)} %get-tuple-element.126.refs_10_.refs_0_, bf16[256,2048]{1,0:T(8,128)(2,1)S(1)} %get-tuple-element.127.refs_1_), custom_call_target="tpu_custom_call" | custom-call | flops 1000000 | bytes 10000 | tf_op jit(solution)/shard_map/weight_grads/pallas_call | solution.py:420
  48.8 1.5 %collective-permute-done.17.passed = bf16[32,2176]{1,0:T(8,128)(2,1)S(1)} collective-permute-done((bf16[32,2176]{1,0:T(8,128)(2,1)S(1)}, bf16[32,2176]{1,0:T(8,128)(2,1)S(1)}, u32[]{:S(2)}, u32[]{:S(2)}) %collective-permute-start.17) | collective-permute-done | bytes 139296 | tf_op jit(solution)/shard_map/ppermute | solution.py:473
  50.8 1.7 %collective-permute-start.19 = (bf16[16,2176]{1,0:T(8,128)(2,1)S(1)}, bf16[16,2176]{1,0:T(8,128)(2,1)S(1)}, u32[]{:S(2)}, u32[]{:S(2)}) collective-permute-start(bf16[16,2176]{1,0:T(8,128)(2,1)S(1)} %get-tuple-element.133), channel_id=1, source_target_pairs={{0,24},{4,28},{8,16},{12,20},{16,8},{20,12},{24,0},{28,4},{1,25},{... | collective-permute-start | bytes 208904 | tf_op jit(solution)/shard_map/ppermute | solution.py:473
  52.5 1.4 %collective-permute-start.20 = (bf16[16,2176]{1,0:T(8,128)(2,1)S(1)}, bf16[16,2176]{1,0:T(8,128)(2,1)S(1)}, u32[]{:S(2)}, u32[]{:S(2)}) collective-permute-start(bf16[16,2176]{1,0:T(8,128)(2,1)S(1)} %get-tuple-element.134), channel_id=1, source_target_pairs={{0,8},{4,12},{8,0},{12,4},{16,24},{20,28},{24,16},{28,20},{1,9},{5... | collective-permute-start | bytes 208904 | tf_op jit(solution)/shard_map/ppermute | solution.py:473
  53.9 2.0 %collective-permute-done.18.refs_0_ = bf16[16,2176]{1,0:T(8,128)(2,1)S(1)} collective-permute-done((bf16[16,2176]{1,0:T(8,128)(2,1)S(1)}, bf16[16,2176]{1,0:T(8,128)(2,1)S(1)}, u32[]{:S(2)}, u32[]{:S(2)}) %collective-permute-start.18) | collective-permute-done | bytes 69664 | tf_op jit(solution)/shard_map/ppermute | solution.py:473
  (46 shorter events, 7.9 us)
Async XLA Ops:
  2.9 8.9 %collective-permute-start = (bf16[8,4096]{1,0:T(8,128)(2,1)}, bf16[8,4096]{1,0:T(8,128)(2,1)S(1)}, u32[]{:S(2)}, u32[]{:S(2)}) collective-permute-start(bf16[8,4096]{1,0:T(8,128)(2,1)} %get-tuple-element.74), channel_id=1, source_target_pairs={{0,4},{4,0},{8,12},{12,8},{16,20},{20,16},{24,28},{28,24},{1,5},{5... | collective-permute-start | bytes 196616 | tf_op jit(solution)/shard_map/ppermute | solution.py:473
  6.0 9.5 %collective-permute-start.1 = (bf16[8,4096]{1,0:T(8,128)(2,1)}, bf16[8,4096]{1,0:T(8,128)(2,1)S(1)}, u32[]{:S(2)}, u32[]{:S(2)}) collective-permute-start(bf16[8,4096]{1,0:T(8,128)(2,1)} %get-tuple-element.75), channel_id=1, source_target_pairs={{0,16},{4,20},{8,24},{12,28},{16,0},{20,4},{24,8},{28,12},{1,17},{... | collective-permute-start | bytes 196616 | tf_op jit(solution)/shard_map/ppermute | solution.py:473
  8.5 8.5 %collective-permute-start.2 = (bf16[8,4096]{1,0:T(8,128)(2,1)}, bf16[8,4096]{1,0:T(8,128)(2,1)S(1)}, u32[]{:S(2)}, u32[]{:S(2)}) collective-permute-start(bf16[8,4096]{1,0:T(8,128)(2,1)} %get-tuple-element.76), channel_id=1, source_target_pairs={{0,8},{4,12},{8,0},{12,4},{16,24},{20,28},{24,16},{28,20},{1,9},{5... | collective-permute-start | bytes 196616 | tf_op jit(solution)/shard_map/ppermute | solution.py:473
  10.1 9.8 %collective-permute-start.3 = (bf16[8,4096]{1,0:T(8,128)(2,1)}, bf16[8,4096]{1,0:T(8,128)(2,1)S(1)}, u32[]{:S(2)}, u32[]{:S(2)}) collective-permute-start(bf16[8,4096]{1,0:T(8,128)(2,1)} %get-tuple-element.79), channel_id=1, source_target_pairs={{0,20},{4,16},{8,28},{12,24},{16,4},{20,0},{24,12},{28,8},{1,21},{... | collective-permute-start | bytes 196616 | tf_op jit(solution)/shard_map/ppermute | solution.py:473
  10.4 9.5 %collective-permute-start.4 = (bf16[8,4096]{1,0:T(8,128)(2,1)}, bf16[8,4096]{1,0:T(8,128)(2,1)S(1)}, u32[]{:S(2)}, u32[]{:S(2)}) collective-permute-start(bf16[8,4096]{1,0:T(8,128)(2,1)} %get-tuple-element.80), channel_id=1, source_target_pairs={{0,12},{4,8},{8,4},{12,0},{16,28},{20,24},{24,20},{28,16},{1,13},{... | collective-permute-start | bytes 196616 | tf_op jit(solution)/shard_map/ppermute | solution.py:473
  11.8 8.1 %collective-permute-start.5 = (bf16[8,4096]{1,0:T(8,128)(2,1)}, bf16[8,4096]{1,0:T(8,128)(2,1)S(1)}, u32[]{:S(2)}, u32[]{:S(2)}) collective-permute-start(bf16[8,4096]{1,0:T(8,128)(2,1)} %get-tuple-element.81), channel_id=1, source_target_pairs={{0,24},{4,28},{8,16},{12,20},{16,8},{20,12},{24,0},{28,4},{1,25},{... | collective-permute-start | bytes 196616 | tf_op jit(solution)/shard_map/ppermute | solution.py:473
  15.4 7.2 %collective-permute-start.6 = (bf16[8,4096]{1,0:T(8,128)(2,1)}, bf16[8,4096]{1,0:T(8,128)(2,1)S(1)}, u32[]{:S(2)}, u32[]{:S(2)}) collective-permute-start(bf16[8,4096]{1,0:T(8,128)(2,1)} %get-tuple-element.82), channel_id=1, source_target_pairs={{0,28},{4,24},{8,20},{12,16},{16,12},{20,8},{24,4},{28,0},{1,29},{... | collective-permute-start | bytes 196616 | tf_op jit(solution)/shard_map/ppermute | solution.py:473
  17.1 13.7 %copy-start = (bf16[1,384,4096]{2,1,0:T(8,128)(2,1)S(1)}, bf16[1,384,4096]{2,1,0:T(8,128)(2,1)}, u32[]{:S(2)}) copy-start(bf16[1,384,4096]{2,1,0:T(8,128)(2,1)} %param.11) | copy-start | bytes 9437188
  17.1 13.7 %copy-start.1 = (bf16[1,384,4096]{2,1,0:T(8,128)(2,1)S(1)}, bf16[1,384,4096]{2,1,0:T(8,128)(2,1)}, u32[]{:S(2)}) copy-start(bf16[1,384,4096]{2,1,0:T(8,128)(2,1)} %param.12) | copy-start | bytes 9437188
  17.1 7.5 %collective-permute-start.7 = (bf16[32,4096]{1,0:T(8,128)(2,1)S(1)}, bf16[32,4096]{1,0:T(8,128)(2,1)S(1)}, u32[]{:S(2)}, u32[]{:S(2)}) collective-permute-start(bf16[32,4096]{1,0:T(8,128)(2,1)S(1)} %pack.4.rows), channel_id=1, source_target_pairs={{0,2},{1,3},{2,0},{3,1},{4,6},{5,7},{6,4},{7,5},{8,10},{9,11},{10,... | collective-permute-start | bytes 786440 | tf_op jit(solution)/shard_map/ppermute | solution.py:473
  22.6 6.5 %collective-permute-start.11 = (bf16[32,4096]{1,0:T(8,128)(2,1)S(1)}, bf16[32,4096]{1,0:T(8,128)(2,1)S(1)}, u32[]{:S(2)}, u32[]{:S(2)}) collective-permute-start(bf16[32,4096]{1,0:T(8,128)(2,1)S(1)} %pack.5.refs_1_), channel_id=1, source_target_pairs={{0,2},{1,3},{2,0},{3,1},{4,6},{5,7},{6,4},{7,5},{8,10},{9,11},{10,... | collective-permute-start | bytes 786440 | tf_op jit(solution)/shard_map/ppermute | solution.py:473
  24.6 4.6 %collective-permute-start.8 = (bf16[32,4096]{1,0:T(8,128)(2,1)S(1)}, bf16[32,4096]{1,0:T(8,128)(2,1)S(1)}, u32[]{:S(2)}, u32[]{:S(2)}) collective-permute-start(bf16[32,4096]{1,0:T(8,128)(2,1)S(1)} %pack.4.rows), channel_id=1, source_target_pairs={{0,1},{1,0},{2,3},{3,2},{4,5},{5,4},{6,7},{7,6},{8,9},{9,8},{10,11... | collective-permute-start | bytes 786440 | tf_op jit(solution)/shard_map/ppermute | solution.py:473
  24.6 4.6 %collective-permute-start.9 = (bf16[32,4096]{1,0:T(8,128)(2,1)S(1)}, bf16[32,4096]{1,0:T(8,128)(2,1)S(1)}, u32[]{:S(2)}, u32[]{:S(2)}) collective-permute-start(bf16[32,4096]{1,0:T(8,128)(2,1)S(1)} %collective-permute-done.7.refs_2_), channel_id=1, source_target_pairs={{0,1},{1,0},{2,3},{3,2},{4,5},{5,4},{6,7},{7,6},{8,9},{9,8},{10,11... | collective-permute-start | bytes 786440 | tf_op jit(solution)/shard_map/ppermute | solution.py:473
  25.1 4.0 %collective-permute-start.10 = (bf16[32,4096]{1,0:T(8,128)(2,1)S(1)}, bf16[32,4096]{1,0:T(8,128)(2,1)S(1)}, u32[]{:S(2)}, u32[]{:S(2)}) collective-permute-start(bf16[32,4096]{1,0:T(8,128)(2,1)S(1)} %pack.5.refs_1_), channel_id=1, source_target_pairs={{0,1},{1,0},{2,3},{3,2},{4,5},{5,4},{6,7},{7,6},{8,9},{9,8},{10,11... | collective-permute-start | bytes 786440 | tf_op jit(solution)/shard_map/ppermute | solution.py:473
  29.2 1.6 %collective-permute-start.12 = (bf16[32,4096]{1,0:T(8,128)(2,1)S(1)}, bf16[32,4096]{1,0:T(8,128)(2,1)S(1)}, u32[]{:S(2)}, u32[]{:S(2)}) collective-permute-start(bf16[32,4096]{1,0:T(8,128)(2,1)S(1)} %collective-permute-done.11.refs_3_), channel_id=1, source_target_pairs={{0,1},{1,0},{2,3},{3,2},{4,5},{5,4},{6,7},{7,6},{8,9},{9,8},{10,11... | collective-permute-start | bytes 786440 | tf_op jit(solution)/shard_map/ppermute | solution.py:473
  36.1 1.8 %collective-permute-start.13 = (bf16[128,1536]{1,0:T(8,128)(2,1)S(1)}, bf16[128,1536]{1,0:T(8,128)(2,1)S(1)}, u32[]{:S(2)}, u32[]{:S(2)}) collective-permute-start(bf16[128,1536]{1,0:T(8,128)(2,1)S(1)} %get-tuple-element.107), channel_id=1, source_target_pairs={{0,1},{1,0},{2,3},{3,2},{4,5},{5,4},{6,7},{7,6},{8,9},{9,8},{10,11... | collective-permute-start | bytes 1179656 | tf_op jit(solution)/shard_map/ppermute | solution.py:473
  36.9 1.5 %collective-permute-start.14 = (bf16[128,640]{1,0:T(8,128)(2,1)S(1)}, bf16[128,640]{1,0:T(8,128)(2,1)S(1)}, u32[]{:S(2)}, u32[]{:S(2)}) collective-permute-start(bf16[128,640]{1,0:T(8,128)(2,1)S(1)} %get-tuple-element.113), channel_id=1, source_target_pairs={{0,1},{1,0},{2,3},{3,2},{4,5},{5,4},{6,7},{7,6},{8,9},{9,8},{10,11... | collective-permute-start | bytes 491528 | tf_op jit(solution)/shard_map/ppermute | solution.py:473
  38.5 6.6 %collective-permute-start.16 = (bf16[32,2176]{1,0:T(8,128)(2,1)S(1)}, bf16[32,2176]{1,0:T(8,128)(2,1)S(1)}, u32[]{:S(2)}, u32[]{:S(2)}) collective-permute-start(bf16[32,2176]{1,0:T(8,128)(2,1)S(1)} %get-tuple-element.117), channel_id=1, source_target_pairs={{0,2},{1,3},{2,0},{3,1},{4,6},{5,7},{6,4},{7,5},{8,10},{9,11},{10,... | collective-permute-start | bytes 417800 | tf_op jit(solution)/shard_map/ppermute | solution.py:473
  40.1 8.6 %collective-permute-start.15 = (bf16[32,2176]{1,0:T(8,128)(2,1)S(1)}, bf16[32,2176]{1,0:T(8,128)(2,1)S(1)}, u32[]{:S(2)}, u32[]{:S(2)}) collective-permute-start(bf16[32,2176]{1,0:T(8,128)(2,1)S(1)} %get-tuple-element.115), channel_id=1, source_target_pairs={{0,2},{1,3},{2,0},{3,1},{4,6},{5,7},{6,4},{7,5},{8,10},{9,11},{10,... | collective-permute-start | bytes 417800 | tf_op jit(solution)/shard_map/ppermute | solution.py:473
  40.6 16.9 %copy-start.5 = (bf16[32,8]{0,1:T(8,128)(2,1)S(1)}, bf16[32,8]{0,1:T(8,128)(2,1)}, u32[]{:S(2)}) copy-start(bf16[32,8]{0,1:T(8,128)(2,1)} %param.9) | copy-start | bytes 1540
  45.1 5.1 %collective-permute-start.17 = (bf16[32,2176]{1,0:T(8,128)(2,1)S(1)}, bf16[32,2176]{1,0:T(8,128)(2,1)S(1)}, u32[]{:S(2)}, u32[]{:S(2)}) collective-permute-start(bf16[32,2176]{1,0:T(8,128)(2,1)S(1)} %add_rows.2), channel_id=1, source_target_pairs={{0,4},{4,0},{8,12},{12,8},{16,20},{20,16},{24,28},{28,24},{1,5},{5... | collective-permute-start | bytes 417800 | tf_op jit(solution)/shard_map/ppermute | solution.py:473
  50.3 5.6 %collective-permute-start.18 = (bf16[16,2176]{1,0:T(8,128)(2,1)S(1)}, bf16[16,2176]{1,0:T(8,128)(2,1)S(1)}, u32[]{:S(2)}, u32[]{:S(2)}) collective-permute-start(bf16[16,2176]{1,0:T(8,128)(2,1)S(1)} %get-tuple-element.132), channel_id=1, source_target_pairs={{0,16},{4,20},{8,24},{12,28},{16,0},{20,4},{24,8},{28,12},{1,17},{... | collective-permute-start | bytes 208904 | tf_op jit(solution)/shard_map/ppermute | solution.py:473
  50.8 6.3 %collective-permute-start.19 = (bf16[16,2176]{1,0:T(8,128)(2,1)S(1)}, bf16[16,2176]{1,0:T(8,128)(2,1)S(1)}, u32[]{:S(2)}, u32[]{:S(2)}) collective-permute-start(bf16[16,2176]{1,0:T(8,128)(2,1)S(1)} %get-tuple-element.133), channel_id=1, source_target_pairs={{0,24},{4,28},{8,16},{12,20},{16,8},{20,12},{24,0},{28,4},{1,25},{... | collective-permute-start | bytes 208904 | tf_op jit(solution)/shard_map/ppermute | solution.py:473
  52.5 5.1 %collective-permute-start.20 = (bf16[16,2176]{1,0:T(8,128)(2,1)S(1)}, bf16[16,2176]{1,0:T(8,128)(2,1)S(1)}, u32[]{:S(2)}, u32[]{:S(2)}) collective-permute-start(bf16[16,2176]{1,0:T(8,128)(2,1)S(1)} %get-tuple-element.134), channel_id=1, source_target_pairs={{0,8},{4,12},{8,0},{12,4},{16,24},{20,28},{24,16},{28,20},{1,9},{5... | collective-permute-start | bytes 208904 | tf_op jit(solution)/shard_map/ppermute | solution.py:473
  (3 other events, 11.6 us)

commit v15 on v14

--- a/solution.py
+++ b/solution.py
@@ -350,18 +350,21 @@
     )(*own, *other)
 
 
-def add_kernel(left, right, out):
-    total = left[...].astype(jnp.float32) + right[...].astype(jnp.float32)
-    out[...] = total.astype(jnp.bfloat16)
-
-
-def add_rows(left, right):
+def add_kernel(left, right, *outs):
+    total = (left[...].astype(jnp.float32) + right[...].astype(jnp.float32)).astype(jnp.bfloat16)
+    block = outs[0].shape[0]
+    for i, out in enumerate(outs):
+        out[...] = total[i * block : (i + 1) * block]
+
+
+def add_rows(left, right, count):
+    rows, width = left.shape
     return pl.pallas_call(
         add_kernel,
-        out_shape=struct(left.shape),
+        out_shape=[struct((rows // count, width))] * count,
         in_specs=[VMEM] * 2,
-        out_specs=VMEM,
-        compiler_params=pltpu.CompilerParams(vmem_limit_bytes=4 * MIB + 16 * left.size),
+        out_specs=[VMEM] * count,
+        compiler_params=pltpu.CompilerParams(vmem_limit_bytes=4 * MIB + 16 * rows * width),
         name="add_rows",
     )(left, right)
 
@@ -482,7 +485,7 @@
 
 
 def return_offsets(count):
-    even = list(range(count // 2, count, 2)) + list(range(count // 2 - 2, -1, -2))
+    even = list(range(count // 2 - 2, -1, -2)) + list(range(count // 2, count, 2))
     return [k ^ 1 for k in even], even
 
 
@@ -556,9 +559,11 @@
     parts = sum_rows(targets, (own_left, own_right), (left, right))
     gate_f, up_f, _ = tie((gate_f, up_f, parts))
     grad_gate, grad_up = weight_grads((gate_f, up_f), token_halves)
+    parts = [list(parts[group::2]) for group in range(2)]
+    parts[1], grad_gate, grad_up = tie((parts[1], grad_gate, grad_up))
     sums = []
     for group in range(2):
-        held = dict(zip(near, parts[group::2]))
+        held = dict(zip(near, parts[group]))
         for bit in reversed(far_bits):
             masks = [mask for mask in held if mask & bit]
             moved = {mask: flip(held.pop(mask), "dp", bit) for mask in masks}
@@ -568,14 +573,15 @@
                 sums.append((held[0], moved[bit]))
             else:
                 for mask in masks:
-                    held[mask ^ bit] = add_rows(held[mask ^ bit], moved[mask])
-    passed = add_rows(*sums[0])
+                    (held[mask ^ bit],) = add_rows(held[mask ^ bit], moved[mask], 1)
+    passed = add_rows(*sums[0], 2)
     hidden, _ = tie((hidden, passed))
     (grad_down,) = weight_grads((hidden,), grad_halves)
-    passed = flip(passed, "expert", 1)
+    passed = [flip(value, "expert", 1) for value in passed]
     kept, moved, grad_down = tie((*sums[1], grad_down))
-    kept, passed = tie((add_rows(kept, moved), passed))
-    returned = exchange(merge_rows(kept, passed), even)
+    kept = add_rows(kept, moved, 2)
+    merged = [block for pair in zip(kept, passed) for block in merge_rows(*pair)]
+    returned = exchange(merged, even)
     token_grad, gate_grad = combine(table, gates, returned, width)
     grads = (grad_gate, grad_up, grad_down)
     return (token_grad, gate_grad.T, *(grad[None] for grad in grads))

time: 58.7 us -> 58.3 us (level)
  waiting for transfers between devices: 17.3 us -> 16.3 us
  starting transfers between devices: 25.6 us -> 26.3 us
    ppermute x21 -> x22, waiting for transfers between devices: 17.3 us -> 16.3 us  [flip(): return lax.ppermute(value, axis, [(i, i ^ bit) for i in range(size)])]
    ppermute x21 -> x22, starting transfers between devices: 25.6 us -> 26.3 us  [flip(): return lax.ppermute(value, axis, [(i, i ^ bit) for i in range(size)])]
  transfers between devices with their start and end apart: 21 -> 22, of which waited for: 12 -> 12; matrix products, arithmetic and copies ran while one was open for 0% -> 0% of each run, Pallas kernels for 10% -> 11%
where the time goes in v15:
time: 58.3 us; the launch traced here: 58.1 us
  starting transfers between devices  26.3 us (45%)
  waiting for transfers between devices  16.3 us (28%)
  Pallas kernels  14.8 us (25%)
  between operations  0.8 us (1%)
    ppermute x22, starting transfers between devices, flip(): return lax.ppermute(value, axis, [(i, i ^ bit) for i in range(size)])  26.3 us
    ppermute x22, waiting for transfers between devices, flip(): return lax.ppermute(value, axis, [(i, i ^ bit) for i in range(size)])  16.3 us
    pallas_call x2, Pallas kernels, weight_grads(): pl.pallas_call(functools.partial(weight_kernel, chunk, count), out_shape=...  5.05 us
    pallas_call x1, Pallas kernels, backward(): pl.pallas_call(functools.partial(backward_kernel, count), out_shape=[stru...  3.3 us
    pallas_call x1, Pallas kernels, dispatch(): pl.pallas_call(functools.partial(dispatch_kernel, n_targets), out_shape=[...  2.28 us
    pallas_call x1, Pallas kernels, forward(): pl.pallas_call(functools.partial(forward_kernel, count), out_shape=[struc...  1.95 us
  transfers between devices with their start and end apart: 22, of which 12 were waited for; matrix products, arithmetic and copies ran while one was open for 0% of the time, Pallas kernels for 11%

profile of v15, /device:TPU:0, one launch (start us, length us, event | category | flops | bytes accessed | tf_op | source)
XLA Modules:
  0.0 58.1 jit_solution(7647870308176267670)
XLA Ops:
  0.6 2.3 %dispatch.1 = (bf16[8,4096]{1,0:T(8,128)(2,1)}, bf16[8,4096]{1,0:T(8,128)(2,1)}, bf16[8,4096]{1,0:T(8,128)(2,1)}, bf16[8,4096]{1,0:T(8,128)(2,1)}, bf16[8,4096]{...) custom-call(s32[8,32]{1,0:T(8,128)} %bitcast.16, ...), custom_call_target="tpu_custom_call" | custom-call | tf_op jit(solution)/shard_map/dispatch/pallas_call | solution.py:91
  2.9 3.0 %collective-permute-start = (bf16[8,4096]{1,0:T(8,128)(2,1)}, bf16[8,4096]{1,0:T(8,128)(2,1)S(1)}, u32[]{:S(2)}, u32[]{:S(2)}) collective-permute-start(bf16[8,4096]{1,0:T(8,128)(2,1)} %get-tuple-element.80), channel_id=1, source_target_pairs={{0,4},{4,0},{8,12},{12,8},{16,20},{20,16},{24,28},{28,24},{1,5},{5... | collective-permute-start | bytes 196616 | tf_op jit(solution)/shard_map/ppermute | solution.py:476
  6.0 2.6 %collective-permute-start.1 = (bf16[8,4096]{1,0:T(8,128)(2,1)}, bf16[8,4096]{1,0:T(8,128)(2,1)S(1)}, u32[]{:S(2)}, u32[]{:S(2)}) collective-permute-start(bf16[8,4096]{1,0:T(8,128)(2,1)} %get-tuple-element.81), channel_id=1, source_target_pairs={{0,16},{4,20},{8,24},{12,28},{16,0},{20,4},{24,8},{28,12},{1,17},{... | collective-permute-start | bytes 196616 | tf_op jit(solution)/shard_map/ppermute | solution.py:476
  8.5 1.6 %collective-permute-start.2 = (bf16[8,4096]{1,0:T(8,128)(2,1)}, bf16[8,4096]{1,0:T(8,128)(2,1)S(1)}, u32[]{:S(2)}, u32[]{:S(2)}) collective-permute-start(bf16[8,4096]{1,0:T(8,128)(2,1)} %get-tuple-element.82), channel_id=1, source_target_pairs={{0,8},{4,12},{8,0},{12,4},{16,24},{20,28},{24,16},{28,20},{1,9},{5... | collective-permute-start | bytes 196616 | tf_op jit(solution)/shard_map/ppermute | solution.py:476
  10.4 1.4 %collective-permute-start.4 = (bf16[8,4096]{1,0:T(8,128)(2,1)}, bf16[8,4096]{1,0:T(8,128)(2,1)S(1)}, u32[]{:S(2)}, u32[]{:S(2)}) collective-permute-start(bf16[8,4096]{1,0:T(8,128)(2,1)} %get-tuple-element.86), channel_id=1, source_target_pairs={{0,12},{4,8},{8,4},{12,0},{16,28},{20,24},{24,20},{28,16},{1,13},{... | collective-permute-start | bytes 196616 | tf_op jit(solution)/shard_map/ppermute | solution.py:476
  11.8 3.6 %collective-permute-start.5 = (bf16[8,4096]{1,0:T(8,128)(2,1)}, bf16[8,4096]{1,0:T(8,128)(2,1)S(1)}, u32[]{:S(2)}, u32[]{:S(2)}) collective-permute-start(bf16[8,4096]{1,0:T(8,128)(2,1)} %get-tuple-element.87), channel_id=1, source_target_pairs={{0,24},{4,28},{8,16},{12,20},{16,8},{20,12},{24,0},{28,4},{1,25},{... | collective-permute-start | bytes 196616 | tf_op jit(solution)/shard_map/ppermute | solution.py:476
  15.4 1.6 %collective-permute-start.6 = (bf16[8,4096]{1,0:T(8,128)(2,1)}, bf16[8,4096]{1,0:T(8,128)(2,1)S(1)}, u32[]{:S(2)}, u32[]{:S(2)}) collective-permute-start(bf16[8,4096]{1,0:T(8,128)(2,1)} %get-tuple-element.88), channel_id=1, source_target_pairs={{0,28},{4,24},{8,20},{12,16},{16,12},{20,8},{24,4},{28,0},{1,29},{... | collective-permute-start | bytes 196616 | tf_op jit(solution)/shard_map/ppermute | solution.py:476
  17.1 1.5 %collective-permute-start.7 = (bf16[32,4096]{1,0:T(8,128)(2,1)S(1)}, bf16[32,4096]{1,0:T(8,128)(2,1)S(1)}, u32[]{:S(2)}, u32[]{:S(2)}) collective-permute-start(bf16[32,4096]{1,0:T(8,128)(2,1)S(1)} %pack.4.rows), channel_id=1, source_target_pairs={{0,2},{1,3},{2,0},{3,1},{4,6},{5,7},{6,4},{7,5},{8,10},{9,11},{10,... | collective-permute-start | bytes 786440 | tf_op jit(solution)/shard_map/ppermute | solution.py:476
  18.7 1.2 %collective-permute-done.3.refs_0_ = bf16[8,4096]{1,0:T(8,128)(2,1)S(1)} collective-permute-done((bf16[8,4096]{1,0:T(8,128)(2,1)}, bf16[8,4096]{1,0:T(8,128)(2,1)S(1)}, u32[]{:S(2)}, u32[]{:S(2)}) %collective-permute-start.3) | collective-permute-done | bytes 65568 | tf_op jit(solution)/shard_map/ppermute | solution.py:476
  19.9 2.7 %collective-permute-done.6.refs_3_ = bf16[8,4096]{1,0:T(8,128)(2,1)S(1)} collective-permute-done((bf16[8,4096]{1,0:T(8,128)(2,1)}, bf16[8,4096]{1,0:T(8,128)(2,1)S(1)}, u32[]{:S(2)}, u32[]{:S(2)}) %collective-permute-start.6) | collective-permute-done | bytes 65568 | tf_op jit(solution)/shard_map/ppermute | solution.py:476
  22.6 1.6 %collective-permute-start.11 = (bf16[32,4096]{1,0:T(8,128)(2,1)S(1)}, bf16[32,4096]{1,0:T(8,128)(2,1)S(1)}, u32[]{:S(2)}, u32[]{:S(2)}) collective-permute-start(bf16[32,4096]{1,0:T(8,128)(2,1)S(1)} %pack.5.refs_1_), channel_id=1, source_target_pairs={{0,2},{1,3},{2,0},{3,1},{4,6},{5,7},{6,4},{7,5},{8,10},{9,11},{10,... | collective-permute-start | bytes 786440 | tf_op jit(solution)/shard_map/ppermute | solution.py:476
  25.3 3.8 %collective-permute-done.11.refs_3_ = bf16[32,4096]{1,0:T(8,128)(2,1)S(1)} collective-permute-done((bf16[32,4096]{1,0:T(8,128)(2,1)S(1)}, bf16[32,4096]{1,0:T(8,128)(2,1)S(1)}, u32[]{:S(2)}, u32[]{:S(2)}) %collective-permute-start.11) | collective-permute-done | bytes 262176 | tf_op jit(solution)/shard_map/ppermute | solution.py:476
  29.3 1.5 %collective-permute-done.12.refs_7_ = bf16[32,4096]{1,0:T(8,128)(2,1)S(1)} collective-permute-done((bf16[32,4096]{1,0:T(8,128)(2,1)S(1)}, bf16[32,4096]{1,0:T(8,128)(2,1)S(1)}, u32[]{:S(2)}, u32[]{:S(2)}) %collective-permute-start.12) | collective-permute-done | bytes 262176 | tf_op jit(solution)/shard_map/ppermute | solution.py:476
  30.8 2.0 %forward.1 = (bf16[256,2048]{1,0:T(8,128)(2,1)S(1)}, f32[384,256]{1,0:T(8,128)S(1)}, f32[384,256]{1,0:T(8,128)S(1)}, bf16[384,256]{1,0:T(8,128)(2,1)S(1)}) custom-call(bf16[32,2048]{1,0:T(8,128)(2,1)S(1)} %get-tuple-element.108.refs_0_, bf16[32,4096]{1,0:T(8,128)(2,1)S(1)} %pack.5.refs_1_, bf16[32,4096]{1,0:T(8,128)(2,1)S(1)} %collective-permute-done.7.refs_2_, ...), custom_call_target="tpu_custom_call" | custom-call | flops 1000000 | bytes 10000 | tf_op jit(solution)/shard_map/forward/pallas_call | solution.py:207
  32.8 3.3 %backward.1 = (bf16[128,1536]{1,0:T(8,128)(2,1)S(1)}, bf16[128,1536]{1,0:T(8,128)(2,1)S(1)}, bf16[256,2048]{1,0:T(8,128)(2,1)S(1)}, bf16[384,256]{1,0:T(8,128)(2...) custom-call(bf16[32,2048]{1,0:T(8,128)(2,1)S(1)} %get-tuple-element.103.refs_0_, ...), custom_call_target="tpu_custom_call" | custom-call | flops 1000000 | bytes 10000 | tf_op jit(solution)/shard_map/backward/pallas_call | solution.py:288
  38.5 1.6 %collective-permute-start.16 = (bf16[32,2176]{1,0:T(8,128)(2,1)S(1)}, bf16[32,2176]{1,0:T(8,128)(2,1)S(1)}, u32[]{:S(2)}, u32[]{:S(2)}) collective-permute-start(bf16[32,2176]{1,0:T(8,128)(2,1)S(1)} %get-tuple-element.125), channel_id=1, source_target_pairs={{0,2},{1,3},{2,0},{3,1},{4,6},{5,7},{6,4},{7,5},{8,10},{9,11},{10,... | collective-permute-start | bytes 417800 | tf_op jit(solution)/shard_map/ppermute | solution.py:476
  40.1 3.1 %weight_grads.2 = (bf16[384,4096]{1,0:T(8,128)(2,1)}, bf16[384,4096]{1,0:T(8,128)(2,1)}) custom-call(bf16[384,256]{1,0:T(8,128)(2,1)S(1)} %get-tuple-element.126.refs_0_, bf16[384,256]{1,0:T(8,128)(2,1)S(1)} %get-tuple-element.127.refs_1_, bf16[256,2048]{1,0:T(8,128)(2,1)S(1)} %get-tuple-element.128.refs_2_), custom_call_target="tpu_custom_call" | custom-call | flops 1000000 | bytes 10000 | tf_op jit(solution)/shard_map/weight_grads/pallas_call | solution.py:423
  43.8 0.8 %collective-permute-done.16.right = bf16[32,2176]{1,0:T(8,128)(2,1)S(1)} collective-permute-done((bf16[32,2176]{1,0:T(8,128)(2,1)S(1)}, bf16[32,2176]{1,0:T(8,128)(2,1)S(1)}, u32[]{:S(2)}, u32[]{:S(2)}) %collective-permute-start.16) | collective-permute-done | bytes 139296 | tf_op jit(solution)/shard_map/ppermute | solution.py:476
  44.6 1.6 %collective-permute-start.19 = (bf16[16,2176]{1,0:T(8,128)(2,1)S(1)}, bf16[16,2176]{1,0:T(8,128)(2,1)S(1)}, u32[]{:S(2)}, u32[]{:S(2)}) collective-permute-start(bf16[16,2176]{1,0:T(8,128)(2,1)S(1)} %get-tuple-element.137), channel_id=1, source_target_pairs={{0,4},{4,0},{8,12},{12,8},{16,20},{20,16},{24,28},{28,24},{1,5},{5... | collective-permute-start | bytes 208904 | tf_op jit(solution)/shard_map/ppermute | solution.py:476
  46.7 2.0 %weight_grads.3 = bf16[384,4096]{1,0:T(8,128)(2,1)} custom-call(bf16[384,256]{1,0:T(8,128)(2,1)S(1)} %get-tuple-element.138.refs_10_.refs_0_, bf16[256,2048]{1,0:T(8,128)(2,1)S(1)} %get-tuple-element.139.refs_1_), custom_call_target="tpu_custom_call" | custom-call | flops 1000000 | bytes 10000 | tf_op jit(solution)/shard_map/weight_grads/pallas_call | solution.py:423
  50.0 1.7 %collective-permute-start.21 = (bf16[16,2176]{1,0:T(8,128)(2,1)S(1)}, bf16[16,2176]{1,0:T(8,128)(2,1)S(1)}, u32[]{:S(2)}, u32[]{:S(2)}) collective-permute-start(bf16[16,2176]{1,0:T(8,128)(2,1)S(1)} %get-tuple-element.147), channel_id=1, source_target_pairs={{0,24},{4,28},{8,16},{12,20},{16,8},{20,12},{24,0},{28,4},{1,25},{... | collective-permute-start | bytes 208904 | tf_op jit(solution)/shard_map/ppermute | solution.py:476
  51.8 1.4 %collective-permute-start.18 = (bf16[16,2176]{1,0:T(8,128)(2,1)S(1)}, bf16[16,2176]{1,0:T(8,128)(2,1)S(1)}, u32[]{:S(2)}, u32[]{:S(2)}) collective-permute-start(bf16[16,2176]{1,0:T(8,128)(2,1)S(1)} %get-tuple-element.143), channel_id=1, source_target_pairs={{0,8},{4,12},{8,0},{12,4},{16,24},{20,28},{24,16},{28,20},{1,9},{5... | collective-permute-start | bytes 208904 | tf_op jit(solution)/shard_map/ppermute | solution.py:476
  53.2 3.3 %collective-permute-done.20.refs_2_ = bf16[16,2176]{1,0:T(8,128)(2,1)S(1)} collective-permute-done((bf16[16,2176]{1,0:T(8,128)(2,1)S(1)}, bf16[16,2176]{1,0:T(8,128)(2,1)S(1)}, u32[]{:S(2)}, u32[]{:S(2)}) %collective-permute-start.20) | collective-permute-done | bytes 69664 | tf_op jit(solution)/shard_map/ppermute | solution.py:476
  57.1 1.0 %combine.1 = (bf16[32,4096]{1,0:T(8,128)(2,1)}, f32[8,32]{1,0:T(8,128)}) custom-call(bf16[64,32]{1,0:T(8,128)(2,1)S(1)} %get-tuple-element.100.first, bf16[64,32]{1,0:T(8,128)(2,1)S(1)} %get-tuple-element.101.second, s32[64,32]{1,0:T(8,128)S(1)} %get-tuple-element.102.choice_ref, bf16[8,32]{1,0:T(8,128)(2,1)S(1)} %bitcast.19, ...), custom_call_target="tpu_custom_call" | custom-call | tf_op jit(solution)/shard_map/combine/pallas_call | solution.py:462
  (49 shorter events, 7.3 us)
Async XLA Ops:
  2.9 8.9 %collective-permute-start = (bf16[8,4096]{1,0:T(8,128)(2,1)}, bf16[8,4096]{1,0:T(8,128)(2,1)S(1)}, u32[]{:S(2)}, u32[]{:S(2)}) collective-permute-start(bf16[8,4096]{1,0:T(8,128)(2,1)} %get-tuple-element.80), channel_id=1, source_target_pairs={{0,4},{4,0},{8,12},{12,8},{16,20},{20,16},{24,28},{28,24},{1,5},{5... | collective-permute-start | bytes 196616 | tf_op jit(solution)/shard_map/ppermute | solution.py:476
  6.0 9.5 %collective-permute-start.1 = (bf16[8,4096]{1,0:T(8,128)(2,1)}, bf16[8,4096]{1,0:T(8,128)(2,1)S(1)}, u32[]{:S(2)}, u32[]{:S(2)}) collective-permute-start(bf16[8,4096]{1,0:T(8,128)(2,1)} %get-tuple-element.81), channel_id=1, source_target_pairs={{0,16},{4,20},{8,24},{12,28},{16,0},{20,4},{24,8},{28,12},{1,17},{... | collective-permute-start | bytes 196616 | tf_op jit(solution)/shard_map/ppermute | solution.py:476
  8.5 8.5 %collective-permute-start.2 = (bf16[8,4096]{1,0:T(8,128)(2,1)}, bf16[8,4096]{1,0:T(8,128)(2,1)S(1)}, u32[]{:S(2)}, u32[]{:S(2)}) collective-permute-start(bf16[8,4096]{1,0:T(8,128)(2,1)} %get-tuple-element.82), channel_id=1, source_target_pairs={{0,8},{4,12},{8,0},{12,4},{16,24},{20,28},{24,16},{28,20},{1,9},{5... | collective-permute-start | bytes 196616 | tf_op jit(solution)/shard_map/ppermute | solution.py:476
  10.1 9.8 %collective-permute-start.3 = (bf16[8,4096]{1,0:T(8,128)(2,1)}, bf16[8,4096]{1,0:T(8,128)(2,1)S(1)}, u32[]{:S(2)}, u32[]{:S(2)}) collective-permute-start(bf16[8,4096]{1,0:T(8,128)(2,1)} %get-tuple-element.85), channel_id=1, source_target_pairs={{0,20},{4,16},{8,28},{12,24},{16,4},{20,0},{24,12},{28,8},{1,21},{... | collective-permute-start | bytes 196616 | tf_op jit(solution)/shard_map/ppermute | solution.py:476
  10.4 9.5 %collective-permute-start.4 = (bf16[8,4096]{1,0:T(8,128)(2,1)}, bf16[8,4096]{1,0:T(8,128)(2,1)S(1)}, u32[]{:S(2)}, u32[]{:S(2)}) collective-permute-start(bf16[8,4096]{1,0:T(8,128)(2,1)} %get-tuple-element.86), channel_id=1, source_target_pairs={{0,12},{4,8},{8,4},{12,0},{16,28},{20,24},{24,20},{28,16},{1,13},{... | collective-permute-start | bytes 196616 | tf_op jit(solution)/shard_map/ppermute | solution.py:476
  11.8 8.1 %collective-permute-start.5 = (bf16[8,4096]{1,0:T(8,128)(2,1)}, bf16[8,4096]{1,0:T(8,128)(2,1)S(1)}, u32[]{:S(2)}, u32[]{:S(2)}) collective-permute-start(bf16[8,4096]{1,0:T(8,128)(2,1)} %get-tuple-element.87), channel_id=1, source_target_pairs={{0,24},{4,28},{8,16},{12,20},{16,8},{20,12},{24,0},{28,4},{1,25},{... | collective-permute-start | bytes 196616 | tf_op jit(solution)/shard_map/ppermute | solution.py:476
  15.4 7.2 %collective-permute-start.6 = (bf16[8,4096]{1,0:T(8,128)(2,1)}, bf16[8,4096]{1,0:T(8,128)(2,1)S(1)}, u32[]{:S(2)}, u32[]{:S(2)}) collective-permute-start(bf16[8,4096]{1,0:T(8,128)(2,1)} %get-tuple-element.88), channel_id=1, source_target_pairs={{0,28},{4,24},{8,20},{12,16},{16,12},{20,8},{24,4},{28,0},{1,29},{... | collective-permute-start | bytes 196616 | tf_op jit(solution)/shard_map/ppermute | solution.py:476
  17.1 13.7 %copy-start = (bf16[1,384,4096]{2,1,0:T(8,128)(2,1)S(1)}, bf16[1,384,4096]{2,1,0:T(8,128)(2,1)}, u32[]{:S(2)}) copy-start(bf16[1,384,4096]{2,1,0:T(8,128)(2,1)} %param.11) | copy-start | bytes 9437188
  17.1 7.5 %collective-permute-start.7 = (bf16[32,4096]{1,0:T(8,128)(2,1)S(1)}, bf16[32,4096]{1,0:T(8,128)(2,1)S(1)}, u32[]{:S(2)}, u32[]{:S(2)}) collective-permute-start(bf16[32,4096]{1,0:T(8,128)(2,1)S(1)} %pack.4.rows), channel_id=1, source_target_pairs={{0,2},{1,3},{2,0},{3,1},{4,6},{5,7},{6,4},{7,5},{8,10},{9,11},{10,... | collective-permute-start | bytes 786440 | tf_op jit(solution)/shard_map/ppermute | solution.py:476
  22.6 6.5 %collective-permute-start.11 = (bf16[32,4096]{1,0:T(8,128)(2,1)S(1)}, bf16[32,4096]{1,0:T(8,128)(2,1)S(1)}, u32[]{:S(2)}, u32[]{:S(2)}) collective-permute-start(bf16[32,4096]{1,0:T(8,128)(2,1)S(1)} %pack.5.refs_1_), channel_id=1, source_target_pairs={{0,2},{1,3},{2,0},{3,1},{4,6},{5,7},{6,4},{7,5},{8,10},{9,11},{10,... | collective-permute-start | bytes 786440 | tf_op jit(solution)/shard_map/ppermute | solution.py:476
  24.6 4.6 %collective-permute-start.8 = (bf16[32,4096]{1,0:T(8,128)(2,1)S(1)}, bf16[32,4096]{1,0:T(8,128)(2,1)S(1)}, u32[]{:S(2)}, u32[]{:S(2)}) collective-permute-start(bf16[32,4096]{1,0:T(8,128)(2,1)S(1)} %pack.4.rows), channel_id=1, source_target_pairs={{0,1},{1,0},{2,3},{3,2},{4,5},{5,4},{6,7},{7,6},{8,9},{9,8},{10,11... | collective-permute-start | bytes 786440 | tf_op jit(solution)/shard_map/ppermute | solution.py:476
  24.6 4.6 %collective-permute-start.9 = (bf16[32,4096]{1,0:T(8,128)(2,1)S(1)}, bf16[32,4096]{1,0:T(8,128)(2,1)S(1)}, u32[]{:S(2)}, u32[]{:S(2)}) collective-permute-start(bf16[32,4096]{1,0:T(8,128)(2,1)S(1)} %collective-permute-done.7.refs_2_), channel_id=1, source_target_pairs={{0,1},{1,0},{2,3},{3,2},{4,5},{5,4},{6,7},{7,6},{8,9},{9,8},{10,11... | collective-permute-start | bytes 786440 | tf_op jit(solution)/shard_map/ppermute | solution.py:476
  25.1 4.0 %collective-permute-start.10 = (bf16[32,4096]{1,0:T(8,128)(2,1)S(1)}, bf16[32,4096]{1,0:T(8,128)(2,1)S(1)}, u32[]{:S(2)}, u32[]{:S(2)}) collective-permute-start(bf16[32,4096]{1,0:T(8,128)(2,1)S(1)} %pack.5.refs_1_), channel_id=1, source_target_pairs={{0,1},{1,0},{2,3},{3,2},{4,5},{5,4},{6,7},{7,6},{8,9},{9,8},{10,11... | collective-permute-start | bytes 786440 | tf_op jit(solution)/shard_map/ppermute | solution.py:476
  29.2 1.6 %collective-permute-start.12 = (bf16[32,4096]{1,0:T(8,128)(2,1)S(1)}, bf16[32,4096]{1,0:T(8,128)(2,1)S(1)}, u32[]{:S(2)}, u32[]{:S(2)}) collective-permute-start(bf16[32,4096]{1,0:T(8,128)(2,1)S(1)} %collective-permute-done.11.refs_3_), channel_id=1, source_target_pairs={{0,1},{1,0},{2,3},{3,2},{4,5},{5,4},{6,7},{7,6},{8,9},{9,8},{10,11... | collective-permute-start | bytes 786440 | tf_op jit(solution)/shard_map/ppermute | solution.py:476
  36.1 1.8 %collective-permute-start.13 = (bf16[128,1536]{1,0:T(8,128)(2,1)S(1)}, bf16[128,1536]{1,0:T(8,128)(2,1)S(1)}, u32[]{:S(2)}, u32[]{:S(2)}) collective-permute-start(bf16[128,1536]{1,0:T(8,128)(2,1)S(1)} %get-tuple-element.113), channel_id=1, source_target_pairs={{0,1},{1,0},{2,3},{3,2},{4,5},{5,4},{6,7},{7,6},{8,9},{9,8},{10,11... | collective-permute-start | bytes 1179656 | tf_op jit(solution)/shard_map/ppermute | solution.py:476
  36.9 1.5 %collective-permute-start.14 = (bf16[128,640]{1,0:T(8,128)(2,1)S(1)}, bf16[128,640]{1,0:T(8,128)(2,1)S(1)}, u32[]{:S(2)}, u32[]{:S(2)}) collective-permute-start(bf16[128,640]{1,0:T(8,128)(2,1)S(1)} %get-tuple-element.119), channel_id=1, source_target_pairs={{0,1},{1,0},{2,3},{3,2},{4,5},{5,4},{6,7},{7,6},{8,9},{9,8},{10,11... | collective-permute-start | bytes 491528 | tf_op jit(solution)/shard_map/ppermute | solution.py:476
  38.5 6.0 %collective-permute-start.16 = (bf16[32,2176]{1,0:T(8,128)(2,1)S(1)}, bf16[32,2176]{1,0:T(8,128)(2,1)S(1)}, u32[]{:S(2)}, u32[]{:S(2)}) collective-permute-start(bf16[32,2176]{1,0:T(8,128)(2,1)S(1)} %get-tuple-element.125), channel_id=1, source_target_pairs={{0,2},{1,3},{2,0},{3,1},{4,6},{5,7},{6,4},{7,5},{8,10},{9,11},{10,... | collective-permute-start | bytes 417800 | tf_op jit(solution)/shard_map/ppermute | solution.py:476
  40.1 17.0 %copy-start.5 = (bf16[32,8]{0,1:T(8,128)(2,1)S(1)}, bf16[32,8]{0,1:T(8,128)(2,1)}, u32[]{:S(2)}) copy-start(bf16[32,8]{0,1:T(8,128)(2,1)} %param.9) | copy-start | bytes 1540
  43.2 5.7 %collective-permute-start.15 = (bf16[32,2176]{1,0:T(8,128)(2,1)S(1)}, bf16[32,2176]{1,0:T(8,128)(2,1)S(1)}, u32[]{:S(2)}, u32[]{:S(2)}) collective-permute-start(bf16[32,2176]{1,0:T(8,128)(2,1)S(1)} %get-tuple-element.132), channel_id=1, source_target_pairs={{0,2},{1,3},{2,0},{3,1},{4,6},{5,7},{6,4},{7,5},{8,10},{9,11},{10,... | collective-permute-start | bytes 417800 | tf_op jit(solution)/shard_map/ppermute | solution.py:476
  44.6 4.9 %collective-permute-start.19 = (bf16[16,2176]{1,0:T(8,128)(2,1)S(1)}, bf16[16,2176]{1,0:T(8,128)(2,1)S(1)}, u32[]{:S(2)}, u32[]{:S(2)}) collective-permute-start(bf16[16,2176]{1,0:T(8,128)(2,1)S(1)} %get-tuple-element.137), channel_id=1, source_target_pairs={{0,4},{4,0},{8,12},{12,8},{16,20},{20,16},{24,28},{28,24},{1,5},{5... | collective-permute-start | bytes 208904 | tf_op jit(solution)/shard_map/ppermute | solution.py:476
  46.2 5.6 %collective-permute-start.17 = (bf16[16,2176]{1,0:T(8,128)(2,1)S(1)}, bf16[16,2176]{1,0:T(8,128)(2,1)S(1)}, u32[]{:S(2)}, u32[]{:S(2)}) collective-permute-start(bf16[16,2176]{1,0:T(8,128)(2,1)S(1)} %get-tuple-element.136), channel_id=1, source_target_pairs={{0,4},{4,0},{8,12},{12,8},{16,20},{20,16},{24,28},{28,24},{1,5},{5... | collective-permute-start | bytes 208904 | tf_op jit(solution)/shard_map/ppermute | solution.py:476
  49.5 6.9 %collective-permute-start.20 = (bf16[16,2176]{1,0:T(8,128)(2,1)S(1)}, bf16[16,2176]{1,0:T(8,128)(2,1)S(1)}, u32[]{:S(2)}, u32[]{:S(2)}) collective-permute-start(bf16[16,2176]{1,0:T(8,128)(2,1)S(1)} %get-tuple-element.146), channel_id=1, source_target_pairs={{0,16},{4,20},{8,24},{12,28},{16,0},{20,4},{24,8},{28,12},{1,17},{... | collective-permute-start | bytes 208904 | tf_op jit(solution)/shard_map/ppermute | solution.py:476
  50.0 6.4 %collective-permute-start.21 = (bf16[16,2176]{1,0:T(8,128)(2,1)S(1)}, bf16[16,2176]{1,0:T(8,128)(2,1)S(1)}, u32[]{:S(2)}, u32[]{:S(2)}) collective-permute-start(bf16[16,2176]{1,0:T(8,128)(2,1)S(1)} %get-tuple-element.147), channel_id=1, source_target_pairs={{0,24},{4,28},{8,16},{12,20},{16,8},{20,12},{24,0},{28,4},{1,25},{... | collective-permute-start | bytes 208904 | tf_op jit(solution)/shard_map/ppermute | solution.py:476
  51.8 5.4 %collective-permute-start.18 = (bf16[16,2176]{1,0:T(8,128)(2,1)S(1)}, bf16[16,2176]{1,0:T(8,128)(2,1)S(1)}, u32[]{:S(2)}, u32[]{:S(2)}) collective-permute-start(bf16[16,2176]{1,0:T(8,128)(2,1)S(1)} %get-tuple-element.143), channel_id=1, source_target_pairs={{0,8},{4,12},{8,0},{12,4},{16,24},{20,28},{24,16},{28,20},{1,9},{5... | collective-permute-start | bytes 208904 | tf_op jit(solution)/shard_map/ppermute | solution.py:476
  (4 other events, 25.3 us)

commit v16 on v15

--- a/solution.py
+++ b/solution.py
@@ -478,10 +478,9 @@
 
 def offsets(count):
     near, far = list(range(1, count // 2)), list(range(count // 2, count))
-    order = [0]
-    for i, k in enumerate(near):
-        order += [k, far[i]]
-    return order + far[len(near) :]
+    mixed = [k for pair in zip(near, far) for k in pair] + far[len(near) :]
+    head, tail = mixed[: count // 2 - 1], mixed[count // 2 - 1 :]
+    return [0] + head + sorted(tail, key=lambda k: (k < count // 2, k))
 
 
 def return_offsets(count):

time: 58.3 us -> 59.6 us (1.022)
  local copies, waits for them, and re-layouts: 0.03 us -> 0.82 us
    unnamed x12, local copies, waits for them, and re-layouts: 0.03 us -> 0.82 us
  transfers between devices with their start and end apart: 22 -> 22, of which waited for: 12 -> 13; matrix products, arithmetic and copies ran while one was open for 0% -> 0% of each run, Pallas kernels for 11% -> 10%
where the time goes in v16:
time: 59.6 us; the launch traced here: 59.4 us
  starting transfers between devices  26.2 us (44%)
  waiting for transfers between devices  16.8 us (28%)
  Pallas kernels  14.8 us (25%)
  local copies, waits for them, and re-layouts  0.82 us (1%)
  between operations  0.8 us (1%)
    ppermute x22, starting transfers between devices, flip(): return lax.ppermute(value, axis, [(i, i ^ bit) for i in range(size)])  26.2 us
    ppermute x22, waiting for transfers between devices, flip(): return lax.ppermute(value, axis, [(i, i ^ bit) for i in range(size)])  16.8 us
    pallas_call x2, Pallas kernels, weight_grads(): pl.pallas_call(functools.partial(weight_kernel, chunk, count), out_shape=...  5.05 us
    pallas_call x1, Pallas kernels, backward(): pl.pallas_call(functools.partial(backward_kernel, count), out_shape=[stru...  3.3 us
    pallas_call x1, Pallas kernels, dispatch(): pl.pallas_call(functools.partial(dispatch_kernel, n_targets), out_shape=[...  2.28 us
    pallas_call x1, Pallas kernels, forward(): pl.pallas_call(functools.partial(forward_kernel, count), out_shape=[struc...  1.95 us
  transfers between devices with their start and end apart: 22, of which 13 were waited for; matrix products, arithmetic and copies ran while one was open for 0% of the time, Pallas kernels for 10%

profile of v16, /device:TPU:0, one launch (start us, length us, event | category | flops | bytes accessed | tf_op | source)
XLA Modules:
  0.0 59.4 jit_solution(6082311555248325781)
XLA Ops:
  0.6 2.3 %dispatch.1 = (bf16[8,4096]{1,0:T(8,128)(2,1)}, bf16[8,4096]{1,0:T(8,128)(2,1)}, bf16[8,4096]{1,0:T(8,128)(2,1)}, bf16[8,4096]{1,0:T(8,128)(2,1)}, bf16[8,4096]{...) custom-call(s32[8,32]{1,0:T(8,128)} %bitcast.16, ...), custom_call_target="tpu_custom_call" | custom-call | tf_op jit(solution)/shard_map/dispatch/pallas_call | solution.py:91
  2.9 3.0 %collective-permute-start = (bf16[8,4096]{1,0:T(8,128)(2,1)}, bf16[8,4096]{1,0:T(8,128)(2,1)S(1)}, u32[]{:S(2)}, u32[]{:S(2)}) collective-permute-start(bf16[8,4096]{1,0:T(8,128)(2,1)} %get-tuple-element.80), channel_id=1, source_target_pairs={{0,4},{4,0},{8,12},{12,8},{16,20},{20,16},{24,28},{28,24},{1,5},{5... | collective-permute-start | bytes 196616 | tf_op jit(solution)/shard_map/ppermute | solution.py:476
  6.0 2.6 %collective-permute-start.1 = (bf16[8,4096]{1,0:T(8,128)(2,1)}, bf16[8,4096]{1,0:T(8,128)(2,1)S(1)}, u32[]{:S(2)}, u32[]{:S(2)}) collective-permute-start(bf16[8,4096]{1,0:T(8,128)(2,1)} %get-tuple-element.81), channel_id=1, source_target_pairs={{0,16},{4,20},{8,24},{12,28},{16,0},{20,4},{24,8},{28,12},{1,17},{... | collective-permute-start | bytes 196616 | tf_op jit(solution)/shard_map/ppermute | solution.py:476
  8.5 1.6 %collective-permute-start.2 = (bf16[8,4096]{1,0:T(8,128)(2,1)}, bf16[8,4096]{1,0:T(8,128)(2,1)S(1)}, u32[]{:S(2)}, u32[]{:S(2)}) collective-permute-start(bf16[8,4096]{1,0:T(8,128)(2,1)} %get-tuple-element.82), channel_id=1, source_target_pairs={{0,8},{4,12},{8,0},{12,4},{16,24},{20,28},{24,16},{28,20},{1,9},{5... | collective-permute-start | bytes 196616 | tf_op jit(solution)/shard_map/ppermute | solution.py:476
  10.4 2.5 %collective-permute-start.4 = (bf16[8,4096]{1,0:T(8,128)(2,1)}, bf16[8,4096]{1,0:T(8,128)(2,1)S(1)}, u32[]{:S(2)}, u32[]{:S(2)}) collective-permute-start(bf16[8,4096]{1,0:T(8,128)(2,1)} %get-tuple-element.86), channel_id=1, source_target_pairs={{0,24},{4,28},{8,16},{12,20},{16,8},{20,12},{24,0},{28,4},{1,25},{... | collective-permute-start | bytes 196616 | tf_op jit(solution)/shard_map/ppermute | solution.py:476
  12.9 2.3 %collective-permute-start.5 = (bf16[8,4096]{1,0:T(8,128)(2,1)}, bf16[8,4096]{1,0:T(8,128)(2,1)S(1)}, u32[]{:S(2)}, u32[]{:S(2)}) collective-permute-start(bf16[8,4096]{1,0:T(8,128)(2,1)} %get-tuple-element.87), channel_id=1, source_target_pairs={{0,28},{4,24},{8,20},{12,16},{16,12},{20,8},{24,4},{28,0},{1,29},{... | collective-permute-start | bytes 196616 | tf_op jit(solution)/shard_map/ppermute | solution.py:476
  15.2 0.8 %copy-done.3 = bf16[8,4096]{1,0:T(8,128)(2,1)S(1)} copy-done((bf16[8,4096]{1,0:T(8,128)(2,1)S(1)}, bf16[8,4096]{1,0:T(8,128)(2,1)}, u32[]{:S(2)}) %copy-start.3) | copy-done | bytes 65560
  16.1 1.6 %collective-permute-start.7 = (bf16[32,4096]{1,0:T(8,128)(2,1)S(1)}, bf16[32,4096]{1,0:T(8,128)(2,1)S(1)}, u32[]{:S(2)}, u32[]{:S(2)}) collective-permute-start(bf16[32,4096]{1,0:T(8,128)(2,1)S(1)} %pack.4.rows), channel_id=1, source_target_pairs={{0,2},{1,3},{2,0},{3,1},{4,6},{5,7},{6,4},{7,5},{8,10},{9,11},{10,... | collective-permute-start | bytes 786440 | tf_op jit(solution)/shard_map/ppermute | solution.py:476
  17.7 1.5 %collective-permute-done.3.refs_0_ = bf16[8,4096]{1,0:T(8,128)(2,1)S(1)} collective-permute-done((bf16[8,4096]{1,0:T(8,128)(2,1)}, bf16[8,4096]{1,0:T(8,128)(2,1)S(1)}, u32[]{:S(2)}, u32[]{:S(2)}) %collective-permute-start.3) | collective-permute-done | bytes 65568 | tf_op jit(solution)/shard_map/ppermute | solution.py:476
  19.1 1.0 %collective-permute-done.5.refs_2_ = bf16[8,4096]{1,0:T(8,128)(2,1)S(1)} collective-permute-done((bf16[8,4096]{1,0:T(8,128)(2,1)}, bf16[8,4096]{1,0:T(8,128)(2,1)S(1)}, u32[]{:S(2)}, u32[]{:S(2)}) %collective-permute-start.5) | collective-permute-done | bytes 65568 | tf_op jit(solution)/shard_map/ppermute | solution.py:476
  20.9 1.6 %collective-permute-start.11 = (bf16[32,4096]{1,0:T(8,128)(2,1)S(1)}, bf16[32,4096]{1,0:T(8,128)(2,1)S(1)}, u32[]{:S(2)}, u32[]{:S(2)}) collective-permute-start(bf16[32,4096]{1,0:T(8,128)(2,1)S(1)} %pack.5.refs_1_), channel_id=1, source_target_pairs={{0,2},{1,3},{2,0},{3,1},{4,6},{5,7},{6,4},{7,5},{8,10},{9,11},{10,... | collective-permute-start | bytes 786440 | tf_op jit(solution)/shard_map/ppermute | solution.py:476
  23.4 4.7 %collective-permute-done.11.refs_3_ = bf16[32,4096]{1,0:T(8,128)(2,1)S(1)} collective-permute-done((bf16[32,4096]{1,0:T(8,128)(2,1)S(1)}, bf16[32,4096]{1,0:T(8,128)(2,1)S(1)}, u32[]{:S(2)}, u32[]{:S(2)}) %collective-permute-start.11) | collective-permute-done | bytes 262176 | tf_op jit(solution)/shard_map/ppermute | solution.py:476
  28.2 1.5 %collective-permute-done.12.refs_7_ = bf16[32,4096]{1,0:T(8,128)(2,1)S(1)} collective-permute-done((bf16[32,4096]{1,0:T(8,128)(2,1)S(1)}, bf16[32,4096]{1,0:T(8,128)(2,1)S(1)}, u32[]{:S(2)}, u32[]{:S(2)}) %collective-permute-start.12) | collective-permute-done | bytes 262176 | tf_op jit(solution)/shard_map/ppermute | solution.py:476
  29.8 2.0 %forward.1 = (bf16[256,2048]{1,0:T(8,128)(2,1)S(1)}, f32[384,256]{1,0:T(8,128)S(1)}, f32[384,256]{1,0:T(8,128)S(1)}, bf16[384,256]{1,0:T(8,128)(2,1)S(1)}) custom-call(bf16[32,2048]{1,0:T(8,128)(2,1)S(1)} %get-tuple-element.108.refs_0_, bf16[32,4096]{1,0:T(8,128)(2,1)S(1)} %pack.5.refs_1_, bf16[32,4096]{1,0:T(8,128)(2,1)S(1)} %collective-permute-done.7.refs_2_, ...), custom_call_target="tpu_custom_call" | custom-call | flops 1000000 | bytes 10000 | tf_op jit(solution)/shard_map/forward/pallas_call | solution.py:207
  31.7 3.3 %backward.1 = (bf16[128,1536]{1,0:T(8,128)(2,1)S(1)}, bf16[128,1536]{1,0:T(8,128)(2,1)S(1)}, bf16[256,2048]{1,0:T(8,128)(2,1)S(1)}, bf16[384,256]{1,0:T(8,128)(2...) custom-call(bf16[32,2048]{1,0:T(8,128)(2,1)S(1)} %get-tuple-element.103.refs_0_, ...), custom_call_target="tpu_custom_call" | custom-call | flops 1000000 | bytes 10000 | tf_op jit(solution)/shard_map/backward/pallas_call | solution.py:288
  37.5 1.6 %collective-permute-start.16 = (bf16[32,2176]{1,0:T(8,128)(2,1)S(1)}, bf16[32,2176]{1,0:T(8,128)(2,1)S(1)}, u32[]{:S(2)}, u32[]{:S(2)}) collective-permute-start(bf16[32,2176]{1,0:T(8,128)(2,1)S(1)} %get-tuple-element.125), channel_id=1, source_target_pairs={{0,2},{1,3},{2,0},{3,1},{4,6},{5,7},{6,4},{7,5},{8,10},{9,11},{10,... | collective-permute-start | bytes 417800 | tf_op jit(solution)/shard_map/ppermute | solution.py:476
  39.1 3.1 %weight_grads.2 = (bf16[384,4096]{1,0:T(8,128)(2,1)}, bf16[384,4096]{1,0:T(8,128)(2,1)}) custom-call(bf16[384,256]{1,0:T(8,128)(2,1)S(1)} %get-tuple-element.126.refs_0_, bf16[384,256]{1,0:T(8,128)(2,1)S(1)} %get-tuple-element.127.refs_1_, bf16[256,2048]{1,0:T(8,128)(2,1)S(1)} %get-tuple-element.128.refs_2_), custom_call_target="tpu_custom_call" | custom-call | flops 1000000 | bytes 10000 | tf_op jit(solution)/shard_map/weight_grads/pallas_call | solution.py:423
  42.8 0.8 %collective-permute-done.16.right = bf16[32,2176]{1,0:T(8,128)(2,1)S(1)} collective-permute-done((bf16[32,2176]{1,0:T(8,128)(2,1)S(1)}, bf16[32,2176]{1,0:T(8,128)(2,1)S(1)}, u32[]{:S(2)}, u32[]{:S(2)}) %collective-permute-start.16) | collective-permute-done | bytes 139296 | tf_op jit(solution)/shard_map/ppermute | solution.py:476
  44.1 1.5 %collective-permute-start.17 = (bf16[16,2176]{1,0:T(8,128)(2,1)S(1)}, bf16[16,2176]{1,0:T(8,128)(2,1)S(1)}, u32[]{:S(2)}, u32[]{:S(2)}) collective-permute-start(bf16[16,2176]{1,0:T(8,128)(2,1)S(1)} %get-tuple-element.136), channel_id=1, source_target_pairs={{0,4},{4,0},{8,12},{12,8},{16,20},{20,16},{24,28},{28,24},{1,5},{5... | collective-permute-start | bytes 208904 | tf_op jit(solution)/shard_map/ppermute | solution.py:476
  45.7 2.0 %weight_grads.3 = bf16[384,4096]{1,0:T(8,128)(2,1)} custom-call(bf16[384,256]{1,0:T(8,128)(2,1)S(1)} %get-tuple-element.138.refs_10_.refs_0_, bf16[256,2048]{1,0:T(8,128)(2,1)S(1)} %get-tuple-element.139.refs_1_), custom_call_target="tpu_custom_call" | custom-call | flops 1000000 | bytes 10000 | tf_op jit(solution)/shard_map/weight_grads/pallas_call | solution.py:423
  48.0 4.3 %collective-permute-start.20 = (bf16[16,2176]{1,0:T(8,128)(2,1)S(1)}, bf16[16,2176]{1,0:T(8,128)(2,1)S(1)}, u32[]{:S(2)}, u32[]{:S(2)}) collective-permute-start(bf16[16,2176]{1,0:T(8,128)(2,1)S(1)} %get-tuple-element.146), channel_id=1, source_target_pairs={{0,16},{4,20},{8,24},{12,28},{16,0},{20,4},{24,8},{28,12},{1,17},{... | collective-permute-start | bytes 208904 | tf_op jit(solution)/shard_map/ppermute | solution.py:476
  53.4 3.2 %collective-permute-done.20.refs_2_ = bf16[16,2176]{1,0:T(8,128)(2,1)S(1)} collective-permute-done((bf16[16,2176]{1,0:T(8,128)(2,1)S(1)}, bf16[16,2176]{1,0:T(8,128)(2,1)S(1)}, u32[]{:S(2)}, u32[]{:S(2)}) %collective-permute-start.20) | collective-permute-done | bytes 69664 | tf_op jit(solution)/shard_map/ppermute | solution.py:476
  56.6 1.9 %collective-permute-done.21.refs_3_ = bf16[16,2176]{1,0:T(8,128)(2,1)S(1)} collective-permute-done((bf16[16,2176]{1,0:T(8,128)(2,1)S(1)}, bf16[16,2176]{1,0:T(8,128)(2,1)S(1)}, u32[]{:S(2)}, u32[]{:S(2)}) %collective-permute-start.21) | collective-permute-done | bytes 69664 | tf_op jit(solution)/shard_map/ppermute | solution.py:476
  58.4 1.0 %combine.1 = (bf16[32,4096]{1,0:T(8,128)(2,1)}, f32[8,32]{1,0:T(8,128)}) custom-call(bf16[64,32]{1,0:T(8,128)(2,1)S(1)} %get-tuple-element.100.first, bf16[64,32]{1,0:T(8,128)(2,1)S(1)} %get-tuple-element.101.second, s32[64,32]{1,0:T(8,128)S(1)} %get-tuple-element.102.choice_ref, bf16[8,32]{1,0:T(8,128)(2,1)S(1)} %bitcast.19, ...), custom_call_target="tpu_custom_call" | custom-call | tf_op jit(solution)/shard_map/combine/pallas_call | solution.py:462
  (49 shorter events, 7.3 us)
Async XLA Ops:
  2.9 9.9 %collective-permute-start = (bf16[8,4096]{1,0:T(8,128)(2,1)}, bf16[8,4096]{1,0:T(8,128)(2,1)S(1)}, u32[]{:S(2)}, u32[]{:S(2)}) collective-permute-start(bf16[8,4096]{1,0:T(8,128)(2,1)} %get-tuple-element.80), channel_id=1, source_target_pairs={{0,4},{4,0},{8,12},{12,8},{16,20},{20,16},{24,28},{28,24},{1,5},{5... | collective-permute-start | bytes 196616 | tf_op jit(solution)/shard_map/ppermute | solution.py:476
  6.0 9.2 %collective-permute-start.1 = (bf16[8,4096]{1,0:T(8,128)(2,1)}, bf16[8,4096]{1,0:T(8,128)(2,1)S(1)}, u32[]{:S(2)}, u32[]{:S(2)}) collective-permute-start(bf16[8,4096]{1,0:T(8,128)(2,1)} %get-tuple-element.81), channel_id=1, source_target_pairs={{0,16},{4,20},{8,24},{12,28},{16,0},{20,4},{24,8},{28,12},{1,17},{... | collective-permute-start | bytes 196616 | tf_op jit(solution)/shard_map/ppermute | solution.py:476
  8.5 6.7 %collective-permute-start.2 = (bf16[8,4096]{1,0:T(8,128)(2,1)}, bf16[8,4096]{1,0:T(8,128)(2,1)S(1)}, u32[]{:S(2)}, u32[]{:S(2)}) collective-permute-start(bf16[8,4096]{1,0:T(8,128)(2,1)} %get-tuple-element.82), channel_id=1, source_target_pairs={{0,8},{4,12},{8,0},{12,4},{16,24},{20,28},{24,16},{28,20},{1,9},{5... | collective-permute-start | bytes 196616 | tf_op jit(solution)/shard_map/ppermute | solution.py:476
  10.1 9.0 %collective-permute-start.3 = (bf16[8,4096]{1,0:T(8,128)(2,1)}, bf16[8,4096]{1,0:T(8,128)(2,1)S(1)}, u32[]{:S(2)}, u32[]{:S(2)}) collective-permute-start(bf16[8,4096]{1,0:T(8,128)(2,1)} %get-tuple-element.85), channel_id=1, source_target_pairs={{0,20},{4,16},{8,28},{12,24},{16,4},{20,0},{24,12},{28,8},{1,21},{... | collective-permute-start | bytes 196616 | tf_op jit(solution)/shard_map/ppermute | solution.py:476
  10.4 8.8 %collective-permute-start.4 = (bf16[8,4096]{1,0:T(8,128)(2,1)}, bf16[8,4096]{1,0:T(8,128)(2,1)S(1)}, u32[]{:S(2)}, u32[]{:S(2)}) collective-permute-start(bf16[8,4096]{1,0:T(8,128)(2,1)} %get-tuple-element.86), channel_id=1, source_target_pairs={{0,24},{4,28},{8,16},{12,20},{16,8},{20,12},{24,0},{28,4},{1,25},{... | collective-permute-start | bytes 196616 | tf_op jit(solution)/shard_map/ppermute | solution.py:476
  12.9 7.3 %collective-permute-start.5 = (bf16[8,4096]{1,0:T(8,128)(2,1)}, bf16[8,4096]{1,0:T(8,128)(2,1)S(1)}, u32[]{:S(2)}, u32[]{:S(2)}) collective-permute-start(bf16[8,4096]{1,0:T(8,128)(2,1)} %get-tuple-element.87), channel_id=1, source_target_pairs={{0,28},{4,24},{8,20},{12,16},{16,12},{20,8},{24,4},{28,0},{1,29},{... | collective-permute-start | bytes 196616 | tf_op jit(solution)/shard_map/ppermute | solution.py:476
  15.2 5.7 %collective-permute-start.6 = (bf16[8,4096]{1,0:T(8,128)(2,1)}, bf16[8,4096]{1,0:T(8,128)(2,1)S(1)}, u32[]{:S(2)}, u32[]{:S(2)}) collective-permute-start(bf16[8,4096]{1,0:T(8,128)(2,1)} %get-tuple-element.88), channel_id=1, source_target_pairs={{0,12},{4,8},{8,4},{12,0},{16,28},{20,24},{24,20},{28,16},{1,13},{... | collective-permute-start | bytes 196616 | tf_op jit(solution)/shard_map/ppermute | solution.py:476
  16.1 13.7 %copy-start = (bf16[1,384,4096]{2,1,0:T(8,128)(2,1)S(1)}, bf16[1,384,4096]{2,1,0:T(8,128)(2,1)}, u32[]{:S(2)}) copy-start(bf16[1,384,4096]{2,1,0:T(8,128)(2,1)} %param.11) | copy-start | bytes 9437188
  16.1 6.6 %collective-permute-start.7 = (bf16[32,4096]{1,0:T(8,128)(2,1)S(1)}, bf16[32,4096]{1,0:T(8,128)(2,1)S(1)}, u32[]{:S(2)}, u32[]{:S(2)}) collective-permute-start(bf16[32,4096]{1,0:T(8,128)(2,1)S(1)} %pack.4.rows), channel_id=1, source_target_pairs={{0,2},{1,3},{2,0},{3,1},{4,6},{5,7},{6,4},{7,5},{8,10},{9,11},{10,... | collective-permute-start | bytes 786440 | tf_op jit(solution)/shard_map/ppermute | solution.py:476
  20.9 7.3 %collective-permute-start.11 = (bf16[32,4096]{1,0:T(8,128)(2,1)S(1)}, bf16[32,4096]{1,0:T(8,128)(2,1)S(1)}, u32[]{:S(2)}, u32[]{:S(2)}) collective-permute-start(bf16[32,4096]{1,0:T(8,128)(2,1)S(1)} %pack.5.refs_1_), channel_id=1, source_target_pairs={{0,2},{1,3},{2,0},{3,1},{4,6},{5,7},{6,4},{7,5},{8,10},{9,11},{10,... | collective-permute-start | bytes 786440 | tf_op jit(solution)/shard_map/ppermute | solution.py:476
  22.7 5.4 %collective-permute-start.8 = (bf16[32,4096]{1,0:T(8,128)(2,1)S(1)}, bf16[32,4096]{1,0:T(8,128)(2,1)S(1)}, u32[]{:S(2)}, u32[]{:S(2)}) collective-permute-start(bf16[32,4096]{1,0:T(8,128)(2,1)S(1)} %pack.4.rows), channel_id=1, source_target_pairs={{0,1},{1,0},{2,3},{3,2},{4,5},{5,4},{6,7},{7,6},{8,9},{9,8},{10,11... | collective-permute-start | bytes 786440 | tf_op jit(solution)/shard_map/ppermute | solution.py:476
  22.7 5.4 %collective-permute-start.9 = (bf16[32,4096]{1,0:T(8,128)(2,1)S(1)}, bf16[32,4096]{1,0:T(8,128)(2,1)S(1)}, u32[]{:S(2)}, u32[]{:S(2)}) collective-permute-start(bf16[32,4096]{1,0:T(8,128)(2,1)S(1)} %collective-permute-done.7.refs_2_), channel_id=1, source_target_pairs={{0,1},{1,0},{2,3},{3,2},{4,5},{5,4},{6,7},{7,6},{8,9},{9,8},{10,11... | collective-permute-start | bytes 786440 | tf_op jit(solution)/shard_map/ppermute | solution.py:476
  23.2 4.9 %collective-permute-start.10 = (bf16[32,4096]{1,0:T(8,128)(2,1)S(1)}, bf16[32,4096]{1,0:T(8,128)(2,1)S(1)}, u32[]{:S(2)}, u32[]{:S(2)}) collective-permute-start(bf16[32,4096]{1,0:T(8,128)(2,1)S(1)} %pack.5.refs_1_), channel_id=1, source_target_pairs={{0,1},{1,0},{2,3},{3,2},{4,5},{5,4},{6,7},{7,6},{8,9},{9,8},{10,11... | collective-permute-start | bytes 786440 | tf_op jit(solution)/shard_map/ppermute | solution.py:476
  28.2 1.6 %collective-permute-start.12 = (bf16[32,4096]{1,0:T(8,128)(2,1)S(1)}, bf16[32,4096]{1,0:T(8,128)(2,1)S(1)}, u32[]{:S(2)}, u32[]{:S(2)}) collective-permute-start(bf16[32,4096]{1,0:T(8,128)(2,1)S(1)} %collective-permute-done.11.refs_3_), channel_id=1, source_target_pairs={{0,1},{1,0},{2,3},{3,2},{4,5},{5,4},{6,7},{7,6},{8,9},{9,8},{10,11... | collective-permute-start | bytes 786440 | tf_op jit(solution)/shard_map/ppermute | solution.py:476
  35.1 1.8 %collective-permute-start.13 = (bf16[128,1536]{1,0:T(8,128)(2,1)S(1)}, bf16[128,1536]{1,0:T(8,128)(2,1)S(1)}, u32[]{:S(2)}, u32[]{:S(2)}) collective-permute-start(bf16[128,1536]{1,0:T(8,128)(2,1)S(1)} %get-tuple-element.113), channel_id=1, source_target_pairs={{0,1},{1,0},{2,3},{3,2},{4,5},{5,4},{6,7},{7,6},{8,9},{9,8},{10,11... | collective-permute-start | bytes 1179656 | tf_op jit(solution)/shard_map/ppermute | solution.py:476
  35.9 1.5 %collective-permute-start.14 = (bf16[128,640]{1,0:T(8,128)(2,1)S(1)}, bf16[128,640]{1,0:T(8,128)(2,1)S(1)}, u32[]{:S(2)}, u32[]{:S(2)}) collective-permute-start(bf16[128,640]{1,0:T(8,128)(2,1)S(1)} %get-tuple-element.119), channel_id=1, source_target_pairs={{0,1},{1,0},{2,3},{3,2},{4,5},{5,4},{6,7},{7,6},{8,9},{9,8},{10,11... | collective-permute-start | bytes 491528 | tf_op jit(solution)/shard_map/ppermute | solution.py:476
  37.5 6.0 %collective-permute-start.16 = (bf16[32,2176]{1,0:T(8,128)(2,1)S(1)}, bf16[32,2176]{1,0:T(8,128)(2,1)S(1)}, u32[]{:S(2)}, u32[]{:S(2)}) collective-permute-start(bf16[32,2176]{1,0:T(8,128)(2,1)S(1)} %get-tuple-element.125), channel_id=1, source_target_pairs={{0,2},{1,3},{2,0},{3,1},{4,6},{5,7},{6,4},{7,5},{8,10},{9,11},{10,... | collective-permute-start | bytes 417800 | tf_op jit(solution)/shard_map/ppermute | solution.py:476
  39.1 19.3 %copy-start.5 = (bf16[32,8]{0,1:T(8,128)(2,1)S(1)}, bf16[32,8]{0,1:T(8,128)(2,1)}, u32[]{:S(2)}) copy-start(bf16[32,8]{0,1:T(8,128)(2,1)} %param.9) | copy-start | bytes 1540
  42.2 5.7 %collective-permute-start.15 = (bf16[32,2176]{1,0:T(8,128)(2,1)S(1)}, bf16[32,2176]{1,0:T(8,128)(2,1)S(1)}, u32[]{:S(2)}, u32[]{:S(2)}) collective-permute-start(bf16[32,2176]{1,0:T(8,128)(2,1)S(1)} %get-tuple-element.132), channel_id=1, source_target_pairs={{0,2},{1,3},{2,0},{3,1},{4,6},{5,7},{6,4},{7,5},{8,10},{9,11},{10,... | collective-permute-start | bytes 417800 | tf_op jit(solution)/shard_map/ppermute | solution.py:476
  43.6 4.4 %collective-permute-start.19 = (bf16[16,2176]{1,0:T(8,128)(2,1)S(1)}, bf16[16,2176]{1,0:T(8,128)(2,1)S(1)}, u32[]{:S(2)}, u32[]{:S(2)}) collective-permute-start(bf16[16,2176]{1,0:T(8,128)(2,1)S(1)} %get-tuple-element.137), channel_id=1, source_target_pairs={{0,4},{4,0},{8,12},{12,8},{16,20},{20,16},{24,28},{28,24},{1,5},{5... | collective-permute-start | bytes 208904 | tf_op jit(solution)/shard_map/ppermute | solution.py:476
  44.1 8.7 %collective-permute-start.17 = (bf16[16,2176]{1,0:T(8,128)(2,1)S(1)}, bf16[16,2176]{1,0:T(8,128)(2,1)S(1)}, u32[]{:S(2)}, u32[]{:S(2)}) collective-permute-start(bf16[16,2176]{1,0:T(8,128)(2,1)S(1)} %get-tuple-element.136), channel_id=1, source_target_pairs={{0,4},{4,0},{8,12},{12,8},{16,20},{20,16},{24,28},{28,24},{1,5},{5... | collective-permute-start | bytes 208904 | tf_op jit(solution)/shard_map/ppermute | solution.py:476
  48.0 8.5 %collective-permute-start.20 = (bf16[16,2176]{1,0:T(8,128)(2,1)S(1)}, bf16[16,2176]{1,0:T(8,128)(2,1)S(1)}, u32[]{:S(2)}, u32[]{:S(2)}) collective-permute-start(bf16[16,2176]{1,0:T(8,128)(2,1)S(1)} %get-tuple-element.146), channel_id=1, source_target_pairs={{0,16},{4,20},{8,24},{12,28},{16,0},{20,4},{24,8},{28,12},{1,17},{... | collective-permute-start | bytes 208904 | tf_op jit(solution)/shard_map/ppermute | solution.py:476
  52.3 6.1 %collective-permute-start.21 = (bf16[16,2176]{1,0:T(8,128)(2,1)S(1)}, bf16[16,2176]{1,0:T(8,128)(2,1)S(1)}, u32[]{:S(2)}, u32[]{:S(2)}) collective-permute-start(bf16[16,2176]{1,0:T(8,128)(2,1)S(1)} %get-tuple-element.147), channel_id=1, source_target_pairs={{0,24},{4,28},{8,16},{12,20},{16,8},{20,12},{24,0},{28,4},{1,25},{... | collective-permute-start | bytes 208904 | tf_op jit(solution)/shard_map/ppermute | solution.py:476
  52.9 5.6 %collective-permute-start.18 = (bf16[16,2176]{1,0:T(8,128)(2,1)S(1)}, bf16[16,2176]{1,0:T(8,128)(2,1)S(1)}, u32[]{:S(2)}, u32[]{:S(2)}) collective-permute-start(bf16[16,2176]{1,0:T(8,128)(2,1)S(1)} %get-tuple-element.143), channel_id=1, source_target_pairs={{0,8},{4,12},{8,0},{12,4},{16,24},{20,28},{24,16},{28,20},{1,9},{5... | collective-permute-start | bytes 208904 | tf_op jit(solution)/shard_map/ppermute | solution.py:476
  (4 other events, 23.7 us)

commit v17 on v15

--- a/solution.py
+++ b/solution.py
@@ -58,7 +58,8 @@
 
 def dispatch_kernel(n_targets, *refs):
     sources, outs = refs[:4], refs[4 : 4 + n_targets]
-    targets, sems = refs[4 + n_targets : -1], refs[-1]
+    targets, blocks = refs[4 + n_targets : 8 + n_targets], refs[8 + n_targets : -2]
+    sems, out_sems = refs[-2:]
     ids_ref, tokens_ref, gates_ref, grads_ref = targets
     copies = [
         pltpu.make_async_copy(source, target, sems.at[i])
@@ -66,14 +67,24 @@
     ]
     for copy in copies:
         copy.start()
+    half = tokens_ref.shape[1] // 2
+    sent = []
+
+    def send(rows, start):
+        span = pl.ds(start, half)
+        for k, (block, out) in enumerate(zip(blocks, outs)):
+            block[:, span] = rows[k * BLOCK : (k + 1) * BLOCK]
+            copy = pltpu.make_async_copy(
+                block.at[:, span], out.at[:, span], out_sems.at[len(sent)]
+            )
+            copy.start()
+            sent.append(copy)
+
     copies[0].wait()
     matches, first, second = choice_table(ids_ref[...], n_targets)
     picks = jnp.concatenate([first.astype(jnp.float32), second.astype(jnp.float32)], axis=1)
     copies[1].wait()
-    rows = pick_rows(picks.astype(jnp.bfloat16), tokens_ref)
-    half = rows.shape[1]
-    for k, out in enumerate(outs):
-        out[:, :half] = rows[k * BLOCK : (k + 1) * BLOCK]
+    send(pick_rows(picks.astype(jnp.bfloat16), tokens_ref), 0)
     copies[2].wait()
     gates = gates_ref[...].astype(jnp.float32)
     scale = jnp.zeros(first.shape, jnp.float32)
@@ -81,20 +92,22 @@
         scale = scale + jnp.where(match, gates[k : k + 1, :], 0.0)
     picks = (picks * jnp.concatenate([scale, scale], axis=1)).astype(jnp.bfloat16)
     copies[3].wait()
-    rows = pick_rows(picks, grads_ref)
-    for k, out in enumerate(outs):
-        out[:, half:] = rows[k * BLOCK : (k + 1) * BLOCK]
+    send(pick_rows(picks, grads_ref), half)
+    for copy in sent:
+        copy.wait()
 
 
 def dispatch(n_targets, ids, tokens, gates, out_grad):
     arrays = (ids, tokens, gates, out_grad)
+    block = (BLOCK, tokens.shape[1])
     return pl.pallas_call(
         functools.partial(dispatch_kernel, n_targets),
-        out_shape=[struct((BLOCK, tokens.shape[1]))] * n_targets,
+        out_shape=[struct(block)] * n_targets,
         in_specs=[HBM] * 4,
-        out_specs=[VMEM] * n_targets,
+        out_specs=[HBM] * n_targets,
         scratch_shapes=[pltpu.VMEM(a.shape, a.dtype) for a in arrays]
-        + [pltpu.SemaphoreType.DMA((4,))],
+        + [pltpu.VMEM(block, jnp.bfloat16)] * n_targets
+        + [pltpu.SemaphoreType.DMA((4,)), pltpu.SemaphoreType.DMA((2 * n_targets,))],
         compiler_params=pltpu.CompilerParams(vmem_limit_bytes=60 * MIB),
         name="dispatch",
     )(*arrays)

time: 58.3 us -> 58.3 us (level)
  no operation moved by 1% of the time
where the time goes in v17:
time: 58.3 us; the launch traced here: 58.1 us
  starting transfers between devices  26.3 us (45%)
  waiting for transfers between devices  16.2 us (28%)
  Pallas kernels  14.8 us (25%)
  between operations  0.8 us (1%)
    ppermute x22, starting transfers between devices, flip(): return lax.ppermute(value, axis, [(i, i ^ bit) for i in range(size)])  26.3 us
    ppermute x22, waiting for transfers between devices, flip(): return lax.ppermute(value, axis, [(i, i ^ bit) for i in range(size)])  16.2 us
    pallas_call x2, Pallas kernels, weight_grads(): pl.pallas_call(functools.partial(weight_kernel, chunk, count), out_shape=...  5.05 us
    pallas_call x1, Pallas kernels, backward(): pl.pallas_call(functools.partial(backward_kernel, count), out_shape=[stru...  3.3 us
    pallas_call x1, Pallas kernels, dispatch(): pl.pallas_call(functools.partial(dispatch_kernel, n_targets), out_shape=[...  2.33 us
    pallas_call x1, Pallas kernels, forward(): pl.pallas_call(functools.partial(forward_kernel, count), out_shape=[struc...  1.95 us
  transfers between devices with their start and end apart: 22, of which 12 were waited for; matrix products, arithmetic and copies ran while one was open for 0% of the time, Pallas kernels for 11%

profile of v17, /device:TPU:0, one launch (start us, length us, event | category | flops | bytes accessed | tf_op | source)
XLA Modules:
  0.0 58.1 jit_solution(14131315384690678319)
XLA Ops:
  0.6 2.3 %dispatch.1 = (bf16[8,4096]{1,0:T(8,128)(2,1)}, bf16[8,4096]{1,0:T(8,128)(2,1)}, bf16[8,4096]{1,0:T(8,128)(2,1)}, bf16[8,4096]{1,0:T(8,128)(2,1)}, bf16[8,4096]{...) custom-call(s32[8,32]{1,0:T(8,128)} %bitcast.16, ...), custom_call_target="tpu_custom_call" | custom-call | tf_op jit(solution)/shard_map/dispatch/pallas_call | solution.py:103
  3.0 3.0 %collective-permute-start = (bf16[8,4096]{1,0:T(8,128)(2,1)}, bf16[8,4096]{1,0:T(8,128)(2,1)S(1)}, u32[]{:S(2)}, u32[]{:S(2)}) collective-permute-start(bf16[8,4096]{1,0:T(8,128)(2,1)} %get-tuple-element.80), channel_id=1, source_target_pairs={{0,4},{4,0},{8,12},{12,8},{16,20},{20,16},{24,28},{28,24},{1,5},{5... | collective-permute-start | bytes 196616 | tf_op jit(solution)/shard_map/ppermute | solution.py:489
  6.0 2.6 %collective-permute-start.1 = (bf16[8,4096]{1,0:T(8,128)(2,1)}, bf16[8,4096]{1,0:T(8,128)(2,1)S(1)}, u32[]{:S(2)}, u32[]{:S(2)}) collective-permute-start(bf16[8,4096]{1,0:T(8,128)(2,1)} %get-tuple-element.81), channel_id=1, source_target_pairs={{0,16},{4,20},{8,24},{12,28},{16,0},{20,4},{24,8},{28,12},{1,17},{... | collective-permute-start | bytes 196616 | tf_op jit(solution)/shard_map/ppermute | solution.py:489
  8.6 1.6 %collective-permute-start.2 = (bf16[8,4096]{1,0:T(8,128)(2,1)}, bf16[8,4096]{1,0:T(8,128)(2,1)S(1)}, u32[]{:S(2)}, u32[]{:S(2)}) collective-permute-start(bf16[8,4096]{1,0:T(8,128)(2,1)} %get-tuple-element.82), channel_id=1, source_target_pairs={{0,8},{4,12},{8,0},{12,4},{16,24},{20,28},{24,16},{28,20},{1,9},{5... | collective-permute-start | bytes 196616 | tf_op jit(solution)/shard_map/ppermute | solution.py:489
  10.4 1.4 %collective-permute-start.4 = (bf16[8,4096]{1,0:T(8,128)(2,1)}, bf16[8,4096]{1,0:T(8,128)(2,1)S(1)}, u32[]{:S(2)}, u32[]{:S(2)}) collective-permute-start(bf16[8,4096]{1,0:T(8,128)(2,1)} %get-tuple-element.86), channel_id=1, source_target_pairs={{0,12},{4,8},{8,4},{12,0},{16,28},{20,24},{24,20},{28,16},{1,13},{... | collective-permute-start | bytes 196616 | tf_op jit(solution)/shard_map/ppermute | solution.py:489
  11.9 3.6 %collective-permute-start.5 = (bf16[8,4096]{1,0:T(8,128)(2,1)}, bf16[8,4096]{1,0:T(8,128)(2,1)S(1)}, u32[]{:S(2)}, u32[]{:S(2)}) collective-permute-start(bf16[8,4096]{1,0:T(8,128)(2,1)} %get-tuple-element.87), channel_id=1, source_target_pairs={{0,24},{4,28},{8,16},{12,20},{16,8},{20,12},{24,0},{28,4},{1,25},{... | collective-permute-start | bytes 196616 | tf_op jit(solution)/shard_map/ppermute | solution.py:489
  15.5 1.6 %collective-permute-start.6 = (bf16[8,4096]{1,0:T(8,128)(2,1)}, bf16[8,4096]{1,0:T(8,128)(2,1)S(1)}, u32[]{:S(2)}, u32[]{:S(2)}) collective-permute-start(bf16[8,4096]{1,0:T(8,128)(2,1)} %get-tuple-element.88), channel_id=1, source_target_pairs={{0,28},{4,24},{8,20},{12,16},{16,12},{20,8},{24,4},{28,0},{1,29},{... | collective-permute-start | bytes 196616 | tf_op jit(solution)/shard_map/ppermute | solution.py:489
  17.2 1.5 %collective-permute-start.7 = (bf16[32,4096]{1,0:T(8,128)(2,1)S(1)}, bf16[32,4096]{1,0:T(8,128)(2,1)S(1)}, u32[]{:S(2)}, u32[]{:S(2)}) collective-permute-start(bf16[32,4096]{1,0:T(8,128)(2,1)S(1)} %pack.4.rows), channel_id=1, source_target_pairs={{0,2},{1,3},{2,0},{3,1},{4,6},{5,7},{6,4},{7,5},{8,10},{9,11},{10,... | collective-permute-start | bytes 786440 | tf_op jit(solution)/shard_map/ppermute | solution.py:489
  18.7 1.2 %collective-permute-done.3.refs_0_ = bf16[8,4096]{1,0:T(8,128)(2,1)S(1)} collective-permute-done((bf16[8,4096]{1,0:T(8,128)(2,1)}, bf16[8,4096]{1,0:T(8,128)(2,1)S(1)}, u32[]{:S(2)}, u32[]{:S(2)}) %collective-permute-start.3) | collective-permute-done | bytes 65568 | tf_op jit(solution)/shard_map/ppermute | solution.py:489
  20.0 2.7 %collective-permute-done.6.refs_3_ = bf16[8,4096]{1,0:T(8,128)(2,1)S(1)} collective-permute-done((bf16[8,4096]{1,0:T(8,128)(2,1)}, bf16[8,4096]{1,0:T(8,128)(2,1)S(1)}, u32[]{:S(2)}, u32[]{:S(2)}) %collective-permute-start.6) | collective-permute-done | bytes 65568 | tf_op jit(solution)/shard_map/ppermute | solution.py:489
  22.7 1.6 %collective-permute-start.11 = (bf16[32,4096]{1,0:T(8,128)(2,1)S(1)}, bf16[32,4096]{1,0:T(8,128)(2,1)S(1)}, u32[]{:S(2)}, u32[]{:S(2)}) collective-permute-start(bf16[32,4096]{1,0:T(8,128)(2,1)S(1)} %pack.5.refs_1_), channel_id=1, source_target_pairs={{0,2},{1,3},{2,0},{3,1},{4,6},{5,7},{6,4},{7,5},{8,10},{9,11},{10,... | collective-permute-start | bytes 786440 | tf_op jit(solution)/shard_map/ppermute | solution.py:489
  25.4 3.8 %collective-permute-done.11.refs_3_ = bf16[32,4096]{1,0:T(8,128)(2,1)S(1)} collective-permute-done((bf16[32,4096]{1,0:T(8,128)(2,1)S(1)}, bf16[32,4096]{1,0:T(8,128)(2,1)S(1)}, u32[]{:S(2)}, u32[]{:S(2)}) %collective-permute-start.11) | collective-permute-done | bytes 262176 | tf_op jit(solution)/shard_map/ppermute | solution.py:489
  29.3 1.5 %collective-permute-done.12.refs_7_ = bf16[32,4096]{1,0:T(8,128)(2,1)S(1)} collective-permute-done((bf16[32,4096]{1,0:T(8,128)(2,1)S(1)}, bf16[32,4096]{1,0:T(8,128)(2,1)S(1)}, u32[]{:S(2)}, u32[]{:S(2)}) %collective-permute-start.12) | collective-permute-done | bytes 262176 | tf_op jit(solution)/shard_map/ppermute | solution.py:489
  30.8 2.0 %forward.1 = (bf16[256,2048]{1,0:T(8,128)(2,1)S(1)}, f32[384,256]{1,0:T(8,128)S(1)}, f32[384,256]{1,0:T(8,128)S(1)}, bf16[384,256]{1,0:T(8,128)(2,1)S(1)}) custom-call(bf16[32,2048]{1,0:T(8,128)(2,1)S(1)} %get-tuple-element.108.refs_0_, bf16[32,4096]{1,0:T(8,128)(2,1)S(1)} %pack.5.refs_1_, bf16[32,4096]{1,0:T(8,128)(2,1)S(1)} %collective-permute-done.7.refs_2_, ...), custom_call_target="tpu_custom_call" | custom-call | flops 1000000 | bytes 10000 | tf_op jit(solution)/shard_map/forward/pallas_call | solution.py:220
  32.8 3.3 %backward.1 = (bf16[128,1536]{1,0:T(8,128)(2,1)S(1)}, bf16[128,1536]{1,0:T(8,128)(2,1)S(1)}, bf16[256,2048]{1,0:T(8,128)(2,1)S(1)}, bf16[384,256]{1,0:T(8,128)(2...) custom-call(bf16[32,2048]{1,0:T(8,128)(2,1)S(1)} %get-tuple-element.103.refs_0_, ...), custom_call_target="tpu_custom_call" | custom-call | flops 1000000 | bytes 10000 | tf_op jit(solution)/shard_map/backward/pallas_call | solution.py:301
  38.6 1.6 %collective-permute-start.16 = (bf16[32,2176]{1,0:T(8,128)(2,1)S(1)}, bf16[32,2176]{1,0:T(8,128)(2,1)S(1)}, u32[]{:S(2)}, u32[]{:S(2)}) collective-permute-start(bf16[32,2176]{1,0:T(8,128)(2,1)S(1)} %get-tuple-element.125), channel_id=1, source_target_pairs={{0,2},{1,3},{2,0},{3,1},{4,6},{5,7},{6,4},{7,5},{8,10},{9,11},{10,... | collective-permute-start | bytes 417800 | tf_op jit(solution)/shard_map/ppermute | solution.py:489
  40.2 3.1 %weight_grads.2 = (bf16[384,4096]{1,0:T(8,128)(2,1)}, bf16[384,4096]{1,0:T(8,128)(2,1)}) custom-call(bf16[384,256]{1,0:T(8,128)(2,1)S(1)} %get-tuple-element.126.refs_0_, bf16[384,256]{1,0:T(8,128)(2,1)S(1)} %get-tuple-element.127.refs_1_, bf16[256,2048]{1,0:T(8,128)(2,1)S(1)} %get-tuple-element.128.refs_2_), custom_call_target="tpu_custom_call" | custom-call | flops 1000000 | bytes 10000 | tf_op jit(solution)/shard_map/weight_grads/pallas_call | solution.py:436
  43.8 0.8 %collective-permute-done.16.right = bf16[32,2176]{1,0:T(8,128)(2,1)S(1)} collective-permute-done((bf16[32,2176]{1,0:T(8,128)(2,1)S(1)}, bf16[32,2176]{1,0:T(8,128)(2,1)S(1)}, u32[]{:S(2)}, u32[]{:S(2)}) %collective-permute-start.16) | collective-permute-done | bytes 139296 | tf_op jit(solution)/shard_map/ppermute | solution.py:489
  44.6 1.6 %collective-permute-start.19 = (bf16[16,2176]{1,0:T(8,128)(2,1)S(1)}, bf16[16,2176]{1,0:T(8,128)(2,1)S(1)}, u32[]{:S(2)}, u32[]{:S(2)}) collective-permute-start(bf16[16,2176]{1,0:T(8,128)(2,1)S(1)} %get-tuple-element.137), channel_id=1, source_target_pairs={{0,4},{4,0},{8,12},{12,8},{16,20},{20,16},{24,28},{28,24},{1,5},{5... | collective-permute-start | bytes 208904 | tf_op jit(solution)/shard_map/ppermute | solution.py:489
  46.7 2.0 %weight_grads.3 = bf16[384,4096]{1,0:T(8,128)(2,1)} custom-call(bf16[384,256]{1,0:T(8,128)(2,1)S(1)} %get-tuple-element.138.refs_10_.refs_0_, bf16[256,2048]{1,0:T(8,128)(2,1)S(1)} %get-tuple-element.139.refs_1_), custom_call_target="tpu_custom_call" | custom-call | flops 1000000 | bytes 10000 | tf_op jit(solution)/shard_map/weight_grads/pallas_call | solution.py:436
  50.1 1.7 %collective-permute-start.21 = (bf16[16,2176]{1,0:T(8,128)(2,1)S(1)}, bf16[16,2176]{1,0:T(8,128)(2,1)S(1)}, u32[]{:S(2)}, u32[]{:S(2)}) collective-permute-start(bf16[16,2176]{1,0:T(8,128)(2,1)S(1)} %get-tuple-element.147), channel_id=1, source_target_pairs={{0,24},{4,28},{8,16},{12,20},{16,8},{20,12},{24,0},{28,4},{1,25},{... | collective-permute-start | bytes 208904 | tf_op jit(solution)/shard_map/ppermute | solution.py:489
  51.8 1.4 %collective-permute-start.18 = (bf16[16,2176]{1,0:T(8,128)(2,1)S(1)}, bf16[16,2176]{1,0:T(8,128)(2,1)S(1)}, u32[]{:S(2)}, u32[]{:S(2)}) collective-permute-start(bf16[16,2176]{1,0:T(8,128)(2,1)S(1)} %get-tuple-element.143), channel_id=1, source_target_pairs={{0,8},{4,12},{8,0},{12,4},{16,24},{20,28},{24,16},{28,20},{1,9},{5... | collective-permute-start | bytes 208904 | tf_op jit(solution)/shard_map/ppermute | solution.py:489
  53.3 3.2 %collective-permute-done.20.refs_2_ = bf16[16,2176]{1,0:T(8,128)(2,1)S(1)} collective-permute-done((bf16[16,2176]{1,0:T(8,128)(2,1)S(1)}, bf16[16,2176]{1,0:T(8,128)(2,1)S(1)}, u32[]{:S(2)}, u32[]{:S(2)}) %collective-permute-start.20) | collective-permute-done | bytes 69664 | tf_op jit(solution)/shard_map/ppermute | solution.py:489
  57.2 1.0 %combine.1 = (bf16[32,4096]{1,0:T(8,128)(2,1)}, f32[8,32]{1,0:T(8,128)}) custom-call(bf16[64,32]{1,0:T(8,128)(2,1)S(1)} %get-tuple-element.100.first, bf16[64,32]{1,0:T(8,128)(2,1)S(1)} %get-tuple-element.101.second, s32[64,32]{1,0:T(8,128)S(1)} %get-tuple-element.102.choice_ref, bf16[8,32]{1,0:T(8,128)(2,1)S(1)} %bitcast.19, ...), custom_call_target="tpu_custom_call" | custom-call | tf_op jit(solution)/shard_map/combine/pallas_call | solution.py:475
  (49 shorter events, 7.3 us)
Async XLA Ops:
  3.0 8.9 %collective-permute-start = (bf16[8,4096]{1,0:T(8,128)(2,1)}, bf16[8,4096]{1,0:T(8,128)(2,1)S(1)}, u32[]{:S(2)}, u32[]{:S(2)}) collective-permute-start(bf16[8,4096]{1,0:T(8,128)(2,1)} %get-tuple-element.80), channel_id=1, source_target_pairs={{0,4},{4,0},{8,12},{12,8},{16,20},{20,16},{24,28},{28,24},{1,5},{5... | collective-permute-start | bytes 196616 | tf_op jit(solution)/shard_map/ppermute | solution.py:489
  6.0 9.5 %collective-permute-start.1 = (bf16[8,4096]{1,0:T(8,128)(2,1)}, bf16[8,4096]{1,0:T(8,128)(2,1)S(1)}, u32[]{:S(2)}, u32[]{:S(2)}) collective-permute-start(bf16[8,4096]{1,0:T(8,128)(2,1)} %get-tuple-element.81), channel_id=1, source_target_pairs={{0,16},{4,20},{8,24},{12,28},{16,0},{20,4},{24,8},{28,12},{1,17},{... | collective-permute-start | bytes 196616 | tf_op jit(solution)/shard_map/ppermute | solution.py:489
  8.6 8.5 %collective-permute-start.2 = (bf16[8,4096]{1,0:T(8,128)(2,1)}, bf16[8,4096]{1,0:T(8,128)(2,1)S(1)}, u32[]{:S(2)}, u32[]{:S(2)}) collective-permute-start(bf16[8,4096]{1,0:T(8,128)(2,1)} %get-tuple-element.82), channel_id=1, source_target_pairs={{0,8},{4,12},{8,0},{12,4},{16,24},{20,28},{24,16},{28,20},{1,9},{5... | collective-permute-start | bytes 196616 | tf_op jit(solution)/shard_map/ppermute | solution.py:489
  10.2 9.8 %collective-permute-start.3 = (bf16[8,4096]{1,0:T(8,128)(2,1)}, bf16[8,4096]{1,0:T(8,128)(2,1)S(1)}, u32[]{:S(2)}, u32[]{:S(2)}) collective-permute-start(bf16[8,4096]{1,0:T(8,128)(2,1)} %get-tuple-element.85), channel_id=1, source_target_pairs={{0,20},{4,16},{8,28},{12,24},{16,4},{20,0},{24,12},{28,8},{1,21},{... | collective-permute-start | bytes 196616 | tf_op jit(solution)/shard_map/ppermute | solution.py:489
  10.4 9.5 %collective-permute-start.4 = (bf16[8,4096]{1,0:T(8,128)(2,1)}, bf16[8,4096]{1,0:T(8,128)(2,1)S(1)}, u32[]{:S(2)}, u32[]{:S(2)}) collective-permute-start(bf16[8,4096]{1,0:T(8,128)(2,1)} %get-tuple-element.86), channel_id=1, source_target_pairs={{0,12},{4,8},{8,4},{12,0},{16,28},{20,24},{24,20},{28,16},{1,13},{... | collective-permute-start | bytes 196616 | tf_op jit(solution)/shard_map/ppermute | solution.py:489
  11.9 8.1 %collective-permute-start.5 = (bf16[8,4096]{1,0:T(8,128)(2,1)}, bf16[8,4096]{1,0:T(8,128)(2,1)S(1)}, u32[]{:S(2)}, u32[]{:S(2)}) collective-permute-start(bf16[8,4096]{1,0:T(8,128)(2,1)} %get-tuple-element.87), channel_id=1, source_target_pairs={{0,24},{4,28},{8,16},{12,20},{16,8},{20,12},{24,0},{28,4},{1,25},{... | collective-permute-start | bytes 196616 | tf_op jit(solution)/shard_map/ppermute | solution.py:489
  15.5 7.2 %collective-permute-start.6 = (bf16[8,4096]{1,0:T(8,128)(2,1)}, bf16[8,4096]{1,0:T(8,128)(2,1)S(1)}, u32[]{:S(2)}, u32[]{:S(2)}) collective-permute-start(bf16[8,4096]{1,0:T(8,128)(2,1)} %get-tuple-element.88), channel_id=1, source_target_pairs={{0,28},{4,24},{8,20},{12,16},{16,12},{20,8},{24,4},{28,0},{1,29},{... | collective-permute-start | bytes 196616 | tf_op jit(solution)/shard_map/ppermute | solution.py:489
  17.1 13.7 %copy-start = (bf16[1,384,4096]{2,1,0:T(8,128)(2,1)S(1)}, bf16[1,384,4096]{2,1,0:T(8,128)(2,1)}, u32[]{:S(2)}) copy-start(bf16[1,384,4096]{2,1,0:T(8,128)(2,1)} %param.11) | copy-start | bytes 9437188
  17.2 7.5 %collective-permute-start.7 = (bf16[32,4096]{1,0:T(8,128)(2,1)S(1)}, bf16[32,4096]{1,0:T(8,128)(2,1)S(1)}, u32[]{:S(2)}, u32[]{:S(2)}) collective-permute-start(bf16[32,4096]{1,0:T(8,128)(2,1)S(1)} %pack.4.rows), channel_id=1, source_target_pairs={{0,2},{1,3},{2,0},{3,1},{4,6},{5,7},{6,4},{7,5},{8,10},{9,11},{10,... | collective-permute-start | bytes 786440 | tf_op jit(solution)/shard_map/ppermute | solution.py:489
  22.7 6.5 %collective-permute-start.11 = (bf16[32,4096]{1,0:T(8,128)(2,1)S(1)}, bf16[32,4096]{1,0:T(8,128)(2,1)S(1)}, u32[]{:S(2)}, u32[]{:S(2)}) collective-permute-start(bf16[32,4096]{1,0:T(8,128)(2,1)S(1)} %pack.5.refs_1_), channel_id=1, source_target_pairs={{0,2},{1,3},{2,0},{3,1},{4,6},{5,7},{6,4},{7,5},{8,10},{9,11},{10,... | collective-permute-start | bytes 786440 | tf_op jit(solution)/shard_map/ppermute | solution.py:489
  24.7 4.6 %collective-permute-start.8 = (bf16[32,4096]{1,0:T(8,128)(2,1)S(1)}, bf16[32,4096]{1,0:T(8,128)(2,1)S(1)}, u32[]{:S(2)}, u32[]{:S(2)}) collective-permute-start(bf16[32,4096]{1,0:T(8,128)(2,1)S(1)} %pack.4.rows), channel_id=1, source_target_pairs={{0,1},{1,0},{2,3},{3,2},{4,5},{5,4},{6,7},{7,6},{8,9},{9,8},{10,11... | collective-permute-start | bytes 786440 | tf_op jit(solution)/shard_map/ppermute | solution.py:489
  24.7 4.6 %collective-permute-start.9 = (bf16[32,4096]{1,0:T(8,128)(2,1)S(1)}, bf16[32,4096]{1,0:T(8,128)(2,1)S(1)}, u32[]{:S(2)}, u32[]{:S(2)}) collective-permute-start(bf16[32,4096]{1,0:T(8,128)(2,1)S(1)} %collective-permute-done.7.refs_2_), channel_id=1, source_target_pairs={{0,1},{1,0},{2,3},{3,2},{4,5},{5,4},{6,7},{7,6},{8,9},{9,8},{10,11... | collective-permute-start | bytes 786440 | tf_op jit(solution)/shard_map/ppermute | solution.py:489
  25.2 4.0 %collective-permute-start.10 = (bf16[32,4096]{1,0:T(8,128)(2,1)S(1)}, bf16[32,4096]{1,0:T(8,128)(2,1)S(1)}, u32[]{:S(2)}, u32[]{:S(2)}) collective-permute-start(bf16[32,4096]{1,0:T(8,128)(2,1)S(1)} %pack.5.refs_1_), channel_id=1, source_target_pairs={{0,1},{1,0},{2,3},{3,2},{4,5},{5,4},{6,7},{7,6},{8,9},{9,8},{10,11... | collective-permute-start | bytes 786440 | tf_op jit(solution)/shard_map/ppermute | solution.py:489
  29.2 1.6 %collective-permute-start.12 = (bf16[32,4096]{1,0:T(8,128)(2,1)S(1)}, bf16[32,4096]{1,0:T(8,128)(2,1)S(1)}, u32[]{:S(2)}, u32[]{:S(2)}) collective-permute-start(bf16[32,4096]{1,0:T(8,128)(2,1)S(1)} %collective-permute-done.11.refs_3_), channel_id=1, source_target_pairs={{0,1},{1,0},{2,3},{3,2},{4,5},{5,4},{6,7},{7,6},{8,9},{9,8},{10,11... | collective-permute-start | bytes 786440 | tf_op jit(solution)/shard_map/ppermute | solution.py:489
  36.1 1.8 %collective-permute-start.13 = (bf16[128,1536]{1,0:T(8,128)(2,1)S(1)}, bf16[128,1536]{1,0:T(8,128)(2,1)S(1)}, u32[]{:S(2)}, u32[]{:S(2)}) collective-permute-start(bf16[128,1536]{1,0:T(8,128)(2,1)S(1)} %get-tuple-element.113), channel_id=1, source_target_pairs={{0,1},{1,0},{2,3},{3,2},{4,5},{5,4},{6,7},{7,6},{8,9},{9,8},{10,11... | collective-permute-start | bytes 1179656 | tf_op jit(solution)/shard_map/ppermute | solution.py:489
  37.0 1.5 %collective-permute-start.14 = (bf16[128,640]{1,0:T(8,128)(2,1)S(1)}, bf16[128,640]{1,0:T(8,128)(2,1)S(1)}, u32[]{:S(2)}, u32[]{:S(2)}) collective-permute-start(bf16[128,640]{1,0:T(8,128)(2,1)S(1)} %get-tuple-element.119), channel_id=1, source_target_pairs={{0,1},{1,0},{2,3},{3,2},{4,5},{5,4},{6,7},{7,6},{8,9},{9,8},{10,11... | collective-permute-start | bytes 491528 | tf_op jit(solution)/shard_map/ppermute | solution.py:489
  38.6 6.0 %collective-permute-start.16 = (bf16[32,2176]{1,0:T(8,128)(2,1)S(1)}, bf16[32,2176]{1,0:T(8,128)(2,1)S(1)}, u32[]{:S(2)}, u32[]{:S(2)}) collective-permute-start(bf16[32,2176]{1,0:T(8,128)(2,1)S(1)} %get-tuple-element.125), channel_id=1, source_target_pairs={{0,2},{1,3},{2,0},{3,1},{4,6},{5,7},{6,4},{7,5},{8,10},{9,11},{10,... | collective-permute-start | bytes 417800 | tf_op jit(solution)/shard_map/ppermute | solution.py:489
  40.1 17.0 %copy-start.5 = (bf16[32,8]{0,1:T(8,128)(2,1)S(1)}, bf16[32,8]{0,1:T(8,128)(2,1)}, u32[]{:S(2)}) copy-start(bf16[32,8]{0,1:T(8,128)(2,1)} %param.9) | copy-start | bytes 1540
  43.2 5.7 %collective-permute-start.15 = (bf16[32,2176]{1,0:T(8,128)(2,1)S(1)}, bf16[32,2176]{1,0:T(8,128)(2,1)S(1)}, u32[]{:S(2)}, u32[]{:S(2)}) collective-permute-start(bf16[32,2176]{1,0:T(8,128)(2,1)S(1)} %get-tuple-element.132), channel_id=1, source_target_pairs={{0,2},{1,3},{2,0},{3,1},{4,6},{5,7},{6,4},{7,5},{8,10},{9,11},{10,... | collective-permute-start | bytes 417800 | tf_op jit(solution)/shard_map/ppermute | solution.py:489
  44.6 5.0 %collective-permute-start.19 = (bf16[16,2176]{1,0:T(8,128)(2,1)S(1)}, bf16[16,2176]{1,0:T(8,128)(2,1)S(1)}, u32[]{:S(2)}, u32[]{:S(2)}) collective-permute-start(bf16[16,2176]{1,0:T(8,128)(2,1)S(1)} %get-tuple-element.137), channel_id=1, source_target_pairs={{0,4},{4,0},{8,12},{12,8},{16,20},{20,16},{24,28},{28,24},{1,5},{5... | collective-permute-start | bytes 208904 | tf_op jit(solution)/shard_map/ppermute | solution.py:489
  46.2 5.6 %collective-permute-start.17 = (bf16[16,2176]{1,0:T(8,128)(2,1)S(1)}, bf16[16,2176]{1,0:T(8,128)(2,1)S(1)}, u32[]{:S(2)}, u32[]{:S(2)}) collective-permute-start(bf16[16,2176]{1,0:T(8,128)(2,1)S(1)} %get-tuple-element.136), channel_id=1, source_target_pairs={{0,4},{4,0},{8,12},{12,8},{16,20},{20,16},{24,28},{28,24},{1,5},{5... | collective-permute-start | bytes 208904 | tf_op jit(solution)/shard_map/ppermute | solution.py:489
  49.6 6.9 %collective-permute-start.20 = (bf16[16,2176]{1,0:T(8,128)(2,1)S(1)}, bf16[16,2176]{1,0:T(8,128)(2,1)S(1)}, u32[]{:S(2)}, u32[]{:S(2)}) collective-permute-start(bf16[16,2176]{1,0:T(8,128)(2,1)S(1)} %get-tuple-element.146), channel_id=1, source_target_pairs={{0,16},{4,20},{8,24},{12,28},{16,0},{20,4},{24,8},{28,12},{1,17},{... | collective-permute-start | bytes 208904 | tf_op jit(solution)/shard_map/ppermute | solution.py:489
  50.1 6.4 %collective-permute-start.21 = (bf16[16,2176]{1,0:T(8,128)(2,1)S(1)}, bf16[16,2176]{1,0:T(8,128)(2,1)S(1)}, u32[]{:S(2)}, u32[]{:S(2)}) collective-permute-start(bf16[16,2176]{1,0:T(8,128)(2,1)S(1)} %get-tuple-element.147), channel_id=1, source_target_pairs={{0,24},{4,28},{8,16},{12,20},{16,8},{20,12},{24,0},{28,4},{1,25},{... | collective-permute-start | bytes 208904 | tf_op jit(solution)/shard_map/ppermute | solution.py:489
  51.8 5.4 %collective-permute-start.18 = (bf16[16,2176]{1,0:T(8,128)(2,1)S(1)}, bf16[16,2176]{1,0:T(8,128)(2,1)S(1)}, u32[]{:S(2)}, u32[]{:S(2)}) collective-permute-start(bf16[16,2176]{1,0:T(8,128)(2,1)S(1)} %get-tuple-element.143), channel_id=1, source_target_pairs={{0,8},{4,12},{8,0},{12,4},{16,24},{20,28},{24,16},{28,20},{1,9},{5... | collective-permute-start | bytes 208904 | tf_op jit(solution)/shard_map/ppermute | solution.py:489
  (4 other events, 25.3 us)

commit v18 on v15

--- a/solution.py
+++ b/solution.py
@@ -481,6 +481,7 @@
     order = [0]
     for i, k in enumerate(near):
         order += [k, far[i]]
+    order[1], order[2] = order[2], order[1]
     return order + far[len(near) :]
 
 

time: 58.3 us -> 58.4 us (level)
  transfers between devices with their start and end apart: 22 -> 22, of which waited for: 12 -> 11; matrix products, arithmetic and copies ran while one was open for 0% -> 0% of each run, Pallas kernels for 11% -> 11%
where the time goes in v18:
time: 58.4 us; the launch traced here: 58.2 us
  starting transfers between devices  25.8 us (44%)
  waiting for transfers between devices  16.8 us (29%)
  Pallas kernels  14.8 us (25%)
  between operations  0.81 us (1%)
    ppermute x22, starting transfers between devices, flip(): return lax.ppermute(value, axis, [(i, i ^ bit) for i in range(size)])  25.8 us
    ppermute x22, waiting for transfers between devices, flip(): return lax.ppermute(value, axis, [(i, i ^ bit) for i in range(size)])  16.8 us
    pallas_call x2, Pallas kernels, weight_grads(): pl.pallas_call(functools.partial(weight_kernel, chunk, count), out_shape=...  5.05 us
    pallas_call x1, Pallas kernels, backward(): pl.pallas_call(functools.partial(backward_kernel, count), out_shape=[stru...  3.3 us
    pallas_call x1, Pallas kernels, dispatch(): pl.pallas_call(functools.partial(dispatch_kernel, n_targets), out_shape=[...  2.28 us
    pallas_call x1, Pallas kernels, forward(): pl.pallas_call(functools.partial(forward_kernel, count), out_shape=[struc...  1.95 us
  transfers between devices with their start and end apart: 22, of which 11 were waited for; matrix products, arithmetic and copies ran while one was open for 0% of the time, Pallas kernels for 11%

profile of v18, /device:TPU:0, one launch (start us, length us, event | category | flops | bytes accessed | tf_op | source)
XLA Modules:
  0.0 58.2 jit_solution(15763851116269545018)
XLA Ops:
  0.6 2.3 %dispatch.1 = (bf16[8,4096]{1,0:T(8,128)(2,1)}, bf16[8,4096]{1,0:T(8,128)(2,1)}, bf16[8,4096]{1,0:T(8,128)(2,1)}, bf16[8,4096]{1,0:T(8,128)(2,1)}, bf16[8,4096]{...) custom-call(s32[8,32]{1,0:T(8,128)} %bitcast.16, ...), custom_call_target="tpu_custom_call" | custom-call | tf_op jit(solution)/shard_map/dispatch/pallas_call | solution.py:91
  2.9 4.1 %collective-permute-start = (bf16[8,4096]{1,0:T(8,128)(2,1)}, bf16[8,4096]{1,0:T(8,128)(2,1)S(1)}, u32[]{:S(2)}, u32[]{:S(2)}) collective-permute-start(bf16[8,4096]{1,0:T(8,128)(2,1)} %get-tuple-element.80), channel_id=1, source_target_pairs={{0,16},{4,20},{8,24},{12,28},{16,0},{20,4},{24,8},{28,12},{1,17},{... | collective-permute-start | bytes 196616 | tf_op jit(solution)/shard_map/ppermute | solution.py:476
  7.0 1.5 %collective-permute-start.1 = (bf16[8,4096]{1,0:T(8,128)(2,1)}, bf16[8,4096]{1,0:T(8,128)(2,1)S(1)}, u32[]{:S(2)}, u32[]{:S(2)}) collective-permute-start(bf16[8,4096]{1,0:T(8,128)(2,1)} %get-tuple-element.81), channel_id=1, source_target_pairs={{0,4},{4,0},{8,12},{12,8},{16,20},{20,16},{24,28},{28,24},{1,5},{5... | collective-permute-start | bytes 196616 | tf_op jit(solution)/shard_map/ppermute | solution.py:476
  8.5 1.6 %collective-permute-start.2 = (bf16[8,4096]{1,0:T(8,128)(2,1)}, bf16[8,4096]{1,0:T(8,128)(2,1)S(1)}, u32[]{:S(2)}, u32[]{:S(2)}) collective-permute-start(bf16[8,4096]{1,0:T(8,128)(2,1)} %get-tuple-element.82), channel_id=1, source_target_pairs={{0,8},{4,12},{8,0},{12,4},{16,24},{20,28},{24,16},{28,20},{1,9},{5... | collective-permute-start | bytes 196616 | tf_op jit(solution)/shard_map/ppermute | solution.py:476
  10.4 1.4 %collective-permute-start.4 = (bf16[8,4096]{1,0:T(8,128)(2,1)}, bf16[8,4096]{1,0:T(8,128)(2,1)S(1)}, u32[]{:S(2)}, u32[]{:S(2)}) collective-permute-start(bf16[8,4096]{1,0:T(8,128)(2,1)} %get-tuple-element.86), channel_id=1, source_target_pairs={{0,12},{4,8},{8,4},{12,0},{16,28},{20,24},{24,20},{28,16},{1,13},{... | collective-permute-start | bytes 196616 | tf_op jit(solution)/shard_map/ppermute | solution.py:476
  11.8 3.6 %collective-permute-start.5 = (bf16[8,4096]{1,0:T(8,128)(2,1)}, bf16[8,4096]{1,0:T(8,128)(2,1)S(1)}, u32[]{:S(2)}, u32[]{:S(2)}) collective-permute-start(bf16[8,4096]{1,0:T(8,128)(2,1)} %get-tuple-element.87), channel_id=1, source_target_pairs={{0,24},{4,28},{8,16},{12,20},{16,8},{20,12},{24,0},{28,4},{1,25},{... | collective-permute-start | bytes 196616 | tf_op jit(solution)/shard_map/ppermute | solution.py:476
  15.4 1.1 %collective-permute-start.6 = (bf16[8,4096]{1,0:T(8,128)(2,1)}, bf16[8,4096]{1,0:T(8,128)(2,1)S(1)}, u32[]{:S(2)}, u32[]{:S(2)}) collective-permute-start(bf16[8,4096]{1,0:T(8,128)(2,1)} %get-tuple-element.88), channel_id=1, source_target_pairs={{0,28},{4,24},{8,20},{12,16},{16,12},{20,8},{24,4},{28,0},{1,29},{... | collective-permute-start | bytes 196616 | tf_op jit(solution)/shard_map/ppermute | solution.py:476
  16.6 1.6 %collective-permute-start.7 = (bf16[32,4096]{1,0:T(8,128)(2,1)S(1)}, bf16[32,4096]{1,0:T(8,128)(2,1)S(1)}, u32[]{:S(2)}, u32[]{:S(2)}) collective-permute-start(bf16[32,4096]{1,0:T(8,128)(2,1)S(1)} %pack.4.rows), channel_id=1, source_target_pairs={{0,2},{1,3},{2,0},{3,1},{4,6},{5,7},{6,4},{7,5},{8,10},{9,11},{10,... | collective-permute-start | bytes 786440 | tf_op jit(solution)/shard_map/ppermute | solution.py:476
  18.2 1.7 %collective-permute-done.3.refs_0_ = bf16[8,4096]{1,0:T(8,128)(2,1)S(1)} collective-permute-done((bf16[8,4096]{1,0:T(8,128)(2,1)}, bf16[8,4096]{1,0:T(8,128)(2,1)S(1)}, u32[]{:S(2)}, u32[]{:S(2)}) %collective-permute-start.3) | collective-permute-done | bytes 65568 | tf_op jit(solution)/shard_map/ppermute | solution.py:476
  19.9 2.7 %collective-permute-done.6.refs_3_ = bf16[8,4096]{1,0:T(8,128)(2,1)S(1)} collective-permute-done((bf16[8,4096]{1,0:T(8,128)(2,1)}, bf16[8,4096]{1,0:T(8,128)(2,1)S(1)}, u32[]{:S(2)}, u32[]{:S(2)}) %collective-permute-start.6) | collective-permute-done | bytes 65568 | tf_op jit(solution)/shard_map/ppermute | solution.py:476
  22.6 1.6 %collective-permute-start.11 = (bf16[32,4096]{1,0:T(8,128)(2,1)S(1)}, bf16[32,4096]{1,0:T(8,128)(2,1)S(1)}, u32[]{:S(2)}, u32[]{:S(2)}) collective-permute-start(bf16[32,4096]{1,0:T(8,128)(2,1)S(1)} %pack.5.refs_1_), channel_id=1, source_target_pairs={{0,2},{1,3},{2,0},{3,1},{4,6},{5,7},{6,4},{7,5},{8,10},{9,11},{10,... | collective-permute-start | bytes 786440 | tf_op jit(solution)/shard_map/ppermute | solution.py:476
  24.9 4.2 %collective-permute-done.11.refs_3_ = bf16[32,4096]{1,0:T(8,128)(2,1)S(1)} collective-permute-done((bf16[32,4096]{1,0:T(8,128)(2,1)S(1)}, bf16[32,4096]{1,0:T(8,128)(2,1)S(1)}, u32[]{:S(2)}, u32[]{:S(2)}) %collective-permute-start.11) | collective-permute-done | bytes 262176 | tf_op jit(solution)/shard_map/ppermute | solution.py:476
  29.2 1.5 %collective-permute-done.12.refs_7_ = bf16[32,4096]{1,0:T(8,128)(2,1)S(1)} collective-permute-done((bf16[32,4096]{1,0:T(8,128)(2,1)S(1)}, bf16[32,4096]{1,0:T(8,128)(2,1)S(1)}, u32[]{:S(2)}, u32[]{:S(2)}) %collective-permute-start.12) | collective-permute-done | bytes 262176 | tf_op jit(solution)/shard_map/ppermute | solution.py:476
  30.7 2.0 %forward.1 = (bf16[256,2048]{1,0:T(8,128)(2,1)S(1)}, f32[384,256]{1,0:T(8,128)S(1)}, f32[384,256]{1,0:T(8,128)S(1)}, bf16[384,256]{1,0:T(8,128)(2,1)S(1)}) custom-call(bf16[32,2048]{1,0:T(8,128)(2,1)S(1)} %get-tuple-element.108.refs_0_, bf16[32,4096]{1,0:T(8,128)(2,1)S(1)} %pack.5.refs_1_, bf16[32,4096]{1,0:T(8,128)(2,1)S(1)} %collective-permute-done.7.refs_2_, ...), custom_call_target="tpu_custom_call" | custom-call | flops 1000000 | bytes 10000 | tf_op jit(solution)/shard_map/forward/pallas_call | solution.py:207
  32.7 3.3 %backward.1 = (bf16[128,1536]{1,0:T(8,128)(2,1)S(1)}, bf16[128,1536]{1,0:T(8,128)(2,1)S(1)}, bf16[256,2048]{1,0:T(8,128)(2,1)S(1)}, bf16[384,256]{1,0:T(8,128)(2...) custom-call(bf16[32,2048]{1,0:T(8,128)(2,1)S(1)} %get-tuple-element.103.refs_0_, ...), custom_call_target="tpu_custom_call" | custom-call | flops 1000000 | bytes 10000 | tf_op jit(solution)/shard_map/backward/pallas_call | solution.py:288
  38.4 1.6 %collective-permute-start.16 = (bf16[32,2176]{1,0:T(8,128)(2,1)S(1)}, bf16[32,2176]{1,0:T(8,128)(2,1)S(1)}, u32[]{:S(2)}, u32[]{:S(2)}) collective-permute-start(bf16[32,2176]{1,0:T(8,128)(2,1)S(1)} %get-tuple-element.125), channel_id=1, source_target_pairs={{0,2},{1,3},{2,0},{3,1},{4,6},{5,7},{6,4},{7,5},{8,10},{9,11},{10,... | collective-permute-start | bytes 417800 | tf_op jit(solution)/shard_map/ppermute | solution.py:476
  40.0 3.1 %weight_grads.2 = (bf16[384,4096]{1,0:T(8,128)(2,1)}, bf16[384,4096]{1,0:T(8,128)(2,1)}) custom-call(bf16[384,256]{1,0:T(8,128)(2,1)S(1)} %get-tuple-element.126.refs_0_, bf16[384,256]{1,0:T(8,128)(2,1)S(1)} %get-tuple-element.127.refs_1_, bf16[256,2048]{1,0:T(8,128)(2,1)S(1)} %get-tuple-element.128.refs_2_), custom_call_target="tpu_custom_call" | custom-call | flops 1000000 | bytes 10000 | tf_op jit(solution)/shard_map/weight_grads/pallas_call | solution.py:423
  43.7 0.8 %collective-permute-done.16.right = bf16[32,2176]{1,0:T(8,128)(2,1)S(1)} collective-permute-done((bf16[32,2176]{1,0:T(8,128)(2,1)S(1)}, bf16[32,2176]{1,0:T(8,128)(2,1)S(1)}, u32[]{:S(2)}, u32[]{:S(2)}) %collective-permute-start.16) | collective-permute-done | bytes 139296 | tf_op jit(solution)/shard_map/ppermute | solution.py:476
  44.5 1.7 %collective-permute-start.19 = (bf16[16,2176]{1,0:T(8,128)(2,1)S(1)}, bf16[16,2176]{1,0:T(8,128)(2,1)S(1)}, u32[]{:S(2)}, u32[]{:S(2)}) collective-permute-start(bf16[16,2176]{1,0:T(8,128)(2,1)S(1)} %get-tuple-element.137), channel_id=1, source_target_pairs={{0,4},{4,0},{8,12},{12,8},{16,20},{20,16},{24,28},{28,24},{1,5},{5... | collective-permute-start | bytes 208904 | tf_op jit(solution)/shard_map/ppermute | solution.py:476
  46.6 2.0 %weight_grads.3 = bf16[384,4096]{1,0:T(8,128)(2,1)} custom-call(bf16[384,256]{1,0:T(8,128)(2,1)S(1)} %get-tuple-element.138.refs_10_.refs_0_, bf16[256,2048]{1,0:T(8,128)(2,1)S(1)} %get-tuple-element.139.refs_1_), custom_call_target="tpu_custom_call" | custom-call | flops 1000000 | bytes 10000 | tf_op jit(solution)/shard_map/weight_grads/pallas_call | solution.py:423
  49.6 2.6 %collective-permute-start.21 = (bf16[16,2176]{1,0:T(8,128)(2,1)S(1)}, bf16[16,2176]{1,0:T(8,128)(2,1)S(1)}, u32[]{:S(2)}, u32[]{:S(2)}) collective-permute-start(bf16[16,2176]{1,0:T(8,128)(2,1)S(1)} %get-tuple-element.147), channel_id=1, source_target_pairs={{0,24},{4,28},{8,16},{12,20},{16,8},{20,12},{24,0},{28,4},{1,25},{... | collective-permute-start | bytes 208904 | tf_op jit(solution)/shard_map/ppermute | solution.py:476
  52.2 0.9 %collective-permute-start.18 = (bf16[16,2176]{1,0:T(8,128)(2,1)S(1)}, bf16[16,2176]{1,0:T(8,128)(2,1)S(1)}, u32[]{:S(2)}, u32[]{:S(2)}) collective-permute-start(bf16[16,2176]{1,0:T(8,128)(2,1)S(1)} %get-tuple-element.143), channel_id=1, source_target_pairs={{0,8},{4,12},{8,0},{12,4},{16,24},{20,28},{24,16},{28,20},{1,9},{5... | collective-permute-start | bytes 208904 | tf_op jit(solution)/shard_map/ppermute | solution.py:476
  53.2 3.6 %collective-permute-done.20.refs_2_ = bf16[16,2176]{1,0:T(8,128)(2,1)S(1)} collective-permute-done((bf16[16,2176]{1,0:T(8,128)(2,1)S(1)}, bf16[16,2176]{1,0:T(8,128)(2,1)S(1)}, u32[]{:S(2)}, u32[]{:S(2)}) %collective-permute-start.20) | collective-permute-done | bytes 69664 | tf_op jit(solution)/shard_map/ppermute | solution.py:476
  57.2 1.0 %combine.1 = (bf16[32,4096]{1,0:T(8,128)(2,1)}, f32[8,32]{1,0:T(8,128)}) custom-call(bf16[64,32]{1,0:T(8,128)(2,1)S(1)} %get-tuple-element.100.first, bf16[64,32]{1,0:T(8,128)(2,1)S(1)} %get-tuple-element.101.second, s32[64,32]{1,0:T(8,128)S(1)} %get-tuple-element.102.choice_ref, bf16[8,32]{1,0:T(8,128)(2,1)S(1)} %bitcast.19, ...), custom_call_target="tpu_custom_call" | custom-call | tf_op jit(solution)/shard_map/combine/pallas_call | solution.py:462
  (49 shorter events, 6.2 us)
Async XLA Ops:
  2.9 8.9 %collective-permute-start = (bf16[8,4096]{1,0:T(8,128)(2,1)}, bf16[8,4096]{1,0:T(8,128)(2,1)S(1)}, u32[]{:S(2)}, u32[]{:S(2)}) collective-permute-start(bf16[8,4096]{1,0:T(8,128)(2,1)} %get-tuple-element.80), channel_id=1, source_target_pairs={{0,16},{4,20},{8,24},{12,28},{16,0},{20,4},{24,8},{28,12},{1,17},{... | collective-permute-start | bytes 196616 | tf_op jit(solution)/shard_map/ppermute | solution.py:476
  7.0 8.4 %collective-permute-start.1 = (bf16[8,4096]{1,0:T(8,128)(2,1)}, bf16[8,4096]{1,0:T(8,128)(2,1)S(1)}, u32[]{:S(2)}, u32[]{:S(2)}) collective-permute-start(bf16[8,4096]{1,0:T(8,128)(2,1)} %get-tuple-element.81), channel_id=1, source_target_pairs={{0,4},{4,0},{8,12},{12,8},{16,20},{20,16},{24,28},{28,24},{1,5},{5... | collective-permute-start | bytes 196616 | tf_op jit(solution)/shard_map/ppermute | solution.py:476
  8.5 8.0 %collective-permute-start.2 = (bf16[8,4096]{1,0:T(8,128)(2,1)}, bf16[8,4096]{1,0:T(8,128)(2,1)S(1)}, u32[]{:S(2)}, u32[]{:S(2)}) collective-permute-start(bf16[8,4096]{1,0:T(8,128)(2,1)} %get-tuple-element.82), channel_id=1, source_target_pairs={{0,8},{4,12},{8,0},{12,4},{16,24},{20,28},{24,16},{28,20},{1,9},{5... | collective-permute-start | bytes 196616 | tf_op jit(solution)/shard_map/ppermute | solution.py:476
  10.1 9.8 %collective-permute-start.3 = (bf16[8,4096]{1,0:T(8,128)(2,1)}, bf16[8,4096]{1,0:T(8,128)(2,1)S(1)}, u32[]{:S(2)}, u32[]{:S(2)}) collective-permute-start(bf16[8,4096]{1,0:T(8,128)(2,1)} %get-tuple-element.85), channel_id=1, source_target_pairs={{0,20},{4,16},{8,28},{12,24},{16,4},{20,0},{24,12},{28,8},{1,21},{... | collective-permute-start | bytes 196616 | tf_op jit(solution)/shard_map/ppermute | solution.py:476
  10.4 9.5 %collective-permute-start.4 = (bf16[8,4096]{1,0:T(8,128)(2,1)}, bf16[8,4096]{1,0:T(8,128)(2,1)S(1)}, u32[]{:S(2)}, u32[]{:S(2)}) collective-permute-start(bf16[8,4096]{1,0:T(8,128)(2,1)} %get-tuple-element.86), channel_id=1, source_target_pairs={{0,12},{4,8},{8,4},{12,0},{16,28},{20,24},{24,20},{28,16},{1,13},{... | collective-permute-start | bytes 196616 | tf_op jit(solution)/shard_map/ppermute | solution.py:476
  11.8 8.1 %collective-permute-start.5 = (bf16[8,4096]{1,0:T(8,128)(2,1)}, bf16[8,4096]{1,0:T(8,128)(2,1)S(1)}, u32[]{:S(2)}, u32[]{:S(2)}) collective-permute-start(bf16[8,4096]{1,0:T(8,128)(2,1)} %get-tuple-element.87), channel_id=1, source_target_pairs={{0,24},{4,28},{8,16},{12,20},{16,8},{20,12},{24,0},{28,4},{1,25},{... | collective-permute-start | bytes 196616 | tf_op jit(solution)/shard_map/ppermute | solution.py:476
  15.4 7.2 %collective-permute-start.6 = (bf16[8,4096]{1,0:T(8,128)(2,1)}, bf16[8,4096]{1,0:T(8,128)(2,1)S(1)}, u32[]{:S(2)}, u32[]{:S(2)}) collective-permute-start(bf16[8,4096]{1,0:T(8,128)(2,1)} %get-tuple-element.88), channel_id=1, source_target_pairs={{0,28},{4,24},{8,20},{12,16},{16,12},{20,8},{24,4},{28,0},{1,29},{... | collective-permute-start | bytes 196616 | tf_op jit(solution)/shard_map/ppermute | solution.py:476
  16.6 14.1 %copy-start = (bf16[1,384,4096]{2,1,0:T(8,128)(2,1)S(1)}, bf16[1,384,4096]{2,1,0:T(8,128)(2,1)}, u32[]{:S(2)}) copy-start(bf16[1,384,4096]{2,1,0:T(8,128)(2,1)} %param.11) | copy-start | bytes 9437188
  16.6 7.5 %collective-permute-start.7 = (bf16[32,4096]{1,0:T(8,128)(2,1)S(1)}, bf16[32,4096]{1,0:T(8,128)(2,1)S(1)}, u32[]{:S(2)}, u32[]{:S(2)}) collective-permute-start(bf16[32,4096]{1,0:T(8,128)(2,1)S(1)} %pack.4.rows), channel_id=1, source_target_pairs={{0,2},{1,3},{2,0},{3,1},{4,6},{5,7},{6,4},{7,5},{8,10},{9,11},{10,... | collective-permute-start | bytes 786440 | tf_op jit(solution)/shard_map/ppermute | solution.py:476
  22.6 6.4 %collective-permute-start.11 = (bf16[32,4096]{1,0:T(8,128)(2,1)S(1)}, bf16[32,4096]{1,0:T(8,128)(2,1)S(1)}, u32[]{:S(2)}, u32[]{:S(2)}) collective-permute-start(bf16[32,4096]{1,0:T(8,128)(2,1)S(1)} %pack.5.refs_1_), channel_id=1, source_target_pairs={{0,2},{1,3},{2,0},{3,1},{4,6},{5,7},{6,4},{7,5},{8,10},{9,11},{10,... | collective-permute-start | bytes 786440 | tf_op jit(solution)/shard_map/ppermute | solution.py:476
  24.2 4.9 %collective-permute-start.8 = (bf16[32,4096]{1,0:T(8,128)(2,1)S(1)}, bf16[32,4096]{1,0:T(8,128)(2,1)S(1)}, u32[]{:S(2)}, u32[]{:S(2)}) collective-permute-start(bf16[32,4096]{1,0:T(8,128)(2,1)S(1)} %pack.4.rows), channel_id=1, source_target_pairs={{0,1},{1,0},{2,3},{3,2},{4,5},{5,4},{6,7},{7,6},{8,9},{9,8},{10,11... | collective-permute-start | bytes 786440 | tf_op jit(solution)/shard_map/ppermute | solution.py:476
  24.2 4.9 %collective-permute-start.9 = (bf16[32,4096]{1,0:T(8,128)(2,1)S(1)}, bf16[32,4096]{1,0:T(8,128)(2,1)S(1)}, u32[]{:S(2)}, u32[]{:S(2)}) collective-permute-start(bf16[32,4096]{1,0:T(8,128)(2,1)S(1)} %collective-permute-done.7.refs_2_), channel_id=1, source_target_pairs={{0,1},{1,0},{2,3},{3,2},{4,5},{5,4},{6,7},{7,6},{8,9},{9,8},{10,11... | collective-permute-start | bytes 786440 | tf_op jit(solution)/shard_map/ppermute | solution.py:476
  24.7 4.4 %collective-permute-start.10 = (bf16[32,4096]{1,0:T(8,128)(2,1)S(1)}, bf16[32,4096]{1,0:T(8,128)(2,1)S(1)}, u32[]{:S(2)}, u32[]{:S(2)}) collective-permute-start(bf16[32,4096]{1,0:T(8,128)(2,1)S(1)} %pack.5.refs_1_), channel_id=1, source_target_pairs={{0,1},{1,0},{2,3},{3,2},{4,5},{5,4},{6,7},{7,6},{8,9},{9,8},{10,11... | collective-permute-start | bytes 786440 | tf_op jit(solution)/shard_map/ppermute | solution.py:476
  29.1 1.6 %collective-permute-start.12 = (bf16[32,4096]{1,0:T(8,128)(2,1)S(1)}, bf16[32,4096]{1,0:T(8,128)(2,1)S(1)}, u32[]{:S(2)}, u32[]{:S(2)}) collective-permute-start(bf16[32,4096]{1,0:T(8,128)(2,1)S(1)} %collective-permute-done.11.refs_3_), channel_id=1, source_target_pairs={{0,1},{1,0},{2,3},{3,2},{4,5},{5,4},{6,7},{7,6},{8,9},{9,8},{10,11... | collective-permute-start | bytes 786440 | tf_op jit(solution)/shard_map/ppermute | solution.py:476
  36.0 1.8 %collective-permute-start.13 = (bf16[128,1536]{1,0:T(8,128)(2,1)S(1)}, bf16[128,1536]{1,0:T(8,128)(2,1)S(1)}, u32[]{:S(2)}, u32[]{:S(2)}) collective-permute-start(bf16[128,1536]{1,0:T(8,128)(2,1)S(1)} %get-tuple-element.113), channel_id=1, source_target_pairs={{0,1},{1,0},{2,3},{3,2},{4,5},{5,4},{6,7},{7,6},{8,9},{9,8},{10,11... | collective-permute-start | bytes 1179656 | tf_op jit(solution)/shard_map/ppermute | solution.py:476
  36.8 1.5 %collective-permute-start.14 = (bf16[128,640]{1,0:T(8,128)(2,1)S(1)}, bf16[128,640]{1,0:T(8,128)(2,1)S(1)}, u32[]{:S(2)}, u32[]{:S(2)}) collective-permute-start(bf16[128,640]{1,0:T(8,128)(2,1)S(1)} %get-tuple-element.119), channel_id=1, source_target_pairs={{0,1},{1,0},{2,3},{3,2},{4,5},{5,4},{6,7},{7,6},{8,9},{9,8},{10,11... | collective-permute-start | bytes 491528 | tf_op jit(solution)/shard_map/ppermute | solution.py:476
  38.4 6.0 %collective-permute-start.16 = (bf16[32,2176]{1,0:T(8,128)(2,1)S(1)}, bf16[32,2176]{1,0:T(8,128)(2,1)S(1)}, u32[]{:S(2)}, u32[]{:S(2)}) collective-permute-start(bf16[32,2176]{1,0:T(8,128)(2,1)S(1)} %get-tuple-element.125), channel_id=1, source_target_pairs={{0,2},{1,3},{2,0},{3,1},{4,6},{5,7},{6,4},{7,5},{8,10},{9,11},{10,... | collective-permute-start | bytes 417800 | tf_op jit(solution)/shard_map/ppermute | solution.py:476
  40.0 17.2 %copy-start.5 = (bf16[32,8]{0,1:T(8,128)(2,1)S(1)}, bf16[32,8]{0,1:T(8,128)(2,1)}, u32[]{:S(2)}) copy-start(bf16[32,8]{0,1:T(8,128)(2,1)} %param.9) | copy-start | bytes 1540
  43.1 5.7 %collective-permute-start.15 = (bf16[32,2176]{1,0:T(8,128)(2,1)S(1)}, bf16[32,2176]{1,0:T(8,128)(2,1)S(1)}, u32[]{:S(2)}, u32[]{:S(2)}) collective-permute-start(bf16[32,2176]{1,0:T(8,128)(2,1)S(1)} %get-tuple-element.132), channel_id=1, source_target_pairs={{0,2},{1,3},{2,0},{3,1},{4,6},{5,7},{6,4},{7,5},{8,10},{9,11},{10,... | collective-permute-start | bytes 417800 | tf_op jit(solution)/shard_map/ppermute | solution.py:476
  44.5 5.0 %collective-permute-start.19 = (bf16[16,2176]{1,0:T(8,128)(2,1)S(1)}, bf16[16,2176]{1,0:T(8,128)(2,1)S(1)}, u32[]{:S(2)}, u32[]{:S(2)}) collective-permute-start(bf16[16,2176]{1,0:T(8,128)(2,1)S(1)} %get-tuple-element.137), channel_id=1, source_target_pairs={{0,4},{4,0},{8,12},{12,8},{16,20},{20,16},{24,28},{28,24},{1,5},{5... | collective-permute-start | bytes 208904 | tf_op jit(solution)/shard_map/ppermute | solution.py:476
  46.1 6.1 %collective-permute-start.17 = (bf16[16,2176]{1,0:T(8,128)(2,1)S(1)}, bf16[16,2176]{1,0:T(8,128)(2,1)S(1)}, u32[]{:S(2)}, u32[]{:S(2)}) collective-permute-start(bf16[16,2176]{1,0:T(8,128)(2,1)S(1)} %get-tuple-element.136), channel_id=1, source_target_pairs={{0,4},{4,0},{8,12},{12,8},{16,20},{20,16},{24,28},{28,24},{1,5},{5... | collective-permute-start | bytes 208904 | tf_op jit(solution)/shard_map/ppermute | solution.py:476
  49.5 7.2 %collective-permute-start.20 = (bf16[16,2176]{1,0:T(8,128)(2,1)S(1)}, bf16[16,2176]{1,0:T(8,128)(2,1)S(1)}, u32[]{:S(2)}, u32[]{:S(2)}) collective-permute-start(bf16[16,2176]{1,0:T(8,128)(2,1)S(1)} %get-tuple-element.146), channel_id=1, source_target_pairs={{0,16},{4,20},{8,24},{12,28},{16,0},{20,4},{24,8},{28,12},{1,17},{... | collective-permute-start | bytes 208904 | tf_op jit(solution)/shard_map/ppermute | solution.py:476
  49.6 7.2 %collective-permute-start.21 = (bf16[16,2176]{1,0:T(8,128)(2,1)S(1)}, bf16[16,2176]{1,0:T(8,128)(2,1)S(1)}, u32[]{:S(2)}, u32[]{:S(2)}) collective-permute-start(bf16[16,2176]{1,0:T(8,128)(2,1)S(1)} %get-tuple-element.147), channel_id=1, source_target_pairs={{0,24},{4,28},{8,16},{12,20},{16,8},{20,12},{24,0},{28,4},{1,25},{... | collective-permute-start | bytes 208904 | tf_op jit(solution)/shard_map/ppermute | solution.py:476
  52.2 5.0 %collective-permute-start.18 = (bf16[16,2176]{1,0:T(8,128)(2,1)S(1)}, bf16[16,2176]{1,0:T(8,128)(2,1)S(1)}, u32[]{:S(2)}, u32[]{:S(2)}) collective-permute-start(bf16[16,2176]{1,0:T(8,128)(2,1)S(1)} %get-tuple-element.143), channel_id=1, source_target_pairs={{0,8},{4,12},{8,0},{12,4},{16,24},{20,28},{24,16},{28,20},{1,9},{5... | collective-permute-start | bytes 208904 | tf_op jit(solution)/shard_map/ppermute | solution.py:476
  (4 other events, 25.3 us)
